TPU v7x, 32 devices: a whole 2x2x4 slice. The times are simulated.
32 devices in a mesh: seq: 8 (over z, y), head: 4 (over x, core).
Axes of the slice: x: 2, y: 2, z: 4, core: 2. Of those that a mesh axis runs over, the one named last changes fastest.
Arguments:
- queries: bfloat16 [4096, 2048], P(('seq', 'head')), may hold values from -27 to 27
- key_vectors: bfloat16 [4096, 2048], P(('seq', 'head')), may hold values from -6 to 6
- value_vectors: bfloat16 [4096, 2048], P(('seq', 'head')), may hold values from -6 to 6
- grad_output: bfloat16 [4096, 2048], P(('seq', 'head')), may hold values from -6 to 6
Outputs:
- grad_queries: bfloat16 [4096, 2048], P(('seq', 'head'))
- grad_keys: bfloat16 [4096, 2048], P(('seq', 'head'))
- grad_values: bfloat16 [4096, 2048], P(('seq', 'head'))
All inputs are finite; a program needn't handle non-finite values.
Results may differ from a plain program's by a relative error of at most 0.009.
Values may be sent and summed in bfloat16 or wider, within the bound.
No kernel may reach another device: no remote copies, remote signals or barrier semaphores. Data moves between devices by JAX's collectives and lax.ppermute only.
A program may use at most 64 MiB of HBM per device.

v0:
```python
import jax
import jax.numpy as jnp
from jax import lax
from jax.sharding import PartitionSpec as P

HEADS = 16
HEAD_DIM = 128
WINDOW = 512


def from_behind(block, axis, distance):
    devices = range(lax.axis_size(axis))
    route = [(i - distance, i) for i in devices if i - distance in devices]
    return lax.ppermute(block, axis, route)


def scores_of(query_rows, key_rows, allowed):
    factor = HEAD_DIM ** (-0.5)
    scores = (
        jnp.einsum("rhe,che->hrc", query_rows, key_rows, preferred_element_type=jnp.float32)
        * factor
    )
    return jnp.where(allowed[None], scores, -1e30)


def stats_of(scores, value_rows, grad_rows):
    row_max = jnp.max(scores, axis=-1)
    log_total = row_max + jnp.log(jnp.sum(jnp.exp(scores - row_max[..., None]), axis=-1))
    probs_low = jnp.exp(scores - log_total[..., None]).astype(jnp.bfloat16)
    attn_out = jnp.einsum("hrc,che->hre", probs_low, value_rows, preferred_element_type=jnp.float32)
    row_dots = jnp.sum(jnp.transpose(grad_rows, (1, 0, 2)).astype(jnp.float32) * attn_out, axis=-1)
    return (log_total, row_dots)


def grads_of(scores, log_total, row_dots, query_rows, key_rows, value_rows, grad_rows):
    factor = HEAD_DIM ** (-0.5)
    attn_probs = jnp.exp(scores - log_total[..., None])
    probs_low = attn_probs.astype(jnp.bfloat16)
    grad_probs = jnp.einsum(
        "rhe,che->hrc", grad_rows, value_rows, preferred_element_type=jnp.float32
    )
    grad_scores = (attn_probs * (grad_probs - row_dots[..., None])).astype(jnp.bfloat16)
    grad_query = (
        jnp.einsum("hrc,che->rhe", grad_scores, key_rows, preferred_element_type=jnp.float32)
        * factor
    )
    grad_key = (
        jnp.einsum("hrc,rhe->che", grad_scores, query_rows, preferred_element_type=jnp.float32)
        * factor
    )
    grad_value = jnp.einsum(
        "hrc,rhe->che", probs_low, grad_rows, preferred_element_type=jnp.float32
    )
    return (grad_query, grad_key, grad_value)


def regrouped(queries, key_vectors, value_vectors, grad_output):
    head_group = HEADS // lax.axis_size("head")
    query_block, key_block, value_block, grad_block = (
        lax.all_to_all(queries, "head", split_axis=1, concat_axis=0, tiled=True),
        lax.all_to_all(key_vectors, "head", split_axis=1, concat_axis=0, tiled=True),
        lax.all_to_all(value_vectors, "head", split_axis=1, concat_axis=0, tiled=True),
        lax.all_to_all(grad_output, "head", split_axis=1, concat_axis=0, tiled=True),
    )
    block_rows = query_block.shape[0]
    shape = (block_rows, head_group, HEAD_DIM)
    query_block = query_block.reshape(shape)
    key_block = key_block.reshape(shape)
    value_block = value_block.reshape(shape)
    grad_block = grad_block.reshape(shape)
    blocks = block_rows // WINDOW
    key_tail = key_block[block_rows - WINDOW :]
    value_tail = value_block[block_rows - WINDOW :]
    key_halo, value_halo = from_behind((key_tail, value_tail), "seq", 1)
    key_ext = jnp.concatenate([key_halo, key_block], axis=0)
    value_ext = jnp.concatenate([value_halo, value_block], axis=0)
    first_shard = lax.axis_index("seq") == 0
    row_ids = jnp.arange(WINDOW, dtype=jnp.int32)[:, None]
    col_ids = jnp.arange(2 * WINDOW, dtype=jnp.int32)[None, :]
    band = (col_ids > row_ids) & (col_ids <= row_ids + WINDOW)

    def one_block(block_index):
        start = block_index * WINDOW
        query_rows = lax.dynamic_slice_in_dim(query_block, start, WINDOW, 0)
        grad_rows = lax.dynamic_slice_in_dim(grad_block, start, WINDOW, 0)
        key_rows = lax.dynamic_slice_in_dim(key_ext, start, 2 * WINDOW, 0)
        value_rows = lax.dynamic_slice_in_dim(value_ext, start, 2 * WINDOW, 0)
        allowed = band & ((col_ids >= WINDOW) | (block_index > 0) | jnp.logical_not(first_shard))
        scores = scores_of(query_rows, key_rows, allowed)
        log_total, row_dots = stats_of(scores, value_rows, grad_rows)
        grad_query, grad_key, grad_value = grads_of(
            scores, log_total, row_dots, query_rows, key_rows, value_rows, grad_rows
        )
        return (
            grad_query.astype(jnp.bfloat16),
            grad_key[:WINDOW],
            grad_key[WINDOW:],
            grad_value[:WINDOW],
            grad_value[WINDOW:],
            log_total,
            row_dots,
        )

    grad_query, key_front, key_back, value_front, value_back, log_total, row_dots = lax.map(
        one_block, jnp.arange(blocks, dtype=jnp.int32)
    )
    grad_key = key_back + jnp.concatenate([key_front[1:], jnp.zeros_like(key_front[:1])], axis=0)
    grad_value = value_back + jnp.concatenate(
        [value_front[1:], jnp.zeros_like(value_front[:1])], axis=0
    )
    key_later, value_later = from_behind((key_front[0], value_front[0]), "seq", -1)
    grad_key = grad_key.at[blocks - 1].add(key_later)
    grad_value = grad_value.at[blocks - 1].add(value_later)
    width = head_group * HEAD_DIM
    return (
        lax.all_to_all(
            grad_query.reshape(block_rows, width), "head", split_axis=0, concat_axis=1, tiled=True
        ),
        lax.all_to_all(
            grad_key.reshape(block_rows, width).astype(jnp.bfloat16),
            "head",
            split_axis=0,
            concat_axis=1,
            tiled=True,
        ),
        lax.all_to_all(
            grad_value.reshape(block_rows, width).astype(jnp.bfloat16),
            "head",
            split_axis=0,
            concat_axis=1,
            tiled=True,
        ),
    )


def per_device(queries, key_vectors, value_vectors, grad_output):
    return regrouped(queries, key_vectors, value_vectors, grad_output)


def solution(mesh):
    placed = (
        P(("seq", "head"), None),
        P(("seq", "head"), None),
        P(("seq", "head"), None),
        P(("seq", "head"), None),
    )
    return jax.shard_map(
        per_device,
        mesh=mesh,
        in_specs=placed,
        out_specs=(P(("seq", "head"), None), P(("seq", "head"), None), P(("seq", "head"), None)),
        check_vma=False,
    )
```

profile of v0, /device:TPU:17, one launch (start us, length us, event | category | flops | bytes accessed | tf_op | source)
XLA Modules:
  0.0 140.7 jit_solution(17991139587422492030)
XLA Ops:
  0.6 1.9 %copy.105 = bf16[16,4,8,512]{3,2,0,1:T(8,128)(2,1)} copy(bf16[16,4,8,512]{3,2,1,0:T(8,128)(2,1)} %bitcast.69) | data formatting | bytes 1048576 | tf_op jit(solution)/shard_map/all_to_all | solution.py:61
  2.6 4.1 %all-to-all-start = ((bf16[128,4,512]{2,0,1:T(8,128)(2,1)}), bf16[128,4,512]{2,0,1:T(8,128)(2,1)S(1)}, u32[]{:S(2)}, u32[]{:S(2)}) async-start(bf16[128,4,512]{2,0,1:T(8,128)(2,1)} %bitcast.60), calls=%async_computation | async-start | bytes 1048576 | tf_op jit(solution)/shard_map/all_to_all | solution.py:61
  6.7 1.9 %copy.104 = bf16[16,4,8,512]{3,2,0,1:T(8,128)(2,1)} copy(bf16[16,4,8,512]{3,2,1,0:T(8,128)(2,1)} %bitcast.70) | data formatting | bytes 1048576 | tf_op jit(solution)/shard_map/all_to_all | solution.py:60
  8.6 6.1 %all-to-all-done = bf16[128,4,512]{2,0,1:T(8,128)(2,1)S(1)} async-done(((bf16[128,4,512]{2,0,1:T(8,128)(2,1)}), bf16[128,4,512]{2,0,1:T(8,128)(2,1)S(1)}, u32[]{:S(2)}, u32[]{:S(2)}) %all-to-all-start) | async-done | bytes 524320 | tf_op jit(solution)/shard_map/all_to_all | solution.py:61
  14.7 4.3 %all-to-all-start.1 = ((bf16[128,4,512]{2,0,1:T(8,128)(2,1)}), bf16[128,4,512]{2,0,1:T(8,128)(2,1)S(1)}, u32[]{:S(2)}, u32[]{:S(2)}) async-start(bf16[128,4,512]{2,0,1:T(8,128)(2,1)} %bitcast.59), calls=%async_computation.1 | async-start | bytes 1048576 | tf_op jit(solution)/shard_map/all_to_all | solution.py:60
  19.0 1.9 %copy.103 = bf16[16,4,8,512]{3,2,0,1:T(8,128)(2,1)} copy(bf16[16,4,8,512]{3,2,1,0:T(8,128)(2,1)} %bitcast.71) | data formatting | bytes 1048576 | tf_op jit(solution)/shard_map/all_to_all | solution.py:62
  20.9 6.1 %all-to-all-done.1 = bf16[128,4,512]{2,0,1:T(8,128)(2,1)S(1)} async-done(((bf16[128,4,512]{2,0,1:T(8,128)(2,1)}), bf16[128,4,512]{2,0,1:T(8,128)(2,1)S(1)}, u32[]{:S(2)}, u32[]{:S(2)}) %all-to-all-start.1) | async-done | bytes 524320 | tf_op jit(solution)/shard_map/all_to_all | solution.py:60
  27.0 4.3 %all-to-all-start.2 = ((bf16[128,4,512]{2,0,1:T(8,128)(2,1)}), bf16[128,4,512]{2,0,1:T(8,128)(2,1)S(1)}, u32[]{:S(2)}, u32[]{:S(2)}) async-start(bf16[128,4,512]{2,0,1:T(8,128)(2,1)} %bitcast.58), calls=%async_computation.2 | async-start | bytes 1048576 | tf_op jit(solution)/shard_map/all_to_all | solution.py:62
  31.3 0.1 reshape.198
  31.4 0.9 copy.58
  32.3 3.1 %collective-permute-start = (bf16[512,4,128]{2,0,1:T(8,128)(2,1)}, bf16[512,4,128]{2,0,1:T(8,128)(2,1)}, u32[]{:S(2)}, u32[]{:S(2)}) collective-permute-start(bf16[512,4,128]{2,0,1:T(8,128)(2,1)} %copy.58), channel_id=1, source_target_pairs={{0,4},{4,8},{8,12},{12,16},{16,20},{20,24},{24,28},{1,5},{5,9},{9,... | collective-permute-start | bytes 1572872 | tf_op jit(solution)/shard_map/ppermute | solution.py:14
  35.4 0.8 copy.102
  36.3 3.1 %all-to-all-done.2 = bf16[128,4,512]{2,0,1:T(8,128)(2,1)S(1)} async-done(((bf16[128,4,512]{2,0,1:T(8,128)(2,1)}), bf16[128,4,512]{2,0,1:T(8,128)(2,1)S(1)}, u32[]{:S(2)}, u32[]{:S(2)}) %all-to-all-start.2) | async-done | bytes 524320 | tf_op jit(solution)/shard_map/all_to_all | solution.py:62
  39.4 4.9 %all-to-all-start.3 = ((bf16[128,4,512]{2,0,1:T(8,128)(2,1)}), bf16[128,4,512]{2,0,1:T(8,128)(2,1)}, u32[]{:S(2)}, u32[]{:S(2)}) async-start(bf16[128,4,512]{2,0,1:T(8,128)(2,1)} %bitcast.57), calls=%async_computation.3 | async-start | bytes 1048576 | tf_op jit(solution)/shard_map/all_to_all | solution.py:63
  44.2 0.1 reshape.200
  44.4 0.9 copy.63
  45.2 3.1 %collective-permute-start.1 = (bf16[512,4,128]{2,0,1:T(8,128)(2,1)}, bf16[512,4,128]{2,0,1:T(8,128)(2,1)}, u32[]{:S(2)}, u32[]{:S(2)}) collective-permute-start(bf16[512,4,128]{2,0,1:T(8,128)(2,1)} %copy.63), channel_id=1, source_target_pairs={{0,4},{4,8},{8,12},{12,16},{16,20},{20,24},{24,28},{1,5},{5,9},{9,... | collective-permute-start | bytes 1572872 | tf_op jit(solution)/shard_map/ppermute | solution.py:14
  48.4 0.4 fusion.4
  48.8 0.1 reshape.199
  49.0 3.4 %all-to-all-done.3 = bf16[128,4,512]{2,0,1:T(8,128)(2,1)} async-done(((bf16[128,4,512]{2,0,1:T(8,128)(2,1)}), bf16[128,4,512]{2,0,1:T(8,128)(2,1)}, u32[]{:S(2)}, u32[]{:S(2)}) %all-to-all-start.3) | async-done | bytes 524320 | tf_op jit(solution)/shard_map/all_to_all | solution.py:63
  52.3 1.2 reshape.201
  53.5 0.3 copy.67
  53.8 0.0 copy-start.2
  53.8 0.0 collective-permute-done
  53.8 1.3 constant_dynamic-update-slice_fusion.1
  55.1 0.1 constant_dynamic-update-slice_fusion
  55.2 6.6 %collective-permute-done.1 = bf16[512,4,128]{2,0,1:T(8,128)(2,1)} collective-permute-done((bf16[512,4,128]{2,0,1:T(8,128)(2,1)}, bf16[512,4,128]{2,0,1:T(8,128)(2,1)}, u32[]{:S(2)}, u32[]{:S(2)}) %collective-permute-start.1) | collective-permute-done | bytes 524320 | tf_op jit(solution)/shard_map/ppermute | solution.py:14
  61.8 1.1 constant_dynamic-update-slice_fusion.3
  62.9 0.1 constant_dynamic-update-slice_fusion.2
  63.0 1.7 %fusion.2 = (f32[4,512]{1,0:T(4,128)S(1)}, f32[4,1024,512]{2,1,0:T(8,128)S(1)}) fusion(pred[512,1024]{0,1:T(8,128)(4,1)S(1)} %fusion.4, bf16[1024,4,128]{2,0,1:T(8,128)(2,1)S(1)} %constant_dynamic-update-slice_fusion, bf16[512,4,128]{2,1,0:T(4,128)(2,1)S(1)} %reshape.199), kind=kOutput, calls=%fused_computation.6 | convolution fusion | flops 543160320 | bytes 10493952 | tf_op jit(solution)/shard_map/while/body/eval_jaxpr/rhe,che->hrc/dot_general | solution.py:20
  64.7 1.8 %exponential_reduce_fusion = f32[4,512]{1,0:T(4,128)S(1)} fusion(f32[4,1024,512]{2,1,0:T(8,128)S(1)} %get-tuple-element.73, f32[4,512]{1,0:T(4,128)S(1)} %get-tuple-element.72, pred[512,1024]{0,1:T(8,128)(4,1)S(1)} %fusion.4), kind=kLoop, calls=%fused_computation.4 | loop fusion | flops 8386560 | bytes 8929280 | tf_op jit(solution)/shard_map/while/body/eval_jaxpr/reduce_sum | solution.py:28
  66.6 2.8 %fusion.6 = f32[4,512]{1,0:T(4,128)S(1)} fusion(bf16[1024,4,128]{2,0,1:T(8,128)(2,1)S(1)} %constant_dynamic-update-slice_fusion.2, bf16[512,4,128]{0,2,1:T(8,128)(2,1)S(1)} %copy.67, f32[4,1024,512]{2,1,0:T(8,128)S(1)} %get-tuple-element.73, f32[4,512]{1,0:T(4,128)S(1)} %log_add_fusion, pred[512,1024]{0,1:T(8,128)(4,1)S(1)} %fusion.4), kind=kOutput, calls=%fused_computation.16 | convolution fusion | flops 546043904 | bytes 10502144 | tf_op jit(solution)/shard_map/while/body/eval_jaxpr/hrc,che->hre/dot_general | solution.py:30
  69.4 0.0 copy-done.2
  69.4 3.0 %fusion = bf16[4,512,1024]{1,2,0:T(8,128)(2,1)S(1)} fusion(f32[4,1024,512]{2,1,0:T(8,128)S(1)} %get-tuple-element.73, f32[4,512]{1,0:T(4,128)S(1)} %fusion.6, f32[4,512]{1,0:T(4,128)S(1)} %log_add_fusion, pred[512,1024]{0,1:T(8,128)(4,1)S(1)} %fusion.4, bf16[1024,4,128]{2,0,1:T(8,128)(2,1)S(1)} %constant_dynamic-update-slice_fusion.2, ...), kind=kOutput, calls=%fused_computation.1 | convolution fusion | flops 549453824 | bytes 14696448 | tf_op jit(solution)/shard_map/while/body/eval_jaxpr/rhe,che->hrc/dot_general | solution.py:39
  72.4 0.0 copy-start.3
  72.4 1.2 multiply_bitcast_fusion
  73.6 1.0 slice.69
  74.7 2.1 %collective-permute-start.2 = (f32[512,4,128]{2,0,1:T(8,128)}, f32[512,4,128]{2,0,1:T(8,128)}, u32[]{:S(2)}, u32[]{:S(2)}) collective-permute-start(f32[512,4,128]{2,0,1:T(8,128)} %slice.69), channel_id=1, source_target_pairs={{4,0},{8,4},{12,8},{16,12},{20,16},{24,20},{28,24},{5,1},{9,5},{13... | collective-permute-start | bytes 3145736 | tf_op jit(solution)/shard_map/ppermute | solution.py:14
  76.8 2.1 %convolution_bitcast_fusion = f32[1024,4,128]{2,0,1:T(8,128)S(1)} fusion(bf16[512,4,128]{0,2,1:T(8,128)(2,1)S(1)} %copy-done.3, f32[4,1024,512]{2,1,0:T(8,128)S(1)} %get-tuple-element.73, f32[4,512]{1,0:T(4,128)S(1)} %log_add_fusion, pred[512,1024]{0,1:T(8,128)(4,1)S(1)} %fusion.4), kind=kOutput, calls=%fused_computation.12 | convolution fusion | flops 545259520 | bytes 11542528 | tf_op jit(solution)/shard_map/while/body/eval_jaxpr/hrc,rhe->che/dot_general | solution.py:51
  79.0 1.2 slice.71
  80.2 0.5 copy-done
  80.6 3.2 %collective-permute-start.3 = (f32[512,4,128]{2,0,1:T(8,128)}, f32[512,4,128]{2,0,1:T(8,128)}, u32[]{:S(2)}, u32[]{:S(2)}) collective-permute-start(f32[512,4,128]{2,0,1:T(8,128)} %slice.71), channel_id=1, source_target_pairs={{4,0},{8,4},{12,8},{16,12},{20,16},{24,20},{28,24},{5,1},{9,5},{13... | collective-permute-start | bytes 3145736 | tf_op jit(solution)/shard_map/ppermute | solution.py:14
  83.8 0.8 fusion.7
  84.6 0.1 all_to_all.98
  84.8 0.9 copy.72
  85.6 4.9 %all-to-all-start.4 = ((bf16[4,128,512]{1,2,0:T(8,128)(2,1)}), bf16[4,128,512]{1,2,0:T(8,128)(2,1)S(1)}, u32[]{:S(2)}, u32[]{:S(2)}) async-start(bf16[4,128,512]{1,2,0:T(8,128)(2,1)} %copy.72), calls=%async_computation.4 | async-start | bytes 1048576 | tf_op jit(solution)/shard_map/all_to_all | solution.py:116
  90.5 10.2 %collective-permute-done.2 = f32[512,4,128]{2,0,1:T(8,128)} collective-permute-done((f32[512,4,128]{2,0,1:T(8,128)}, f32[512,4,128]{2,0,1:T(8,128)}, u32[]{:S(2)}, u32[]{:S(2)}) %collective-permute-start.2) | collective-permute-done | bytes 1048608 | tf_op jit(solution)/shard_map/ppermute | solution.py:14
  100.7 1.3 fusion.9
  102.0 0.4 copy.74
  102.5 1.0 convert_element_type.44
  103.4 0.0 all-to-all-done.4
  103.4 6.5 %all-to-all-start.5 = ((bf16[4,128,512]{2,1,0:T(8,128)(2,1)}), bf16[4,128,512]{2,1,0:T(8,128)(2,1)S(1)}, u32[]{:S(2)}, u32[]{:S(2)}) async-start(bf16[4,128,512]{2,1,0:T(8,128)(2,1)} %convert_element_type.44), calls=%async_computation.5 | async-start | bytes 1048576 | tf_op jit(solution)/shard_map/all_to_all | solution.py:119
  110.0 13.2 %collective-permute-done.3 = f32[512,4,128]{2,0,1:T(8,128)} collective-permute-done((f32[512,4,128]{2,0,1:T(8,128)}, f32[512,4,128]{2,0,1:T(8,128)}, u32[]{:S(2)}, u32[]{:S(2)}) %collective-permute-start.3) | collective-permute-done | bytes 1048608 | tf_op jit(solution)/shard_map/ppermute | solution.py:14
  123.2 1.6 %fusion.8 = bf16[512,4,128]{2,0,1:T(8,128)(2,1)S(1)} fusion(f32[512,4,128]{2,0,1:T(8,128)} %collective-permute-done.3, f32[1024,4,128]{2,0,1:T(8,128)} %copy-done), kind=kLoop, calls=%fused_computation.19 | loop fusion | flops 524288 | bytes 2621440 | tf_op jit(solution)/shard_map/convert_element_type | solution.py:127
  124.8 0.4 copy.77
  125.2 1.0 convert_element_type.46
  126.2 0.0 all-to-all-done.5
  126.2 5.2 %all-to-all-start.6 = ((bf16[4,128,512]{2,1,0:T(8,128)(2,1)}), bf16[4,128,512]{2,1,0:T(8,128)(2,1)S(1)}, u32[]{:S(2)}, u32[]{:S(2)}) async-start(bf16[4,128,512]{2,1,0:T(8,128)(2,1)} %convert_element_type.46), calls=%async_computation.6 | async-start | bytes 1048576 | tf_op jit(solution)/shard_map/all_to_all | solution.py:126
  131.4 1.0 copy.79
  132.4 0.3 copy.75
  132.7 1.0 copy.80
  133.7 5.7 %all-to-all-done.6 = bf16[4,128,512]{2,1,0:T(8,128)(2,1)S(1)} async-done(((bf16[4,128,512]{2,1,0:T(8,128)(2,1)}), bf16[4,128,512]{2,1,0:T(8,128)(2,1)S(1)}, u32[]{:S(2)}, u32[]{:S(2)}) %all-to-all-start.6) | async-done | bytes 524320 | tf_op jit(solution)/shard_map/all_to_all | solution.py:126
  139.4 0.3 copy.78
  139.7 1.0 copy.81
  (7 shorter events, 0.0 us)
Async XLA Ops:
  0.6 34.8 %copy-start.1 = (bf16[128,2048]{1,0:T(8,128)(2,1)S(1)}, bf16[128,2048]{1,0:T(8,128)(2,1)}, u32[]{:S(2)}) copy-start(bf16[128,2048]{1,0:T(8,128)(2,1)} %param.11) | copy-start | bytes 1572868
  2.6 12.1 %all-to-all-start = ((bf16[128,4,512]{2,0,1:T(8,128)(2,1)}), bf16[128,4,512]{2,0,1:T(8,128)(2,1)S(1)}, u32[]{:S(2)}, u32[]{:S(2)}) async-start(bf16[128,4,512]{2,0,1:T(8,128)(2,1)} %bitcast.60), calls=%async_computation | async-start | bytes 1048576 | tf_op jit(solution)/shard_map/all_to_all | solution.py:61
  14.7 12.3 %all-to-all-start.1 = ((bf16[128,4,512]{2,0,1:T(8,128)(2,1)}), bf16[128,4,512]{2,0,1:T(8,128)(2,1)S(1)}, u32[]{:S(2)}, u32[]{:S(2)}) async-start(bf16[128,4,512]{2,0,1:T(8,128)(2,1)} %bitcast.59), calls=%async_computation.1 | async-start | bytes 1048576 | tf_op jit(solution)/shard_map/all_to_all | solution.py:60
  27.0 12.4 %all-to-all-start.2 = ((bf16[128,4,512]{2,0,1:T(8,128)(2,1)}), bf16[128,4,512]{2,0,1:T(8,128)(2,1)S(1)}, u32[]{:S(2)}, u32[]{:S(2)}) async-start(bf16[128,4,512]{2,0,1:T(8,128)(2,1)} %bitcast.58), calls=%async_computation.2 | async-start | bytes 1048576 | tf_op jit(solution)/shard_map/all_to_all | solution.py:62
  32.3 21.6 %collective-permute-start = (bf16[512,4,128]{2,0,1:T(8,128)(2,1)}, bf16[512,4,128]{2,0,1:T(8,128)(2,1)}, u32[]{:S(2)}, u32[]{:S(2)}) collective-permute-start(bf16[512,4,128]{2,0,1:T(8,128)(2,1)} %copy.58), channel_id=1, source_target_pairs={{0,4},{4,8},{8,12},{12,16},{16,20},{20,24},{24,28},{1,5},{5,9},{9,... | collective-permute-start | bytes 1572872 | tf_op jit(solution)/shard_map/ppermute | solution.py:14
  39.4 12.9 %all-to-all-start.3 = ((bf16[128,4,512]{2,0,1:T(8,128)(2,1)}), bf16[128,4,512]{2,0,1:T(8,128)(2,1)}, u32[]{:S(2)}, u32[]{:S(2)}) async-start(bf16[128,4,512]{2,0,1:T(8,128)(2,1)} %bitcast.57), calls=%async_computation.3 | async-start | bytes 1048576 | tf_op jit(solution)/shard_map/all_to_all | solution.py:63
  45.2 16.6 %collective-permute-start.1 = (bf16[512,4,128]{2,0,1:T(8,128)(2,1)}, bf16[512,4,128]{2,0,1:T(8,128)(2,1)}, u32[]{:S(2)}, u32[]{:S(2)}) collective-permute-start(bf16[512,4,128]{2,0,1:T(8,128)(2,1)} %copy.63), channel_id=1, source_target_pairs={{0,4},{4,8},{8,12},{12,16},{16,20},{20,24},{24,28},{1,5},{5,9},{9,... | collective-permute-start | bytes 1572872 | tf_op jit(solution)/shard_map/ppermute | solution.py:14
  53.8 15.6 %copy-start.2 = (bf16[512,4,128]{0,2,1:T(8,128)(2,1)}, bf16[512,4,128]{0,2,1:T(8,128)(2,1)S(1)}, u32[]{:S(2)}) copy-start(bf16[512,4,128]{0,2,1:T(8,128)(2,1)S(1)} %copy.67) | copy-start | bytes 1572868
  72.4 4.4 %copy-start.3 = (bf16[512,4,128]{0,2,1:T(8,128)(2,1)S(1)}, bf16[512,4,128]{0,2,1:T(8,128)(2,1)}, u32[]{:S(2)}) copy-start(bf16[512,4,128]{0,2,1:T(8,128)(2,1)} %copy-done.2) | copy-start | bytes 1572868
  74.7 26.0 %collective-permute-start.2 = (f32[512,4,128]{2,0,1:T(8,128)}, f32[512,4,128]{2,0,1:T(8,128)}, u32[]{:S(2)}, u32[]{:S(2)}) collective-permute-start(f32[512,4,128]{2,0,1:T(8,128)} %slice.69), channel_id=1, source_target_pairs={{4,0},{8,4},{12,8},{16,12},{20,16},{24,20},{28,24},{5,1},{9,5},{13... | collective-permute-start | bytes 3145736 | tf_op jit(solution)/shard_map/ppermute | solution.py:14
  79.0 1.7 %copy-start = (f32[1024,4,128]{2,0,1:T(8,128)}, f32[1024,4,128]{2,0,1:T(8,128)S(1)}, u32[]{:S(2)}) copy-start(f32[1024,4,128]{2,0,1:T(8,128)S(1)} %convolution_bitcast_fusion) | copy-start | bytes 6291460
  80.6 42.6 %collective-permute-start.3 = (f32[512,4,128]{2,0,1:T(8,128)}, f32[512,4,128]{2,0,1:T(8,128)}, u32[]{:S(2)}, u32[]{:S(2)}) collective-permute-start(f32[512,4,128]{2,0,1:T(8,128)} %slice.71), channel_id=1, source_target_pairs={{4,0},{8,4},{12,8},{16,12},{20,16},{24,20},{28,24},{5,1},{9,5},{13... | collective-permute-start | bytes 3145736 | tf_op jit(solution)/shard_map/ppermute | solution.py:14
  85.6 17.8 %all-to-all-start.4 = ((bf16[4,128,512]{1,2,0:T(8,128)(2,1)}), bf16[4,128,512]{1,2,0:T(8,128)(2,1)S(1)}, u32[]{:S(2)}, u32[]{:S(2)}) async-start(bf16[4,128,512]{1,2,0:T(8,128)(2,1)} %copy.72), calls=%async_computation.4 | async-start | bytes 1048576 | tf_op jit(solution)/shard_map/all_to_all | solution.py:116
  103.4 22.8 %all-to-all-start.5 = ((bf16[4,128,512]{2,1,0:T(8,128)(2,1)}), bf16[4,128,512]{2,1,0:T(8,128)(2,1)S(1)}, u32[]{:S(2)}, u32[]{:S(2)}) async-start(bf16[4,128,512]{2,1,0:T(8,128)(2,1)} %convert_element_type.44), calls=%async_computation.5 | async-start | bytes 1048576 | tf_op jit(solution)/shard_map/all_to_all | solution.py:119
  126.2 13.2 %all-to-all-start.6 = ((bf16[4,128,512]{2,1,0:T(8,128)(2,1)}), bf16[4,128,512]{2,1,0:T(8,128)(2,1)S(1)}, u32[]{:S(2)}, u32[]{:S(2)}) async-start(bf16[4,128,512]{2,1,0:T(8,128)(2,1)} %convert_element_type.46), calls=%async_computation.6 | async-start | bytes 1048576 | tf_op jit(solution)/shard_map/all_to_all | solution.py:126
where the time goes:
time: 142 us; the launch traced here: 141 us
  waiting for transfers between devices  54.3 us (38%)
  starting transfers between devices  45.8 us (32%)
  local copies, waits for them, and re-layouts  22.8 us (16%)
  matrix products  11.6 us (8%)
  other arithmetic  5.28 us (4%)
    ppermute x4, waiting for transfers between devices, from_behind(): return lax.ppermute(block, axis, route)  30 us
    ppermute x4, starting transfers between devices, from_behind(): return lax.ppermute(block, axis, route)  11.6 us
    all_to_all x1, starting transfers between devices, regrouped(): lax.all_to_all(grad_key.reshape(block_rows, width).astype(jnp.bfloat16),...  6.54 us
    all_to_all x1, waiting for transfers between devices, regrouped(): lax.all_to_all(key_vectors, 'head', split_axis=1, concat_axis=0, tiled=True)  6.1 us
    all_to_all x1, waiting for transfers between devices, regrouped(): lax.all_to_all(queries, 'head', split_axis=1, concat_axis=0, tiled=True)  6.1 us
    unnamed x13, local copies, waits for them, and re-layouts  5.86 us
    all_to_all x1, waiting for transfers between devices, regrouped(): lax.all_to_all(grad_value.reshape(block_rows, width).astype(jnp.bfloat16)...  5.68 us
    all_to_all x1, starting transfers between devices, regrouped(): lax.all_to_all(grad_value.reshape(block_rows, width).astype(jnp.bfloat16)...  5.19 us
  transfers between devices with their start and end apart: 11, of which 8 were waited for; matrix products, arithmetic and copies ran while one was open for 16% of the time, Pallas kernels for 0%

commit v1 on v0

v1 whole, which is shorter than its diff:
```python
import functools
import math

import jax
import jax.numpy as jnp
from jax import lax
from jax.experimental import pallas as pl
from jax.experimental.pallas import tpu as pltpu
from jax.sharding import Mesh, PartitionSpec as P

HEADS = 16
HEAD_DIM = 128
WINDOW = 512
TILE = 256
AXES = ("chunk", "part", "head")
GROUP = ("part", "head")
SCALE = HEAD_DIM ** (-0.5)
SCALE_LOG2 = SCALE * math.log2(math.e)
MASKED = -1e30
HBM = pl.BlockSpec(memory_space=pl.ANY)
VMEM_LIMIT = 48 * 1024 * 1024


def bf16(*shape):
    return jax.ShapeDtypeStruct(shape, jnp.bfloat16)


def f32(*shape):
    return jax.ShapeDtypeStruct(shape, jnp.float32)


def params():
    return pltpu.CompilerParams(vmem_limit_bytes=VMEM_LIMIT)


def group_index():
    return lax.axis_index("part") * lax.axis_size("head") + lax.axis_index("head")


def group_size():
    return lax.axis_size("part") * lax.axis_size("head")


def copy_all(pairs, sems):
    copies = [pltpu.make_async_copy(src, dst, sems.at[i]) for i, (src, dst) in enumerate(pairs)]
    for copy in copies:
        copy.start()
    for copy in copies:
        copy.wait()


def aligned(index, step):
    return pl.multiple_of(index * step, step)


def pack_kernel(n, *refs):
    q, k, v, g = refs[:4]
    crit = refs[4 : 4 + n]
    rest = refs[4 + n : 4 + 2 * n]
    sems = refs[-1]
    me = group_index()
    width = q.shape[1] // n
    late = me >= n // 2

    def send(first, second):
        pairs = []
        for out, pair in ((crit, first), (rest, second)):
            for m in range(n):
                cols = pl.ds(aligned(jnp.bitwise_xor(me, m), width), width)
                for t in range(2):
                    pairs.append((pair[t].at[:, cols], out[m].at[t]))
        copy_all(pairs, sems)

    @pl.when(late)
    def _():
        send((k, v), (q, g))

    @pl.when(jnp.logical_not(late))
    def _():
        send((q, g), (k, v))


def halo_kernel(n, *refs):
    crit = refs[:n]
    kv, qg = refs[n], refs[n + 1]
    sems = refs[-1]
    me = group_index()
    rows = crit[0].shape[1]
    ends = WINDOW // rows
    for phase in range(2):
        for m in range(n):
            other = jnp.bitwise_xor(me, m)

            @pl.when(other >= n - ends)
            def _():
                at = aligned(other - (n - ends), rows)
                copy = pltpu.make_async_copy(crit[m], kv.at[:, pl.ds(at, rows)], sems.at[m])
                copy.start() if phase == 0 else copy.wait()

            @pl.when(other < ends)
            def _():
                at = aligned(other, rows)
                copy = pltpu.make_async_copy(crit[m], qg.at[:, pl.ds(at, rows)], sems.at[m])
                copy.start() if phase == 0 else copy.wait()


def dot(a, b, dims):
    return lax.dot_general(a, b, (dims, ((), ())), preferred_element_type=jnp.float32)


NT = ((1,), (1,))
NN = ((1,), (0,))
TN = ((0,), (0,))


def main_kernel(n, heads, *refs):
    crit = refs[:n]
    rest = refs[n : 2 * n]
    kv_halo = refs[2 * n]
    dq_out = refs[2 * n + 1 : 3 * n + 1]
    front_out, back_out, stat_out = refs[3 * n + 1 : 3 * n + 4]
    x, dq, dk, dv, front, stat, sems = refs[3 * n + 4 :]
    me = group_index()
    first = lax.axis_index("chunk") == 0
    rows = crit[0].shape[1]
    total = n * rows
    pairs = [(kv_halo, x.at[pl.ds(2, 2), pl.ds(0, WINDOW)])]
    for m in range(n):
        other = jnp.bitwise_xor(me, m)
        kind = (other >= n // 2).astype(jnp.int32)
        at = pl.ds(pl.multiple_of(WINDOW + other * rows, rows), rows)
        pairs.append((crit[m], x.at[pl.ds(2 * kind, 2), at]))
        pairs.append((rest[m], x.at[pl.ds(2 - 2 * kind, 2), at]))
    copy_all(pairs, sems)
    stat[...] = jnp.zeros_like(stat)

    row = lax.broadcasted_iota(jnp.int32, (TILE, TILE), 0)
    col = lax.broadcasted_iota(jnp.int32, (TILE, TILE), 1)

    @pl.loop(0, total // TILE)
    def _(i):
        start = aligned(i, TILE)
        keys = pl.ds(start, 3 * TILE)
        mine = pl.ds(pl.multiple_of(WINDOW + start, TILE), TILE)
        low = jnp.where(first, WINDOW - start, 0)
        for h in range(heads):
            lanes = slice(h * HEAD_DIM, (h + 1) * HEAD_DIM)
            qb = x[0, mine, lanes]
            gb = x[1, mine, lanes]
            kb = x[2, keys, lanes]
            vb = x[3, keys, lanes]
            s = dot(kb, qb, NT) * SCALE_LOG2
            s0 = jnp.where(row > jnp.maximum(col, low - 1), s[:TILE], MASKED)
            s1 = jnp.where(row >= low - TILE, s[TILE : 2 * TILE], MASKED)
            s2 = jnp.where(row <= col, s[2 * TILE :], MASKED)
            s = jnp.concatenate([s0, s1, s2], axis=0)
            top = jnp.max(s, axis=0, keepdims=True)
            e = jnp.exp2(s - top)
            inverse = 1.0 / jnp.sum(e, axis=0, keepdims=True)
            p = e * inverse
            p_low = p.astype(jnp.bfloat16)
            dp = dot(vb, gb, NT)
            dots = jnp.sum(p_low.astype(jnp.float32) * dp, axis=0, keepdims=True)
            ds = (p * (dp - dots)).astype(jnp.bfloat16)
            dq[mine, lanes] = (dot(ds, kb, TN) * SCALE).astype(jnp.bfloat16)
            add_v = dot(p_low, gb, NN)
            add_k = dot(ds, qb, NN)
            older = pl.ds(start, 2 * TILE)
            dv[older, lanes] += add_v[: 2 * TILE]
            dk[older, lanes] += add_k[: 2 * TILE]
            dv[mine, lanes] = add_v[2 * TILE :]
            dk[mine, lanes] = add_k[2 * TILE :]

            @pl.when(i < WINDOW // TILE)
            def _():
                at = pl.ds(start, TILE)
                stat[3 * h : 3 * h + 1, at] = top
                stat[3 * h + 1 : 3 * h + 2, at] = inverse
                stat[3 * h + 2 : 3 * h + 3, at] = dots

    done = total - WINDOW
    front[0] = (dk[pl.ds(WINDOW, done)] * SCALE).astype(jnp.bfloat16)
    front[1] = dv[pl.ds(WINDOW, done)].astype(jnp.bfloat16)
    pairs = [
        (stat, stat_out),
        (front, front_out),
        (dk.at[pl.ds(total, WINDOW)], back_out.at[0]),
        (dv.at[pl.ds(total, WINDOW)], back_out.at[1]),
    ]
    for m in range(n):
        other = jnp.bitwise_xor(me, m)
        at = pl.ds(pl.multiple_of(WINDOW + other * rows, rows), rows)
        pairs.append((dq.at[at], dq_out[m]))
    copy_all(pairs, sems)


def edge_kernel(n, heads, *refs):
    crit = refs[:n]
    qg_halo, front_in, back_in, stat_in = refs[n : n + 4]
    out = refs[n + 4 : 2 * n + 4]
    kv, qg, full, back, stat, sems = refs[2 * n + 4 :]
    me = group_index()
    rows = crit[0].shape[1]
    total = n * rows
    done = total - WINDOW
    ends = WINDOW // rows
    for phase in range(2):
        for m in range(n):
            other = jnp.bitwise_xor(me, m)

            @pl.when(other >= n - ends)
            def _():
                at = aligned(other - (n - ends), rows)
                copy = pltpu.make_async_copy(crit[m], kv.at[:, pl.ds(at, rows)], sems.at[4 + m])
                copy.start() if phase == 0 else copy.wait()

        if phase == 0:
            copy_all(
                [(qg_halo, qg), (front_in, full.at[:, pl.ds(0, done)]), (back_in, back), (stat_in, stat)],
                sems,
            )

    row = lax.broadcasted_iota(jnp.int32, (TILE, TILE), 0)
    col = lax.broadcasted_iota(jnp.int32, (TILE, TILE), 1)
    for h in range(heads):
        lanes = slice(h * HEAD_DIM, (h + 1) * HEAD_DIM)
        for j in range(WINDOW // TILE):
            at = slice(j * TILE, (j + 1) * TILE)
            qb = qg[0, at, lanes]
            gb = qg[1, at, lanes]
            kb = kv[0, j * TILE :, lanes]
            vb = kv[1, j * TILE :, lanes]
            s = dot(kb, qb, NT) * SCALE_LOG2
            s0 = jnp.where(row > col, s[:TILE], MASKED)
            s = jnp.concatenate([s0, s[TILE:]], axis=0) if j == 0 else s0
            top = stat[3 * h : 3 * h + 1, at]
            inverse = stat[3 * h + 1 : 3 * h + 2, at]
            dots = stat[3 * h + 2 : 3 * h + 3, at]
            p = jnp.exp2(s - top) * inverse
            dp = dot(vb, gb, NT)
            ds = (p * (dp - dots)).astype(jnp.bfloat16)
            back[0, j * TILE :, lanes] += dot(ds, qb, NN)
            back[1, j * TILE :, lanes] += dot(p.astype(jnp.bfloat16), gb, NN)
    full[0, done:] = (back[0] * SCALE).astype(jnp.bfloat16)
    full[1, done:] = back[1].astype(jnp.bfloat16)
    pairs = []
    for m in range(n):
        at = pl.ds(aligned(jnp.bitwise_xor(me, m), rows), rows)
        pairs.append((full.at[:, at], out[m]))
    copy_all(pairs, sems)


def unpack_kernel(n, *refs):
    dq_in = refs[:n]
    dkv_in = refs[n : 2 * n]
    dq, dk, dv, sems = refs[2 * n :]
    me = group_index()
    width = dq_in[0].shape[1]
    pairs = []
    for m in range(n):
        cols = pl.ds(aligned(jnp.bitwise_xor(me, m), width), width)
        pairs.append((dq_in[m], dq.at[:, cols]))
        pairs.append((dkv_in[m].at[0], dk.at[:, cols]))
        pairs.append((dkv_in[m].at[1], dv.at[:, cols]))
    copy_all(pairs, sems)


def call(kernel, outs, scratch, sems, *operands):
    return pl.pallas_call(
        kernel,
        out_shape=outs,
        in_specs=[HBM] * len(operands),
        out_specs=jax.tree.map(lambda _: HBM, outs),
        scratch_shapes=[*scratch, pltpu.SemaphoreType.DMA((sems,))],
        compiler_params=params(),
    )(*operands)


def exchanged(pieces):
    n = len(pieces)
    return [pieces[0]] + [
        lax.ppermute(pieces[m], GROUP, [(i, i ^ m) for i in range(n)]) for m in range(1, n)
    ]


def per_device(queries, key_vectors, value_vectors, grad_output):
    n = group_size()
    chunks = lax.axis_size("chunk")
    rows, model = queries.shape
    heads = HEADS // n
    width = model // n
    total = n * rows
    piece = bf16(2, rows, width)
    packed = call(
        functools.partial(pack_kernel, n), [piece] * (2 * n), [], 4 * n,
        queries, key_vectors, value_vectors, grad_output,
    )
    crit = exchanged(packed[:n])
    end = bf16(2, WINDOW, width)
    kv_send, qg_send = call(functools.partial(halo_kernel, n), [end, end], [], n, *crit)
    forward = [(i, i + 1) for i in range(chunks - 1)]
    backward = [(i + 1, i) for i in range(chunks - 1)]
    kv_halo = lax.ppermute(kv_send, "chunk", forward)
    qg_halo = lax.ppermute(qg_send, "chunk", backward)
    rest = exchanged(packed[n:])
    done = total - WINDOW
    stat_rows = -(-3 * heads // 8) * 8
    *dq, front, back, stat = call(
        functools.partial(main_kernel, n, heads),
        [bf16(rows, width)] * n
        + [bf16(2, done, width), f32(2, WINDOW, width), f32(stat_rows, WINDOW)],
        [
            pltpu.VMEM((4, WINDOW + total, width), jnp.bfloat16),
            pltpu.VMEM((WINDOW + total, width), jnp.bfloat16),
            pltpu.VMEM((WINDOW + total, width), jnp.float32),
            pltpu.VMEM((WINDOW + total, width), jnp.float32),
            pltpu.VMEM((2, done, width), jnp.bfloat16),
            pltpu.VMEM((stat_rows, WINDOW), jnp.float32),
        ],
        2 * n + 4,
        *crit, *rest, kv_halo,
    )
    stat_halo = lax.ppermute(stat, "chunk", backward)
    dq = exchanged(dq)
    dkv = call(
        functools.partial(edge_kernel, n, heads),
        [piece] * n,
        [
            pltpu.VMEM((2, WINDOW, width), jnp.bfloat16),
            pltpu.VMEM((2, WINDOW, width), jnp.bfloat16),
            pltpu.VMEM((2, total, width), jnp.bfloat16),
            pltpu.VMEM((2, WINDOW, width), jnp.float32),
            pltpu.VMEM((stat_rows, WINDOW), jnp.float32),
        ],
        n + 4,
        *crit, qg_halo, front, back, stat_halo,
    )
    dkv = exchanged(dkv)
    out = bf16(rows, model)
    return tuple(
        call(functools.partial(unpack_kernel, n), [out] * 3, [], 3 * n, *dq, *dkv)
    )


def solution(mesh):
    seq, head = mesh.devices.shape
    part = max(1, min(seq, HEADS // 2 // head))
    fine = Mesh(mesh.devices.reshape(seq // part, part, head), AXES)
    placed = P(AXES, None)
    return jax.shard_map(
        per_device,
        mesh=fine,
        in_specs=(placed,) * 4,
        out_specs=(placed,) * 3,
        check_vma=False,
    )
```

time: 142 us -> 91.7 us (0.65)
  waiting for transfers between devices: 54.3 us -> 26.9 us
  local copies, waits for them, and re-layouts: 22.8 us -> 4.16 us
  Pallas kernels: 0 us -> 18.1 us
  matrix products: 11.6 us -> 0 us
  other arithmetic: 5.28 us -> 0 us
  starting transfers between devices: 45.8 us -> 40.7 us
    all_to_all x7 -> x0, starting transfers between devices: 34.2 us -> none  [the longest x1 6.54 us: regrouped(): lax.all_to_all(grad_key.reshape(block_rows, width).astype(jnp.bfloat16),...]
    ppermute x4 -> x31, starting transfers between devices: 11.6 us -> 40.7 us  [the longest x28 33.3 us: exchanged(): lax.ppermute(pieces[m], GROUP, [(i, i ^ m) for i in range(n)])]
    all_to_all x7 -> x0, waiting for transfers between devices: 24.3 us -> none  [the longest x1 6.1 us: regrouped(): lax.all_to_all(key_vectors, 'head', split_axis=1, concat_axis=0, tiled=True)]
    pallas_call x0 -> x5, Pallas kernels: none -> 18.1 us  [call(): pl.pallas_call(kernel, out_shape=outs, in_specs=[HBM] * len(operands), ou...]
    dot_general x6 -> x0, matrix products: 11.6 us -> none  [the longest x1 3 us: grads_of(): jnp.einsum('rhe,che->hrc', grad_rows, value_rows, preferred_element_type=...]
    all_to_all x8 -> x0, local copies, waits for them, and re-layouts: 8.07 us -> none  [the longest x1 1.94 us: regrouped(): lax.all_to_all(key_vectors, 'head', split_axis=1, concat_axis=0, tiled=True)]
    reshape x7 -> x0, local copies, waits for them, and re-layouts: 3.58 us -> none  [the longest x2 1.48 us: regrouped(): grad_block = grad_block.reshape(shape)]
    ppermute x4 -> x31, waiting for transfers between devices: 30 us -> 26.9 us  [the longest x28 26.9 us: exchanged(): lax.ppermute(pieces[m], GROUP, [(i, i ^ m) for i in range(n)])]
  transfers between devices with their start and end apart: 11 -> 31, of which waited for: 8 -> 10; matrix products, arithmetic and copies ran while one was open for 16% -> 0% of each run, Pallas kernels for 0% -> 17%
where the time goes in v1:
time: 91.7 us; the launch traced here: 90.6 us
  starting transfers between devices  40.7 us (44%)
  waiting for transfers between devices  26.9 us (29%)
  Pallas kernels  18.1 us (20%)
  local copies, waits for them, and re-layouts  4.16 us (5%)
    ppermute x28, starting transfers between devices, exchanged(): lax.ppermute(pieces[m], GROUP, [(i, i ^ m) for i in range(n)])  33.3 us
    ppermute x28, waiting for transfers between devices, exchanged(): lax.ppermute(pieces[m], GROUP, [(i, i ^ m) for i in range(n)])  26.9 us
    pallas_call x5, Pallas kernels, call(): pl.pallas_call(kernel, out_shape=outs, in_specs=[HBM] * len(operands), ou...  18.1 us
    unnamed x8, local copies, waits for them, and re-layouts  4.16 us
    ppermute x1, starting transfers between devices, per_device(): kv_halo = lax.ppermute(kv_send, 'chunk', forward)  3.2 us
    ppermute x1, starting transfers between devices, per_device(): stat_halo = lax.ppermute(stat, 'chunk', backward)  2.09 us
    ppermute x1, starting transfers between devices, per_device(): qg_halo = lax.ppermute(qg_send, 'chunk', backward)  2.08 us
  transfers between devices with their start and end apart: 31, of which 10 were waited for; matrix products, arithmetic and copies ran while one was open for 0% of the time, Pallas kernels for 17%

profile of v1, /device:TPU:17, one launch (start us, length us, event | category | flops | bytes accessed | tf_op | source)
XLA Modules:
  0.0 90.6 jit_solution(13089890314071277079)
XLA Ops:
  0.6 1.0 %copy-done = bf16[128,2048]{1,0:T(8,128)(2,1)S(1)} copy-done((bf16[128,2048]{1,0:T(8,128)(2,1)S(1)}, bf16[128,2048]{1,0:T(8,128)(2,1)}, u32[]{:S(2)}) %copy-start) | copy-done | bytes 524312
  1.7 1.0 %copy-done.1 = bf16[128,2048]{1,0:T(8,128)(2,1)S(1)} copy-done((bf16[128,2048]{1,0:T(8,128)(2,1)S(1)}, bf16[128,2048]{1,0:T(8,128)(2,1)}, u32[]{:S(2)}) %copy-start.1) | copy-done | bytes 524312
  2.7 1.0 %copy-done.2 = bf16[128,2048]{1,0:T(8,128)(2,1)S(1)} copy-done((bf16[128,2048]{1,0:T(8,128)(2,1)S(1)}, bf16[128,2048]{1,0:T(8,128)(2,1)}, u32[]{:S(2)}) %copy-start.2) | copy-done | bytes 524312
  3.8 1.0 %copy-done.3 = bf16[128,2048]{1,0:T(8,128)(2,1)S(1)} copy-done((bf16[128,2048]{1,0:T(8,128)(2,1)S(1)}, bf16[128,2048]{1,0:T(8,128)(2,1)}, u32[]{:S(2)}) %copy-start.3) | copy-done | bytes 524312
  4.8 0.8 shard_map.67
  5.6 0.7 collective-permute-start
  6.3 1.2 %collective-permute-start.1 = (bf16[2,128,256]{2,1,0:T(8,128)(2,1)S(1)}, bf16[2,128,256]{2,1,0:T(8,128)(2,1)S(1)}, u32[]{:S(2)}, u32[]{:S(2)}) collective-permute-start(bf16[2,128,256]{2,1,0:T(8,128)(2,1)S(1)} %get-tuple-element.42), channel_id=1, source_target_pairs={{0,2},{1,3},{2,0},{3,1},{4,6},{5,7},{6,4},{7,5},{8,10},{9,11},{10,... | collective-permute-start | bytes 393224 | tf_op jit(solution)/shard_map/ppermute | solution.py:282
  7.5 0.5 collective-permute-start.2
  8.0 1.2 %collective-permute-start.3 = (bf16[2,128,256]{2,1,0:T(8,128)(2,1)S(1)}, bf16[2,128,256]{2,1,0:T(8,128)(2,1)S(1)}, u32[]{:S(2)}, u32[]{:S(2)}) collective-permute-start(bf16[2,128,256]{2,1,0:T(8,128)(2,1)S(1)} %get-tuple-element.44), channel_id=1, source_target_pairs={{0,4},{1,5},{2,6},{3,7},{4,0},{5,1},{6,2},{7,3},{8,12},{9,13},{10,... | collective-permute-start | bytes 393224 | tf_op jit(solution)/shard_map/ppermute | solution.py:282
  9.2 0.6 collective-permute-start.4
  9.8 0.0 collective-permute-done.refs_1_
  9.8 2.2 %collective-permute-start.5 = (bf16[2,128,256]{2,1,0:T(8,128)(2,1)S(1)}, bf16[2,128,256]{2,1,0:T(8,128)(2,1)S(1)}, u32[]{:S(2)}, u32[]{:S(2)}) collective-permute-start(bf16[2,128,256]{2,1,0:T(8,128)(2,1)S(1)} %get-tuple-element.46), channel_id=1, source_target_pairs={{0,6},{1,7},{2,4},{3,5},{4,2},{5,3},{6,0},{7,1},{8,14},{9,15},{10,... | collective-permute-start | bytes 393224 | tf_op jit(solution)/shard_map/ppermute | solution.py:282
  12.0 0.0 collective-permute-done.1.refs_2_
  12.0 2.7 %collective-permute-start.6 = (bf16[2,128,256]{2,1,0:T(8,128)(2,1)S(1)}, bf16[2,128,256]{2,1,0:T(8,128)(2,1)S(1)}, u32[]{:S(2)}, u32[]{:S(2)}) collective-permute-start(bf16[2,128,256]{2,1,0:T(8,128)(2,1)S(1)} %get-tuple-element.47), channel_id=1, source_target_pairs={{0,7},{1,6},{2,5},{3,4},{4,3},{5,2},{6,1},{7,0},{8,15},{9,14},{10,... | collective-permute-start | bytes 393224 | tf_op jit(solution)/shard_map/ppermute | solution.py:282
  14.7 0.4 collective-permute-done.2.refs_3_
  15.1 0.0 collective-permute-done.3.refs_4_
  15.1 6.6 %collective-permute-done.4.refs_5_ = bf16[2,128,256]{2,1,0:T(8,128)(2,1)S(1)} collective-permute-done((bf16[2,128,256]{2,1,0:T(8,128)(2,1)S(1)}, bf16[2,128,256]{2,1,0:T(8,128)(2,1)S(1)}, u32[]{:S(2)}, u32[]{:S(2)}) %collective-permute-start.4) | collective-permute-done | bytes 131104 | tf_op jit(solution)/shard_map/ppermute | solution.py:282
  21.7 0.0 collective-permute-done.5.refs_6_
  21.7 0.0 collective-permute-done.6.refs_7_
  21.7 0.8 shard_map.68
  22.5 3.2 %collective-permute-start.14 = (bf16[2,512,256]{2,1,0:T(8,128)(2,1)S(1)}, bf16[2,512,256]{2,1,0:T(8,128)(2,1)S(1)}, u32[]{:S(2)}, u32[]{:S(2)}) collective-permute-start(bf16[2,512,256]{2,1,0:T(8,128)(2,1)S(1)} %get-tuple-element.56), channel_id=1, source_target_pairs={{0,8},{8,16},{16,24},{1,9},{9,17},{17,25},{2,10},{10,18},{18,26},{... | collective-permute-start | bytes 1572872 | tf_op jit(solution)/shard_map/ppermute | solution.py:303
  25.7 2.1 %collective-permute-start.22 = (bf16[2,512,256]{2,1,0:T(8,128)(2,1)S(1)}, bf16[2,512,256]{2,1,0:T(8,128)(2,1)S(1)}, u32[]{:S(2)}, u32[]{:S(2)}) collective-permute-start(bf16[2,512,256]{2,1,0:T(8,128)(2,1)S(1)} %get-tuple-element.65), channel_id=1, source_target_pairs={{8,0},{16,8},{24,16},{9,1},{17,9},{25,17},{10,2},{18,10},{26,18},{... | collective-permute-start | bytes 1572872 | tf_op jit(solution)/shard_map/ppermute | solution.py:304
  27.8 0.8 collective-permute-start.7
  28.6 1.2 %collective-permute-start.8 = (bf16[2,128,256]{2,1,0:T(8,128)(2,1)S(1)}, bf16[2,128,256]{2,1,0:T(8,128)(2,1)S(1)}, u32[]{:S(2)}, u32[]{:S(2)}) collective-permute-start(bf16[2,128,256]{2,1,0:T(8,128)(2,1)S(1)} %get-tuple-element.50), channel_id=1, source_target_pairs={{0,2},{1,3},{2,0},{3,1},{4,6},{5,7},{6,4},{7,5},{8,10},{9,11},{10,... | collective-permute-start | bytes 393224 | tf_op jit(solution)/shard_map/ppermute | solution.py:282
  29.8 0.5 collective-permute-start.9
  30.3 1.2 %collective-permute-start.10 = (bf16[2,128,256]{2,1,0:T(8,128)(2,1)S(1)}, bf16[2,128,256]{2,1,0:T(8,128)(2,1)S(1)}, u32[]{:S(2)}, u32[]{:S(2)}) collective-permute-start(bf16[2,128,256]{2,1,0:T(8,128)(2,1)S(1)} %get-tuple-element.52), channel_id=1, source_target_pairs={{0,4},{1,5},{2,6},{3,7},{4,0},{5,1},{6,2},{7,3},{8,12},{9,13},{10,... | collective-permute-start | bytes 393224 | tf_op jit(solution)/shard_map/ppermute | solution.py:282
  31.5 2.1 %collective-permute-done.8.refs_10_ = bf16[2,128,256]{2,1,0:T(8,128)(2,1)S(1)} collective-permute-done((bf16[2,128,256]{2,1,0:T(8,128)(2,1)S(1)}, bf16[2,128,256]{2,1,0:T(8,128)(2,1)S(1)}, u32[]{:S(2)}, u32[]{:S(2)}) %collective-permute-start.8) | collective-permute-done | bytes 131104 | tf_op jit(solution)/shard_map/ppermute | solution.py:282
  33.6 2.4 %collective-permute-start.11 = (bf16[2,128,256]{2,1,0:T(8,128)(2,1)S(1)}, bf16[2,128,256]{2,1,0:T(8,128)(2,1)S(1)}, u32[]{:S(2)}, u32[]{:S(2)}) collective-permute-start(bf16[2,128,256]{2,1,0:T(8,128)(2,1)S(1)} %get-tuple-element.53), channel_id=1, source_target_pairs={{0,5},{1,4},{2,7},{3,6},{4,1},{5,0},{6,3},{7,2},{8,13},{9,12},{10,... | collective-permute-start | bytes 393224 | tf_op jit(solution)/shard_map/ppermute | solution.py:282
  36.1 0.8 collective-permute-done.9.refs_11_
  36.9 2.2 %collective-permute-start.12 = (bf16[2,128,256]{2,1,0:T(8,128)(2,1)S(1)}, bf16[2,128,256]{2,1,0:T(8,128)(2,1)S(1)}, u32[]{:S(2)}, u32[]{:S(2)}) collective-permute-start(bf16[2,128,256]{2,1,0:T(8,128)(2,1)S(1)} %get-tuple-element.54), channel_id=1, source_target_pairs={{0,6},{1,7},{2,4},{3,5},{4,2},{5,3},{6,0},{7,1},{8,14},{9,15},{10,... | collective-permute-start | bytes 393224 | tf_op jit(solution)/shard_map/ppermute | solution.py:282
  39.1 0.0 collective-permute-done.10.refs_12_
  39.1 0.3 collective-permute-start.13
  39.4 1.0 %collective-permute-done.11.refs_13_ = bf16[2,128,256]{2,1,0:T(8,128)(2,1)S(1)} collective-permute-done((bf16[2,128,256]{2,1,0:T(8,128)(2,1)S(1)}, bf16[2,128,256]{2,1,0:T(8,128)(2,1)S(1)}, u32[]{:S(2)}, u32[]{:S(2)}) %collective-permute-start.11) | collective-permute-done | bytes 131104 | tf_op jit(solution)/shard_map/ppermute | solution.py:282
  40.3 2.7 %collective-permute-done.12.refs_14_ = bf16[2,128,256]{2,1,0:T(8,128)(2,1)S(1)} collective-permute-done((bf16[2,128,256]{2,1,0:T(8,128)(2,1)S(1)}, bf16[2,128,256]{2,1,0:T(8,128)(2,1)S(1)}, u32[]{:S(2)}, u32[]{:S(2)}) %collective-permute-start.12) | collective-permute-done | bytes 131104 | tf_op jit(solution)/shard_map/ppermute | solution.py:282
  43.0 2.8 %collective-permute-done.13.refs_15_ = bf16[2,128,256]{2,1,0:T(8,128)(2,1)S(1)} collective-permute-done((bf16[2,128,256]{2,1,0:T(8,128)(2,1)S(1)}, bf16[2,128,256]{2,1,0:T(8,128)(2,1)S(1)}, u32[]{:S(2)}, u32[]{:S(2)}) %collective-permute-start.13) | collective-permute-done | bytes 131104 | tf_op jit(solution)/shard_map/ppermute | solution.py:282
  45.8 12.6 %shard_map.69 = (bf16[128,256]{1,0:T(8,128)(2,1)S(1)}, bf16[128,256]{1,0:T(8,128)(2,1)S(1)}, bf16[128,256]{1,0:T(8,128)(2,1)S(1)}, bf16[128,256]{1,0:T(8,128)(2,...) custom-call(bf16[2,128,256]{2,1,0:T(8,128)(2,1)S(1)} %get-tuple-elem, ...), custom_call_target="tpu_custom_call" | custom-call | tf_op jit(solution)/shard_map/pallas_call | solution.py:269
  58.5 0.4 collective-permute-start.15
  58.9 2.1 %collective-permute-start.23 = (f32[8,512]{1,0:T(8,128)S(1)}, f32[8,512]{1,0:T(8,128)S(1)}, u32[]{:S(2)}, u32[]{:S(2)}) collective-permute-start(f32[8,512]{1,0:T(8,128)S(1)} %get-tuple-element.68), channel_id=1, source_target_pairs={{8,0},{16,8},{24,16},{9,1},{17,9},{25,17},{10,2},{18,10},{26,18},{... | collective-permute-start | bytes 49160 | tf_op jit(solution)/shard_map/ppermute | solution.py:323
  61.0 1.3 %collective-permute-start.16 = (bf16[128,256]{1,0:T(8,128)(2,1)S(1)}, bf16[128,256]{1,0:T(8,128)(2,1)S(1)}, u32[]{:S(2)}, u32[]{:S(2)}) collective-permute-start(bf16[128,256]{1,0:T(8,128)(2,1)S(1)} %get-tuple-element.59), channel_id=1, source_target_pairs={{0,2},{1,3},{2,0},{3,1},{4,6},{5,7},{6,4},{7,5},{8,10},{9,11},{10,... | collective-permute-start | bytes 196616 | tf_op jit(solution)/shard_map/ppermute | solution.py:282
  62.3 0.9 collective-permute-start.17
  63.2 0.0 collective-permute-done.22.refs_8_
  63.2 1.2 %collective-permute-start.18 = (bf16[128,256]{1,0:T(8,128)(2,1)S(1)}, bf16[128,256]{1,0:T(8,128)(2,1)S(1)}, u32[]{:S(2)}, u32[]{:S(2)}) collective-permute-start(bf16[128,256]{1,0:T(8,128)(2,1)S(1)} %get-tuple-element.61), channel_id=1, source_target_pairs={{0,4},{1,5},{2,6},{3,7},{4,0},{5,1},{6,2},{7,3},{8,12},{9,13},{10,... | collective-permute-start | bytes 196616 | tf_op jit(solution)/shard_map/ppermute | solution.py:282
  64.4 2.5 %shard_map.70 = (bf16[2,128,256]{2,1,0:T(8,128)(2,1)S(1)}, bf16[2,128,256]{2,1,0:T(8,128)(2,1)S(1)}, bf16[2,128,256]{2,1,0:T(8,128)(2,1)S(1)}, bf16[2,128,256]{2...) custom-call(bf16[2,128,256]{2,1,0:T(8,128)(2,1)S(1)} %get-tuple-elem, ...), custom_call_target="tpu_custom_call" | custom-call | tf_op jit(solution)/shard_map/pallas_call | solution.py:269
  67.0 0.3 collective-permute-start.24
  67.3 0.0 collective-permute-done.15.refs_1_
  67.3 1.2 %collective-permute-start.25 = (bf16[2,128,256]{2,1,0:T(8,128)(2,1)S(1)}, bf16[2,128,256]{2,1,0:T(8,128)(2,1)S(1)}, u32[]{:S(2)}, u32[]{:S(2)}) collective-permute-start(bf16[2,128,256]{2,1,0:T(8,128)(2,1)S(1)} %get-tuple-element.71), channel_id=1, source_target_pairs={{0,2},{1,3},{2,0},{3,1},{4,6},{5,7},{6,4},{7,5},{8,10},{9,11},{10,... | collective-permute-start | bytes 393224 | tf_op jit(solution)/shard_map/ppermute | solution.py:282
  68.5 1.6 %collective-permute-start.19 = (bf16[128,256]{1,0:T(8,128)(2,1)S(1)}, bf16[128,256]{1,0:T(8,128)(2,1)S(1)}, u32[]{:S(2)}, u32[]{:S(2)}) collective-permute-start(bf16[128,256]{1,0:T(8,128)(2,1)S(1)} %get-tuple-element.62), channel_id=1, source_target_pairs={{0,5},{1,4},{2,7},{3,6},{4,1},{5,0},{6,3},{7,2},{8,13},{9,12},{10,... | collective-permute-start | bytes 196616 | tf_op jit(solution)/shard_map/ppermute | solution.py:282
  70.1 0.0 collective-permute-done.17.refs_3_
  70.1 0.2 collective-permute-start.20
  70.4 0.0 collective-permute-done.18.refs_4_
  70.4 2.4 %collective-permute-start.21 = (bf16[128,256]{1,0:T(8,128)(2,1)S(1)}, bf16[128,256]{1,0:T(8,128)(2,1)S(1)}, u32[]{:S(2)}, u32[]{:S(2)}) collective-permute-start(bf16[128,256]{1,0:T(8,128)(2,1)S(1)} %get-tuple-element.64), channel_id=1, source_target_pairs={{0,7},{1,6},{2,5},{3,4},{4,3},{5,2},{6,1},{7,0},{8,15},{9,14},{10,... | collective-permute-start | bytes 196616 | tf_op jit(solution)/shard_map/ppermute | solution.py:282
  72.8 0.0 collective-permute-done.19.refs_5_
  72.8 0.5 collective-permute-start.26
  73.4 1.5 %collective-permute-done.20.refs_6_ = bf16[128,256]{1,0:T(8,128)(2,1)S(1)} collective-permute-done((bf16[128,256]{1,0:T(8,128)(2,1)S(1)}, bf16[128,256]{1,0:T(8,128)(2,1)S(1)}, u32[]{:S(2)}, u32[]{:S(2)}) %collective-permute-start.20) | collective-permute-done | bytes 65568 | tf_op jit(solution)/shard_map/ppermute | solution.py:282
  74.9 2.1 %collective-permute-start.27 = (bf16[2,128,256]{2,1,0:T(8,128)(2,1)S(1)}, bf16[2,128,256]{2,1,0:T(8,128)(2,1)S(1)}, u32[]{:S(2)}, u32[]{:S(2)}) collective-permute-start(bf16[2,128,256]{2,1,0:T(8,128)(2,1)S(1)} %get-tuple-element.73), channel_id=1, source_target_pairs={{0,4},{1,5},{2,6},{3,7},{4,0},{5,1},{6,2},{7,3},{8,12},{9,13},{10,... | collective-permute-start | bytes 393224 | tf_op jit(solution)/shard_map/ppermute | solution.py:282
  77.0 0.7 collective-permute-start.28
  77.7 0.0 collective-permute-done.24.refs_9_
  77.7 2.5 %collective-permute-start.29 = (bf16[2,128,256]{2,1,0:T(8,128)(2,1)S(1)}, bf16[2,128,256]{2,1,0:T(8,128)(2,1)S(1)}, u32[]{:S(2)}, u32[]{:S(2)}) collective-permute-start(bf16[2,128,256]{2,1,0:T(8,128)(2,1)S(1)} %get-tuple-element.75), channel_id=1, source_target_pairs={{0,6},{1,7},{2,4},{3,5},{4,2},{5,3},{6,0},{7,1},{8,14},{9,15},{10,... | collective-permute-start | bytes 393224 | tf_op jit(solution)/shard_map/ppermute | solution.py:282
  80.3 0.0 collective-permute-done.25.refs_10_
  80.3 0.0 collective-permute-start.30
  80.3 0.0 collective-permute-done.26.refs_11_
  80.3 5.5 %collective-permute-done.27.refs_12_ = bf16[2,128,256]{2,1,0:T(8,128)(2,1)S(1)} collective-permute-done((bf16[2,128,256]{2,1,0:T(8,128)(2,1)S(1)}, bf16[2,128,256]{2,1,0:T(8,128)(2,1)S(1)}, u32[]{:S(2)}, u32[]{:S(2)}) %collective-permute-start.27) | collective-permute-done | bytes 131104 | tf_op jit(solution)/shard_map/ppermute | solution.py:282
  85.8 3.4 %collective-permute-done.28.refs_13_ = bf16[2,128,256]{2,1,0:T(8,128)(2,1)S(1)} collective-permute-done((bf16[2,128,256]{2,1,0:T(8,128)(2,1)S(1)}, bf16[2,128,256]{2,1,0:T(8,128)(2,1)S(1)}, u32[]{:S(2)}, u32[]{:S(2)}) %collective-permute-start.28) | collective-permute-done | bytes 131104 | tf_op jit(solution)/shard_map/ppermute | solution.py:282
  89.2 1.3 %shard_map.71 = (bf16[128,2048]{1,0:T(8,128)(2,1)}, bf16[128,2048]{1,0:T(8,128)(2,1)}, bf16[128,2048]{1,0:T(8,128)(2,1)}) custom-call(bf16[128,256]{1,0:T(8,128)(2,1)S(1)} %get-tuple-element.57.refs_0_, bf16[128,256]{1,0:T(8,128)(2,1)S(1)} %collective-permute-done.15.refs_1_, bf16[128,256]{1,0:T(8,128)(2,1)S(1)} %collective-permute-done.16.refs_2_, ...), custom_call_target="tpu_custom_call" | custom-call | tf_op jit(solution)/shard_map/pallas_call | solution.py:269
  (11 shorter events, 0.0 us)
Async XLA Ops:
  0.6 1.0 %copy-start = (bf16[128,2048]{1,0:T(8,128)(2,1)S(1)}, bf16[128,2048]{1,0:T(8,128)(2,1)}, u32[]{:S(2)}) copy-start(bf16[128,2048]{1,0:T(8,128)(2,1)} %refs_0_.1) | copy-start | bytes 1572868
  1.7 1.0 %copy-start.1 = (bf16[128,2048]{1,0:T(8,128)(2,1)S(1)}, bf16[128,2048]{1,0:T(8,128)(2,1)}, u32[]{:S(2)}) copy-start(bf16[128,2048]{1,0:T(8,128)(2,1)} %refs_1_.1) | copy-start | bytes 1572868
  2.7 1.0 %copy-start.2 = (bf16[128,2048]{1,0:T(8,128)(2,1)S(1)}, bf16[128,2048]{1,0:T(8,128)(2,1)}, u32[]{:S(2)}) copy-start(bf16[128,2048]{1,0:T(8,128)(2,1)} %refs_2_.1) | copy-start | bytes 1572868
  3.8 1.0 %copy-start.3 = (bf16[128,2048]{1,0:T(8,128)(2,1)S(1)}, bf16[128,2048]{1,0:T(8,128)(2,1)}, u32[]{:S(2)}) copy-start(bf16[128,2048]{1,0:T(8,128)(2,1)} %refs_3_.1) | copy-start | bytes 1572868
  5.6 4.3 %collective-permute-start = (bf16[2,128,256]{2,1,0:T(8,128)(2,1)S(1)}, bf16[2,128,256]{2,1,0:T(8,128)(2,1)S(1)}, u32[]{:S(2)}, u32[]{:S(2)}) collective-permute-start(bf16[2,128,256]{2,1,0:T(8,128)(2,1)S(1)} %get-tuple-element.41), channel_id=1, source_target_pairs={{0,1},{1,0},{2,3},{3,2},{4,5},{5,4},{6,7},{7,6},{8,9},{9,8},{10,11... | collective-permute-start | bytes 393224 | tf_op jit(solution)/shard_map/ppermute | solution.py:282
  6.3 5.7 %collective-permute-start.1 = (bf16[2,128,256]{2,1,0:T(8,128)(2,1)S(1)}, bf16[2,128,256]{2,1,0:T(8,128)(2,1)S(1)}, u32[]{:S(2)}, u32[]{:S(2)}) collective-permute-start(bf16[2,128,256]{2,1,0:T(8,128)(2,1)S(1)} %get-tuple-element.42), channel_id=1, source_target_pairs={{0,2},{1,3},{2,0},{3,1},{4,6},{5,7},{6,4},{7,5},{8,10},{9,11},{10,... | collective-permute-start | bytes 393224 | tf_op jit(solution)/shard_map/ppermute | solution.py:282
  7.5 7.6 %collective-permute-start.2 = (bf16[2,128,256]{2,1,0:T(8,128)(2,1)S(1)}, bf16[2,128,256]{2,1,0:T(8,128)(2,1)S(1)}, u32[]{:S(2)}, u32[]{:S(2)}) collective-permute-start(bf16[2,128,256]{2,1,0:T(8,128)(2,1)S(1)} %get-tuple-element.43), channel_id=1, source_target_pairs={{0,3},{1,2},{2,1},{3,0},{4,7},{5,6},{6,5},{7,4},{8,11},{9,10},{10,... | collective-permute-start | bytes 393224 | tf_op jit(solution)/shard_map/ppermute | solution.py:282
  8.0 7.1 %collective-permute-start.3 = (bf16[2,128,256]{2,1,0:T(8,128)(2,1)S(1)}, bf16[2,128,256]{2,1,0:T(8,128)(2,1)S(1)}, u32[]{:S(2)}, u32[]{:S(2)}) collective-permute-start(bf16[2,128,256]{2,1,0:T(8,128)(2,1)S(1)} %get-tuple-element.44), channel_id=1, source_target_pairs={{0,4},{1,5},{2,6},{3,7},{4,0},{5,1},{6,2},{7,3},{8,12},{9,13},{10,... | collective-permute-start | bytes 393224 | tf_op jit(solution)/shard_map/ppermute | solution.py:282
  9.2 12.4 %collective-permute-start.4 = (bf16[2,128,256]{2,1,0:T(8,128)(2,1)S(1)}, bf16[2,128,256]{2,1,0:T(8,128)(2,1)S(1)}, u32[]{:S(2)}, u32[]{:S(2)}) collective-permute-start(bf16[2,128,256]{2,1,0:T(8,128)(2,1)S(1)} %get-tuple-element.45), channel_id=1, source_target_pairs={{0,5},{1,4},{2,7},{3,6},{4,1},{5,0},{6,3},{7,2},{8,13},{9,12},{10,... | collective-permute-start | bytes 393224 | tf_op jit(solution)/shard_map/ppermute | solution.py:282
  9.8 11.9 %collective-permute-start.5 = (bf16[2,128,256]{2,1,0:T(8,128)(2,1)S(1)}, bf16[2,128,256]{2,1,0:T(8,128)(2,1)S(1)}, u32[]{:S(2)}, u32[]{:S(2)}) collective-permute-start(bf16[2,128,256]{2,1,0:T(8,128)(2,1)S(1)} %get-tuple-element.46), channel_id=1, source_target_pairs={{0,6},{1,7},{2,4},{3,5},{4,2},{5,3},{6,0},{7,1},{8,14},{9,15},{10,... | collective-permute-start | bytes 393224 | tf_op jit(solution)/shard_map/ppermute | solution.py:282
  12.0 9.7 %collective-permute-start.6 = (bf16[2,128,256]{2,1,0:T(8,128)(2,1)S(1)}, bf16[2,128,256]{2,1,0:T(8,128)(2,1)S(1)}, u32[]{:S(2)}, u32[]{:S(2)}) collective-permute-start(bf16[2,128,256]{2,1,0:T(8,128)(2,1)S(1)} %get-tuple-element.47), channel_id=1, source_target_pairs={{0,7},{1,6},{2,5},{3,4},{4,3},{5,2},{6,1},{7,0},{8,15},{9,14},{10,... | collective-permute-start | bytes 393224 | tf_op jit(solution)/shard_map/ppermute | solution.py:282
  22.5 23.3 %collective-permute-start.14 = (bf16[2,512,256]{2,1,0:T(8,128)(2,1)S(1)}, bf16[2,512,256]{2,1,0:T(8,128)(2,1)S(1)}, u32[]{:S(2)}, u32[]{:S(2)}) collective-permute-start(bf16[2,512,256]{2,1,0:T(8,128)(2,1)S(1)} %get-tuple-element.56), channel_id=1, source_target_pairs={{0,8},{8,16},{16,24},{1,9},{9,17},{17,25},{2,10},{10,18},{18,26},{... | collective-permute-start | bytes 1572872 | tf_op jit(solution)/shard_map/ppermute | solution.py:303
  25.7 37.5 %collective-permute-start.22 = (bf16[2,512,256]{2,1,0:T(8,128)(2,1)S(1)}, bf16[2,512,256]{2,1,0:T(8,128)(2,1)S(1)}, u32[]{:S(2)}, u32[]{:S(2)}) collective-permute-start(bf16[2,512,256]{2,1,0:T(8,128)(2,1)S(1)} %get-tuple-element.65), channel_id=1, source_target_pairs={{8,0},{16,8},{24,16},{9,1},{17,9},{25,17},{10,2},{18,10},{26,18},{... | collective-permute-start | bytes 1572872 | tf_op jit(solution)/shard_map/ppermute | solution.py:304
  27.8 2.5 %collective-permute-start.7 = (bf16[2,128,256]{2,1,0:T(8,128)(2,1)S(1)}, bf16[2,128,256]{2,1,0:T(8,128)(2,1)S(1)}, u32[]{:S(2)}, u32[]{:S(2)}) collective-permute-start(bf16[2,128,256]{2,1,0:T(8,128)(2,1)S(1)} %get-tuple-element.49), channel_id=1, source_target_pairs={{0,1},{1,0},{2,3},{3,2},{4,5},{5,4},{6,7},{7,6},{8,9},{9,8},{10,11... | collective-permute-start | bytes 393224 | tf_op jit(solution)/shard_map/ppermute | solution.py:282
  28.6 5.1 %collective-permute-start.8 = (bf16[2,128,256]{2,1,0:T(8,128)(2,1)S(1)}, bf16[2,128,256]{2,1,0:T(8,128)(2,1)S(1)}, u32[]{:S(2)}, u32[]{:S(2)}) collective-permute-start(bf16[2,128,256]{2,1,0:T(8,128)(2,1)S(1)} %get-tuple-element.50), channel_id=1, source_target_pairs={{0,2},{1,3},{2,0},{3,1},{4,6},{5,7},{6,4},{7,5},{8,10},{9,11},{10,... | collective-permute-start | bytes 393224 | tf_op jit(solution)/shard_map/ppermute | solution.py:282
  29.8 7.1 %collective-permute-start.9 = (bf16[2,128,256]{2,1,0:T(8,128)(2,1)S(1)}, bf16[2,128,256]{2,1,0:T(8,128)(2,1)S(1)}, u32[]{:S(2)}, u32[]{:S(2)}) collective-permute-start(bf16[2,128,256]{2,1,0:T(8,128)(2,1)S(1)} %get-tuple-element.51), channel_id=1, source_target_pairs={{0,3},{1,2},{2,1},{3,0},{4,7},{5,6},{6,5},{7,4},{8,11},{9,10},{10,... | collective-permute-start | bytes 393224 | tf_op jit(solution)/shard_map/ppermute | solution.py:282
  30.3 8.8 %collective-permute-start.10 = (bf16[2,128,256]{2,1,0:T(8,128)(2,1)S(1)}, bf16[2,128,256]{2,1,0:T(8,128)(2,1)S(1)}, u32[]{:S(2)}, u32[]{:S(2)}) collective-permute-start(bf16[2,128,256]{2,1,0:T(8,128)(2,1)S(1)} %get-tuple-element.52), channel_id=1, source_target_pairs={{0,4},{1,5},{2,6},{3,7},{4,0},{5,1},{6,2},{7,3},{8,12},{9,13},{10,... | collective-permute-start | bytes 393224 | tf_op jit(solution)/shard_map/ppermute | solution.py:282
  33.6 6.7 %collective-permute-start.11 = (bf16[2,128,256]{2,1,0:T(8,128)(2,1)S(1)}, bf16[2,128,256]{2,1,0:T(8,128)(2,1)S(1)}, u32[]{:S(2)}, u32[]{:S(2)}) collective-permute-start(bf16[2,128,256]{2,1,0:T(8,128)(2,1)S(1)} %get-tuple-element.53), channel_id=1, source_target_pairs={{0,5},{1,4},{2,7},{3,6},{4,1},{5,0},{6,3},{7,2},{8,13},{9,12},{10,... | collective-permute-start | bytes 393224 | tf_op jit(solution)/shard_map/ppermute | solution.py:282
  36.9 6.1 %collective-permute-start.12 = (bf16[2,128,256]{2,1,0:T(8,128)(2,1)S(1)}, bf16[2,128,256]{2,1,0:T(8,128)(2,1)S(1)}, u32[]{:S(2)}, u32[]{:S(2)}) collective-permute-start(bf16[2,128,256]{2,1,0:T(8,128)(2,1)S(1)} %get-tuple-element.54), channel_id=1, source_target_pairs={{0,6},{1,7},{2,4},{3,5},{4,2},{5,3},{6,0},{7,1},{8,14},{9,15},{10,... | collective-permute-start | bytes 393224 | tf_op jit(solution)/shard_map/ppermute | solution.py:282
  39.1 6.8 %collective-permute-start.13 = (bf16[2,128,256]{2,1,0:T(8,128)(2,1)S(1)}, bf16[2,128,256]{2,1,0:T(8,128)(2,1)S(1)}, u32[]{:S(2)}, u32[]{:S(2)}) collective-permute-start(bf16[2,128,256]{2,1,0:T(8,128)(2,1)S(1)} %get-tuple-element.55), channel_id=1, source_target_pairs={{0,7},{1,6},{2,5},{3,4},{4,3},{5,2},{6,1},{7,0},{8,15},{9,14},{10,... | collective-permute-start | bytes 393224 | tf_op jit(solution)/shard_map/ppermute | solution.py:282
  58.5 8.8 %collective-permute-start.15 = (bf16[128,256]{1,0:T(8,128)(2,1)S(1)}, bf16[128,256]{1,0:T(8,128)(2,1)S(1)}, u32[]{:S(2)}, u32[]{:S(2)}) collective-permute-start(bf16[128,256]{1,0:T(8,128)(2,1)S(1)} %get-tuple-element.58), channel_id=1, source_target_pairs={{0,1},{1,0},{2,3},{3,2},{4,5},{5,4},{6,7},{7,6},{8,9},{9,8},{10,11... | collective-permute-start | bytes 196616 | tf_op jit(solution)/shard_map/ppermute | solution.py:282
  58.9 5.5 %collective-permute-start.23 = (f32[8,512]{1,0:T(8,128)S(1)}, f32[8,512]{1,0:T(8,128)S(1)}, u32[]{:S(2)}, u32[]{:S(2)}) collective-permute-start(f32[8,512]{1,0:T(8,128)S(1)} %get-tuple-element.68), channel_id=1, source_target_pairs={{8,0},{16,8},{24,16},{9,1},{17,9},{25,17},{10,2},{18,10},{26,18},{... | collective-permute-start | bytes 49160 | tf_op jit(solution)/shard_map/ppermute | solution.py:323
  61.0 7.5 %collective-permute-start.16 = (bf16[128,256]{1,0:T(8,128)(2,1)S(1)}, bf16[128,256]{1,0:T(8,128)(2,1)S(1)}, u32[]{:S(2)}, u32[]{:S(2)}) collective-permute-start(bf16[128,256]{1,0:T(8,128)(2,1)S(1)} %get-tuple-element.59), channel_id=1, source_target_pairs={{0,2},{1,3},{2,0},{3,1},{4,6},{5,7},{6,4},{7,5},{8,10},{9,11},{10,... | collective-permute-start | bytes 196616 | tf_op jit(solution)/shard_map/ppermute | solution.py:282
  62.3 7.8 %collective-permute-start.17 = (bf16[128,256]{1,0:T(8,128)(2,1)S(1)}, bf16[128,256]{1,0:T(8,128)(2,1)S(1)}, u32[]{:S(2)}, u32[]{:S(2)}) collective-permute-start(bf16[128,256]{1,0:T(8,128)(2,1)S(1)} %get-tuple-element.60), channel_id=1, source_target_pairs={{0,3},{1,2},{2,1},{3,0},{4,7},{5,6},{6,5},{7,4},{8,11},{9,10},{10,... | collective-permute-start | bytes 196616 | tf_op jit(solution)/shard_map/ppermute | solution.py:282
  63.2 7.2 %collective-permute-start.18 = (bf16[128,256]{1,0:T(8,128)(2,1)S(1)}, bf16[128,256]{1,0:T(8,128)(2,1)S(1)}, u32[]{:S(2)}, u32[]{:S(2)}) collective-permute-start(bf16[128,256]{1,0:T(8,128)(2,1)S(1)} %get-tuple-element.61), channel_id=1, source_target_pairs={{0,4},{1,5},{2,6},{3,7},{4,0},{5,1},{6,2},{7,3},{8,12},{9,13},{10,... | collective-permute-start | bytes 196616 | tf_op jit(solution)/shard_map/ppermute | solution.py:282
  67.0 10.8 %collective-permute-start.24 = (bf16[2,128,256]{2,1,0:T(8,128)(2,1)S(1)}, bf16[2,128,256]{2,1,0:T(8,128)(2,1)S(1)}, u32[]{:S(2)}, u32[]{:S(2)}) collective-permute-start(bf16[2,128,256]{2,1,0:T(8,128)(2,1)S(1)} %get-tuple-element.70), channel_id=1, source_target_pairs={{0,1},{1,0},{2,3},{3,2},{4,5},{5,4},{6,7},{7,6},{8,9},{9,8},{10,11... | collective-permute-start | bytes 393224 | tf_op jit(solution)/shard_map/ppermute | solution.py:282
  67.3 12.9 %collective-permute-start.25 = (bf16[2,128,256]{2,1,0:T(8,128)(2,1)S(1)}, bf16[2,128,256]{2,1,0:T(8,128)(2,1)S(1)}, u32[]{:S(2)}, u32[]{:S(2)}) collective-permute-start(bf16[2,128,256]{2,1,0:T(8,128)(2,1)S(1)} %get-tuple-element.71), channel_id=1, source_target_pairs={{0,2},{1,3},{2,0},{3,1},{4,6},{5,7},{6,4},{7,5},{8,10},{9,11},{10,... | collective-permute-start | bytes 393224 | tf_op jit(solution)/shard_map/ppermute | solution.py:282
  68.5 4.3 %collective-permute-start.19 = (bf16[128,256]{1,0:T(8,128)(2,1)S(1)}, bf16[128,256]{1,0:T(8,128)(2,1)S(1)}, u32[]{:S(2)}, u32[]{:S(2)}) collective-permute-start(bf16[128,256]{1,0:T(8,128)(2,1)S(1)} %get-tuple-element.62), channel_id=1, source_target_pairs={{0,5},{1,4},{2,7},{3,6},{4,1},{5,0},{6,3},{7,2},{8,13},{9,12},{10,... | collective-permute-start | bytes 196616 | tf_op jit(solution)/shard_map/ppermute | solution.py:282
  70.1 4.8 %collective-permute-start.20 = (bf16[128,256]{1,0:T(8,128)(2,1)S(1)}, bf16[128,256]{1,0:T(8,128)(2,1)S(1)}, u32[]{:S(2)}, u32[]{:S(2)}) collective-permute-start(bf16[128,256]{1,0:T(8,128)(2,1)S(1)} %get-tuple-element.63), channel_id=1, source_target_pairs={{0,6},{1,7},{2,4},{3,5},{4,2},{5,3},{6,0},{7,1},{8,14},{9,15},{10,... | collective-permute-start | bytes 196616 | tf_op jit(solution)/shard_map/ppermute | solution.py:282
  70.4 6.7 %collective-permute-start.21 = (bf16[128,256]{1,0:T(8,128)(2,1)S(1)}, bf16[128,256]{1,0:T(8,128)(2,1)S(1)}, u32[]{:S(2)}, u32[]{:S(2)}) collective-permute-start(bf16[128,256]{1,0:T(8,128)(2,1)S(1)} %get-tuple-element.64), channel_id=1, source_target_pairs={{0,7},{1,6},{2,5},{3,4},{4,3},{5,2},{6,1},{7,0},{8,15},{9,14},{10,... | collective-permute-start | bytes 196616 | tf_op jit(solution)/shard_map/ppermute | solution.py:282
  72.8 7.4 %collective-permute-start.26 = (bf16[2,128,256]{2,1,0:T(8,128)(2,1)S(1)}, bf16[2,128,256]{2,1,0:T(8,128)(2,1)S(1)}, u32[]{:S(2)}, u32[]{:S(2)}) collective-permute-start(bf16[2,128,256]{2,1,0:T(8,128)(2,1)S(1)} %get-tuple-element.72), channel_id=1, source_target_pairs={{0,3},{1,2},{2,1},{3,0},{4,7},{5,6},{6,5},{7,4},{8,11},{9,10},{10,... | collective-permute-start | bytes 393224 | tf_op jit(solution)/shard_map/ppermute | solution.py:282
  74.9 10.9 %collective-permute-start.27 = (bf16[2,128,256]{2,1,0:T(8,128)(2,1)S(1)}, bf16[2,128,256]{2,1,0:T(8,128)(2,1)S(1)}, u32[]{:S(2)}, u32[]{:S(2)}) collective-permute-start(bf16[2,128,256]{2,1,0:T(8,128)(2,1)S(1)} %get-tuple-element.73), channel_id=1, source_target_pairs={{0,4},{1,5},{2,6},{3,7},{4,0},{5,1},{6,2},{7,3},{8,12},{9,13},{10,... | collective-permute-start | bytes 393224 | tf_op jit(solution)/shard_map/ppermute | solution.py:282
  77.0 12.2 %collective-permute-start.28 = (bf16[2,128,256]{2,1,0:T(8,128)(2,1)S(1)}, bf16[2,128,256]{2,1,0:T(8,128)(2,1)S(1)}, u32[]{:S(2)}, u32[]{:S(2)}) collective-permute-start(bf16[2,128,256]{2,1,0:T(8,128)(2,1)S(1)} %get-tuple-element.74), channel_id=1, source_target_pairs={{0,5},{1,4},{2,7},{3,6},{4,1},{5,0},{6,3},{7,2},{8,13},{9,12},{10,... | collective-permute-start | bytes 393224 | tf_op jit(solution)/shard_map/ppermute | solution.py:282
  77.7 11.5 %collective-permute-start.29 = (bf16[2,128,256]{2,1,0:T(8,128)(2,1)S(1)}, bf16[2,128,256]{2,1,0:T(8,128)(2,1)S(1)}, u32[]{:S(2)}, u32[]{:S(2)}) collective-permute-start(bf16[2,128,256]{2,1,0:T(8,128)(2,1)S(1)} %get-tuple-element.75), channel_id=1, source_target_pairs={{0,6},{1,7},{2,4},{3,5},{4,2},{5,3},{6,0},{7,1},{8,14},{9,15},{10,... | collective-permute-start | bytes 393224 | tf_op jit(solution)/shard_map/ppermute | solution.py:282
  80.3 9.0 %collective-permute-start.30 = (bf16[2,128,256]{2,1,0:T(8,128)(2,1)S(1)}, bf16[2,128,256]{2,1,0:T(8,128)(2,1)S(1)}, u32[]{:S(2)}, u32[]{:S(2)}) collective-permute-start(bf16[2,128,256]{2,1,0:T(8,128)(2,1)S(1)} %get-tuple-element.76), channel_id=1, source_target_pairs={{0,7},{1,6},{2,5},{3,4},{4,3},{5,2},{6,1},{7,0},{8,15},{9,14},{10,... | collective-permute-start | bytes 393224 | tf_op jit(solution)/shard_map/ppermute | solution.py:282

commit v2 on v1

v2 whole, which is shorter than its diff:
```python
import functools
import math

import jax
import jax.numpy as jnp
from jax import lax
from jax.experimental import pallas as pl
from jax.experimental.pallas import tpu as pltpu
from jax.sharding import Mesh, PartitionSpec as P

HEADS = 16
HEAD_DIM = 128
WINDOW = 512
TILE = 256
HALF = 128
AXES = ("chunk", "part", "head")
GROUP = ("part", "head")
SCALE = HEAD_DIM ** (-0.5)
SCALE_LOG2 = SCALE * math.log2(math.e)
MASKED = -1e30
VMEM_LIMIT = 48 * 1024 * 1024
NT = ((1,), (1,))
NN = ((1,), (0,))
ORDER = (0, 1, 6, 7, 2, 4, 3, 5)
LATE_FLOPS = 16000000000
HALO_FLOPS = 0


def bf16(*shape):
    return jax.ShapeDtypeStruct(shape, jnp.bfloat16)


def f32(*shape):
    return jax.ShapeDtypeStruct(shape, jnp.float32)


def group_index():
    return lax.axis_index("part") * lax.axis_size("head") + lax.axis_index("head")


def group_size():
    return lax.axis_size("part") * lax.axis_size("head")


def aligned(index, step):
    return pl.multiple_of(index * step, step)


def copy_all(pairs, sems):
    copies = [pltpu.make_async_copy(src, dst, sems.at[i]) for i, (src, dst) in enumerate(pairs)]
    for copy in copies:
        copy.start()
    for copy in copies:
        copy.wait()


def copy_where(conditions, sems):
    for phase in range(2):
        for slot, flag, src, dst in conditions:

            @pl.when(flag)
            def _():
                copy = pltpu.make_async_copy(src, dst, sems.at[slot])
                copy.start() if phase == 0 else copy.wait()


def dot(a, b, dims):
    return lax.dot_general(a, b, (dims, ((), ())), preferred_element_type=jnp.float32)


def pack_kernel(n, *refs):
    sources = refs[:4]
    crit = refs[4 : 4 + n]
    rest = refs[4 + n : 4 + 2 * n]
    stage, sems = refs[4 + 2 * n :]
    me = group_index()
    width = stage.shape[2] // n
    late = (me >= n // 2).astype(jnp.int32)
    copy_all([(source, stage.at[i]) for i, source in enumerate(sources)], sems)
    pairs = []
    for m in range(n):
        cols = pl.ds(aligned(jnp.bitwise_xor(me, m), width), width)
        pairs.append((stage.at[pl.ds(2 * late, 2), :, cols], crit[m]))
        pairs.append((stage.at[pl.ds(2 - 2 * late, 2), :, cols], rest[m]))
    copy_all(pairs, sems)


def halo_kernel(n, *refs):
    crit = by_slot(refs[:n])
    kv, qg, sems = refs[n:]
    me = group_index()
    rows = crit[0].shape[1]
    ends = WINDOW // rows
    copies = []
    for m in range(n):
        other = jnp.bitwise_xor(me, m)
        at = pl.ds(aligned(other - (n - ends), rows), rows)
        copies.append((m, other >= n - ends, crit[m], kv.at[:, at]))
        at = pl.ds(aligned(other, rows), rows)
        copies.append((m, other < ends, crit[m], qg.at[:, at]))
    copy_where(copies, sems)


def softmax_block(qb, gb, kb, vb, bias, blind):
    row = lax.broadcasted_iota(jnp.int32, (HALF, HALF), 0)
    col = lax.broadcasted_iota(jnp.int32, (HALF, HALF), 1)
    s = dot(kb, qb, NT)
    dp = dot(vb, gb, NT)
    span = WINDOW // HALF + 1
    nothing = jnp.zeros((HALF, HALF), jnp.bfloat16)
    p_parts, ds_parts, stats = [], [], []
    for c in range(TILE // HALF):
        cols = slice(c * HALF, (c + 1) * HALF)
        parts = [s[(c + r) * HALF : (c + r + 1) * HALF, cols] for r in range(span)]
        parts[0] = jnp.where(row > col, parts[0], MASKED)
        parts[-1] = jnp.where(row <= col, parts[-1], MASKED)
        parts = [b + bias if (c + r) * HALF < blind else b for r, b in enumerate(parts)]
        sc = jnp.concatenate(parts, axis=0)
        dpc = dp[c * HALF : (c + span) * HALF, cols]
        top = jnp.max(sc, axis=0, keepdims=True) * SCALE_LOG2
        e = jnp.exp2(sc * SCALE_LOG2 - top)
        inverse = 1.0 / jnp.sum(e, axis=0, keepdims=True)
        p = e * inverse
        dots = jnp.sum(p * dpc, axis=0, keepdims=True)
        ds = (p * (dpc - dots)).astype(jnp.bfloat16)
        pad = [nothing] * c, [nothing] * (TILE // HALF - 1 - c)
        p_parts.append(jnp.concatenate([*pad[0], p.astype(jnp.bfloat16), *pad[1]], axis=0))
        ds_parts.append(jnp.concatenate([*pad[0], ds, *pad[1]], axis=0))
        stats.append((top, inverse, dots))
    return jnp.concatenate(p_parts, axis=1), jnp.concatenate(ds_parts, axis=1), stats


def late_kernel(n, heads, *refs):
    crit = by_slot(refs[:n])
    rest = by_slot(refs[n : 2 * n])
    dq_out, dkv_out, x, dq, dkv, sems = refs[2 * n :]
    me = group_index()
    rows = crit[0].shape[1]
    total = n * rows
    pairs = []
    for m in range(n):
        other = jnp.bitwise_xor(me, m)
        kind = (other >= n // 2).astype(jnp.int32)
        at = pl.ds(aligned(other, rows), rows)
        pairs.append((crit[m], x.at[pl.ds(2 * kind, 2), at]))
        pairs.append((rest[m], x.at[pl.ds(2 - 2 * kind, 2), at]))
    copy_all(pairs, sems)
    for h in range(heads):
        lanes = slice(h * HEAD_DIM, (h + 1) * HEAD_DIM)
        key_t = x[2, :, lanes].T
        for start in range(0, total - WINDOW, TILE):
            keys = slice(start, start + 3 * TILE)
            mine = slice(start + WINDOW, start + WINDOW + TILE)
            qb, gb = x[0, mine, lanes], x[1, mine, lanes]
            p_low, ds, _ = softmax_block(qb, gb, x[2, keys, lanes], x[3, keys, lanes], 0.0, 0)
            out = slice(start, start + TILE)
            dq[out, lanes] = (dot(key_t[:, keys], ds, NN) * SCALE).T.astype(jnp.bfloat16)
            for t, add in enumerate((dot(ds, qb, NN), dot(p_low, gb, NN))):
                if start == 0:
                    dkv[t, keys, lanes] = add
                else:
                    older = slice(start, start + 2 * TILE)
                    dkv[t, older, lanes] += add[: 2 * TILE]
                    dkv[t, mine, lanes] = add[2 * TILE :]
    copy_all([(dq, dq_out), (dkv, dkv_out)], sems)


def early_kernel(n, heads, *refs):
    crit = by_slot(refs[:n])
    rest = by_slot(refs[n : 2 * n])
    kv_halo, dq_in, dkv_in = refs[2 * n : 2 * n + 3]
    dq_out = refs[2 * n + 3 : 3 * n + 3]
    dkv_out, stat_out, x, dq, dkv, stat, sems = refs[3 * n + 3 :]
    me = group_index()
    first = lax.axis_index("chunk") == 0
    rows = crit[0].shape[1]
    total = n * rows
    ends = WINDOW // rows
    copies = []
    for m in range(n):
        other = jnp.bitwise_xor(me, m)
        need = other < ends
        at = pl.ds(aligned(other, rows), rows)
        copies.append((2 * m, need, crit[m], x.at[pl.ds(0, 2), at]))
        at = pl.ds(pl.multiple_of(WINDOW + other * rows, rows), rows)
        copies.append((2 * m + 1, need, rest[m], x.at[pl.ds(2, 2), at]))
    always = jnp.bool_(True)
    copies.append((2 * n, always, kv_halo, x.at[pl.ds(2, 2), pl.ds(0, WINDOW)]))
    copies.append((2 * n + 1, always, dkv_in.at[:, pl.ds(0, WINDOW)], dkv))
    copies.append((2 * n + 2, always, dq_in, dq.at[pl.ds(WINDOW, total - WINDOW)]))
    copy_where(copies, sems)
    stat[...] = jnp.zeros_like(stat)
    bias = jnp.where(first, MASKED, 0.0)
    for h in range(heads):
        lanes = slice(h * HEAD_DIM, (h + 1) * HEAD_DIM)
        key_t = x[2, :, lanes].T
        for start in range(0, WINDOW, TILE):
            keys = slice(start, start + 3 * TILE)
            mine = slice(start, start + TILE)
            qb, gb = x[0, mine, lanes], x[1, mine, lanes]
            p_low, ds, stats = softmax_block(
                qb, gb, x[2, keys, lanes], x[3, keys, lanes], bias, WINDOW - start
            )
            dq[mine, lanes] = (dot(key_t[:, keys], ds, NN) * SCALE).T.astype(jnp.bfloat16)
            own = slice(0, start + TILE)
            dkv[0, own, lanes] += dot(ds[WINDOW - start :], qb, NN)
            dkv[1, own, lanes] += dot(p_low[WINDOW - start :], gb, NN)
            for c, rows_of in enumerate(stats):
                at = slice(start + c * HALF, start + (c + 1) * HALF)
                for k, value in enumerate(rows_of):
                    stat[3 * h + k : 3 * h + k + 1, at] = value
    x[2, :WINDOW] = (dkv[0] * SCALE).astype(jnp.bfloat16)
    x[3, :WINDOW] = dkv[1].astype(jnp.bfloat16)
    pairs = [(stat, stat_out), (x.at[pl.ds(2, 2), pl.ds(0, WINDOW)], dkv_out)]
    for m in range(n):
        at = pl.ds(aligned(jnp.bitwise_xor(me, m), rows), rows)
        pairs.append((dq.at[at], dq_out[m]))
    copy_all(pairs, sems)


def edge_kernel(n, heads, *refs):
    crit = by_slot(refs[:n])
    qg_halo, front, dkv_in, stat_in = refs[n : n + 4]
    out = refs[n + 4 : 2 * n + 4]
    kv, qg, full, dkv, stat, sems = refs[2 * n + 4 :]
    me = group_index()
    rows = crit[0].shape[1]
    total = n * rows
    done = total - WINDOW
    ends = WINDOW // rows
    always = jnp.bool_(True)
    copies = [
        (n, always, qg_halo, qg),
        (n + 1, always, front, full.at[:, pl.ds(0, WINDOW)]),
        (n + 2, always, dkv_in.at[:, pl.ds(WINDOW, done)], dkv),
        (n + 3, always, stat_in, stat),
    ]
    for m in range(n):
        other = jnp.bitwise_xor(me, m)
        at = pl.ds(aligned(other - (n - ends), rows), rows)
        copies.append((m, other >= n - ends, crit[m], kv.at[:, at]))
    copy_where(copies, sems)
    row = lax.broadcasted_iota(jnp.int32, (TILE, TILE), 0)
    col = lax.broadcasted_iota(jnp.int32, (TILE, TILE), 1)
    for h in range(heads):
        lanes = slice(h * HEAD_DIM, (h + 1) * HEAD_DIM)
        for start in range(0, WINDOW, TILE):
            mine = slice(start, start + TILE)
            keys = slice(start, WINDOW)
            qb, gb = qg[0, mine, lanes], qg[1, mine, lanes]
            s = dot(kv[0, keys, lanes], qb, NT)
            newest = jnp.where(row > col, s[:TILE], MASKED)
            s = newest if len(s) == TILE else jnp.concatenate([newest, s[TILE:]], axis=0)
            top, inverse, dots = (stat[3 * h + k : 3 * h + k + 1, mine] for k in range(3))
            p = jnp.exp2(s * SCALE_LOG2 - top) * inverse
            dp = dot(kv[1, keys, lanes], gb, NT)
            ds = (p * (dp - dots)).astype(jnp.bfloat16)
            at = slice(done - WINDOW + start, done)
            dkv[0, at, lanes] += dot(ds, qb, NN)
            dkv[1, at, lanes] += dot(p.astype(jnp.bfloat16), gb, NN)
    full[0, WINDOW:] = (dkv[0] * SCALE).astype(jnp.bfloat16)
    full[1, WINDOW:] = dkv[1].astype(jnp.bfloat16)
    pairs = []
    for m in range(n):
        at = pl.ds(aligned(jnp.bitwise_xor(me, m), rows), rows)
        pairs.append((full.at[:, at], out[m]))
    copy_all(pairs, sems)


def unpack_kernel(n, *refs):
    dq_in = by_slot(refs[:n])
    dkv_in = by_slot(refs[n : 2 * n])
    dq, dk, dv, sems = refs[2 * n :]
    me = group_index()
    width = dq_in[0].shape[1]
    pairs = []
    for m in range(n):
        cols = pl.ds(aligned(jnp.bitwise_xor(me, m), width), width)
        pairs.append((dq_in[m], dq.at[:, cols]))
        pairs.append((dkv_in[m].at[0], dk.at[:, cols]))
        pairs.append((dkv_in[m].at[1], dv.at[:, cols]))
    copy_all(pairs, sems)


def call(kernel, outs, scratch, sems, *operands, space=pl.ANY, limit=VMEM_LIMIT, flops=0):
    return pl.pallas_call(
        kernel,
        out_shape=outs,
        in_specs=[pl.BlockSpec(memory_space=space)] * len(operands),
        out_specs=jax.tree.map(lambda _: pl.BlockSpec(memory_space=pl.ANY), outs),
        scratch_shapes=[*scratch, pltpu.SemaphoreType.DMA((sems,))],
        compiler_params=pltpu.CompilerParams(vmem_limit_bytes=limit),
        cost_estimate=pl.CostEstimate(flops=flops, bytes_accessed=0, transcendentals=0) if flops else None,
    )(*operands)


def vmem(shape):
    return pltpu.VMEM(shape.shape, shape.dtype)


def order_of(n):
    return [m for m in ORDER if m < n] + list(range(len(ORDER), n))


def by_slot(refs):
    order = order_of(len(refs))
    return [refs[order.index(m)] for m in range(len(refs))]


def exchanged(pieces):
    n = len(pieces)
    return [
        lax.ppermute(pieces[m], GROUP, [(i, i ^ m) for i in range(n)]) if m else pieces[0]
        for m in order_of(n)
    ]


def per_device(queries, key_vectors, value_vectors, grad_output):
    n = group_size()
    chunks = lax.axis_size("chunk")
    rows, model = queries.shape
    heads = HEADS // n
    width = model // n
    total = n * rows
    done = total - WINDOW
    piece = bf16(2, rows, width)
    packed = call(
        functools.partial(pack_kernel, n),
        [piece] * (2 * n),
        [vmem(bf16(4, rows, model))], 2 * n,
        queries, grad_output, key_vectors, value_vectors, space=pltpu.HBM, limit=None,
    )
    crit = exchanged(packed[:n])
    end = bf16(2, WINDOW, width)
    kv_send, qg_send = call(
        functools.partial(halo_kernel, n), [end, end], [], n, *crit, flops=HALO_FLOPS
    )
    forward = [(i, i + 1) for i in range(chunks - 1)]
    backward = [(i + 1, i) for i in range(chunks - 1)]
    kv_halo = lax.ppermute(kv_send, "chunk", forward)
    qg_halo = lax.ppermute(qg_send, "chunk", backward)
    rest = exchanged(packed[n:])
    stat_out = f32(-(-3 * heads // 8) * 8, WINDOW)
    partial_out = f32(2, total, width)
    dq_late, partial = call(
        functools.partial(late_kernel, n, heads),
        [bf16(done, width), partial_out],
        [vmem(bf16(4, total, width)), vmem(bf16(done, width)), vmem(partial_out)], 2 * n,
        *crit, *rest, flops=LATE_FLOPS,
    )
    *dq, front, stat = call(
        functools.partial(early_kernel, n, heads),
        [bf16(rows, width)] * n + [end, stat_out],
        [
            vmem(bf16(4, 2 * WINDOW, width)),
            vmem(bf16(total, width)),
            vmem(f32(2, WINDOW, width)),
            vmem(stat_out),
        ],
        2 * n + 3,
        *crit, *rest, kv_halo, dq_late, partial,
    )
    stat_halo = lax.ppermute(stat, "chunk", backward)
    dq = exchanged(dq)
    dkv = call(
        functools.partial(edge_kernel, n, heads),
        [piece] * n,
        [vmem(end), vmem(end), vmem(bf16(2, total, width)), vmem(f32(2, done, width)), vmem(stat_out)],
        n + 4,
        *crit, qg_halo, front, partial, stat_halo,
    )
    dkv = exchanged(dkv)
    out = bf16(rows, model)
    return tuple(
        call(functools.partial(unpack_kernel, n), [out] * 3, [], 3 * n, *dq, *dkv)
    )


def solution(mesh):
    seq, head = mesh.devices.shape
    part = max(1, min(seq, HEADS // 2 // head))
    fine = Mesh(mesh.devices.reshape(seq // part, part, head), AXES)
    placed = P(AXES, None)
    return jax.shard_map(
        per_device,
        mesh=fine,
        in_specs=(placed,) * 4,
        out_specs=(placed,) * 3,
        check_vma=False,
    )
```

time: 91.7 us -> 79.1 us (0.86)
  waiting for transfers between devices: 26.9 us -> 16.4 us
  local copies, waits for them, and re-layouts: 4.16 us -> 1.81 us
    ppermute x28, waiting for transfers between devices: 26.9 us -> 12.3 us  [exchanged(): lax.ppermute(pieces[m], GROUP, [(i, i ^ m) for i in range(n)])]
    ppermute x1, waiting for transfers between devices: 0.01 us -> 4.11 us  [per_device(): kv_halo = lax.ppermute(kv_send, 'chunk', forward)]
    unnamed x8 -> x4, local copies, waits for them, and re-layouts: 4.16 us -> 1.81 us
    pallas_call x5 -> x6, Pallas kernels: 18.1 us -> 18.5 us  [call(): pl.pallas_call(kernel, out_shape=outs, in_specs=[pl.BlockSpec(memory_spac...]
  transfers between devices with their start and end apart: 31 -> 31, of which waited for: 10 -> 10; matrix products, arithmetic and copies ran while one was open for 0% -> 0% of each run, Pallas kernels for 17% -> 18%
where the time goes in v2:
time: 79.1 us; the launch traced here: 77.8 us
  starting transfers between devices  40.4 us (51%)
  Pallas kernels  18.5 us (23%)
  waiting for transfers between devices  16.4 us (21%)
  local copies, waits for them, and re-layouts  1.81 us (2%)
    ppermute x28, starting transfers between devices, exchanged(): lax.ppermute(pieces[m], GROUP, [(i, i ^ m) for i in range(n)])  33.1 us
    pallas_call x6, Pallas kernels, call(): pl.pallas_call(kernel, out_shape=outs, in_specs=[pl.BlockSpec(memory_spac...  18.5 us
    ppermute x28, waiting for transfers between devices, exchanged(): lax.ppermute(pieces[m], GROUP, [(i, i ^ m) for i in range(n)])  12.3 us
    ppermute x1, waiting for transfers between devices, per_device(): kv_halo = lax.ppermute(kv_send, 'chunk', forward)  4.11 us
    ppermute x1, starting transfers between devices, per_device(): kv_halo = lax.ppermute(kv_send, 'chunk', forward)  3.19 us
    ppermute x1, starting transfers between devices, per_device(): qg_halo = lax.ppermute(qg_send, 'chunk', backward)  2.08 us
    ppermute x1, starting transfers between devices, per_device(): stat_halo = lax.ppermute(stat, 'chunk', backward)  2.07 us
    unnamed x4, local copies, waits for them, and re-layouts  1.81 us
  transfers between devices with their start and end apart: 31, of which 10 were waited for; matrix products, arithmetic and copies ran while one was open for 0% of the time, Pallas kernels for 18%

profile of v2, /device:TPU:17, one launch (start us, length us, event | category | flops | bytes accessed | tf_op | source)
XLA Modules:
  0.0 77.8 jit_solution(16690770871203959344)
XLA Ops:
  0.6 3.0 %shard_map.67 = (bf16[2,128,256]{2,1,0:T(8,128)(2,1)}, bf16[2,128,256]{2,1,0:T(8,128)(2,1)}, bf16[2,128,256]{2,1,0:T(8,128)(2,1)}, bf16[2,128,256]{2,1,0:T(8,128...) custom-call(bf16[128,2048]{1,0:T(8,128)(2,1)} %refs_0_.1, ...), custom_call_target="tpu_custom_call" | custom-call | tf_op jit(solution)/shard_map/pallas_call | solution.py:286
  3.6 0.7 collective-permute-start
  4.3 2.2 %collective-permute-start.1 = (bf16[2,128,256]{2,1,0:T(8,128)(2,1)}, bf16[2,128,256]{2,1,0:T(8,128)(2,1)S(1)}, u32[]{:S(2)}, u32[]{:S(2)}) collective-permute-start(bf16[2,128,256]{2,1,0:T(8,128)(2,1)} %get-tuple-element.43), channel_id=1, source_target_pairs={{0,6},{1,7},{2,4},{3,5},{4,2},{5,3},{6,0},{7,1},{8,14},{9,15},{10,... | collective-permute-start | bytes 393224 | tf_op jit(solution)/shard_map/ppermute | solution.py:313
  6.5 0.4 collective-permute-start.2
  6.9 1.2 %collective-permute-start.3 = (bf16[2,128,256]{2,1,0:T(8,128)(2,1)}, bf16[2,128,256]{2,1,0:T(8,128)(2,1)S(1)}, u32[]{:S(2)}, u32[]{:S(2)}) collective-permute-start(bf16[2,128,256]{2,1,0:T(8,128)(2,1)} %get-tuple-element.45), channel_id=1, source_target_pairs={{0,2},{1,3},{2,0},{3,1},{4,6},{5,7},{6,4},{7,5},{8,10},{9,11},{10,... | collective-permute-start | bytes 393224 | tf_op jit(solution)/shard_map/ppermute | solution.py:313
  8.2 1.2 %collective-permute-start.4 = (bf16[2,128,256]{2,1,0:T(8,128)(2,1)}, bf16[2,128,256]{2,1,0:T(8,128)(2,1)S(1)}, u32[]{:S(2)}, u32[]{:S(2)}) collective-permute-start(bf16[2,128,256]{2,1,0:T(8,128)(2,1)} %get-tuple-element.46), channel_id=1, source_target_pairs={{0,4},{1,5},{2,6},{3,7},{4,0},{5,1},{6,2},{7,3},{8,12},{9,13},{10,... | collective-permute-start | bytes 393224 | tf_op jit(solution)/shard_map/ppermute | solution.py:313
  9.4 0.0 collective-permute-done.refs_1_
  9.4 0.9 %collective-permute-start.5 = (bf16[2,128,256]{2,1,0:T(8,128)(2,1)}, bf16[2,128,256]{2,1,0:T(8,128)(2,1)S(1)}, u32[]{:S(2)}, u32[]{:S(2)}) collective-permute-start(bf16[2,128,256]{2,1,0:T(8,128)(2,1)} %get-tuple-element.47), channel_id=1, source_target_pairs={{0,3},{1,2},{2,1},{3,0},{4,7},{5,6},{6,5},{7,4},{8,11},{9,10},{10,... | collective-permute-start | bytes 393224 | tf_op jit(solution)/shard_map/ppermute | solution.py:313
  10.3 0.3 collective-permute-done.1.refs_2_
  10.5 2.5 %collective-permute-start.6 = (bf16[2,128,256]{2,1,0:T(8,128)(2,1)}, bf16[2,128,256]{2,1,0:T(8,128)(2,1)S(1)}, u32[]{:S(2)}, u32[]{:S(2)}) collective-permute-start(bf16[2,128,256]{2,1,0:T(8,128)(2,1)} %get-tuple-element.48), channel_id=1, source_target_pairs={{0,5},{1,4},{2,7},{3,6},{4,1},{5,0},{6,3},{7,2},{8,13},{9,12},{10,... | collective-permute-start | bytes 393224 | tf_op jit(solution)/shard_map/ppermute | solution.py:313
  13.0 0.9 %collective-permute-done.2.refs_3_ = bf16[2,128,256]{2,1,0:T(8,128)(2,1)S(1)} collective-permute-done((bf16[2,128,256]{2,1,0:T(8,128)(2,1)}, bf16[2,128,256]{2,1,0:T(8,128)(2,1)S(1)}, u32[]{:S(2)}, u32[]{:S(2)}) %collective-permute-start.2) | collective-permute-done | bytes 131104 | tf_op jit(solution)/shard_map/ppermute | solution.py:313
  13.9 0.0 collective-permute-start.7
  13.9 2.3 %collective-permute-done.3.refs_4_ = bf16[2,128,256]{2,1,0:T(8,128)(2,1)S(1)} collective-permute-done((bf16[2,128,256]{2,1,0:T(8,128)(2,1)}, bf16[2,128,256]{2,1,0:T(8,128)(2,1)S(1)}, u32[]{:S(2)}, u32[]{:S(2)}) %collective-permute-start.3) | collective-permute-done | bytes 131104 | tf_op jit(solution)/shard_map/ppermute | solution.py:313
  16.2 1.2 %collective-permute-start.8 = (bf16[2,128,256]{2,1,0:T(8,128)(2,1)}, bf16[2,128,256]{2,1,0:T(8,128)(2,1)S(1)}, u32[]{:S(2)}, u32[]{:S(2)}) collective-permute-start(bf16[2,128,256]{2,1,0:T(8,128)(2,1)} %get-tuple-element.51), channel_id=1, source_target_pairs={{0,6},{1,7},{2,4},{3,5},{4,2},{5,3},{6,0},{7,1},{8,14},{9,15},{10,... | collective-permute-start | bytes 393224 | tf_op jit(solution)/shard_map/ppermute | solution.py:313
  17.4 0.0 collective-permute-done.4.refs_5_
  17.4 2.7 %collective-permute-start.9 = (bf16[2,128,256]{2,1,0:T(8,128)(2,1)}, bf16[2,128,256]{2,1,0:T(8,128)(2,1)S(1)}, u32[]{:S(2)}, u32[]{:S(2)}) collective-permute-start(bf16[2,128,256]{2,1,0:T(8,128)(2,1)} %get-tuple-element.52), channel_id=1, source_target_pairs={{0,7},{1,6},{2,5},{3,4},{4,3},{5,2},{6,1},{7,0},{8,15},{9,14},{10,... | collective-permute-start | bytes 393224 | tf_op jit(solution)/shard_map/ppermute | solution.py:313
  20.1 1.2 %collective-permute-start.10 = (bf16[2,128,256]{2,1,0:T(8,128)(2,1)}, bf16[2,128,256]{2,1,0:T(8,128)(2,1)S(1)}, u32[]{:S(2)}, u32[]{:S(2)}) collective-permute-start(bf16[2,128,256]{2,1,0:T(8,128)(2,1)} %get-tuple-element.53), channel_id=1, source_target_pairs={{0,2},{1,3},{2,0},{3,1},{4,6},{5,7},{6,4},{7,5},{8,10},{9,11},{10,... | collective-permute-start | bytes 393224 | tf_op jit(solution)/shard_map/ppermute | solution.py:313
  21.3 0.0 collective-permute-done.6.refs_7_
  21.3 0.2 collective-permute-start.11
  21.5 0.0 collective-permute-done.7.refs_9_
  21.5 1.0 %collective-permute-start.12 = (bf16[2,128,256]{2,1,0:T(8,128)(2,1)}, bf16[2,128,256]{2,1,0:T(8,128)(2,1)S(1)}, u32[]{:S(2)}, u32[]{:S(2)}) collective-permute-start(bf16[2,128,256]{2,1,0:T(8,128)(2,1)} %get-tuple-element.55), channel_id=1, source_target_pairs={{0,3},{1,2},{2,1},{3,0},{4,7},{5,6},{6,5},{7,4},{8,11},{9,10},{10,... | collective-permute-start | bytes 393224 | tf_op jit(solution)/shard_map/ppermute | solution.py:313
  22.5 1.8 %collective-permute-start.13 = (bf16[2,128,256]{2,1,0:T(8,128)(2,1)}, bf16[2,128,256]{2,1,0:T(8,128)(2,1)S(1)}, u32[]{:S(2)}, u32[]{:S(2)}) collective-permute-start(bf16[2,128,256]{2,1,0:T(8,128)(2,1)} %get-tuple-element.56), channel_id=1, source_target_pairs={{0,5},{1,4},{2,7},{3,6},{4,1},{5,0},{6,3},{7,2},{8,13},{9,12},{10,... | collective-permute-start | bytes 393224 | tf_op jit(solution)/shard_map/ppermute | solution.py:313
  24.3 0.9 %copy-done = bf16[2,128,256]{2,1,0:T(8,128)(2,1)S(1)} copy-done((bf16[2,128,256]{2,1,0:T(8,128)(2,1)S(1)}, bf16[2,128,256]{2,1,0:T(8,128)(2,1)}, u32[]{:S(2)}) %copy-start) | copy-done | bytes 131096
  25.2 0.9 %shard_map.68 = (bf16[2,512,256]{2,1,0:T(8,128)(2,1)S(1)}, bf16[2,512,256]{2,1,0:T(8,128)(2,1)S(1)}) custom-call(bf16[2,128,256]{2,1,0:T(8,128)(2,1)S(1)} %copy-done, bf16[2,128,256]{2,1,0:T(8,128)(2,1)S(1)} %collective-permute-done.refs_1_, bf16[2,128,256]{2,1,0:T(8,128)(2,1)S(1)} %collective-permute-done.1.refs_2_, ...), custom_call_target="tpu_custom_call" | custom-call | tf_op jit(solution)/shard_map/pallas_call | solution.py:286
  26.1 0.3 collective-permute-done.9.refs_11_
  26.3 3.2 %collective-permute-start.14 = (bf16[2,512,256]{2,1,0:T(8,128)(2,1)S(1)}, bf16[2,512,256]{2,1,0:T(8,128)(2,1)S(1)}, u32[]{:S(2)}, u32[]{:S(2)}) collective-permute-start(bf16[2,512,256]{2,1,0:T(8,128)(2,1)S(1)} %get-tuple-element.57), channel_id=1, source_target_pairs={{0,8},{8,16},{16,24},{1,9},{9,17},{17,25},{2,10},{10,18},{18,26},{... | collective-permute-start | bytes 1572872 | tf_op jit(solution)/shard_map/ppermute | solution.py:340
  29.5 0.0 collective-permute-done.10.refs_12_
  29.5 2.1 %collective-permute-start.22 = (bf16[2,512,256]{2,1,0:T(8,128)(2,1)S(1)}, bf16[2,512,256]{2,1,0:T(8,128)(2,1)S(1)}, u32[]{:S(2)}, u32[]{:S(2)}) collective-permute-start(bf16[2,512,256]{2,1,0:T(8,128)(2,1)S(1)} %get-tuple-element.68), channel_id=1, source_target_pairs={{8,0},{16,8},{24,16},{9,1},{17,9},{25,17},{10,2},{18,10},{26,18},{... | collective-permute-start | bytes 1572872 | tf_op jit(solution)/shard_map/ppermute | solution.py:341
  31.6 0.0 collective-permute-done.11.refs_13_
  31.6 0.0 collective-permute-done.12.refs_14_
  31.6 0.0 collective-permute-done.13.refs_15_
  31.7 0.9 %copy-done.1 = bf16[2,128,256]{2,1,0:T(8,128)(2,1)S(1)} copy-done((bf16[2,128,256]{2,1,0:T(8,128)(2,1)S(1)}, bf16[2,128,256]{2,1,0:T(8,128)(2,1)}, u32[]{:S(2)}) %copy-start.1) | copy-done | bytes 131096
  32.6 5.3 %shard_map.69 = (bf16[512,256]{1,0:T(8,128)(2,1)S(1)}, f32[2,1024,256]{2,1,0:T(8,128)S(1)}) custom-call(bf16[2,128,256]{2,1,0:T(8,128)(2,1)S(1)} %copy-done, bf16[2,128,256]{2,1,0:T(8,128)(2,1)S(1)} %collective-permute-done.refs_1_, bf16[2,128,256]{2,1,0:T(8,128)(2,1)S(1)} %collective-permute-done.1.refs_2_, ...), custom_call_target="tpu_custom_call" | custom-call | flops 16000000000 | tf_op jit(solution)/shard_map/pallas_call | solution.py:286
  37.9 4.1 %collective-permute-done.14.refs_16_ = bf16[2,512,256]{2,1,0:T(8,128)(2,1)S(1)} collective-permute-done((bf16[2,512,256]{2,1,0:T(8,128)(2,1)S(1)}, bf16[2,512,256]{2,1,0:T(8,128)(2,1)S(1)}, u32[]{:S(2)}, u32[]{:S(2)}) %collective-permute-start.14) | collective-permute-done | bytes 524320 | tf_op jit(solution)/shard_map/ppermute | solution.py:340
  42.0 5.3 %shard_map.70 = (bf16[128,256]{1,0:T(8,128)(2,1)S(1)}, bf16[128,256]{1,0:T(8,128)(2,1)S(1)}, bf16[128,256]{1,0:T(8,128)(2,1)S(1)}, bf16[128,256]{1,0:T(8,128)(2,...) custom-call(bf16[2,128,256]{2,1,0:T(8,128)(2,1)S(1)} %copy-done, ...), custom_call_target="tpu_custom_call" | custom-call | tf_op jit(solution)/shard_map/pallas_call | solution.py:286
  47.3 0.6 collective-permute-start.15
  47.9 2.1 %collective-permute-start.23 = (f32[8,512]{1,0:T(8,128)S(1)}, f32[8,512]{1,0:T(8,128)S(1)}, u32[]{:S(2)}, u32[]{:S(2)}) collective-permute-start(f32[8,512]{1,0:T(8,128)S(1)} %get-tuple-element.70), channel_id=1, source_target_pairs={{8,0},{16,8},{24,16},{9,1},{17,9},{25,17},{10,2},{18,10},{26,18},{... | collective-permute-start | bytes 49160 | tf_op jit(solution)/shard_map/ppermute | solution.py:363
  50.0 1.0 %collective-permute-start.16 = (bf16[128,256]{1,0:T(8,128)(2,1)S(1)}, bf16[128,256]{1,0:T(8,128)(2,1)S(1)}, u32[]{:S(2)}, u32[]{:S(2)}) collective-permute-start(bf16[128,256]{1,0:T(8,128)(2,1)S(1)} %get-tuple-element.62), channel_id=1, source_target_pairs={{0,6},{1,7},{2,4},{3,5},{4,2},{5,3},{6,0},{7,1},{8,14},{9,15},{10,... | collective-permute-start | bytes 196616 | tf_op jit(solution)/shard_map/ppermute | solution.py:313
  51.0 1.9 %collective-permute-start.17 = (bf16[128,256]{1,0:T(8,128)(2,1)S(1)}, bf16[128,256]{1,0:T(8,128)(2,1)S(1)}, u32[]{:S(2)}, u32[]{:S(2)}) collective-permute-start(bf16[128,256]{1,0:T(8,128)(2,1)S(1)} %get-tuple-element.63), channel_id=1, source_target_pairs={{0,7},{1,6},{2,5},{3,4},{4,3},{5,2},{6,1},{7,0},{8,15},{9,14},{10,... | collective-permute-start | bytes 196616 | tf_op jit(solution)/shard_map/ppermute | solution.py:313
  52.9 0.0 collective-permute-done.22.refs_8_
  52.9 2.0 %collective-permute-start.18 = (bf16[128,256]{1,0:T(8,128)(2,1)S(1)}, bf16[128,256]{1,0:T(8,128)(2,1)S(1)}, u32[]{:S(2)}, u32[]{:S(2)}) collective-permute-start(bf16[128,256]{1,0:T(8,128)(2,1)S(1)} %get-tuple-element.64), channel_id=1, source_target_pairs={{0,2},{1,3},{2,0},{3,1},{4,6},{5,7},{6,4},{7,5},{8,10},{9,11},{10,... | collective-permute-start | bytes 196616 | tf_op jit(solution)/shard_map/ppermute | solution.py:313
  54.9 2.7 %shard_map.71 = (bf16[2,128,256]{2,1,0:T(8,128)(2,1)S(1)}, bf16[2,128,256]{2,1,0:T(8,128)(2,1)S(1)}, bf16[2,128,256]{2,1,0:T(8,128)(2,1)S(1)}, bf16[2,128,256]{2...) custom-call(bf16[2,128,256]{2,1,0:T(8,128)(2,1)S(1)} %copy-done, ...), custom_call_target="tpu_custom_call" | custom-call | tf_op jit(solution)/shard_map/pallas_call | solution.py:286
  57.6 0.3 collective-permute-start.24
  57.9 0.2 collective-permute-start.25
  58.1 0.0 collective-permute-done.16.refs_2_
  58.1 1.5 %collective-permute-start.19 = (bf16[128,256]{1,0:T(8,128)(2,1)S(1)}, bf16[128,256]{1,0:T(8,128)(2,1)S(1)}, u32[]{:S(2)}, u32[]{:S(2)}) collective-permute-start(bf16[128,256]{1,0:T(8,128)(2,1)S(1)} %get-tuple-element.65), channel_id=1, source_target_pairs={{0,4},{1,5},{2,6},{3,7},{4,0},{5,1},{6,2},{7,3},{8,12},{9,13},{10,... | collective-permute-start | bytes 196616 | tf_op jit(solution)/shard_map/ppermute | solution.py:313
  59.6 0.0 collective-permute-done.17.refs_3_
  59.6 1.8 %collective-permute-start.20 = (bf16[128,256]{1,0:T(8,128)(2,1)S(1)}, bf16[128,256]{1,0:T(8,128)(2,1)S(1)}, u32[]{:S(2)}, u32[]{:S(2)}) collective-permute-start(bf16[128,256]{1,0:T(8,128)(2,1)S(1)} %get-tuple-element.66), channel_id=1, source_target_pairs={{0,3},{1,2},{2,1},{3,0},{4,7},{5,6},{6,5},{7,4},{8,11},{9,10},{10,... | collective-permute-start | bytes 196616 | tf_op jit(solution)/shard_map/ppermute | solution.py:313
  61.3 0.0 collective-permute-done.18.refs_4_
  61.3 0.0 collective-permute-start.21
  61.3 1.6 %collective-permute-done.19.refs_5_ = bf16[128,256]{1,0:T(8,128)(2,1)S(1)} collective-permute-done((bf16[128,256]{1,0:T(8,128)(2,1)S(1)}, bf16[128,256]{1,0:T(8,128)(2,1)S(1)}, u32[]{:S(2)}, u32[]{:S(2)}) %collective-permute-start.19) | collective-permute-done | bytes 65568 | tf_op jit(solution)/shard_map/ppermute | solution.py:313
  63.0 3.3 %collective-permute-start.26 = (bf16[2,128,256]{2,1,0:T(8,128)(2,1)S(1)}, bf16[2,128,256]{2,1,0:T(8,128)(2,1)S(1)}, u32[]{:S(2)}, u32[]{:S(2)}) collective-permute-start(bf16[2,128,256]{2,1,0:T(8,128)(2,1)S(1)} %get-tuple-element.74), channel_id=1, source_target_pairs={{0,7},{1,6},{2,5},{3,4},{4,3},{5,2},{6,1},{7,0},{8,15},{9,14},{10,... | collective-permute-start | bytes 393224 | tf_op jit(solution)/shard_map/ppermute | solution.py:313
  66.3 0.0 collective-permute-done.20.refs_6_
  66.3 0.5 collective-permute-start.27
  66.8 1.8 %collective-permute-start.28 = (bf16[2,128,256]{2,1,0:T(8,128)(2,1)S(1)}, bf16[2,128,256]{2,1,0:T(8,128)(2,1)S(1)}, u32[]{:S(2)}, u32[]{:S(2)}) collective-permute-start(bf16[2,128,256]{2,1,0:T(8,128)(2,1)S(1)} %get-tuple-element.76), channel_id=1, source_target_pairs={{0,4},{1,5},{2,6},{3,7},{4,0},{5,1},{6,2},{7,3},{8,12},{9,13},{10,... | collective-permute-start | bytes 393224 | tf_op jit(solution)/shard_map/ppermute | solution.py:313
  68.6 0.6 collective-permute-start.29
  69.2 0.0 collective-permute-done.25.refs_10_
  69.2 0.4 collective-permute-start.30
  69.6 0.0 collective-permute-done.26.refs_11_
  69.6 3.9 %collective-permute-done.27.refs_12_ = bf16[2,128,256]{2,1,0:T(8,128)(2,1)S(1)} collective-permute-done((bf16[2,128,256]{2,1,0:T(8,128)(2,1)S(1)}, bf16[2,128,256]{2,1,0:T(8,128)(2,1)S(1)}, u32[]{:S(2)}, u32[]{:S(2)}) %collective-permute-start.27) | collective-permute-done | bytes 131104 | tf_op jit(solution)/shard_map/ppermute | solution.py:313
  73.5 0.2 collective-permute-done.28.refs_13_
  73.7 2.7 %collective-permute-done.29.refs_14_ = bf16[2,128,256]{2,1,0:T(8,128)(2,1)S(1)} collective-permute-done((bf16[2,128,256]{2,1,0:T(8,128)(2,1)S(1)}, bf16[2,128,256]{2,1,0:T(8,128)(2,1)S(1)}, u32[]{:S(2)}, u32[]{:S(2)}) %collective-permute-start.29) | collective-permute-done | bytes 131104 | tf_op jit(solution)/shard_map/ppermute | solution.py:313
  76.4 0.1 collective-permute-done.30.refs_15_
  76.5 1.3 %shard_map.72 = (bf16[128,2048]{1,0:T(8,128)(2,1)}, bf16[128,2048]{1,0:T(8,128)(2,1)}, bf16[128,2048]{1,0:T(8,128)(2,1)}) custom-call(bf16[128,256]{1,0:T(8,128)(2,1)S(1)} %get-tuple-element.60.refs_0_, bf16[128,256]{1,0:T(8,128)(2,1)S(1)} %collective-permute-done.15.refs_1_, bf16[128,256]{1,0:T(8,128)(2,1)S(1)} %collective-permute-done.16.refs_2_, ...), custom_call_target="tpu_custom_call" | custom-call | tf_op jit(solution)/shard_map/pallas_call | solution.py:286
  (8 shorter events, 0.0 us)
Async XLA Ops:
  3.6 5.8 %collective-permute-start = (bf16[2,128,256]{2,1,0:T(8,128)(2,1)}, bf16[2,128,256]{2,1,0:T(8,128)(2,1)S(1)}, u32[]{:S(2)}, u32[]{:S(2)}) collective-permute-start(bf16[2,128,256]{2,1,0:T(8,128)(2,1)} %get-tuple-element.42), channel_id=1, source_target_pairs={{0,1},{1,0},{2,3},{3,2},{4,5},{5,4},{6,7},{7,6},{8,9},{9,8},{10,11... | collective-permute-start | bytes 393224 | tf_op jit(solution)/shard_map/ppermute | solution.py:313
  4.3 6.2 %collective-permute-start.1 = (bf16[2,128,256]{2,1,0:T(8,128)(2,1)}, bf16[2,128,256]{2,1,0:T(8,128)(2,1)S(1)}, u32[]{:S(2)}, u32[]{:S(2)}) collective-permute-start(bf16[2,128,256]{2,1,0:T(8,128)(2,1)} %get-tuple-element.43), channel_id=1, source_target_pairs={{0,6},{1,7},{2,4},{3,5},{4,2},{5,3},{6,0},{7,1},{8,14},{9,15},{10,... | collective-permute-start | bytes 393224 | tf_op jit(solution)/shard_map/ppermute | solution.py:313
  6.5 7.4 %collective-permute-start.2 = (bf16[2,128,256]{2,1,0:T(8,128)(2,1)}, bf16[2,128,256]{2,1,0:T(8,128)(2,1)S(1)}, u32[]{:S(2)}, u32[]{:S(2)}) collective-permute-start(bf16[2,128,256]{2,1,0:T(8,128)(2,1)} %get-tuple-element.44), channel_id=1, source_target_pairs={{0,7},{1,6},{2,5},{3,4},{4,3},{5,2},{6,1},{7,0},{8,15},{9,14},{10,... | collective-permute-start | bytes 393224 | tf_op jit(solution)/shard_map/ppermute | solution.py:313
  6.9 9.3 %collective-permute-start.3 = (bf16[2,128,256]{2,1,0:T(8,128)(2,1)}, bf16[2,128,256]{2,1,0:T(8,128)(2,1)S(1)}, u32[]{:S(2)}, u32[]{:S(2)}) collective-permute-start(bf16[2,128,256]{2,1,0:T(8,128)(2,1)} %get-tuple-element.45), channel_id=1, source_target_pairs={{0,2},{1,3},{2,0},{3,1},{4,6},{5,7},{6,4},{7,5},{8,10},{9,11},{10,... | collective-permute-start | bytes 393224 | tf_op jit(solution)/shard_map/ppermute | solution.py:313
  8.2 9.2 %collective-permute-start.4 = (bf16[2,128,256]{2,1,0:T(8,128)(2,1)}, bf16[2,128,256]{2,1,0:T(8,128)(2,1)S(1)}, u32[]{:S(2)}, u32[]{:S(2)}) collective-permute-start(bf16[2,128,256]{2,1,0:T(8,128)(2,1)} %get-tuple-element.46), channel_id=1, source_target_pairs={{0,4},{1,5},{2,6},{3,7},{4,0},{5,1},{6,2},{7,3},{8,12},{9,13},{10,... | collective-permute-start | bytes 393224 | tf_op jit(solution)/shard_map/ppermute | solution.py:313
  9.4 10.7 %collective-permute-start.5 = (bf16[2,128,256]{2,1,0:T(8,128)(2,1)}, bf16[2,128,256]{2,1,0:T(8,128)(2,1)S(1)}, u32[]{:S(2)}, u32[]{:S(2)}) collective-permute-start(bf16[2,128,256]{2,1,0:T(8,128)(2,1)} %get-tuple-element.47), channel_id=1, source_target_pairs={{0,3},{1,2},{2,1},{3,0},{4,7},{5,6},{6,5},{7,4},{8,11},{9,10},{10,... | collective-permute-start | bytes 393224 | tf_op jit(solution)/shard_map/ppermute | solution.py:313
  10.5 10.8 %collective-permute-start.6 = (bf16[2,128,256]{2,1,0:T(8,128)(2,1)}, bf16[2,128,256]{2,1,0:T(8,128)(2,1)S(1)}, u32[]{:S(2)}, u32[]{:S(2)}) collective-permute-start(bf16[2,128,256]{2,1,0:T(8,128)(2,1)} %get-tuple-element.48), channel_id=1, source_target_pairs={{0,5},{1,4},{2,7},{3,6},{4,1},{5,0},{6,3},{7,2},{8,13},{9,12},{10,... | collective-permute-start | bytes 393224 | tf_op jit(solution)/shard_map/ppermute | solution.py:313
  13.9 7.6 %collective-permute-start.7 = (bf16[2,128,256]{2,1,0:T(8,128)(2,1)}, bf16[2,128,256]{2,1,0:T(8,128)(2,1)S(1)}, u32[]{:S(2)}, u32[]{:S(2)}) collective-permute-start(bf16[2,128,256]{2,1,0:T(8,128)(2,1)} %get-tuple-element.50), channel_id=1, source_target_pairs={{0,1},{1,0},{2,3},{3,2},{4,5},{5,4},{6,7},{7,6},{8,9},{9,8},{10,11... | collective-permute-start | bytes 393224 | tf_op jit(solution)/shard_map/ppermute | solution.py:313
  16.2 6.3 %collective-permute-start.8 = (bf16[2,128,256]{2,1,0:T(8,128)(2,1)}, bf16[2,128,256]{2,1,0:T(8,128)(2,1)S(1)}, u32[]{:S(2)}, u32[]{:S(2)}) collective-permute-start(bf16[2,128,256]{2,1,0:T(8,128)(2,1)} %get-tuple-element.51), channel_id=1, source_target_pairs={{0,6},{1,7},{2,4},{3,5},{4,2},{5,3},{6,0},{7,1},{8,14},{9,15},{10,... | collective-permute-start | bytes 393224 | tf_op jit(solution)/shard_map/ppermute | solution.py:313
  17.4 8.9 %collective-permute-start.9 = (bf16[2,128,256]{2,1,0:T(8,128)(2,1)}, bf16[2,128,256]{2,1,0:T(8,128)(2,1)S(1)}, u32[]{:S(2)}, u32[]{:S(2)}) collective-permute-start(bf16[2,128,256]{2,1,0:T(8,128)(2,1)} %get-tuple-element.52), channel_id=1, source_target_pairs={{0,7},{1,6},{2,5},{3,4},{4,3},{5,2},{6,1},{7,0},{8,15},{9,14},{10,... | collective-permute-start | bytes 393224 | tf_op jit(solution)/shard_map/ppermute | solution.py:313
  20.1 9.4 %collective-permute-start.10 = (bf16[2,128,256]{2,1,0:T(8,128)(2,1)}, bf16[2,128,256]{2,1,0:T(8,128)(2,1)S(1)}, u32[]{:S(2)}, u32[]{:S(2)}) collective-permute-start(bf16[2,128,256]{2,1,0:T(8,128)(2,1)} %get-tuple-element.53), channel_id=1, source_target_pairs={{0,2},{1,3},{2,0},{3,1},{4,6},{5,7},{6,4},{7,5},{8,10},{9,11},{10,... | collective-permute-start | bytes 393224 | tf_op jit(solution)/shard_map/ppermute | solution.py:313
  21.3 10.3 %collective-permute-start.11 = (bf16[2,128,256]{2,1,0:T(8,128)(2,1)}, bf16[2,128,256]{2,1,0:T(8,128)(2,1)S(1)}, u32[]{:S(2)}, u32[]{:S(2)}) collective-permute-start(bf16[2,128,256]{2,1,0:T(8,128)(2,1)} %get-tuple-element.54), channel_id=1, source_target_pairs={{0,4},{1,5},{2,6},{3,7},{4,0},{5,1},{6,2},{7,3},{8,12},{9,13},{10,... | collective-permute-start | bytes 393224 | tf_op jit(solution)/shard_map/ppermute | solution.py:313
  21.5 10.1 %collective-permute-start.12 = (bf16[2,128,256]{2,1,0:T(8,128)(2,1)}, bf16[2,128,256]{2,1,0:T(8,128)(2,1)S(1)}, u32[]{:S(2)}, u32[]{:S(2)}) collective-permute-start(bf16[2,128,256]{2,1,0:T(8,128)(2,1)} %get-tuple-element.55), channel_id=1, source_target_pairs={{0,3},{1,2},{2,1},{3,0},{4,7},{5,6},{6,5},{7,4},{8,11},{9,10},{10,... | collective-permute-start | bytes 393224 | tf_op jit(solution)/shard_map/ppermute | solution.py:313
  22.5 9.1 %collective-permute-start.13 = (bf16[2,128,256]{2,1,0:T(8,128)(2,1)}, bf16[2,128,256]{2,1,0:T(8,128)(2,1)S(1)}, u32[]{:S(2)}, u32[]{:S(2)}) collective-permute-start(bf16[2,128,256]{2,1,0:T(8,128)(2,1)} %get-tuple-element.56), channel_id=1, source_target_pairs={{0,5},{1,4},{2,7},{3,6},{4,1},{5,0},{6,3},{7,2},{8,13},{9,12},{10,... | collective-permute-start | bytes 393224 | tf_op jit(solution)/shard_map/ppermute | solution.py:313
  24.3 0.9 %copy-start = (bf16[2,128,256]{2,1,0:T(8,128)(2,1)S(1)}, bf16[2,128,256]{2,1,0:T(8,128)(2,1)}, u32[]{:S(2)}) copy-start(bf16[2,128,256]{2,1,0:T(8,128)(2,1)} %get-tuple-element.41.refs_0_) | copy-start | bytes 393220
  26.3 15.7 %collective-permute-start.14 = (bf16[2,512,256]{2,1,0:T(8,128)(2,1)S(1)}, bf16[2,512,256]{2,1,0:T(8,128)(2,1)S(1)}, u32[]{:S(2)}, u32[]{:S(2)}) collective-permute-start(bf16[2,512,256]{2,1,0:T(8,128)(2,1)S(1)} %get-tuple-element.57), channel_id=1, source_target_pairs={{0,8},{8,16},{16,24},{1,9},{9,17},{17,25},{2,10},{10,18},{18,26},{... | collective-permute-start | bytes 1572872 | tf_op jit(solution)/shard_map/ppermute | solution.py:340
  29.5 23.3 %collective-permute-start.22 = (bf16[2,512,256]{2,1,0:T(8,128)(2,1)S(1)}, bf16[2,512,256]{2,1,0:T(8,128)(2,1)S(1)}, u32[]{:S(2)}, u32[]{:S(2)}) collective-permute-start(bf16[2,512,256]{2,1,0:T(8,128)(2,1)S(1)} %get-tuple-element.68), channel_id=1, source_target_pairs={{8,0},{16,8},{24,16},{9,1},{17,9},{25,17},{10,2},{18,10},{26,18},{... | collective-permute-start | bytes 1572872 | tf_op jit(solution)/shard_map/ppermute | solution.py:341
  31.7 0.9 %copy-start.1 = (bf16[2,128,256]{2,1,0:T(8,128)(2,1)S(1)}, bf16[2,128,256]{2,1,0:T(8,128)(2,1)}, u32[]{:S(2)}) copy-start(bf16[2,128,256]{2,1,0:T(8,128)(2,1)} %get-tuple-element.49.refs_8_) | copy-start | bytes 393220
  47.3 10.6 %collective-permute-start.15 = (bf16[128,256]{1,0:T(8,128)(2,1)S(1)}, bf16[128,256]{1,0:T(8,128)(2,1)S(1)}, u32[]{:S(2)}, u32[]{:S(2)}) collective-permute-start(bf16[128,256]{1,0:T(8,128)(2,1)S(1)} %get-tuple-element.61), channel_id=1, source_target_pairs={{0,1},{1,0},{2,3},{3,2},{4,5},{5,4},{6,7},{7,6},{8,9},{9,8},{10,11... | collective-permute-start | bytes 196616 | tf_op jit(solution)/shard_map/ppermute | solution.py:313
  47.9 7.0 %collective-permute-start.23 = (f32[8,512]{1,0:T(8,128)S(1)}, f32[8,512]{1,0:T(8,128)S(1)}, u32[]{:S(2)}, u32[]{:S(2)}) collective-permute-start(f32[8,512]{1,0:T(8,128)S(1)} %get-tuple-element.70), channel_id=1, source_target_pairs={{8,0},{16,8},{24,16},{9,1},{17,9},{25,17},{10,2},{18,10},{26,18},{... | collective-permute-start | bytes 49160 | tf_op jit(solution)/shard_map/ppermute | solution.py:363
  50.0 8.1 %collective-permute-start.16 = (bf16[128,256]{1,0:T(8,128)(2,1)S(1)}, bf16[128,256]{1,0:T(8,128)(2,1)S(1)}, u32[]{:S(2)}, u32[]{:S(2)}) collective-permute-start(bf16[128,256]{1,0:T(8,128)(2,1)S(1)} %get-tuple-element.62), channel_id=1, source_target_pairs={{0,6},{1,7},{2,4},{3,5},{4,2},{5,3},{6,0},{7,1},{8,14},{9,15},{10,... | collective-permute-start | bytes 196616 | tf_op jit(solution)/shard_map/ppermute | solution.py:313
  51.0 8.6 %collective-permute-start.17 = (bf16[128,256]{1,0:T(8,128)(2,1)S(1)}, bf16[128,256]{1,0:T(8,128)(2,1)S(1)}, u32[]{:S(2)}, u32[]{:S(2)}) collective-permute-start(bf16[128,256]{1,0:T(8,128)(2,1)S(1)} %get-tuple-element.63), channel_id=1, source_target_pairs={{0,7},{1,6},{2,5},{3,4},{4,3},{5,2},{6,1},{7,0},{8,15},{9,14},{10,... | collective-permute-start | bytes 196616 | tf_op jit(solution)/shard_map/ppermute | solution.py:313
  52.9 8.5 %collective-permute-start.18 = (bf16[128,256]{1,0:T(8,128)(2,1)S(1)}, bf16[128,256]{1,0:T(8,128)(2,1)S(1)}, u32[]{:S(2)}, u32[]{:S(2)}) collective-permute-start(bf16[128,256]{1,0:T(8,128)(2,1)S(1)} %get-tuple-element.64), channel_id=1, source_target_pairs={{0,2},{1,3},{2,0},{3,1},{4,6},{5,7},{6,4},{7,5},{8,10},{9,11},{10,... | collective-permute-start | bytes 196616 | tf_op jit(solution)/shard_map/ppermute | solution.py:313
  57.6 10.9 %collective-permute-start.24 = (bf16[2,128,256]{2,1,0:T(8,128)(2,1)S(1)}, bf16[2,128,256]{2,1,0:T(8,128)(2,1)S(1)}, u32[]{:S(2)}, u32[]{:S(2)}) collective-permute-start(bf16[2,128,256]{2,1,0:T(8,128)(2,1)S(1)} %get-tuple-element.72), channel_id=1, source_target_pairs={{0,1},{1,0},{2,3},{3,2},{4,5},{5,4},{6,7},{7,6},{8,9},{9,8},{10,11... | collective-permute-start | bytes 393224 | tf_op jit(solution)/shard_map/ppermute | solution.py:313
  57.9 11.3 %collective-permute-start.25 = (bf16[2,128,256]{2,1,0:T(8,128)(2,1)S(1)}, bf16[2,128,256]{2,1,0:T(8,128)(2,1)S(1)}, u32[]{:S(2)}, u32[]{:S(2)}) collective-permute-start(bf16[2,128,256]{2,1,0:T(8,128)(2,1)S(1)} %get-tuple-element.73), channel_id=1, source_target_pairs={{0,6},{1,7},{2,4},{3,5},{4,2},{5,3},{6,0},{7,1},{8,14},{9,15},{10,... | collective-permute-start | bytes 393224 | tf_op jit(solution)/shard_map/ppermute | solution.py:313
  58.1 4.9 %collective-permute-start.19 = (bf16[128,256]{1,0:T(8,128)(2,1)S(1)}, bf16[128,256]{1,0:T(8,128)(2,1)S(1)}, u32[]{:S(2)}, u32[]{:S(2)}) collective-permute-start(bf16[128,256]{1,0:T(8,128)(2,1)S(1)} %get-tuple-element.65), channel_id=1, source_target_pairs={{0,4},{1,5},{2,6},{3,7},{4,0},{5,1},{6,2},{7,3},{8,12},{9,13},{10,... | collective-permute-start | bytes 196616 | tf_op jit(solution)/shard_map/ppermute | solution.py:313
  59.6 6.7 %collective-permute-start.20 = (bf16[128,256]{1,0:T(8,128)(2,1)S(1)}, bf16[128,256]{1,0:T(8,128)(2,1)S(1)}, u32[]{:S(2)}, u32[]{:S(2)}) collective-permute-start(bf16[128,256]{1,0:T(8,128)(2,1)S(1)} %get-tuple-element.66), channel_id=1, source_target_pairs={{0,3},{1,2},{2,1},{3,0},{4,7},{5,6},{6,5},{7,4},{8,11},{9,10},{10,... | collective-permute-start | bytes 196616 | tf_op jit(solution)/shard_map/ppermute | solution.py:313
  61.3 5.4 %collective-permute-start.21 = (bf16[128,256]{1,0:T(8,128)(2,1)S(1)}, bf16[128,256]{1,0:T(8,128)(2,1)S(1)}, u32[]{:S(2)}, u32[]{:S(2)}) collective-permute-start(bf16[128,256]{1,0:T(8,128)(2,1)S(1)} %get-tuple-element.67), channel_id=1, source_target_pairs={{0,5},{1,4},{2,7},{3,6},{4,1},{5,0},{6,3},{7,2},{8,13},{9,12},{10,... | collective-permute-start | bytes 196616 | tf_op jit(solution)/shard_map/ppermute | solution.py:313
  63.0 6.6 %collective-permute-start.26 = (bf16[2,128,256]{2,1,0:T(8,128)(2,1)S(1)}, bf16[2,128,256]{2,1,0:T(8,128)(2,1)S(1)}, u32[]{:S(2)}, u32[]{:S(2)}) collective-permute-start(bf16[2,128,256]{2,1,0:T(8,128)(2,1)S(1)} %get-tuple-element.74), channel_id=1, source_target_pairs={{0,7},{1,6},{2,5},{3,4},{4,3},{5,2},{6,1},{7,0},{8,15},{9,14},{10,... | collective-permute-start | bytes 393224 | tf_op jit(solution)/shard_map/ppermute | solution.py:313
  66.3 7.2 %collective-permute-start.27 = (bf16[2,128,256]{2,1,0:T(8,128)(2,1)S(1)}, bf16[2,128,256]{2,1,0:T(8,128)(2,1)S(1)}, u32[]{:S(2)}, u32[]{:S(2)}) collective-permute-start(bf16[2,128,256]{2,1,0:T(8,128)(2,1)S(1)} %get-tuple-element.75), channel_id=1, source_target_pairs={{0,2},{1,3},{2,0},{3,1},{4,6},{5,7},{6,4},{7,5},{8,10},{9,11},{10,... | collective-permute-start | bytes 393224 | tf_op jit(solution)/shard_map/ppermute | solution.py:313
  66.8 6.9 %collective-permute-start.28 = (bf16[2,128,256]{2,1,0:T(8,128)(2,1)S(1)}, bf16[2,128,256]{2,1,0:T(8,128)(2,1)S(1)}, u32[]{:S(2)}, u32[]{:S(2)}) collective-permute-start(bf16[2,128,256]{2,1,0:T(8,128)(2,1)S(1)} %get-tuple-element.76), channel_id=1, source_target_pairs={{0,4},{1,5},{2,6},{3,7},{4,0},{5,1},{6,2},{7,3},{8,12},{9,13},{10,... | collective-permute-start | bytes 393224 | tf_op jit(solution)/shard_map/ppermute | solution.py:313
  68.6 7.9 %collective-permute-start.29 = (bf16[2,128,256]{2,1,0:T(8,128)(2,1)S(1)}, bf16[2,128,256]{2,1,0:T(8,128)(2,1)S(1)}, u32[]{:S(2)}, u32[]{:S(2)}) collective-permute-start(bf16[2,128,256]{2,1,0:T(8,128)(2,1)S(1)} %get-tuple-element.77), channel_id=1, source_target_pairs={{0,3},{1,2},{2,1},{3,0},{4,7},{5,6},{6,5},{7,4},{8,11},{9,10},{10,... | collective-permute-start | bytes 393224 | tf_op jit(solution)/shard_map/ppermute | solution.py:313
  69.2 7.3 %collective-permute-start.30 = (bf16[2,128,256]{2,1,0:T(8,128)(2,1)S(1)}, bf16[2,128,256]{2,1,0:T(8,128)(2,1)S(1)}, u32[]{:S(2)}, u32[]{:S(2)}) collective-permute-start(bf16[2,128,256]{2,1,0:T(8,128)(2,1)S(1)} %get-tuple-element.78), channel_id=1, source_target_pairs={{0,5},{1,4},{2,7},{3,6},{4,1},{5,0},{6,3},{7,2},{8,13},{9,12},{10,... | collective-permute-start | bytes 393224 | tf_op jit(solution)/shard_map/ppermute | solution.py:313

commit v3 on v2

v3 whole, which is shorter than its diff:
```python
import functools
import math

import jax
import jax.numpy as jnp
from jax import lax
from jax.experimental import pallas as pl
from jax.experimental.pallas import tpu as pltpu
from jax.sharding import Mesh, PartitionSpec as P

HEADS = 16
HEAD_DIM = 128
WINDOW = 512
TILE = 256
HALF = 128
AXES = ("chunk", "part", "head")
GROUP = ("part", "head")
SCALE = HEAD_DIM ** (-0.5)
SCALE_LOG2 = SCALE * math.log2(math.e)
MASKED = -1e30
VMEM_LIMIT = 48 * 1024 * 1024
NT = ((1,), (1,))
NN = ((1,), (0,))
CRIT_ORDER = (0, 1, 6, 7, 2, 4, 3, 5)
REST_ORDER = (0, 1, 6, 7, 2, 4, 3, 5)
DQ_ORDER = (0, 1, 6, 7, 2, 4, 3, 5)
DKV_ORDER = (0, 1, 6, 7, 2, 4, 3, 5)
QG_FIRST = False
EDGE_FLOPS = 4000000000
LATE_FLOPS = 4000000000


def bf16(*shape):
    return jax.ShapeDtypeStruct(shape, jnp.bfloat16)


def f32(*shape):
    return jax.ShapeDtypeStruct(shape, jnp.float32)


def group_index():
    return lax.axis_index("part") * lax.axis_size("head") + lax.axis_index("head")


def group_size():
    return lax.axis_size("part") * lax.axis_size("head")


def aligned(index, step):
    return pl.multiple_of(index * step, step)


def copy_all(pairs, sems):
    copies = [pltpu.make_async_copy(src, dst, sems.at[i]) for i, (src, dst) in enumerate(pairs)]
    for copy in copies:
        copy.start()
    for copy in copies:
        copy.wait()


def dot(a, b, dims):
    return lax.dot_general(a, b, (dims, ((), ())), preferred_element_type=jnp.float32)


def pack_kernel(n, *refs):
    q, g, k, v = refs[:4]
    crit = refs[4 : 4 + n]
    rest = refs[4 + n : 4 + 2 * n]
    stage, sems = refs[4 + 2 * n :]
    me = group_index()
    width = stage.shape[2] // n

    def run(first, second):
        loads = [
            pltpu.make_async_copy(source, stage.at[i], sems.at[i])
            for i, source in enumerate((*first, *second))
        ]
        for load in loads:
            load.start()
        for i, load in enumerate(loads):
            load.wait()
            for m in range(n):
                cols = pl.ds(aligned(jnp.bitwise_xor(me, m), width), width)
                (crit if i < 2 else rest)[m][i % 2] = stage[i, :, cols]

    @pl.when(me >= n // 2)
    def _():
        run((k, v), (q, g))

    @pl.when(me < n // 2)
    def _():
        run((q, g), (k, v))


def place_all(pieces, late, early, me):
    n = len(pieces)
    rows = pieces[0].shape[1]

    def run(near, far):
        for m in range(n):
            at = pl.ds(aligned(jnp.bitwise_and(jnp.bitwise_xor(me, m), n // 2 - 1), rows), rows)
            (near if m < n // 2 else far)[:, at] = pieces[m][...]

    @pl.when(me >= n // 2)
    def _():
        run(late, early)

    @pl.when(me < n // 2)
    def _():
        run(early, late)


def halo_kernel(n, *refs):
    crit = by_slot(CRIT_ORDER, refs[:n])
    kv_late, qg_early, *sends = refs[n:]
    place_all(crit, kv_late, qg_early, group_index())
    if sends:
        sends[0][...] = kv_late[:, kv_late.shape[1] - WINDOW :]
        sends[1][...] = qg_early[:, :WINDOW]


def load(parts, t, lo, hi, lanes):
    out, start = [], 0
    for ref in parts:
        a, b = max(lo - start, 0), min(hi - start, ref.shape[1])
        if a < b:
            out.append(ref[t, a:b, lanes])
        start += ref.shape[1]
    return out[0] if len(out) == 1 else jnp.concatenate(out, axis=0)


def softmax_block(qb, gb, kb, vb, bias, blind):
    row = lax.broadcasted_iota(jnp.int32, (HALF, HALF), 0)
    col = lax.broadcasted_iota(jnp.int32, (HALF, HALF), 1)
    s = dot(kb, qb, NT)
    dp = dot(vb, gb, NT)
    span = WINDOW // HALF + 1
    nothing = jnp.zeros((HALF, HALF), jnp.bfloat16)
    p_parts, ds_parts, stats = [], [], []
    for c in range(TILE // HALF):
        cols = slice(c * HALF, (c + 1) * HALF)
        parts = [s[(c + r) * HALF : (c + r + 1) * HALF, cols] for r in range(span)]
        parts[0] = jnp.where(row > col, parts[0], MASKED)
        parts[-1] = jnp.where(row <= col, parts[-1], MASKED)
        parts = [b + bias if (c + r) * HALF < blind else b for r, b in enumerate(parts)]
        sc = jnp.concatenate(parts, axis=0)
        dpc = dp[c * HALF : (c + span) * HALF, cols]
        top = jnp.max(sc, axis=0, keepdims=True) * SCALE_LOG2
        e = jnp.exp2(sc * SCALE_LOG2 - top)
        inverse = 1.0 / jnp.sum(e, axis=0, keepdims=True)
        p = e * inverse
        dots = jnp.sum(p * dpc, axis=0, keepdims=True)
        ds = (p * (dpc - dots)).astype(jnp.bfloat16)
        pad = [nothing] * c, [nothing] * (TILE // HALF - 1 - c)
        p_parts.append(jnp.concatenate([*pad[0], p.astype(jnp.bfloat16), *pad[1]], axis=0))
        ds_parts.append(jnp.concatenate([*pad[0], ds, *pad[1]], axis=0))
        stats.append((top, inverse, dots))
    return jnp.concatenate(p_parts, axis=1), jnp.concatenate(ds_parts, axis=1), stats


def late_kernel(n, heads, *refs):
    rest = by_slot(REST_ORDER, refs[:n])
    kv_late, qg_early, qg_late, kv_early, dq, dkv = refs[n:]
    place_all(rest, qg_late, kv_early, group_index())
    total = dkv.shape[1]
    qg, kv = (qg_early, qg_late), (kv_early, kv_late)
    for h in range(heads):
        lanes = slice(h * HEAD_DIM, (h + 1) * HEAD_DIM)
        key_t = load(kv, 0, 0, total, lanes).T
        for start in range(0, total - WINDOW, TILE):
            keys = slice(start, start + 3 * TILE)
            mine = slice(start + WINDOW, start + WINDOW + TILE)
            qb, gb = (load(qg, t, start + WINDOW, start + WINDOW + TILE, lanes) for t in range(2))
            kb, vb = (load(kv, t, start, start + 3 * TILE, lanes) for t in range(2))
            p_low, ds, _ = softmax_block(qb, gb, kb, vb, 0.0, 0)
            out = slice(start, start + TILE)
            dq[out, lanes] = (dot(key_t[:, keys], ds, NN) * SCALE).T.astype(jnp.bfloat16)
            for t, add in enumerate((dot(ds, qb, NN), dot(p_low, gb, NN))):
                if start == 0:
                    dkv[t, keys, lanes] = add
                else:
                    older = slice(start, start + 2 * TILE)
                    dkv[t, older, lanes] += add[: 2 * TILE]
                    dkv[t, mine, lanes] = add[2 * TILE :]


def early_kernel(n, heads, *refs):
    qg_early, qg_late, kv_early, kv_late, kv_halo, dq_in, dkv_in = refs[:7]
    refs = refs[7 + QG_FIRST :]
    dq_out = refs[:n]
    front, stat, dq, acc = refs[n:]
    me = group_index()
    rows = dq_out[0].shape[0]
    first = lax.axis_index("chunk") == 0
    stat[...] = jnp.zeros_like(stat)
    dq[WINDOW:] = dq_in[...]
    acc[...] = dkv_in[:, :WINDOW]
    bias = jnp.where(first, MASKED, 0.0)
    qg, kv = (qg_early, qg_late), (kv_halo, kv_early, kv_late)
    for h in range(heads):
        lanes = slice(h * HEAD_DIM, (h + 1) * HEAD_DIM)
        key_t = load(kv, 0, 0, 2 * WINDOW, lanes).T
        for start in range(0, WINDOW, TILE):
            keys = slice(start, start + 3 * TILE)
            mine = slice(start, start + TILE)
            qb, gb = (load(qg, t, start, start + TILE, lanes) for t in range(2))
            kb, vb = (load(kv, t, start, start + 3 * TILE, lanes) for t in range(2))
            p_low, ds, stats = softmax_block(qb, gb, kb, vb, bias, WINDOW - start)
            dq[mine, lanes] = (dot(key_t[:, keys], ds, NN) * SCALE).T.astype(jnp.bfloat16)
            own = slice(0, start + TILE)
            acc[0, own, lanes] += dot(ds[WINDOW - start :], qb, NN)
            acc[1, own, lanes] += dot(p_low[WINDOW - start :], gb, NN)
            for c, rows_of in enumerate(stats):
                at = slice(start + c * HALF, start + (c + 1) * HALF)
                for k, value in enumerate(rows_of):
                    stat[3 * h + k : 3 * h + k + 1, at] = value
    for m in range(n):
        dq_out[m][...] = dq[pl.ds(aligned(jnp.bitwise_xor(me, m), rows), rows)]
    front[0] = (acc[0] * SCALE).astype(jnp.bfloat16)
    front[1] = acc[1].astype(jnp.bfloat16)


def edge_kernel(n, heads, *refs):
    kv_early, kv_late, qg, front, dkv_in, stat = refs[:6]
    out = refs[6 : 6 + n]
    full, acc = refs[6 + n :]
    me = group_index()
    total = dkv_in.shape[1]
    done = total - WINDOW
    rows = total // n
    kv = (kv_early, kv_late)
    row = lax.broadcasted_iota(jnp.int32, (TILE, TILE), 0)
    col = lax.broadcasted_iota(jnp.int32, (TILE, TILE), 1)
    acc[...] = dkv_in[:, WINDOW:]
    for h in range(heads):
        lanes = slice(h * HEAD_DIM, (h + 1) * HEAD_DIM)
        for start in range(0, WINDOW, TILE):
            mine = slice(start, start + TILE)
            qb, gb = qg[0, mine, lanes], qg[1, mine, lanes]
            kb, vb = (load(kv, t, done + start, total, lanes) for t in range(2))
            s = dot(kb, qb, NT)
            newest = jnp.where(row > col, s[:TILE], MASKED)
            s = newest if len(s) == TILE else jnp.concatenate([newest, s[TILE:]], axis=0)
            top, inverse, dots = (stat[3 * h + k : 3 * h + k + 1, mine] for k in range(3))
            p = jnp.exp2(s * SCALE_LOG2 - top) * inverse
            dp = dot(vb, gb, NT)
            ds = (p * (dp - dots)).astype(jnp.bfloat16)
            at = slice(done - WINDOW + start, done)
            acc[0, at, lanes] += dot(ds, qb, NN)
            acc[1, at, lanes] += dot(p.astype(jnp.bfloat16), gb, NN)
    full[:, :WINDOW] = front[...]
    full[0, WINDOW:] = (acc[0] * SCALE).astype(jnp.bfloat16)
    full[1, WINDOW:] = acc[1].astype(jnp.bfloat16)
    for m in range(n):
        out[m][...] = full[:, pl.ds(aligned(jnp.bitwise_xor(me, m), rows), rows)]


def unpack_kernel(n, *refs):
    dq_in = by_slot(DQ_ORDER, refs[:n])
    dkv_in = by_slot(DKV_ORDER, refs[n : 2 * n])
    dq, dk, dv, sems = refs[2 * n :]
    me = group_index()
    width = dq_in[0].shape[1]
    pairs = []
    for m in range(n):
        cols = pl.ds(aligned(jnp.bitwise_xor(me, m), width), width)
        pairs.append((dq_in[m], dq.at[:, cols]))
        pairs.append((dkv_in[m].at[0], dk.at[:, cols]))
        pairs.append((dkv_in[m].at[1], dv.at[:, cols]))
    copy_all(pairs, sems)


def call(kernel, outs, scratch, sems, *operands, space=pl.ANY, limit=VMEM_LIMIT, flops=0):
    held = pl.BlockSpec(memory_space=pltpu.VMEM)
    loose = pl.BlockSpec(memory_space=space)
    arrays = [x[0] if isinstance(x, tuple) else x for x in operands]
    return pl.pallas_call(
        kernel,
        out_shape=outs,
        in_specs=[held if isinstance(x, tuple) else loose for x in operands],
        out_specs=[held if not isinstance(x, jax.ShapeDtypeStruct) else pl.BlockSpec(memory_space=pl.ANY) for x in outs],
        scratch_shapes=[*scratch, *([pltpu.SemaphoreType.DMA((sems,))] if sems else [])],
        compiler_params=pltpu.CompilerParams(vmem_limit_bytes=limit),
        cost_estimate=pl.CostEstimate(flops=flops, bytes_accessed=0, transcendentals=0) if flops else None,
    )(*arrays)


def held(arrays):
    return [(x,) for x in arrays]


def vmem(shape):
    return pltpu.VMEM(shape.shape, shape.dtype)


def order_of(order, n):
    return [m for m in order if m < n] + list(range(len(order), n))


def by_slot(order, refs):
    order = order_of(order, len(refs))
    return [refs[order.index(m)] for m in range(len(refs))]


def exchanged(order, pieces):
    n = len(pieces)
    return [
        lax.ppermute(pieces[m], GROUP, [(i, i ^ m) for i in range(n)]) if m else pieces[0]
        for m in order_of(order, n)
    ]


def per_device(queries, key_vectors, value_vectors, grad_output):
    n = group_size()
    chunks = lax.axis_size("chunk")
    rows, model = queries.shape
    heads = HEADS // n
    width = model // n
    total = n * rows
    done = total - WINDOW
    piece = bf16(2, rows, width)
    packed = call(
        functools.partial(pack_kernel, n),
        [vmem(piece)] * (2 * n),
        [vmem(bf16(4, rows, model))], 4,
        queries, grad_output, key_vectors, value_vectors, space=pltpu.HBM, limit=None,
    )
    crit = exchanged(CRIT_ORDER, packed[:n])
    half = total // 2
    end = vmem(bf16(2, WINDOW, width))
    halves = vmem(bf16(2, half, width))
    sends = call(
        functools.partial(halo_kernel, n),
        [halves, halves] + [end, end] * (half > WINDOW), [], 0, *held(crit),
    )
    kv_late, qg_early = sends[:2]
    kv_send, qg_send = sends[-2:]
    forward = [(i, i + 1) for i in range(chunks - 1)]
    backward = [(i + 1, i) for i in range(chunks - 1)]
    kv_halo = lax.ppermute(kv_send, "chunk", forward)
    qg_halo = lax.ppermute(qg_send, "chunk", backward)
    rest = exchanged(REST_ORDER, packed[n:])
    stat_out = vmem(f32(-(-3 * heads // 8) * 8, WINDOW))
    qg_late, kv_early, dq_late, partial = call(
        functools.partial(late_kernel, n, heads),
        [halves, halves, vmem(bf16(done, width)), vmem(f32(2, total, width))],
        [], 0,
        *held(rest), (kv_late,), (qg_early,), flops=LATE_FLOPS,
    )
    *dq, front, stat = call(
        functools.partial(early_kernel, n, heads),
        [vmem(bf16(rows, width))] * n + [end, stat_out],
        [vmem(bf16(total, width)), vmem(f32(2, WINDOW, width))], 0,
        *held((qg_early, qg_late, kv_early, kv_late, kv_halo, dq_late, partial)),
        *([qg_halo] if QG_FIRST else []),
    )
    stat_halo = lax.ppermute(stat, "chunk", backward)
    dq = exchanged(DQ_ORDER, dq)
    dkv = call(
        functools.partial(edge_kernel, n, heads),
        [vmem(piece)] * n, [vmem(bf16(2, total, width)), vmem(f32(2, done, width))], 0,
        *held((kv_early, kv_late, qg_halo, front, partial, stat_halo)), flops=EDGE_FLOPS,
    )
    dkv = exchanged(DKV_ORDER, dkv)
    out = bf16(rows, model)
    return tuple(
        call(functools.partial(unpack_kernel, n), [out] * 3, [], 3 * n, *held(dq), *held(dkv))
    )


def solution(mesh):
    seq, head = mesh.devices.shape
    part = max(1, min(seq, HEADS // 2 // head))
    fine = Mesh(mesh.devices.reshape(seq // part, part, head), AXES)
    placed = P(AXES, None)
    return jax.shard_map(
        per_device,
        mesh=fine,
        in_specs=(placed,) * 4,
        out_specs=(placed,) * 3,
        check_vma=False,
    )
```

time: 79.1 us -> 70.8 us (0.90); the launches traced: 77.8 us -> 70.6 us
  Pallas kernels: 18.5 us -> 11 us
  waiting for transfers between devices: 16.4 us -> 20.6 us
  starting transfers between devices: 40.4 us -> 38.2 us
  local copies, waits for them, and re-layouts: 1.81 us -> 0 us
    ppermute x28, waiting for transfers between devices: 12.3 us -> 20.6 us  [exchanged(): lax.ppermute(pieces[m], GROUP, [(i, i ^ m) for i in range(n)])]
    pallas_call x6, Pallas kernels: 18.5 us -> 11 us  [call(): pl.pallas_call(kernel, out_shape=outs, in_specs=[held if isinstance(x, tu...]
    ppermute x1, waiting for transfers between devices: 4.11 us -> 0.01 us  [per_device(): kv_halo = lax.ppermute(kv_send, 'chunk', forward)]
    ppermute x28, starting transfers between devices: 33.1 us -> 30.9 us  [exchanged(): lax.ppermute(pieces[m], GROUP, [(i, i ^ m) for i in range(n)])]
    unnamed x4 -> x0, local copies, waits for them, and re-layouts: 1.81 us -> none
  transfers between devices with their start and end apart: 31 -> 31, of which waited for: 10 -> 11; matrix products, arithmetic and copies ran while one was open for 0% -> 0% of each run, Pallas kernels for 18% -> 11%
where the time goes in v3:
time: 70.8 us; the launch traced here: 70.6 us
  starting transfers between devices  38.2 us (54%)
  waiting for transfers between devices  20.6 us (29%)
  Pallas kernels  11 us (16%)
  between operations  0.74 us (1%)
    ppermute x28, starting transfers between devices, exchanged(): lax.ppermute(pieces[m], GROUP, [(i, i ^ m) for i in range(n)])  30.9 us
    ppermute x28, waiting for transfers between devices, exchanged(): lax.ppermute(pieces[m], GROUP, [(i, i ^ m) for i in range(n)])  20.6 us
    pallas_call x6, Pallas kernels, call(): pl.pallas_call(kernel, out_shape=outs, in_specs=[held if isinstance(x, tu...  11 us
    ppermute x1, starting transfers between devices, per_device(): kv_halo = lax.ppermute(kv_send, 'chunk', forward)  3.2 us
    ppermute x1, starting transfers between devices, per_device(): stat_halo = lax.ppermute(stat, 'chunk', backward)  2.11 us
    ppermute x1, starting transfers between devices, per_device(): qg_halo = lax.ppermute(qg_send, 'chunk', backward)  2.08 us
  transfers between devices with their start and end apart: 31, of which 11 were waited for; matrix products, arithmetic and copies ran while one was open for 0% of the time, Pallas kernels for 11%

profile of v3, /device:TPU:17, one launch (start us, length us, event | category | flops | bytes accessed | tf_op | source)
XLA Modules:
  0.0 70.6 jit_solution(3582206048144683756)
XLA Ops:
  0.6 1.6 %shard_map.67 = (bf16[2,128,256]{2,1,0:T(8,128)(2,1)S(1)}, bf16[2,128,256]{2,1,0:T(8,128)(2,1)S(1)}, bf16[2,128,256]{2,1,0:T(8,128)(2,1)S(1)}, bf16[2,128,256]{2...) custom-call(bf16[128,2048]{1,0:T(8,128)(2,1)} %refs_0_.1, ...), custom_call_target="tpu_custom_call" | custom-call | tf_op jit(solution)/shard_map/pallas_call | solution.py:277
  2.3 0.7 %collective-permute-start = (bf16[2,128,256]{2,1,0:T(8,128)(2,1)S(1)}, bf16[2,128,256]{2,1,0:T(8,128)(2,1)S(1)}, u32[]{:S(2)}, u32[]{:S(2)}) collective-permute-start(bf16[2,128,256]{2,1,0:T(8,128)(2,1)S(1)} %get-tuple-element.44), channel_id=1, source_target_pairs={{0,1},{1,0},{2,3},{3,2},{4,5},{5,4},{6,7},{7,6},{8,9},{9,8},{10,11... | collective-permute-start | bytes 393224 | tf_op jit(solution)/shard_map/ppermute | solution.py:308
  3.0 2.2 %collective-permute-start.1 = (bf16[2,128,256]{2,1,0:T(8,128)(2,1)S(1)}, bf16[2,128,256]{2,1,0:T(8,128)(2,1)S(1)}, u32[]{:S(2)}, u32[]{:S(2)}) collective-permute-start(bf16[2,128,256]{2,1,0:T(8,128)(2,1)S(1)} %get-tuple-element.45), channel_id=1, source_target_pairs={{0,6},{1,7},{2,4},{3,5},{4,2},{5,3},{6,0},{7,1},{8,14},{9,15},{10,... | collective-permute-start | bytes 393224 | tf_op jit(solution)/shard_map/ppermute | solution.py:308
  5.2 0.4 collective-permute-start.2
  5.6 1.2 %collective-permute-start.3 = (bf16[2,128,256]{2,1,0:T(8,128)(2,1)S(1)}, bf16[2,128,256]{2,1,0:T(8,128)(2,1)S(1)}, u32[]{:S(2)}, u32[]{:S(2)}) collective-permute-start(bf16[2,128,256]{2,1,0:T(8,128)(2,1)S(1)} %get-tuple-element.47), channel_id=1, source_target_pairs={{0,2},{1,3},{2,0},{3,1},{4,6},{5,7},{6,4},{7,5},{8,10},{9,11},{10,... | collective-permute-start | bytes 393224 | tf_op jit(solution)/shard_map/ppermute | solution.py:308
  6.8 1.2 %collective-permute-start.4 = (bf16[2,128,256]{2,1,0:T(8,128)(2,1)S(1)}, bf16[2,128,256]{2,1,0:T(8,128)(2,1)S(1)}, u32[]{:S(2)}, u32[]{:S(2)}) collective-permute-start(bf16[2,128,256]{2,1,0:T(8,128)(2,1)S(1)} %get-tuple-element.48), channel_id=1, source_target_pairs={{0,4},{1,5},{2,6},{3,7},{4,0},{5,1},{6,2},{7,3},{8,12},{9,13},{10,... | collective-permute-start | bytes 393224 | tf_op jit(solution)/shard_map/ppermute | solution.py:308
  8.1 0.0 collective-permute-done.refs_1_
  8.1 0.9 %collective-permute-start.5 = (bf16[2,128,256]{2,1,0:T(8,128)(2,1)S(1)}, bf16[2,128,256]{2,1,0:T(8,128)(2,1)S(1)}, u32[]{:S(2)}, u32[]{:S(2)}) collective-permute-start(bf16[2,128,256]{2,1,0:T(8,128)(2,1)S(1)} %get-tuple-element.49), channel_id=1, source_target_pairs={{0,3},{1,2},{2,1},{3,0},{4,7},{5,6},{6,5},{7,4},{8,11},{9,10},{10,... | collective-permute-start | bytes 393224 | tf_op jit(solution)/shard_map/ppermute | solution.py:308
  8.9 0.0 collective-permute-done.1.refs_2_
  9.0 2.5 %collective-permute-start.6 = (bf16[2,128,256]{2,1,0:T(8,128)(2,1)S(1)}, bf16[2,128,256]{2,1,0:T(8,128)(2,1)S(1)}, u32[]{:S(2)}, u32[]{:S(2)}) collective-permute-start(bf16[2,128,256]{2,1,0:T(8,128)(2,1)S(1)} %get-tuple-element.50), channel_id=1, source_target_pairs={{0,5},{1,4},{2,7},{3,6},{4,1},{5,0},{6,3},{7,2},{8,13},{9,12},{10,... | collective-permute-start | bytes 393224 | tf_op jit(solution)/shard_map/ppermute | solution.py:308
  11.5 0.9 %collective-permute-done.2.refs_3_ = bf16[2,128,256]{2,1,0:T(8,128)(2,1)S(1)} collective-permute-done((bf16[2,128,256]{2,1,0:T(8,128)(2,1)S(1)}, bf16[2,128,256]{2,1,0:T(8,128)(2,1)S(1)}, u32[]{:S(2)}, u32[]{:S(2)}) %collective-permute-start.2) | collective-permute-done | bytes 131104 | tf_op jit(solution)/shard_map/ppermute | solution.py:308
  12.4 1.3 %collective-permute-start.10 = (bf16[2,128,256]{2,1,0:T(8,128)(2,1)S(1)}, bf16[2,128,256]{2,1,0:T(8,128)(2,1)S(1)}, u32[]{:S(2)}, u32[]{:S(2)}) collective-permute-start(bf16[2,128,256]{2,1,0:T(8,128)(2,1)S(1)} %get-tuple-element.56), channel_id=1, source_target_pairs={{0,2},{1,3},{2,0},{3,1},{4,6},{5,7},{6,4},{7,5},{8,10},{9,11},{10,... | collective-permute-start | bytes 393224 | tf_op jit(solution)/shard_map/ppermute | solution.py:308
  13.7 1.0 %collective-permute-done.3.refs_4_ = bf16[2,128,256]{2,1,0:T(8,128)(2,1)S(1)} collective-permute-done((bf16[2,128,256]{2,1,0:T(8,128)(2,1)S(1)}, bf16[2,128,256]{2,1,0:T(8,128)(2,1)S(1)}, u32[]{:S(2)}, u32[]{:S(2)}) %collective-permute-start.3) | collective-permute-done | bytes 131104 | tf_op jit(solution)/shard_map/ppermute | solution.py:308
  14.7 0.3 collective-permute-start.11
  15.0 0.0 collective-permute-done.4.refs_5_
  15.1 2.6 %collective-permute-start.12 = (bf16[2,128,256]{2,1,0:T(8,128)(2,1)S(1)}, bf16[2,128,256]{2,1,0:T(8,128)(2,1)S(1)}, u32[]{:S(2)}, u32[]{:S(2)}) collective-permute-start(bf16[2,128,256]{2,1,0:T(8,128)(2,1)S(1)} %get-tuple-element.58), channel_id=1, source_target_pairs={{0,3},{1,2},{2,1},{3,0},{4,7},{5,6},{6,5},{7,4},{8,11},{9,10},{10,... | collective-permute-start | bytes 393224 | tf_op jit(solution)/shard_map/ppermute | solution.py:308
  17.6 0.5 collective-permute-done.5.refs_6_
  18.1 0.0 collective-permute-start.13
  18.1 0.0 collective-permute-done.6.refs_7_
  18.1 0.1 shard_map.68
  18.2 3.2 %collective-permute-start.14 = (bf16[2,512,256]{2,1,0:T(8,128)(2,1)S(1)}, bf16[2,512,256]{2,1,0:T(8,128)(2,1)S(1)}, u32[]{:S(2)}, u32[]{:S(2)}) collective-permute-start(bf16[2,512,256]{2,1,0:T(8,128)(2,1)S(1)} %get-tuple-element.60.refs_8_.refs_3_.refs_1_), channel_id=1, source_target_pairs={{0,8},{8,16},{16,24},{1,9},{9,17},{17,25},{2,10},{10,18},{18,26},{... | collective-permute-start | bytes 1572872 | tf_op jit(solution)/shard_map/ppermute | solution.py:340
  21.4 0.0 collective-permute-done.10.refs_4_
  21.4 2.1 %collective-permute-start.22 = (bf16[2,512,256]{2,1,0:T(8,128)(2,1)S(1)}, bf16[2,512,256]{2,1,0:T(8,128)(2,1)S(1)}, u32[]{:S(2)}, u32[]{:S(2)}) collective-permute-start(bf16[2,512,256]{2,1,0:T(8,128)(2,1)S(1)} %get-tuple-element.51.refs_9_.refs_0_), channel_id=1, source_target_pairs={{8,0},{16,8},{24,16},{9,1},{17,9},{25,17},{10,2},{18,10},{26,18},{... | collective-permute-start | bytes 1572872 | tf_op jit(solution)/shard_map/ppermute | solution.py:341
  23.5 0.0 collective-permute-done.11.refs_5_
  23.5 1.7 %collective-permute-start.7 = (bf16[2,128,256]{2,1,0:T(8,128)(2,1)S(1)}, bf16[2,128,256]{2,1,0:T(8,128)(2,1)S(1)}, u32[]{:S(2)}, u32[]{:S(2)}) collective-permute-start(bf16[2,128,256]{2,1,0:T(8,128)(2,1)S(1)} %get-tuple-element.53), channel_id=1, source_target_pairs={{0,1},{1,0},{2,3},{3,2},{4,5},{5,4},{6,7},{7,6},{8,9},{9,8},{10,11... | collective-permute-start | bytes 393224 | tf_op jit(solution)/shard_map/ppermute | solution.py:308
  25.3 0.0 collective-permute-done.12.refs_6_
  25.3 1.7 %collective-permute-start.8 = (bf16[2,128,256]{2,1,0:T(8,128)(2,1)S(1)}, bf16[2,128,256]{2,1,0:T(8,128)(2,1)S(1)}, u32[]{:S(2)}, u32[]{:S(2)}) collective-permute-start(bf16[2,128,256]{2,1,0:T(8,128)(2,1)S(1)} %get-tuple-element.54), channel_id=1, source_target_pairs={{0,6},{1,7},{2,4},{3,5},{4,2},{5,3},{6,0},{7,1},{8,14},{9,15},{10,... | collective-permute-start | bytes 393224 | tf_op jit(solution)/shard_map/ppermute | solution.py:308
  27.0 0.0 collective-permute-done.13.refs_7_
  27.0 0.9 %collective-permute-start.9 = (bf16[2,128,256]{2,1,0:T(8,128)(2,1)S(1)}, bf16[2,128,256]{2,1,0:T(8,128)(2,1)S(1)}, u32[]{:S(2)}, u32[]{:S(2)}) collective-permute-start(bf16[2,128,256]{2,1,0:T(8,128)(2,1)S(1)} %get-tuple-element.55), channel_id=1, source_target_pairs={{0,7},{1,6},{2,5},{3,4},{4,3},{5,2},{6,1},{7,0},{8,15},{9,14},{10,... | collective-permute-start | bytes 393224 | tf_op jit(solution)/shard_map/ppermute | solution.py:308
  27.9 0.0 collective-permute-done.7.refs_1_
  27.9 3.3 %collective-permute-done.8.refs_2_ = bf16[2,128,256]{2,1,0:T(8,128)(2,1)S(1)} collective-permute-done((bf16[2,128,256]{2,1,0:T(8,128)(2,1)S(1)}, bf16[2,128,256]{2,1,0:T(8,128)(2,1)S(1)}, u32[]{:S(2)}, u32[]{:S(2)}) %collective-permute-start.8) | collective-permute-done | bytes 131104 | tf_op jit(solution)/shard_map/ppermute | solution.py:308
  31.2 3.0 %collective-permute-done.9.refs_3_ = bf16[2,128,256]{2,1,0:T(8,128)(2,1)S(1)} collective-permute-done((bf16[2,128,256]{2,1,0:T(8,128)(2,1)S(1)}, bf16[2,128,256]{2,1,0:T(8,128)(2,1)S(1)}, u32[]{:S(2)}, u32[]{:S(2)}) %collective-permute-start.9) | collective-permute-done | bytes 131104 | tf_op jit(solution)/shard_map/ppermute | solution.py:308
  34.2 3.5 %shard_map.69 = (bf16[2,512,256]{2,1,0:T(8,128)(2,1)S(1)}, bf16[2,512,256]{2,1,0:T(8,128)(2,1)S(1)}, bf16[512,256]{1,0:T(8,128)(2,1)S(1)}, f32[2,1024,256]{2,1,0:T(8,128)S(1)}) custom-call(bf16[2,128,256]{2,1,0:T(8,128)(2,1)S(1)} %get-tuple-element.52.refs_0_, bf16[2,128,256]{2,1,0:T(8,128)(2,1)S(1)} %collective-permute-done.7.refs_1_, ...), custom_call_target="tpu_custom_call" | custom-call | flops 4000000000 | tf_op jit(solution)/shard_map/pallas_call | solution.py:277
  37.7 0.0 collective-permute-done.14.refs_4_
  37.7 3.2 %shard_map.70 = (bf16[128,256]{1,0:T(8,128)(2,1)S(1)}, bf16[128,256]{1,0:T(8,128)(2,1)S(1)}, bf16[128,256]{1,0:T(8,128)(2,1)S(1)}, bf16[128,256]{1,0:T(8,128)(2,...) custom-call(bf16[2,512,256]{2,1,0:T(8,128)(2,1)S(1)} %get-tuple-elem, ...), custom_call_target="tpu_custom_call" | custom-call | tf_op jit(solution)/shard_map/pallas_call | solution.py:277
  41.0 2.1 %collective-permute-start.23 = (f32[8,512]{1,0:T(8,128)S(1)}, f32[8,512]{1,0:T(8,128)S(1)}, u32[]{:S(2)}, u32[]{:S(2)}) collective-permute-start(f32[8,512]{1,0:T(8,128)S(1)} %get-tuple-element.74), channel_id=1, source_target_pairs={{8,0},{16,8},{24,16},{9,1},{17,9},{25,17},{10,2},{18,10},{26,18},{... | collective-permute-start | bytes 49160 | tf_op jit(solution)/shard_map/ppermute | solution.py:357
  43.1 0.6 collective-permute-start.15
  43.7 1.7 %collective-permute-start.16 = (bf16[128,256]{1,0:T(8,128)(2,1)S(1)}, bf16[128,256]{1,0:T(8,128)(2,1)S(1)}, u32[]{:S(2)}, u32[]{:S(2)}) collective-permute-start(bf16[128,256]{1,0:T(8,128)(2,1)S(1)} %get-tuple-element.67), channel_id=1, source_target_pairs={{0,6},{1,7},{2,4},{3,5},{4,2},{5,3},{6,0},{7,1},{8,14},{9,15},{10,... | collective-permute-start | bytes 196616 | tf_op jit(solution)/shard_map/ppermute | solution.py:308
  45.3 0.9 %collective-permute-start.17 = (bf16[128,256]{1,0:T(8,128)(2,1)S(1)}, bf16[128,256]{1,0:T(8,128)(2,1)S(1)}, u32[]{:S(2)}, u32[]{:S(2)}) collective-permute-start(bf16[128,256]{1,0:T(8,128)(2,1)S(1)} %get-tuple-element.68), channel_id=1, source_target_pairs={{0,7},{1,6},{2,5},{3,4},{4,3},{5,2},{6,1},{7,0},{8,15},{9,14},{10,... | collective-permute-start | bytes 196616 | tf_op jit(solution)/shard_map/ppermute | solution.py:308
  46.3 1.0 %collective-permute-start.18 = (bf16[128,256]{1,0:T(8,128)(2,1)S(1)}, bf16[128,256]{1,0:T(8,128)(2,1)S(1)}, u32[]{:S(2)}, u32[]{:S(2)}) collective-permute-start(bf16[128,256]{1,0:T(8,128)(2,1)S(1)} %get-tuple-element.69), channel_id=1, source_target_pairs={{0,2},{1,3},{2,0},{3,1},{4,6},{5,7},{6,4},{7,5},{8,10},{9,11},{10,... | collective-permute-start | bytes 196616 | tf_op jit(solution)/shard_map/ppermute | solution.py:308
  47.3 1.2 %shard_map.71 = (bf16[2,128,256]{2,1,0:T(8,128)(2,1)S(1)}, bf16[2,128,256]{2,1,0:T(8,128)(2,1)S(1)}, bf16[2,128,256]{2,1,0:T(8,128)(2,1)S(1)}, bf16[2,128,256]{2...) custom-call(bf16[2,512,256]{2,1,0:T(8,128)(2,1)S(1)} %get-tuple-elem, ...), custom_call_target="tpu_custom_call" | custom-call | flops 4000000000 | tf_op jit(solution)/shard_map/pallas_call | solution.py:277
  48.5 0.5 collective-permute-start.24
  49.0 0.0 collective-permute-done.15.refs_1_
  49.0 0.9 %collective-permute-start.25 = (bf16[2,128,256]{2,1,0:T(8,128)(2,1)S(1)}, bf16[2,128,256]{2,1,0:T(8,128)(2,1)S(1)}, u32[]{:S(2)}, u32[]{:S(2)}) collective-permute-start(bf16[2,128,256]{2,1,0:T(8,128)(2,1)S(1)} %get-tuple-element.77), channel_id=1, source_target_pairs={{0,6},{1,7},{2,4},{3,5},{4,2},{5,3},{6,0},{7,1},{8,14},{9,15},{10,... | collective-permute-start | bytes 393224 | tf_op jit(solution)/shard_map/ppermute | solution.py:308
  50.0 0.0 collective-permute-done.16.refs_2_
  50.0 0.7 %collective-permute-start.19 = (bf16[128,256]{1,0:T(8,128)(2,1)S(1)}, bf16[128,256]{1,0:T(8,128)(2,1)S(1)}, u32[]{:S(2)}, u32[]{:S(2)}) collective-permute-start(bf16[128,256]{1,0:T(8,128)(2,1)S(1)} %get-tuple-element.70), channel_id=1, source_target_pairs={{0,4},{1,5},{2,6},{3,7},{4,0},{5,1},{6,2},{7,3},{8,12},{9,13},{10,... | collective-permute-start | bytes 196616 | tf_op jit(solution)/shard_map/ppermute | solution.py:308
  50.7 0.0 collective-permute-done.17.refs_3_
  50.7 1.5 %collective-permute-start.20 = (bf16[128,256]{1,0:T(8,128)(2,1)S(1)}, bf16[128,256]{1,0:T(8,128)(2,1)S(1)}, u32[]{:S(2)}, u32[]{:S(2)}) collective-permute-start(bf16[128,256]{1,0:T(8,128)(2,1)S(1)} %get-tuple-element.71), channel_id=1, source_target_pairs={{0,3},{1,2},{2,1},{3,0},{4,7},{5,6},{6,5},{7,4},{8,11},{9,10},{10,... | collective-permute-start | bytes 196616 | tf_op jit(solution)/shard_map/ppermute | solution.py:308
  52.2 0.0 collective-permute-done.18.refs_4_
  52.2 0.7 %collective-permute-start.21 = (bf16[128,256]{1,0:T(8,128)(2,1)S(1)}, bf16[128,256]{1,0:T(8,128)(2,1)S(1)}, u32[]{:S(2)}, u32[]{:S(2)}) collective-permute-start(bf16[128,256]{1,0:T(8,128)(2,1)S(1)} %get-tuple-element.72), channel_id=1, source_target_pairs={{0,5},{1,4},{2,7},{3,6},{4,1},{5,0},{6,3},{7,2},{8,13},{9,12},{10,... | collective-permute-start | bytes 196616 | tf_op jit(solution)/shard_map/ppermute | solution.py:308
  52.9 3.9 %collective-permute-done.19.refs_5_ = bf16[128,256]{1,0:T(8,128)(2,1)S(1)} collective-permute-done((bf16[128,256]{1,0:T(8,128)(2,1)S(1)}, bf16[128,256]{1,0:T(8,128)(2,1)S(1)}, u32[]{:S(2)}, u32[]{:S(2)}) %collective-permute-start.19) | collective-permute-done | bytes 65568 | tf_op jit(solution)/shard_map/ppermute | solution.py:308
  56.8 1.4 %collective-permute-start.26 = (bf16[2,128,256]{2,1,0:T(8,128)(2,1)S(1)}, bf16[2,128,256]{2,1,0:T(8,128)(2,1)S(1)}, u32[]{:S(2)}, u32[]{:S(2)}) collective-permute-start(bf16[2,128,256]{2,1,0:T(8,128)(2,1)S(1)} %get-tuple-element.78), channel_id=1, source_target_pairs={{0,7},{1,6},{2,5},{3,4},{4,3},{5,2},{6,1},{7,0},{8,15},{9,14},{10,... | collective-permute-start | bytes 393224 | tf_op jit(solution)/shard_map/ppermute | solution.py:308
  58.2 1.2 %collective-permute-start.27 = (bf16[2,128,256]{2,1,0:T(8,128)(2,1)S(1)}, bf16[2,128,256]{2,1,0:T(8,128)(2,1)S(1)}, u32[]{:S(2)}, u32[]{:S(2)}) collective-permute-start(bf16[2,128,256]{2,1,0:T(8,128)(2,1)S(1)} %get-tuple-element.79), channel_id=1, source_target_pairs={{0,2},{1,3},{2,0},{3,1},{4,6},{5,7},{6,4},{7,5},{8,10},{9,11},{10,... | collective-permute-start | bytes 393224 | tf_op jit(solution)/shard_map/ppermute | solution.py:308
  59.4 0.0 collective-permute-done.21.refs_7_
  59.4 0.5 collective-permute-start.28
  59.9 0.0 collective-permute-done.24.refs_9_
  59.9 0.9 %collective-permute-start.29 = (bf16[2,128,256]{2,1,0:T(8,128)(2,1)S(1)}, bf16[2,128,256]{2,1,0:T(8,128)(2,1)S(1)}, u32[]{:S(2)}, u32[]{:S(2)}) collective-permute-start(bf16[2,128,256]{2,1,0:T(8,128)(2,1)S(1)} %get-tuple-element.81), channel_id=1, source_target_pairs={{0,3},{1,2},{2,1},{3,0},{4,7},{5,6},{6,5},{7,4},{8,11},{9,10},{10,... | collective-permute-start | bytes 393224 | tf_op jit(solution)/shard_map/ppermute | solution.py:308
  60.8 0.6 collective-permute-start.30
  61.4 2.1 %collective-permute-done.26.refs_11_ = bf16[2,128,256]{2,1,0:T(8,128)(2,1)S(1)} collective-permute-done((bf16[2,128,256]{2,1,0:T(8,128)(2,1)S(1)}, bf16[2,128,256]{2,1,0:T(8,128)(2,1)S(1)}, u32[]{:S(2)}, u32[]{:S(2)}) %collective-permute-start.26) | collective-permute-done | bytes 131104 | tf_op jit(solution)/shard_map/ppermute | solution.py:308
  63.5 2.7 %collective-permute-done.27.refs_12_ = bf16[2,128,256]{2,1,0:T(8,128)(2,1)S(1)} collective-permute-done((bf16[2,128,256]{2,1,0:T(8,128)(2,1)S(1)}, bf16[2,128,256]{2,1,0:T(8,128)(2,1)S(1)}, u32[]{:S(2)}, u32[]{:S(2)}) %collective-permute-start.27) | collective-permute-done | bytes 131104 | tf_op jit(solution)/shard_map/ppermute | solution.py:308
  66.2 0.2 collective-permute-done.28.refs_13_
  66.4 2.0 %collective-permute-done.29.refs_14_ = bf16[2,128,256]{2,1,0:T(8,128)(2,1)S(1)} collective-permute-done((bf16[2,128,256]{2,1,0:T(8,128)(2,1)S(1)}, bf16[2,128,256]{2,1,0:T(8,128)(2,1)S(1)}, u32[]{:S(2)}, u32[]{:S(2)}) %collective-permute-start.29) | collective-permute-done | bytes 131104 | tf_op jit(solution)/shard_map/ppermute | solution.py:308
  68.5 0.8 %collective-permute-done.30.refs_15_ = bf16[2,128,256]{2,1,0:T(8,128)(2,1)S(1)} collective-permute-done((bf16[2,128,256]{2,1,0:T(8,128)(2,1)S(1)}, bf16[2,128,256]{2,1,0:T(8,128)(2,1)S(1)}, u32[]{:S(2)}, u32[]{:S(2)}) %collective-permute-start.30) | collective-permute-done | bytes 131104 | tf_op jit(solution)/shard_map/ppermute | solution.py:308
  69.2 1.3 %shard_map.72 = (bf16[128,2048]{1,0:T(8,128)(2,1)}, bf16[128,2048]{1,0:T(8,128)(2,1)}, bf16[128,2048]{1,0:T(8,128)(2,1)}) custom-call(bf16[128,256]{1,0:T(8,128)(2,1)S(1)} %get-tuple-element.65.refs_0_, bf16[128,256]{1,0:T(8,128)(2,1)S(1)} %collective-permute-done.15.refs_1_, bf16[128,256]{1,0:T(8,128)(2,1)S(1)} %collective-permute-done.16.refs_2_, ...), custom_call_target="tpu_custom_call" | custom-call | tf_op jit(solution)/shard_map/pallas_call | solution.py:277
  (4 shorter events, 0.0 us)
Async XLA Ops:
  2.3 5.8 %collective-permute-start = (bf16[2,128,256]{2,1,0:T(8,128)(2,1)S(1)}, bf16[2,128,256]{2,1,0:T(8,128)(2,1)S(1)}, u32[]{:S(2)}, u32[]{:S(2)}) collective-permute-start(bf16[2,128,256]{2,1,0:T(8,128)(2,1)S(1)} %get-tuple-element.44), channel_id=1, source_target_pairs={{0,1},{1,0},{2,3},{3,2},{4,5},{5,4},{6,7},{7,6},{8,9},{9,8},{10,11... | collective-permute-start | bytes 393224 | tf_op jit(solution)/shard_map/ppermute | solution.py:308
  3.0 6.0 %collective-permute-start.1 = (bf16[2,128,256]{2,1,0:T(8,128)(2,1)S(1)}, bf16[2,128,256]{2,1,0:T(8,128)(2,1)S(1)}, u32[]{:S(2)}, u32[]{:S(2)}) collective-permute-start(bf16[2,128,256]{2,1,0:T(8,128)(2,1)S(1)} %get-tuple-element.45), channel_id=1, source_target_pairs={{0,6},{1,7},{2,4},{3,5},{4,2},{5,3},{6,0},{7,1},{8,14},{9,15},{10,... | collective-permute-start | bytes 393224 | tf_op jit(solution)/shard_map/ppermute | solution.py:308
  5.2 7.2 %collective-permute-start.2 = (bf16[2,128,256]{2,1,0:T(8,128)(2,1)S(1)}, bf16[2,128,256]{2,1,0:T(8,128)(2,1)S(1)}, u32[]{:S(2)}, u32[]{:S(2)}) collective-permute-start(bf16[2,128,256]{2,1,0:T(8,128)(2,1)S(1)} %get-tuple-element.46), channel_id=1, source_target_pairs={{0,7},{1,6},{2,5},{3,4},{4,3},{5,2},{6,1},{7,0},{8,15},{9,14},{10,... | collective-permute-start | bytes 393224 | tf_op jit(solution)/shard_map/ppermute | solution.py:308
  5.6 9.1 %collective-permute-start.3 = (bf16[2,128,256]{2,1,0:T(8,128)(2,1)S(1)}, bf16[2,128,256]{2,1,0:T(8,128)(2,1)S(1)}, u32[]{:S(2)}, u32[]{:S(2)}) collective-permute-start(bf16[2,128,256]{2,1,0:T(8,128)(2,1)S(1)} %get-tuple-element.47), channel_id=1, source_target_pairs={{0,2},{1,3},{2,0},{3,1},{4,6},{5,7},{6,4},{7,5},{8,10},{9,11},{10,... | collective-permute-start | bytes 393224 | tf_op jit(solution)/shard_map/ppermute | solution.py:308
  6.8 8.2 %collective-permute-start.4 = (bf16[2,128,256]{2,1,0:T(8,128)(2,1)S(1)}, bf16[2,128,256]{2,1,0:T(8,128)(2,1)S(1)}, u32[]{:S(2)}, u32[]{:S(2)}) collective-permute-start(bf16[2,128,256]{2,1,0:T(8,128)(2,1)S(1)} %get-tuple-element.48), channel_id=1, source_target_pairs={{0,4},{1,5},{2,6},{3,7},{4,0},{5,1},{6,2},{7,3},{8,12},{9,13},{10,... | collective-permute-start | bytes 393224 | tf_op jit(solution)/shard_map/ppermute | solution.py:308
  8.1 10.0 %collective-permute-start.5 = (bf16[2,128,256]{2,1,0:T(8,128)(2,1)S(1)}, bf16[2,128,256]{2,1,0:T(8,128)(2,1)S(1)}, u32[]{:S(2)}, u32[]{:S(2)}) collective-permute-start(bf16[2,128,256]{2,1,0:T(8,128)(2,1)S(1)} %get-tuple-element.49), channel_id=1, source_target_pairs={{0,3},{1,2},{2,1},{3,0},{4,7},{5,6},{6,5},{7,4},{8,11},{9,10},{10,... | collective-permute-start | bytes 393224 | tf_op jit(solution)/shard_map/ppermute | solution.py:308
  9.0 9.1 %collective-permute-start.6 = (bf16[2,128,256]{2,1,0:T(8,128)(2,1)S(1)}, bf16[2,128,256]{2,1,0:T(8,128)(2,1)S(1)}, u32[]{:S(2)}, u32[]{:S(2)}) collective-permute-start(bf16[2,128,256]{2,1,0:T(8,128)(2,1)S(1)} %get-tuple-element.50), channel_id=1, source_target_pairs={{0,5},{1,4},{2,7},{3,6},{4,1},{5,0},{6,3},{7,2},{8,13},{9,12},{10,... | collective-permute-start | bytes 393224 | tf_op jit(solution)/shard_map/ppermute | solution.py:308
  12.4 9.1 %collective-permute-start.10 = (bf16[2,128,256]{2,1,0:T(8,128)(2,1)S(1)}, bf16[2,128,256]{2,1,0:T(8,128)(2,1)S(1)}, u32[]{:S(2)}, u32[]{:S(2)}) collective-permute-start(bf16[2,128,256]{2,1,0:T(8,128)(2,1)S(1)} %get-tuple-element.56), channel_id=1, source_target_pairs={{0,2},{1,3},{2,0},{3,1},{4,6},{5,7},{6,4},{7,5},{8,10},{9,11},{10,... | collective-permute-start | bytes 393224 | tf_op jit(solution)/shard_map/ppermute | solution.py:308
  14.7 8.8 %collective-permute-start.11 = (bf16[2,128,256]{2,1,0:T(8,128)(2,1)S(1)}, bf16[2,128,256]{2,1,0:T(8,128)(2,1)S(1)}, u32[]{:S(2)}, u32[]{:S(2)}) collective-permute-start(bf16[2,128,256]{2,1,0:T(8,128)(2,1)S(1)} %get-tuple-element.57), channel_id=1, source_target_pairs={{0,4},{1,5},{2,6},{3,7},{4,0},{5,1},{6,2},{7,3},{8,12},{9,13},{10,... | collective-permute-start | bytes 393224 | tf_op jit(solution)/shard_map/ppermute | solution.py:308
  15.1 10.2 %collective-permute-start.12 = (bf16[2,128,256]{2,1,0:T(8,128)(2,1)S(1)}, bf16[2,128,256]{2,1,0:T(8,128)(2,1)S(1)}, u32[]{:S(2)}, u32[]{:S(2)}) collective-permute-start(bf16[2,128,256]{2,1,0:T(8,128)(2,1)S(1)} %get-tuple-element.58), channel_id=1, source_target_pairs={{0,3},{1,2},{2,1},{3,0},{4,7},{5,6},{6,5},{7,4},{8,11},{9,10},{10,... | collective-permute-start | bytes 393224 | tf_op jit(solution)/shard_map/ppermute | solution.py:308
  18.1 8.8 %collective-permute-start.13 = (bf16[2,128,256]{2,1,0:T(8,128)(2,1)S(1)}, bf16[2,128,256]{2,1,0:T(8,128)(2,1)S(1)}, u32[]{:S(2)}, u32[]{:S(2)}) collective-permute-start(bf16[2,128,256]{2,1,0:T(8,128)(2,1)S(1)} %get-tuple-element.59), channel_id=1, source_target_pairs={{0,5},{1,4},{2,7},{3,6},{4,1},{5,0},{6,3},{7,2},{8,13},{9,12},{10,... | collective-permute-start | bytes 393224 | tf_op jit(solution)/shard_map/ppermute | solution.py:308
  18.2 19.5 %collective-permute-start.14 = (bf16[2,512,256]{2,1,0:T(8,128)(2,1)S(1)}, bf16[2,512,256]{2,1,0:T(8,128)(2,1)S(1)}, u32[]{:S(2)}, u32[]{:S(2)}) collective-permute-start(bf16[2,512,256]{2,1,0:T(8,128)(2,1)S(1)} %get-tuple-element.60.refs_8_.refs_3_.refs_1_), channel_id=1, source_target_pairs={{0,8},{8,16},{16,24},{1,9},{9,17},{17,25},{2,10},{10,18},{18,26},{... | collective-permute-start | bytes 1572872 | tf_op jit(solution)/shard_map/ppermute | solution.py:340
  21.4 24.8 %collective-permute-start.22 = (bf16[2,512,256]{2,1,0:T(8,128)(2,1)S(1)}, bf16[2,512,256]{2,1,0:T(8,128)(2,1)S(1)}, u32[]{:S(2)}, u32[]{:S(2)}) collective-permute-start(bf16[2,512,256]{2,1,0:T(8,128)(2,1)S(1)} %get-tuple-element.51.refs_9_.refs_0_), channel_id=1, source_target_pairs={{8,0},{16,8},{24,16},{9,1},{17,9},{25,17},{10,2},{18,10},{26,18},{... | collective-permute-start | bytes 1572872 | tf_op jit(solution)/shard_map/ppermute | solution.py:341
  23.5 4.4 %collective-permute-start.7 = (bf16[2,128,256]{2,1,0:T(8,128)(2,1)S(1)}, bf16[2,128,256]{2,1,0:T(8,128)(2,1)S(1)}, u32[]{:S(2)}, u32[]{:S(2)}) collective-permute-start(bf16[2,128,256]{2,1,0:T(8,128)(2,1)S(1)} %get-tuple-element.53), channel_id=1, source_target_pairs={{0,1},{1,0},{2,3},{3,2},{4,5},{5,4},{6,7},{7,6},{8,9},{9,8},{10,11... | collective-permute-start | bytes 393224 | tf_op jit(solution)/shard_map/ppermute | solution.py:308
  25.3 6.0 %collective-permute-start.8 = (bf16[2,128,256]{2,1,0:T(8,128)(2,1)S(1)}, bf16[2,128,256]{2,1,0:T(8,128)(2,1)S(1)}, u32[]{:S(2)}, u32[]{:S(2)}) collective-permute-start(bf16[2,128,256]{2,1,0:T(8,128)(2,1)S(1)} %get-tuple-element.54), channel_id=1, source_target_pairs={{0,6},{1,7},{2,4},{3,5},{4,2},{5,3},{6,0},{7,1},{8,14},{9,15},{10,... | collective-permute-start | bytes 393224 | tf_op jit(solution)/shard_map/ppermute | solution.py:308
  27.0 7.3 %collective-permute-start.9 = (bf16[2,128,256]{2,1,0:T(8,128)(2,1)S(1)}, bf16[2,128,256]{2,1,0:T(8,128)(2,1)S(1)}, u32[]{:S(2)}, u32[]{:S(2)}) collective-permute-start(bf16[2,128,256]{2,1,0:T(8,128)(2,1)S(1)} %get-tuple-element.55), channel_id=1, source_target_pairs={{0,7},{1,6},{2,5},{3,4},{4,3},{5,2},{6,1},{7,0},{8,15},{9,14},{10,... | collective-permute-start | bytes 393224 | tf_op jit(solution)/shard_map/ppermute | solution.py:308
  41.0 6.3 %collective-permute-start.23 = (f32[8,512]{1,0:T(8,128)S(1)}, f32[8,512]{1,0:T(8,128)S(1)}, u32[]{:S(2)}, u32[]{:S(2)}) collective-permute-start(f32[8,512]{1,0:T(8,128)S(1)} %get-tuple-element.74), channel_id=1, source_target_pairs={{8,0},{16,8},{24,16},{9,1},{17,9},{25,17},{10,2},{18,10},{26,18},{... | collective-permute-start | bytes 49160 | tf_op jit(solution)/shard_map/ppermute | solution.py:357
  43.1 6.0 %collective-permute-start.15 = (bf16[128,256]{1,0:T(8,128)(2,1)S(1)}, bf16[128,256]{1,0:T(8,128)(2,1)S(1)}, u32[]{:S(2)}, u32[]{:S(2)}) collective-permute-start(bf16[128,256]{1,0:T(8,128)(2,1)S(1)} %get-tuple-element.66), channel_id=1, source_target_pairs={{0,1},{1,0},{2,3},{3,2},{4,5},{5,4},{6,7},{7,6},{8,9},{9,8},{10,11... | collective-permute-start | bytes 196616 | tf_op jit(solution)/shard_map/ppermute | solution.py:308
  43.7 6.3 %collective-permute-start.16 = (bf16[128,256]{1,0:T(8,128)(2,1)S(1)}, bf16[128,256]{1,0:T(8,128)(2,1)S(1)}, u32[]{:S(2)}, u32[]{:S(2)}) collective-permute-start(bf16[128,256]{1,0:T(8,128)(2,1)S(1)} %get-tuple-element.67), channel_id=1, source_target_pairs={{0,6},{1,7},{2,4},{3,5},{4,2},{5,3},{6,0},{7,1},{8,14},{9,15},{10,... | collective-permute-start | bytes 196616 | tf_op jit(solution)/shard_map/ppermute | solution.py:308
  45.3 5.4 %collective-permute-start.17 = (bf16[128,256]{1,0:T(8,128)(2,1)S(1)}, bf16[128,256]{1,0:T(8,128)(2,1)S(1)}, u32[]{:S(2)}, u32[]{:S(2)}) collective-permute-start(bf16[128,256]{1,0:T(8,128)(2,1)S(1)} %get-tuple-element.68), channel_id=1, source_target_pairs={{0,7},{1,6},{2,5},{3,4},{4,3},{5,2},{6,1},{7,0},{8,15},{9,14},{10,... | collective-permute-start | bytes 196616 | tf_op jit(solution)/shard_map/ppermute | solution.py:308
  46.3 6.0 %collective-permute-start.18 = (bf16[128,256]{1,0:T(8,128)(2,1)S(1)}, bf16[128,256]{1,0:T(8,128)(2,1)S(1)}, u32[]{:S(2)}, u32[]{:S(2)}) collective-permute-start(bf16[128,256]{1,0:T(8,128)(2,1)S(1)} %get-tuple-element.69), channel_id=1, source_target_pairs={{0,2},{1,3},{2,0},{3,1},{4,6},{5,7},{6,4},{7,5},{8,10},{9,11},{10,... | collective-permute-start | bytes 196616 | tf_op jit(solution)/shard_map/ppermute | solution.py:308
  48.5 11.4 %collective-permute-start.24 = (bf16[2,128,256]{2,1,0:T(8,128)(2,1)S(1)}, bf16[2,128,256]{2,1,0:T(8,128)(2,1)S(1)}, u32[]{:S(2)}, u32[]{:S(2)}) collective-permute-start(bf16[2,128,256]{2,1,0:T(8,128)(2,1)S(1)} %get-tuple-element.76), channel_id=1, source_target_pairs={{0,1},{1,0},{2,3},{3,2},{4,5},{5,4},{6,7},{7,6},{8,9},{9,8},{10,11... | collective-permute-start | bytes 393224 | tf_op jit(solution)/shard_map/ppermute | solution.py:308
  49.0 11.7 %collective-permute-start.25 = (bf16[2,128,256]{2,1,0:T(8,128)(2,1)S(1)}, bf16[2,128,256]{2,1,0:T(8,128)(2,1)S(1)}, u32[]{:S(2)}, u32[]{:S(2)}) collective-permute-start(bf16[2,128,256]{2,1,0:T(8,128)(2,1)S(1)} %get-tuple-element.77), channel_id=1, source_target_pairs={{0,6},{1,7},{2,4},{3,5},{4,2},{5,3},{6,0},{7,1},{8,14},{9,15},{10,... | collective-permute-start | bytes 393224 | tf_op jit(solution)/shard_map/ppermute | solution.py:308
  50.0 6.8 %collective-permute-start.19 = (bf16[128,256]{1,0:T(8,128)(2,1)S(1)}, bf16[128,256]{1,0:T(8,128)(2,1)S(1)}, u32[]{:S(2)}, u32[]{:S(2)}) collective-permute-start(bf16[128,256]{1,0:T(8,128)(2,1)S(1)} %get-tuple-element.70), channel_id=1, source_target_pairs={{0,4},{1,5},{2,6},{3,7},{4,0},{5,1},{6,2},{7,3},{8,12},{9,13},{10,... | collective-permute-start | bytes 196616 | tf_op jit(solution)/shard_map/ppermute | solution.py:308
  50.7 7.4 %collective-permute-start.20 = (bf16[128,256]{1,0:T(8,128)(2,1)S(1)}, bf16[128,256]{1,0:T(8,128)(2,1)S(1)}, u32[]{:S(2)}, u32[]{:S(2)}) collective-permute-start(bf16[128,256]{1,0:T(8,128)(2,1)S(1)} %get-tuple-element.71), channel_id=1, source_target_pairs={{0,3},{1,2},{2,1},{3,0},{4,7},{5,6},{6,5},{7,4},{8,11},{9,10},{10,... | collective-permute-start | bytes 196616 | tf_op jit(solution)/shard_map/ppermute | solution.py:308
  52.2 7.2 %collective-permute-start.21 = (bf16[128,256]{1,0:T(8,128)(2,1)S(1)}, bf16[128,256]{1,0:T(8,128)(2,1)S(1)}, u32[]{:S(2)}, u32[]{:S(2)}) collective-permute-start(bf16[128,256]{1,0:T(8,128)(2,1)S(1)} %get-tuple-element.72), channel_id=1, source_target_pairs={{0,5},{1,4},{2,7},{3,6},{4,1},{5,0},{6,3},{7,2},{8,13},{9,12},{10,... | collective-permute-start | bytes 196616 | tf_op jit(solution)/shard_map/ppermute | solution.py:308
  56.8 6.7 %collective-permute-start.26 = (bf16[2,128,256]{2,1,0:T(8,128)(2,1)S(1)}, bf16[2,128,256]{2,1,0:T(8,128)(2,1)S(1)}, u32[]{:S(2)}, u32[]{:S(2)}) collective-permute-start(bf16[2,128,256]{2,1,0:T(8,128)(2,1)S(1)} %get-tuple-element.78), channel_id=1, source_target_pairs={{0,7},{1,6},{2,5},{3,4},{4,3},{5,2},{6,1},{7,0},{8,15},{9,14},{10,... | collective-permute-start | bytes 393224 | tf_op jit(solution)/shard_map/ppermute | solution.py:308
  58.2 8.1 %collective-permute-start.27 = (bf16[2,128,256]{2,1,0:T(8,128)(2,1)S(1)}, bf16[2,128,256]{2,1,0:T(8,128)(2,1)S(1)}, u32[]{:S(2)}, u32[]{:S(2)}) collective-permute-start(bf16[2,128,256]{2,1,0:T(8,128)(2,1)S(1)} %get-tuple-element.79), channel_id=1, source_target_pairs={{0,2},{1,3},{2,0},{3,1},{4,6},{5,7},{6,4},{7,5},{8,10},{9,11},{10,... | collective-permute-start | bytes 393224 | tf_op jit(solution)/shard_map/ppermute | solution.py:308
  59.4 7.0 %collective-permute-start.28 = (bf16[2,128,256]{2,1,0:T(8,128)(2,1)S(1)}, bf16[2,128,256]{2,1,0:T(8,128)(2,1)S(1)}, u32[]{:S(2)}, u32[]{:S(2)}) collective-permute-start(bf16[2,128,256]{2,1,0:T(8,128)(2,1)S(1)} %get-tuple-element.80), channel_id=1, source_target_pairs={{0,4},{1,5},{2,6},{3,7},{4,0},{5,1},{6,2},{7,3},{8,12},{9,13},{10,... | collective-permute-start | bytes 393224 | tf_op jit(solution)/shard_map/ppermute | solution.py:308
  59.9 8.6 %collective-permute-start.29 = (bf16[2,128,256]{2,1,0:T(8,128)(2,1)S(1)}, bf16[2,128,256]{2,1,0:T(8,128)(2,1)S(1)}, u32[]{:S(2)}, u32[]{:S(2)}) collective-permute-start(bf16[2,128,256]{2,1,0:T(8,128)(2,1)S(1)} %get-tuple-element.81), channel_id=1, source_target_pairs={{0,3},{1,2},{2,1},{3,0},{4,7},{5,6},{6,5},{7,4},{8,11},{9,10},{10,... | collective-permute-start | bytes 393224 | tf_op jit(solution)/shard_map/ppermute | solution.py:308
  60.8 8.5 %collective-permute-start.30 = (bf16[2,128,256]{2,1,0:T(8,128)(2,1)S(1)}, bf16[2,128,256]{2,1,0:T(8,128)(2,1)S(1)}, u32[]{:S(2)}, u32[]{:S(2)}) collective-permute-start(bf16[2,128,256]{2,1,0:T(8,128)(2,1)S(1)} %get-tuple-element.82), channel_id=1, source_target_pairs={{0,5},{1,4},{2,7},{3,6},{4,1},{5,0},{6,3},{7,2},{8,13},{9,12},{10,... | collective-permute-start | bytes 393224 | tf_op jit(solution)/shard_map/ppermute | solution.py:308

commit v4 on v3

--- a/solution.py
+++ b/solution.py
@@ -21,10 +21,10 @@
 VMEM_LIMIT = 48 * 1024 * 1024
 NT = ((1,), (1,))
 NN = ((1,), (0,))
-CRIT_ORDER = (0, 1, 6, 7, 2, 4, 3, 5)
-REST_ORDER = (0, 1, 6, 7, 2, 4, 3, 5)
-DQ_ORDER = (0, 1, 6, 7, 2, 4, 3, 5)
-DKV_ORDER = (0, 1, 6, 7, 2, 4, 3, 5)
+CRIT_ORDER = (0, 6, 7, 2, 4, 1, 3, 5)
+REST_ORDER = (0, 3, 5, 1, 6, 7, 2, 4)
+DQ_ORDER = (0, 3, 1, 2)
+DKV_ORDER = (0, 6, 2, 4, 7, 3, 5, 1)
 QG_FIRST = False
 EDGE_FLOPS = 4000000000
 LATE_FLOPS = 4000000000
@@ -187,10 +187,10 @@
 def early_kernel(n, heads, *refs):
     qg_early, qg_late, kv_early, kv_late, kv_halo, dq_in, dkv_in = refs[:7]
     refs = refs[7 + QG_FIRST :]
-    dq_out = refs[:n]
-    front, stat, dq, acc = refs[n:]
+    dq_out = refs[: n // 2]
+    front, stat, dq, acc = refs[n // 2 :]
     me = group_index()
-    rows = dq_out[0].shape[0]
+    rows = dq_out[0].shape[1]
     first = lax.axis_index("chunk") == 0
     stat[...] = jnp.zeros_like(stat)
     dq[WINDOW:] = dq_in[...]
@@ -215,7 +215,7 @@
                 for k, value in enumerate(rows_of):
                     stat[3 * h + k : 3 * h + k + 1, at] = value
     for m in range(n):
-        dq_out[m][...] = dq[pl.ds(aligned(jnp.bitwise_xor(me, m), rows), rows)]
+        dq_out[m // 2][m % 2] = dq[pl.ds(aligned(jnp.bitwise_xor(me, m), rows), rows)]
     front[0] = (acc[0] * SCALE).astype(jnp.bfloat16)
     front[1] = acc[1].astype(jnp.bfloat16)
 
@@ -255,16 +255,24 @@
         out[m][...] = full[:, pl.ds(aligned(jnp.bitwise_xor(me, m), rows), rows)]
 
 
+def core_kernel(*refs):
+    *pieces, out = refs
+    for slot, piece in enumerate(by_slot(DQ_ORDER, pieces)):
+        out[slot] = piece[1]
+
+
 def unpack_kernel(n, *refs):
-    dq_in = by_slot(DQ_ORDER, refs[:n])
-    dkv_in = by_slot(DKV_ORDER, refs[n : 2 * n])
-    dq, dk, dv, sems = refs[2 * n :]
+    chips = n // 2
+    dq_in = by_slot(DQ_ORDER, refs[:chips])
+    other = refs[chips]
+    dkv_in = by_slot(DKV_ORDER, refs[chips + 1 : chips + 1 + n])
+    dq, dk, dv, sems = refs[chips + 1 + n :]
     me = group_index()
-    width = dq_in[0].shape[1]
+    width = other.shape[2]
     pairs = []
     for m in range(n):
         cols = pl.ds(aligned(jnp.bitwise_xor(me, m), width), width)
-        pairs.append((dq_in[m], dq.at[:, cols]))
+        pairs.append((other.at[m // 2] if m % 2 else dq_in[m // 2].at[0], dq.at[:, cols]))
         pairs.append((dkv_in[m].at[0], dk.at[:, cols]))
         pairs.append((dkv_in[m].at[1], dv.at[:, cols]))
     copy_all(pairs, sems)
@@ -302,10 +310,10 @@
     return [refs[order.index(m)] for m in range(len(refs))]
 
 
-def exchanged(order, pieces):
+def exchanged(order, pieces, step=1):
     n = len(pieces)
     return [
-        lax.ppermute(pieces[m], GROUP, [(i, i ^ m) for i in range(n)]) if m else pieces[0]
+        lax.ppermute(pieces[m], GROUP, [(i, i ^ (step * m)) for i in range(step * n)]) if m else pieces[0]
         for m in order_of(order, n)
     ]
 
@@ -349,13 +357,17 @@
     )
     *dq, front, stat = call(
         functools.partial(early_kernel, n, heads),
-        [vmem(bf16(rows, width))] * n + [end, stat_out],
+        [vmem(bf16(2, rows, width))] * (n // 2) + [end, stat_out],
         [vmem(bf16(total, width)), vmem(f32(2, WINDOW, width))], 0,
         *held((qg_early, qg_late, kv_early, kv_late, kv_halo, dq_late, partial)),
         *([qg_halo] if QG_FIRST else []),
     )
     stat_halo = lax.ppermute(stat, "chunk", backward)
-    dq = exchanged(DQ_ORDER, dq)
+    dq = exchanged(DQ_ORDER, dq, 2)
+    other, = call(
+        core_kernel, [vmem(bf16(n // 2, rows, width))], [], 0, *held(dq)
+    )
+    other = lax.ppermute(other, GROUP, [(i, i ^ 1) for i in range(n)])
     dkv = call(
         functools.partial(edge_kernel, n, heads),
         [vmem(piece)] * n, [vmem(bf16(2, total, width)), vmem(f32(2, done, width))], 0,
@@ -364,7 +376,7 @@
     dkv = exchanged(DKV_ORDER, dkv)
     out = bf16(rows, model)
     return tuple(
-        call(functools.partial(unpack_kernel, n), [out] * 3, [], 3 * n, *held(dq), *held(dkv))
+        call(functools.partial(unpack_kernel, n), [out] * 3, [], 3 * n, *held(dq), (other,), *held(dkv))
     )
 
 

time: 70.8 us -> 64.2 us (0.907)
  waiting for transfers between devices: 20.6 us -> 14.6 us
    ppermute x28 -> x25, waiting for transfers between devices: 20.6 us -> 14.4 us  [the longest x24 14.4 us: exchanged(): lax.ppermute(pieces[m], GROUP, [(i, i ^ step * m) for i in range(step * n)])]
    ppermute x28 -> x25, starting transfers between devices: 30.9 us -> 30.2 us  [the longest x24 26.9 us: exchanged(): lax.ppermute(pieces[m], GROUP, [(i, i ^ step * m) for i in range(step * n)])]
    pallas_call x6 -> x7, Pallas kernels: 11 us -> 11 us  [call(): pl.pallas_call(kernel, out_shape=outs, in_specs=[held if isinstance(x, tu...]
  transfers between devices with their start and end apart: 31 -> 28, of which waited for: 11 -> 10; matrix products, arithmetic and copies ran while one was open for 0% -> 0% of each run, Pallas kernels for 11% -> 13%
where the time goes in v4:
time: 64.2 us; the launch traced here: 64 us
  starting transfers between devices  37.6 us (59%)
  waiting for transfers between devices  14.6 us (23%)
  Pallas kernels  11 us (17%)
  between operations  0.74 us (1%)
    ppermute x24, starting transfers between devices, exchanged(): lax.ppermute(pieces[m], GROUP, [(i, i ^ step * m) for i in range(step * n)])  26.9 us
    ppermute x24, waiting for transfers between devices, exchanged(): lax.ppermute(pieces[m], GROUP, [(i, i ^ step * m) for i in range(step * n)])  14.4 us
    pallas_call x7, Pallas kernels, call(): pl.pallas_call(kernel, out_shape=outs, in_specs=[held if isinstance(x, tu...  11 us
    ppermute x1, starting transfers between devices, per_device(): other = lax.ppermute(other, GROUP, [(i, i ^ 1) for i in range(n)])  3.31 us
    ppermute x1, starting transfers between devices, per_device(): kv_halo = lax.ppermute(kv_send, 'chunk', forward)  3.2 us
    ppermute x1, starting transfers between devices, per_device(): qg_halo = lax.ppermute(qg_send, 'chunk', backward)  2.08 us
    ppermute x1, starting transfers between devices, per_device(): stat_halo = lax.ppermute(stat, 'chunk', backward)  2.08 us
  transfers between devices with their start and end apart: 28, of which 10 were waited for; matrix products, arithmetic and copies ran while one was open for 0% of the time, Pallas kernels for 13%

profile of v4, /device:TPU:17, one launch (start us, length us, event | category | flops | bytes accessed | tf_op | source)
XLA Modules:
  0.0 64.0 jit_solution(7963594389380813680)
XLA Ops:
  0.6 1.6 %shard_map.67 = (bf16[2,128,256]{2,1,0:T(8,128)(2,1)S(1)}, bf16[2,128,256]{2,1,0:T(8,128)(2,1)S(1)}, bf16[2,128,256]{2,1,0:T(8,128)(2,1)S(1)}, bf16[2,128,256]{2...) custom-call(bf16[128,2048]{1,0:T(8,128)(2,1)} %refs_0_.1, ...), custom_call_target="tpu_custom_call" | custom-call | tf_op jit(solution)/shard_map/pallas_call | solution.py:285
  2.3 2.2 %collective-permute-start = (bf16[2,128,256]{2,1,0:T(8,128)(2,1)S(1)}, bf16[2,128,256]{2,1,0:T(8,128)(2,1)S(1)}, u32[]{:S(2)}, u32[]{:S(2)}) collective-permute-start(bf16[2,128,256]{2,1,0:T(8,128)(2,1)S(1)} %get-tuple-element.40), channel_id=1, source_target_pairs={{0,6},{1,7},{2,4},{3,5},{4,2},{5,3},{6,0},{7,1},{8,14},{9,15},{10,... | collective-permute-start | bytes 393224 | tf_op jit(solution)/shard_map/ppermute | solution.py:316
  4.5 1.0 %collective-permute-start.1 = (bf16[2,128,256]{2,1,0:T(8,128)(2,1)S(1)}, bf16[2,128,256]{2,1,0:T(8,128)(2,1)S(1)}, u32[]{:S(2)}, u32[]{:S(2)}) collective-permute-start(bf16[2,128,256]{2,1,0:T(8,128)(2,1)S(1)} %get-tuple-element.41), channel_id=1, source_target_pairs={{0,7},{1,6},{2,5},{3,4},{4,3},{5,2},{6,1},{7,0},{8,15},{9,14},{10,... | collective-permute-start | bytes 393224 | tf_op jit(solution)/shard_map/ppermute | solution.py:316
  5.6 1.2 %collective-permute-start.2 = (bf16[2,128,256]{2,1,0:T(8,128)(2,1)S(1)}, bf16[2,128,256]{2,1,0:T(8,128)(2,1)S(1)}, u32[]{:S(2)}, u32[]{:S(2)}) collective-permute-start(bf16[2,128,256]{2,1,0:T(8,128)(2,1)S(1)} %get-tuple-element.42), channel_id=1, source_target_pairs={{0,2},{1,3},{2,0},{3,1},{4,6},{5,7},{6,4},{7,5},{8,10},{9,11},{10,... | collective-permute-start | bytes 393224 | tf_op jit(solution)/shard_map/ppermute | solution.py:316
  6.8 1.2 %collective-permute-start.3 = (bf16[2,128,256]{2,1,0:T(8,128)(2,1)S(1)}, bf16[2,128,256]{2,1,0:T(8,128)(2,1)S(1)}, u32[]{:S(2)}, u32[]{:S(2)}) collective-permute-start(bf16[2,128,256]{2,1,0:T(8,128)(2,1)S(1)} %get-tuple-element.43), channel_id=1, source_target_pairs={{0,4},{1,5},{2,6},{3,7},{4,0},{5,1},{6,2},{7,3},{8,12},{9,13},{10,... | collective-permute-start | bytes 393224 | tf_op jit(solution)/shard_map/ppermute | solution.py:316
  8.0 0.1 collective-permute-start.4
  8.1 0.0 collective-permute-done.refs_1_
  8.1 3.0 %collective-permute-start.5 = (bf16[2,128,256]{2,1,0:T(8,128)(2,1)S(1)}, bf16[2,128,256]{2,1,0:T(8,128)(2,1)S(1)}, u32[]{:S(2)}, u32[]{:S(2)}) collective-permute-start(bf16[2,128,256]{2,1,0:T(8,128)(2,1)S(1)} %get-tuple-element.45), channel_id=1, source_target_pairs={{0,3},{1,2},{2,1},{3,0},{4,7},{5,6},{6,5},{7,4},{8,11},{9,10},{10,... | collective-permute-start | bytes 393224 | tf_op jit(solution)/shard_map/ppermute | solution.py:316
  11.1 0.2 collective-permute-done.1.refs_2_
  11.3 1.0 %collective-permute-start.6 = (bf16[2,128,256]{2,1,0:T(8,128)(2,1)S(1)}, bf16[2,128,256]{2,1,0:T(8,128)(2,1)S(1)}, u32[]{:S(2)}, u32[]{:S(2)}) collective-permute-start(bf16[2,128,256]{2,1,0:T(8,128)(2,1)S(1)} %get-tuple-element.46), channel_id=1, source_target_pairs={{0,5},{1,4},{2,7},{3,6},{4,1},{5,0},{6,3},{7,2},{8,13},{9,12},{10,... | collective-permute-start | bytes 393224 | tf_op jit(solution)/shard_map/ppermute | solution.py:316
  12.4 1.2 %collective-permute-done.2.refs_3_ = bf16[2,128,256]{2,1,0:T(8,128)(2,1)S(1)} collective-permute-done((bf16[2,128,256]{2,1,0:T(8,128)(2,1)S(1)}, bf16[2,128,256]{2,1,0:T(8,128)(2,1)S(1)}, u32[]{:S(2)}, u32[]{:S(2)}) %collective-permute-start.2) | collective-permute-done | bytes 131104 | tf_op jit(solution)/shard_map/ppermute | solution.py:316
  13.6 1.3 %collective-permute-start.10 = (bf16[2,128,256]{2,1,0:T(8,128)(2,1)S(1)}, bf16[2,128,256]{2,1,0:T(8,128)(2,1)S(1)}, u32[]{:S(2)}, u32[]{:S(2)}) collective-permute-start(bf16[2,128,256]{2,1,0:T(8,128)(2,1)S(1)} %get-tuple-element.52), channel_id=1, source_target_pairs={{0,6},{1,7},{2,4},{3,5},{4,2},{5,3},{6,0},{7,1},{8,14},{9,15},{10,... | collective-permute-start | bytes 393224 | tf_op jit(solution)/shard_map/ppermute | solution.py:316
  14.9 0.0 collective-permute-done.3.refs_4_
  14.9 3.3 %collective-permute-start.11 = (bf16[2,128,256]{2,1,0:T(8,128)(2,1)S(1)}, bf16[2,128,256]{2,1,0:T(8,128)(2,1)S(1)}, u32[]{:S(2)}, u32[]{:S(2)}) collective-permute-start(bf16[2,128,256]{2,1,0:T(8,128)(2,1)S(1)} %get-tuple-element.53), channel_id=1, source_target_pairs={{0,7},{1,6},{2,5},{3,4},{4,3},{5,2},{6,1},{7,0},{8,15},{9,14},{10,... | collective-permute-start | bytes 393224 | tf_op jit(solution)/shard_map/ppermute | solution.py:316
  18.2 0.0 collective-permute-done.4.refs_5_
  18.2 1.6 %collective-permute-start.12 = (bf16[2,128,256]{2,1,0:T(8,128)(2,1)S(1)}, bf16[2,128,256]{2,1,0:T(8,128)(2,1)S(1)}, u32[]{:S(2)}, u32[]{:S(2)}) collective-permute-start(bf16[2,128,256]{2,1,0:T(8,128)(2,1)S(1)} %get-tuple-element.54), channel_id=1, source_target_pairs={{0,2},{1,3},{2,0},{3,1},{4,6},{5,7},{6,4},{7,5},{8,10},{9,11},{10,... | collective-permute-start | bytes 393224 | tf_op jit(solution)/shard_map/ppermute | solution.py:316
  19.8 0.0 collective-permute-done.5.refs_6_
  19.8 0.0 collective-permute-start.13
  19.8 0.0 collective-permute-done.6.refs_7_
  19.8 0.1 shard_map.68
  19.9 3.2 %collective-permute-start.14 = (bf16[2,512,256]{2,1,0:T(8,128)(2,1)S(1)}, bf16[2,512,256]{2,1,0:T(8,128)(2,1)S(1)}, u32[]{:S(2)}, u32[]{:S(2)}) collective-permute-start(bf16[2,512,256]{2,1,0:T(8,128)(2,1)S(1)} %get-tuple-element.56.refs_8_.refs_3_.refs_1_), channel_id=1, source_target_pairs={{0,8},{8,16},{16,24},{1,9},{9,17},{17,25},{2,10},{10,18},{18,26},{... | collective-permute-start | bytes 1572872 | tf_op jit(solution)/shard_map/ppermute | solution.py:348
  23.1 0.0 collective-permute-done.10.refs_4_
  23.1 2.1 %collective-permute-start.19 = (bf16[2,512,256]{2,1,0:T(8,128)(2,1)S(1)}, bf16[2,512,256]{2,1,0:T(8,128)(2,1)S(1)}, u32[]{:S(2)}, u32[]{:S(2)}) collective-permute-start(bf16[2,512,256]{2,1,0:T(8,128)(2,1)S(1)} %get-tuple-element.47.refs_9_.refs_0_), channel_id=1, source_target_pairs={{8,0},{16,8},{24,16},{9,1},{17,9},{25,17},{10,2},{18,10},{26,18},{... | collective-permute-start | bytes 1572872 | tf_op jit(solution)/shard_map/ppermute | solution.py:349
  25.2 0.0 collective-permute-done.11.refs_5_
  25.2 1.6 %collective-permute-start.7 = (bf16[2,128,256]{2,1,0:T(8,128)(2,1)S(1)}, bf16[2,128,256]{2,1,0:T(8,128)(2,1)S(1)}, u32[]{:S(2)}, u32[]{:S(2)}) collective-permute-start(bf16[2,128,256]{2,1,0:T(8,128)(2,1)S(1)} %get-tuple-element.49), channel_id=1, source_target_pairs={{0,3},{1,2},{2,1},{3,0},{4,7},{5,6},{6,5},{7,4},{8,11},{9,10},{10,... | collective-permute-start | bytes 393224 | tf_op jit(solution)/shard_map/ppermute | solution.py:316
  26.7 0.0 collective-permute-done.12.refs_6_
  26.8 0.6 collective-permute-start.8
  27.4 0.0 collective-permute-done.13.refs_7_
  27.4 0.0 collective-permute-start.9
  27.4 3.3 %collective-permute-done.7.refs_1_ = bf16[2,128,256]{2,1,0:T(8,128)(2,1)S(1)} collective-permute-done((bf16[2,128,256]{2,1,0:T(8,128)(2,1)S(1)}, bf16[2,128,256]{2,1,0:T(8,128)(2,1)S(1)}, u32[]{:S(2)}, u32[]{:S(2)}) %collective-permute-start.7) | collective-permute-done | bytes 131104 | tf_op jit(solution)/shard_map/ppermute | solution.py:316
  30.7 1.3 %collective-permute-done.8.refs_2_ = bf16[2,128,256]{2,1,0:T(8,128)(2,1)S(1)} collective-permute-done((bf16[2,128,256]{2,1,0:T(8,128)(2,1)S(1)}, bf16[2,128,256]{2,1,0:T(8,128)(2,1)S(1)}, u32[]{:S(2)}, u32[]{:S(2)}) %collective-permute-start.8) | collective-permute-done | bytes 131104 | tf_op jit(solution)/shard_map/ppermute | solution.py:316
  31.9 0.0 collective-permute-done.9.refs_3_
  31.9 3.5 %shard_map.69 = (bf16[2,512,256]{2,1,0:T(8,128)(2,1)S(1)}, bf16[2,512,256]{2,1,0:T(8,128)(2,1)S(1)}, bf16[512,256]{1,0:T(8,128)(2,1)S(1)}, f32[2,1024,256]{2,1,0:T(8,128)S(1)}) custom-call(bf16[2,128,256]{2,1,0:T(8,128)(2,1)S(1)} %get-tuple-element.48.refs_0_, bf16[2,128,256]{2,1,0:T(8,128)(2,1)S(1)} %collective-permute-done.7.refs_1_, ...), custom_call_target="tpu_custom_call" | custom-call | flops 4000000000 | tf_op jit(solution)/shard_map/pallas_call | solution.py:285
  35.4 0.2 collective-permute-done.14.refs_4_
  35.6 3.2 %shard_map.70 = (bf16[2,128,256]{2,1,0:T(8,128)(2,1)S(1)}, bf16[2,128,256]{2,1,0:T(8,128)(2,1)S(1)}, bf16[2,128,256]{2,1,0:T(8,128)(2,1)S(1)}, bf16[2,128,256]{2...) custom-call(bf16[2,512,256]{2,1,0:T(8,128)(2,1)S(1)} %get-tuple-element.47.refs_9_.refs_0_, ...), custom_call_target="tpu_custom_call" | custom-call | tf_op jit(solution)/shard_map/pallas_call | solution.py:285
  38.9 2.1 %collective-permute-start.20 = (f32[8,512]{1,0:T(8,128)S(1)}, f32[8,512]{1,0:T(8,128)S(1)}, u32[]{:S(2)}, u32[]{:S(2)}) collective-permute-start(f32[8,512]{1,0:T(8,128)S(1)} %get-tuple-element.66), channel_id=1, source_target_pairs={{8,0},{16,8},{24,16},{9,1},{17,9},{25,17},{10,2},{18,10},{26,18},{... | collective-permute-start | bytes 49160 | tf_op jit(solution)/shard_map/ppermute | solution.py:365
  40.9 1.1 %collective-permute-start.15 = (bf16[2,128,256]{2,1,0:T(8,128)(2,1)S(1)}, bf16[2,128,256]{2,1,0:T(8,128)(2,1)S(1)}, u32[]{:S(2)}, u32[]{:S(2)}) collective-permute-start(bf16[2,128,256]{2,1,0:T(8,128)(2,1)S(1)} %get-tuple-element.62), channel_id=1, source_target_pairs={{0,6},{1,7},{2,4},{3,5},{4,2},{5,3},{6,0},{7,1},{8,14},{9,15},{10,... | collective-permute-start | bytes 393224 | tf_op jit(solution)/shard_map/ppermute | solution.py:316
  42.1 0.9 %collective-permute-start.16 = (bf16[2,128,256]{2,1,0:T(8,128)(2,1)S(1)}, bf16[2,128,256]{2,1,0:T(8,128)(2,1)S(1)}, u32[]{:S(2)}, u32[]{:S(2)}) collective-permute-start(bf16[2,128,256]{2,1,0:T(8,128)(2,1)S(1)} %get-tuple-element.63), channel_id=1, source_target_pairs={{0,2},{1,3},{2,0},{3,1},{4,6},{5,7},{6,4},{7,5},{8,10},{9,11},{10,... | collective-permute-start | bytes 393224 | tf_op jit(solution)/shard_map/ppermute | solution.py:316
  43.0 0.7 %collective-permute-start.17 = (bf16[2,128,256]{2,1,0:T(8,128)(2,1)S(1)}, bf16[2,128,256]{2,1,0:T(8,128)(2,1)S(1)}, u32[]{:S(2)}, u32[]{:S(2)}) collective-permute-start(bf16[2,128,256]{2,1,0:T(8,128)(2,1)S(1)} %get-tuple-element.64), channel_id=1, source_target_pairs={{0,4},{1,5},{2,6},{3,7},{4,0},{5,1},{6,2},{7,3},{8,12},{9,13},{10,... | collective-permute-start | bytes 393224 | tf_op jit(solution)/shard_map/ppermute | solution.py:316
  43.7 0.0 collective-permute-done.19.refs_2_
  43.7 0.0 collective-permute-done.20.refs_5_
  43.7 1.2 %shard_map.72 = (bf16[2,128,256]{2,1,0:T(8,128)(2,1)S(1)}, bf16[2,128,256]{2,1,0:T(8,128)(2,1)S(1)}, bf16[2,128,256]{2,1,0:T(8,128)(2,1)S(1)}, bf16[2,128,256]{2...) custom-call(bf16[2,512,256]{2,1,0:T(8,128)(2,1)S(1)} %get-tuple-elem, ...), custom_call_target="tpu_custom_call" | custom-call | flops 4000000000 | tf_op jit(solution)/shard_map/pallas_call | solution.py:285
  44.9 1.1 %collective-permute-start.21 = (bf16[2,128,256]{2,1,0:T(8,128)(2,1)S(1)}, bf16[2,128,256]{2,1,0:T(8,128)(2,1)S(1)}, u32[]{:S(2)}, u32[]{:S(2)}) collective-permute-start(bf16[2,128,256]{2,1,0:T(8,128)(2,1)S(1)} %get-tuple-element.68), channel_id=1, source_target_pairs={{0,6},{1,7},{2,4},{3,5},{4,2},{5,3},{6,0},{7,1},{8,14},{9,15},{10,... | collective-permute-start | bytes 393224 | tf_op jit(solution)/shard_map/ppermute | solution.py:316
  46.0 0.9 %collective-permute-start.22 = (bf16[2,128,256]{2,1,0:T(8,128)(2,1)S(1)}, bf16[2,128,256]{2,1,0:T(8,128)(2,1)S(1)}, u32[]{:S(2)}, u32[]{:S(2)}) collective-permute-start(bf16[2,128,256]{2,1,0:T(8,128)(2,1)S(1)} %get-tuple-element.69), channel_id=1, source_target_pairs={{0,2},{1,3},{2,0},{3,1},{4,6},{5,7},{6,4},{7,5},{8,10},{9,11},{10,... | collective-permute-start | bytes 393224 | tf_op jit(solution)/shard_map/ppermute | solution.py:316
  46.9 0.0 collective-permute-done.15.refs_1_
  46.9 0.7 %collective-permute-start.23 = (bf16[2,128,256]{2,1,0:T(8,128)(2,1)S(1)}, bf16[2,128,256]{2,1,0:T(8,128)(2,1)S(1)}, u32[]{:S(2)}, u32[]{:S(2)}) collective-permute-start(bf16[2,128,256]{2,1,0:T(8,128)(2,1)S(1)} %get-tuple-element.70), channel_id=1, source_target_pairs={{0,4},{1,5},{2,6},{3,7},{4,0},{5,1},{6,2},{7,3},{8,12},{9,13},{10,... | collective-permute-start | bytes 393224 | tf_op jit(solution)/shard_map/ppermute | solution.py:316
  47.6 1.1 %collective-permute-done.16.refs_2_ = bf16[2,128,256]{2,1,0:T(8,128)(2,1)S(1)} collective-permute-done((bf16[2,128,256]{2,1,0:T(8,128)(2,1)S(1)}, bf16[2,128,256]{2,1,0:T(8,128)(2,1)S(1)}, u32[]{:S(2)}, u32[]{:S(2)}) %collective-permute-start.16) | collective-permute-done | bytes 131104 | tf_op jit(solution)/shard_map/ppermute | solution.py:316
  48.7 1.5 %collective-permute-done.17.refs_3_ = bf16[2,128,256]{2,1,0:T(8,128)(2,1)S(1)} collective-permute-done((bf16[2,128,256]{2,1,0:T(8,128)(2,1)S(1)}, bf16[2,128,256]{2,1,0:T(8,128)(2,1)S(1)}, u32[]{:S(2)}, u32[]{:S(2)}) %collective-permute-start.17) | collective-permute-done | bytes 131104 | tf_op jit(solution)/shard_map/ppermute | solution.py:316
  50.2 3.3 %collective-permute-start.18 = (bf16[4,128,256]{2,1,0:T(8,128)(2,1)S(1)}, bf16[4,128,256]{2,1,0:T(8,128)(2,1)S(1)}, u32[]{:S(2)}, u32[]{:S(2)}) collective-permute-start(bf16[4,128,256]{2,1,0:T(8,128)(2,1)S(1)} %shard_map.71), channel_id=1, source_target_pairs={{0,1},{1,0},{2,3},{3,2},{4,5},{5,4},{6,7},{7,6},{8,9},{9,8},{10,11... | collective-permute-start | bytes 786440 | tf_op jit(solution)/shard_map/ppermute | solution.py:370
  53.5 0.8 %collective-permute-start.24 = (bf16[2,128,256]{2,1,0:T(8,128)(2,1)S(1)}, bf16[2,128,256]{2,1,0:T(8,128)(2,1)S(1)}, u32[]{:S(2)}, u32[]{:S(2)}) collective-permute-start(bf16[2,128,256]{2,1,0:T(8,128)(2,1)S(1)} %get-tuple-element.71), channel_id=1, source_target_pairs={{0,7},{1,6},{2,5},{3,4},{4,3},{5,2},{6,1},{7,0},{8,15},{9,14},{10,... | collective-permute-start | bytes 393224 | tf_op jit(solution)/shard_map/ppermute | solution.py:316
  54.4 0.0 collective-permute-done.21.refs_6_
  54.4 1.3 %collective-permute-start.25 = (bf16[2,128,256]{2,1,0:T(8,128)(2,1)S(1)}, bf16[2,128,256]{2,1,0:T(8,128)(2,1)S(1)}, u32[]{:S(2)}, u32[]{:S(2)}) collective-permute-start(bf16[2,128,256]{2,1,0:T(8,128)(2,1)S(1)} %get-tuple-element.72), channel_id=1, source_target_pairs={{0,3},{1,2},{2,1},{3,0},{4,7},{5,6},{6,5},{7,4},{8,11},{9,10},{10,... | collective-permute-start | bytes 393224 | tf_op jit(solution)/shard_map/ppermute | solution.py:316
  55.7 0.0 collective-permute-done.22.refs_7_
  55.7 0.8 %collective-permute-start.26 = (bf16[2,128,256]{2,1,0:T(8,128)(2,1)S(1)}, bf16[2,128,256]{2,1,0:T(8,128)(2,1)S(1)}, u32[]{:S(2)}, u32[]{:S(2)}) collective-permute-start(bf16[2,128,256]{2,1,0:T(8,128)(2,1)S(1)} %get-tuple-element.73), channel_id=1, source_target_pairs={{0,5},{1,4},{2,7},{3,6},{4,1},{5,0},{6,3},{7,2},{8,13},{9,12},{10,... | collective-permute-start | bytes 393224 | tf_op jit(solution)/shard_map/ppermute | solution.py:316
  56.4 0.0 collective-permute-done.23.refs_8_
  56.4 0.4 collective-permute-start.27
  56.9 3.3 %collective-permute-done.24.refs_9_ = bf16[2,128,256]{2,1,0:T(8,128)(2,1)S(1)} collective-permute-done((bf16[2,128,256]{2,1,0:T(8,128)(2,1)S(1)}, bf16[2,128,256]{2,1,0:T(8,128)(2,1)S(1)}, u32[]{:S(2)}, u32[]{:S(2)}) %collective-permute-start.24) | collective-permute-done | bytes 131104 | tf_op jit(solution)/shard_map/ppermute | solution.py:316
  60.2 2.0 %collective-permute-done.25.refs_10_ = bf16[2,128,256]{2,1,0:T(8,128)(2,1)S(1)} collective-permute-done((bf16[2,128,256]{2,1,0:T(8,128)(2,1)S(1)}, bf16[2,128,256]{2,1,0:T(8,128)(2,1)S(1)}, u32[]{:S(2)}, u32[]{:S(2)}) %collective-permute-start.25) | collective-permute-done | bytes 131104 | tf_op jit(solution)/shard_map/ppermute | solution.py:316
  62.2 0.5 collective-permute-done.26.refs_11_
  62.7 0.0 collective-permute-done.27.refs_12_
  62.7 0.0 collective-permute-done.18.refs_4_
  62.7 1.3 %shard_map.73 = (bf16[128,2048]{1,0:T(8,128)(2,1)}, bf16[128,2048]{1,0:T(8,128)(2,1)}, bf16[128,2048]{1,0:T(8,128)(2,1)}) custom-call(bf16[2,128,256]{2,1,0:T(8,128)(2,1)S(1)} %get-tuple-element.61.refs_0_, bf16[2,128,256]{2,1,0:T(8,128)(2,1)S(1)} %collective-permute-done.15.refs_1_, bf16[2,128,256]{2,1,0:T(8,128)(2,1)S(1)} %collective-permute-done.16.refs_2_, ...), custom_call_target="tpu_custom_call" | custom-call | tf_op jit(solution)/shard_map/pallas_call | solution.py:285
  (1 shorter events, 0.0 us)
Async XLA Ops:
  2.3 5.8 %collective-permute-start = (bf16[2,128,256]{2,1,0:T(8,128)(2,1)S(1)}, bf16[2,128,256]{2,1,0:T(8,128)(2,1)S(1)}, u32[]{:S(2)}, u32[]{:S(2)}) collective-permute-start(bf16[2,128,256]{2,1,0:T(8,128)(2,1)S(1)} %get-tuple-element.40), channel_id=1, source_target_pairs={{0,6},{1,7},{2,4},{3,5},{4,2},{5,3},{6,0},{7,1},{8,14},{9,15},{10,... | collective-permute-start | bytes 393224 | tf_op jit(solution)/shard_map/ppermute | solution.py:316
  4.5 6.8 %collective-permute-start.1 = (bf16[2,128,256]{2,1,0:T(8,128)(2,1)S(1)}, bf16[2,128,256]{2,1,0:T(8,128)(2,1)S(1)}, u32[]{:S(2)}, u32[]{:S(2)}) collective-permute-start(bf16[2,128,256]{2,1,0:T(8,128)(2,1)S(1)} %get-tuple-element.41), channel_id=1, source_target_pairs={{0,7},{1,6},{2,5},{3,4},{4,3},{5,2},{6,1},{7,0},{8,15},{9,14},{10,... | collective-permute-start | bytes 393224 | tf_op jit(solution)/shard_map/ppermute | solution.py:316
  5.6 8.0 %collective-permute-start.2 = (bf16[2,128,256]{2,1,0:T(8,128)(2,1)S(1)}, bf16[2,128,256]{2,1,0:T(8,128)(2,1)S(1)}, u32[]{:S(2)}, u32[]{:S(2)}) collective-permute-start(bf16[2,128,256]{2,1,0:T(8,128)(2,1)S(1)} %get-tuple-element.42), channel_id=1, source_target_pairs={{0,2},{1,3},{2,0},{3,1},{4,6},{5,7},{6,4},{7,5},{8,10},{9,11},{10,... | collective-permute-start | bytes 393224 | tf_op jit(solution)/shard_map/ppermute | solution.py:316
  6.8 8.1 %collective-permute-start.3 = (bf16[2,128,256]{2,1,0:T(8,128)(2,1)S(1)}, bf16[2,128,256]{2,1,0:T(8,128)(2,1)S(1)}, u32[]{:S(2)}, u32[]{:S(2)}) collective-permute-start(bf16[2,128,256]{2,1,0:T(8,128)(2,1)S(1)} %get-tuple-element.43), channel_id=1, source_target_pairs={{0,4},{1,5},{2,6},{3,7},{4,0},{5,1},{6,2},{7,3},{8,12},{9,13},{10,... | collective-permute-start | bytes 393224 | tf_op jit(solution)/shard_map/ppermute | solution.py:316
  8.0 10.2 %collective-permute-start.4 = (bf16[2,128,256]{2,1,0:T(8,128)(2,1)S(1)}, bf16[2,128,256]{2,1,0:T(8,128)(2,1)S(1)}, u32[]{:S(2)}, u32[]{:S(2)}) collective-permute-start(bf16[2,128,256]{2,1,0:T(8,128)(2,1)S(1)} %get-tuple-element.44), channel_id=1, source_target_pairs={{0,1},{1,0},{2,3},{3,2},{4,5},{5,4},{6,7},{7,6},{8,9},{9,8},{10,11... | collective-permute-start | bytes 393224 | tf_op jit(solution)/shard_map/ppermute | solution.py:316
  8.1 11.7 %collective-permute-start.5 = (bf16[2,128,256]{2,1,0:T(8,128)(2,1)S(1)}, bf16[2,128,256]{2,1,0:T(8,128)(2,1)S(1)}, u32[]{:S(2)}, u32[]{:S(2)}) collective-permute-start(bf16[2,128,256]{2,1,0:T(8,128)(2,1)S(1)} %get-tuple-element.45), channel_id=1, source_target_pairs={{0,3},{1,2},{2,1},{3,0},{4,7},{5,6},{6,5},{7,4},{8,11},{9,10},{10,... | collective-permute-start | bytes 393224 | tf_op jit(solution)/shard_map/ppermute | solution.py:316
  11.3 8.4 %collective-permute-start.6 = (bf16[2,128,256]{2,1,0:T(8,128)(2,1)S(1)}, bf16[2,128,256]{2,1,0:T(8,128)(2,1)S(1)}, u32[]{:S(2)}, u32[]{:S(2)}) collective-permute-start(bf16[2,128,256]{2,1,0:T(8,128)(2,1)S(1)} %get-tuple-element.46), channel_id=1, source_target_pairs={{0,5},{1,4},{2,7},{3,6},{4,1},{5,0},{6,3},{7,2},{8,13},{9,12},{10,... | collective-permute-start | bytes 393224 | tf_op jit(solution)/shard_map/ppermute | solution.py:316
  13.6 9.5 %collective-permute-start.10 = (bf16[2,128,256]{2,1,0:T(8,128)(2,1)S(1)}, bf16[2,128,256]{2,1,0:T(8,128)(2,1)S(1)}, u32[]{:S(2)}, u32[]{:S(2)}) collective-permute-start(bf16[2,128,256]{2,1,0:T(8,128)(2,1)S(1)} %get-tuple-element.52), channel_id=1, source_target_pairs={{0,6},{1,7},{2,4},{3,5},{4,2},{5,3},{6,0},{7,1},{8,14},{9,15},{10,... | collective-permute-start | bytes 393224 | tf_op jit(solution)/shard_map/ppermute | solution.py:316
  14.9 10.3 %collective-permute-start.11 = (bf16[2,128,256]{2,1,0:T(8,128)(2,1)S(1)}, bf16[2,128,256]{2,1,0:T(8,128)(2,1)S(1)}, u32[]{:S(2)}, u32[]{:S(2)}) collective-permute-start(bf16[2,128,256]{2,1,0:T(8,128)(2,1)S(1)} %get-tuple-element.53), channel_id=1, source_target_pairs={{0,7},{1,6},{2,5},{3,4},{4,3},{5,2},{6,1},{7,0},{8,15},{9,14},{10,... | collective-permute-start | bytes 393224 | tf_op jit(solution)/shard_map/ppermute | solution.py:316
  18.2 8.6 %collective-permute-start.12 = (bf16[2,128,256]{2,1,0:T(8,128)(2,1)S(1)}, bf16[2,128,256]{2,1,0:T(8,128)(2,1)S(1)}, u32[]{:S(2)}, u32[]{:S(2)}) collective-permute-start(bf16[2,128,256]{2,1,0:T(8,128)(2,1)S(1)} %get-tuple-element.54), channel_id=1, source_target_pairs={{0,2},{1,3},{2,0},{3,1},{4,6},{5,7},{6,4},{7,5},{8,10},{9,11},{10,... | collective-permute-start | bytes 393224 | tf_op jit(solution)/shard_map/ppermute | solution.py:316
  19.8 7.6 %collective-permute-start.13 = (bf16[2,128,256]{2,1,0:T(8,128)(2,1)S(1)}, bf16[2,128,256]{2,1,0:T(8,128)(2,1)S(1)}, u32[]{:S(2)}, u32[]{:S(2)}) collective-permute-start(bf16[2,128,256]{2,1,0:T(8,128)(2,1)S(1)} %get-tuple-element.55), channel_id=1, source_target_pairs={{0,4},{1,5},{2,6},{3,7},{4,0},{5,1},{6,2},{7,3},{8,12},{9,13},{10,... | collective-permute-start | bytes 393224 | tf_op jit(solution)/shard_map/ppermute | solution.py:316
  19.9 15.7 %collective-permute-start.14 = (bf16[2,512,256]{2,1,0:T(8,128)(2,1)S(1)}, bf16[2,512,256]{2,1,0:T(8,128)(2,1)S(1)}, u32[]{:S(2)}, u32[]{:S(2)}) collective-permute-start(bf16[2,512,256]{2,1,0:T(8,128)(2,1)S(1)} %get-tuple-element.56.refs_8_.refs_3_.refs_1_), channel_id=1, source_target_pairs={{0,8},{8,16},{16,24},{1,9},{9,17},{17,25},{2,10},{10,18},{18,26},{... | collective-permute-start | bytes 1572872 | tf_op jit(solution)/shard_map/ppermute | solution.py:348
  23.1 20.6 %collective-permute-start.19 = (bf16[2,512,256]{2,1,0:T(8,128)(2,1)S(1)}, bf16[2,512,256]{2,1,0:T(8,128)(2,1)S(1)}, u32[]{:S(2)}, u32[]{:S(2)}) collective-permute-start(bf16[2,512,256]{2,1,0:T(8,128)(2,1)S(1)} %get-tuple-element.47.refs_9_.refs_0_), channel_id=1, source_target_pairs={{8,0},{16,8},{24,16},{9,1},{17,9},{25,17},{10,2},{18,10},{26,18},{... | collective-permute-start | bytes 1572872 | tf_op jit(solution)/shard_map/ppermute | solution.py:349
  25.2 5.5 %collective-permute-start.7 = (bf16[2,128,256]{2,1,0:T(8,128)(2,1)S(1)}, bf16[2,128,256]{2,1,0:T(8,128)(2,1)S(1)}, u32[]{:S(2)}, u32[]{:S(2)}) collective-permute-start(bf16[2,128,256]{2,1,0:T(8,128)(2,1)S(1)} %get-tuple-element.49), channel_id=1, source_target_pairs={{0,3},{1,2},{2,1},{3,0},{4,7},{5,6},{6,5},{7,4},{8,11},{9,10},{10,... | collective-permute-start | bytes 393224 | tf_op jit(solution)/shard_map/ppermute | solution.py:316
  26.8 5.2 %collective-permute-start.8 = (bf16[2,128,256]{2,1,0:T(8,128)(2,1)S(1)}, bf16[2,128,256]{2,1,0:T(8,128)(2,1)S(1)}, u32[]{:S(2)}, u32[]{:S(2)}) collective-permute-start(bf16[2,128,256]{2,1,0:T(8,128)(2,1)S(1)} %get-tuple-element.50), channel_id=1, source_target_pairs={{0,5},{1,4},{2,7},{3,6},{4,1},{5,0},{6,3},{7,2},{8,13},{9,12},{10,... | collective-permute-start | bytes 393224 | tf_op jit(solution)/shard_map/ppermute | solution.py:316
  27.4 4.6 %collective-permute-start.9 = (bf16[2,128,256]{2,1,0:T(8,128)(2,1)S(1)}, bf16[2,128,256]{2,1,0:T(8,128)(2,1)S(1)}, u32[]{:S(2)}, u32[]{:S(2)}) collective-permute-start(bf16[2,128,256]{2,1,0:T(8,128)(2,1)S(1)} %get-tuple-element.51), channel_id=1, source_target_pairs={{0,1},{1,0},{2,3},{3,2},{4,5},{5,4},{6,7},{7,6},{8,9},{9,8},{10,11... | collective-permute-start | bytes 393224 | tf_op jit(solution)/shard_map/ppermute | solution.py:316
  38.9 4.8 %collective-permute-start.20 = (f32[8,512]{1,0:T(8,128)S(1)}, f32[8,512]{1,0:T(8,128)S(1)}, u32[]{:S(2)}, u32[]{:S(2)}) collective-permute-start(f32[8,512]{1,0:T(8,128)S(1)} %get-tuple-element.66), channel_id=1, source_target_pairs={{8,0},{16,8},{24,16},{9,1},{17,9},{25,17},{10,2},{18,10},{26,18},{... | collective-permute-start | bytes 49160 | tf_op jit(solution)/shard_map/ppermute | solution.py:365
  40.9 6.0 %collective-permute-start.15 = (bf16[2,128,256]{2,1,0:T(8,128)(2,1)S(1)}, bf16[2,128,256]{2,1,0:T(8,128)(2,1)S(1)}, u32[]{:S(2)}, u32[]{:S(2)}) collective-permute-start(bf16[2,128,256]{2,1,0:T(8,128)(2,1)S(1)} %get-tuple-element.62), channel_id=1, source_target_pairs={{0,6},{1,7},{2,4},{3,5},{4,2},{5,3},{6,0},{7,1},{8,14},{9,15},{10,... | collective-permute-start | bytes 393224 | tf_op jit(solution)/shard_map/ppermute | solution.py:316
  42.1 6.7 %collective-permute-start.16 = (bf16[2,128,256]{2,1,0:T(8,128)(2,1)S(1)}, bf16[2,128,256]{2,1,0:T(8,128)(2,1)S(1)}, u32[]{:S(2)}, u32[]{:S(2)}) collective-permute-start(bf16[2,128,256]{2,1,0:T(8,128)(2,1)S(1)} %get-tuple-element.63), channel_id=1, source_target_pairs={{0,2},{1,3},{2,0},{3,1},{4,6},{5,7},{6,4},{7,5},{8,10},{9,11},{10,... | collective-permute-start | bytes 393224 | tf_op jit(solution)/shard_map/ppermute | solution.py:316
  43.0 7.3 %collective-permute-start.17 = (bf16[2,128,256]{2,1,0:T(8,128)(2,1)S(1)}, bf16[2,128,256]{2,1,0:T(8,128)(2,1)S(1)}, u32[]{:S(2)}, u32[]{:S(2)}) collective-permute-start(bf16[2,128,256]{2,1,0:T(8,128)(2,1)S(1)} %get-tuple-element.64), channel_id=1, source_target_pairs={{0,4},{1,5},{2,6},{3,7},{4,0},{5,1},{6,2},{7,3},{8,12},{9,13},{10,... | collective-permute-start | bytes 393224 | tf_op jit(solution)/shard_map/ppermute | solution.py:316
  44.9 9.4 %collective-permute-start.21 = (bf16[2,128,256]{2,1,0:T(8,128)(2,1)S(1)}, bf16[2,128,256]{2,1,0:T(8,128)(2,1)S(1)}, u32[]{:S(2)}, u32[]{:S(2)}) collective-permute-start(bf16[2,128,256]{2,1,0:T(8,128)(2,1)S(1)} %get-tuple-element.68), channel_id=1, source_target_pairs={{0,6},{1,7},{2,4},{3,5},{4,2},{5,3},{6,0},{7,1},{8,14},{9,15},{10,... | collective-permute-start | bytes 393224 | tf_op jit(solution)/shard_map/ppermute | solution.py:316
  46.0 9.6 %collective-permute-start.22 = (bf16[2,128,256]{2,1,0:T(8,128)(2,1)S(1)}, bf16[2,128,256]{2,1,0:T(8,128)(2,1)S(1)}, u32[]{:S(2)}, u32[]{:S(2)}) collective-permute-start(bf16[2,128,256]{2,1,0:T(8,128)(2,1)S(1)} %get-tuple-element.69), channel_id=1, source_target_pairs={{0,2},{1,3},{2,0},{3,1},{4,6},{5,7},{6,4},{7,5},{8,10},{9,11},{10,... | collective-permute-start | bytes 393224 | tf_op jit(solution)/shard_map/ppermute | solution.py:316
  46.9 9.5 %collective-permute-start.23 = (bf16[2,128,256]{2,1,0:T(8,128)(2,1)S(1)}, bf16[2,128,256]{2,1,0:T(8,128)(2,1)S(1)}, u32[]{:S(2)}, u32[]{:S(2)}) collective-permute-start(bf16[2,128,256]{2,1,0:T(8,128)(2,1)S(1)} %get-tuple-element.70), channel_id=1, source_target_pairs={{0,4},{1,5},{2,6},{3,7},{4,0},{5,1},{6,2},{7,3},{8,12},{9,13},{10,... | collective-permute-start | bytes 393224 | tf_op jit(solution)/shard_map/ppermute | solution.py:316
  50.2 12.5 %collective-permute-start.18 = (bf16[4,128,256]{2,1,0:T(8,128)(2,1)S(1)}, bf16[4,128,256]{2,1,0:T(8,128)(2,1)S(1)}, u32[]{:S(2)}, u32[]{:S(2)}) collective-permute-start(bf16[4,128,256]{2,1,0:T(8,128)(2,1)S(1)} %shard_map.71), channel_id=1, source_target_pairs={{0,1},{1,0},{2,3},{3,2},{4,5},{5,4},{6,7},{7,6},{8,9},{9,8},{10,11... | collective-permute-start | bytes 786440 | tf_op jit(solution)/shard_map/ppermute | solution.py:370
  53.5 6.7 %collective-permute-start.24 = (bf16[2,128,256]{2,1,0:T(8,128)(2,1)S(1)}, bf16[2,128,256]{2,1,0:T(8,128)(2,1)S(1)}, u32[]{:S(2)}, u32[]{:S(2)}) collective-permute-start(bf16[2,128,256]{2,1,0:T(8,128)(2,1)S(1)} %get-tuple-element.71), channel_id=1, source_target_pairs={{0,7},{1,6},{2,5},{3,4},{4,3},{5,2},{6,1},{7,0},{8,15},{9,14},{10,... | collective-permute-start | bytes 393224 | tf_op jit(solution)/shard_map/ppermute | solution.py:316
  54.4 7.8 %collective-permute-start.25 = (bf16[2,128,256]{2,1,0:T(8,128)(2,1)S(1)}, bf16[2,128,256]{2,1,0:T(8,128)(2,1)S(1)}, u32[]{:S(2)}, u32[]{:S(2)}) collective-permute-start(bf16[2,128,256]{2,1,0:T(8,128)(2,1)S(1)} %get-tuple-element.72), channel_id=1, source_target_pairs={{0,3},{1,2},{2,1},{3,0},{4,7},{5,6},{6,5},{7,4},{8,11},{9,10},{10,... | collective-permute-start | bytes 393224 | tf_op jit(solution)/shard_map/ppermute | solution.py:316
  55.7 7.0 %collective-permute-start.26 = (bf16[2,128,256]{2,1,0:T(8,128)(2,1)S(1)}, bf16[2,128,256]{2,1,0:T(8,128)(2,1)S(1)}, u32[]{:S(2)}, u32[]{:S(2)}) collective-permute-start(bf16[2,128,256]{2,1,0:T(8,128)(2,1)S(1)} %get-tuple-element.73), channel_id=1, source_target_pairs={{0,5},{1,4},{2,7},{3,6},{4,1},{5,0},{6,3},{7,2},{8,13},{9,12},{10,... | collective-permute-start | bytes 393224 | tf_op jit(solution)/shard_map/ppermute | solution.py:316
  56.4 6.2 %collective-permute-start.27 = (bf16[2,128,256]{2,1,0:T(8,128)(2,1)S(1)}, bf16[2,128,256]{2,1,0:T(8,128)(2,1)S(1)}, u32[]{:S(2)}, u32[]{:S(2)}) collective-permute-start(bf16[2,128,256]{2,1,0:T(8,128)(2,1)S(1)} %get-tuple-element.74), channel_id=1, source_target_pairs={{0,1},{1,0},{2,3},{3,2},{4,5},{5,4},{6,7},{7,6},{8,9},{9,8},{10,11... | collective-permute-start | bytes 393224 | tf_op jit(solution)/shard_map/ppermute | solution.py:316

commit v5 on v4

--- a/solution.py
+++ b/solution.py
@@ -25,7 +25,7 @@
 REST_ORDER = (0, 3, 5, 1, 6, 7, 2, 4)
 DQ_ORDER = (0, 3, 1, 2)
 DKV_ORDER = (0, 6, 2, 4, 7, 3, 5, 1)
-QG_FIRST = False
+DEPTH = 2
 EDGE_FLOPS = 4000000000
 LATE_FLOPS = 4000000000
 
@@ -129,11 +129,9 @@
     return out[0] if len(out) == 1 else jnp.concatenate(out, axis=0)
 
 
-def softmax_block(qb, gb, kb, vb, bias, blind):
+def softmax_block(s, dp, bias, blind):
     row = lax.broadcasted_iota(jnp.int32, (HALF, HALF), 0)
     col = lax.broadcasted_iota(jnp.int32, (HALF, HALF), 1)
-    s = dot(kb, qb, NT)
-    dp = dot(vb, gb, NT)
     span = WINDOW // HALF + 1
     nothing = jnp.zeros((HALF, HALF), jnp.bfloat16)
     p_parts, ds_parts, stats = [], [], []
@@ -158,35 +156,56 @@
     return jnp.concatenate(p_parts, axis=1), jnp.concatenate(ds_parts, axis=1), stats
 
 
+def staged(blocks, first, second, third):
+    made, held_back = {}, {}
+    for i in range(len(blocks) + DEPTH):
+        if i < len(blocks):
+            made[i] = first(*blocks[i])
+        j = i - DEPTH // 2
+        if 0 <= j < len(blocks):
+            held_back[j] = second(*blocks[j], *made.pop(j))
+        k = i - DEPTH
+        if 0 <= k < len(blocks):
+            third(*blocks[k], *held_back.pop(k))
+
+
 def late_kernel(n, heads, *refs):
     rest = by_slot(REST_ORDER, refs[:n])
     kv_late, qg_early, qg_late, kv_early, dq, dkv = refs[n:]
     place_all(rest, qg_late, kv_early, group_index())
     total = dkv.shape[1]
     qg, kv = (qg_early, qg_late), (kv_early, kv_late)
-    for h in range(heads):
-        lanes = slice(h * HEAD_DIM, (h + 1) * HEAD_DIM)
-        key_t = load(kv, 0, 0, total, lanes).T
-        for start in range(0, total - WINDOW, TILE):
-            keys = slice(start, start + 3 * TILE)
-            mine = slice(start + WINDOW, start + WINDOW + TILE)
-            qb, gb = (load(qg, t, start + WINDOW, start + WINDOW + TILE, lanes) for t in range(2))
-            kb, vb = (load(kv, t, start, start + 3 * TILE, lanes) for t in range(2))
-            p_low, ds, _ = softmax_block(qb, gb, kb, vb, 0.0, 0)
-            out = slice(start, start + TILE)
-            dq[out, lanes] = (dot(key_t[:, keys], ds, NN) * SCALE).T.astype(jnp.bfloat16)
-            for t, add in enumerate((dot(ds, qb, NN), dot(p_low, gb, NN))):
-                if start == 0:
-                    dkv[t, keys, lanes] = add
-                else:
-                    older = slice(start, start + 2 * TILE)
-                    dkv[t, older, lanes] += add[: 2 * TILE]
-                    dkv[t, mine, lanes] = add[2 * TILE :]
+    blocks = [(h, start) for h in range(heads) for start in range(0, total - WINDOW, TILE)]
+    lanes_of = [slice(h * HEAD_DIM, (h + 1) * HEAD_DIM) for h in range(heads)]
+    key_ts = [load(kv, 0, 0, total, lanes).T for lanes in lanes_of]
+
+    def products(h, start):
+        qb, gb = (load(qg, t, start + WINDOW, start + WINDOW + TILE, lanes_of[h]) for t in range(2))
+        kb, vb = (load(kv, t, start, start + 3 * TILE, lanes_of[h]) for t in range(2))
+        return dot(kb, qb, NT), dot(vb, gb, NT)
+
+    def gradients(h, start, p_low, ds):
+        lanes = lanes_of[h]
+        keys = slice(start, start + 3 * TILE)
+        mine = slice(start + WINDOW, start + WINDOW + TILE)
+        qb, gb = (load(qg, t, start + WINDOW, start + WINDOW + TILE, lanes) for t in range(2))
+        dq[slice(start, start + TILE), lanes] = (
+            (dot(key_ts[h][:, keys], ds, NN) * SCALE).T.astype(jnp.bfloat16)
+        )
+        for t, add in enumerate((dot(ds, qb, NN), dot(p_low, gb, NN))):
+            if start == 0:
+                dkv[t, keys, lanes] = add
+            else:
+                older = slice(start, start + 2 * TILE)
+                dkv[t, older, lanes] += add[: 2 * TILE]
+                dkv[t, mine, lanes] = add[2 * TILE :]
+
+    staged(blocks, products, lambda h, start, s, dp: softmax_block(s, dp, 0.0, 0)[:2], gradients)
 
 
 def early_kernel(n, heads, *refs):
     qg_early, qg_late, kv_early, kv_late, kv_halo, dq_in, dkv_in = refs[:7]
-    refs = refs[7 + QG_FIRST :]
+    refs = refs[7:]
     dq_out = refs[: n // 2]
     front, stat, dq, acc = refs[n // 2 :]
     me = group_index()
@@ -197,23 +216,35 @@
     acc[...] = dkv_in[:, :WINDOW]
     bias = jnp.where(first, MASKED, 0.0)
     qg, kv = (qg_early, qg_late), (kv_halo, kv_early, kv_late)
-    for h in range(heads):
-        lanes = slice(h * HEAD_DIM, (h + 1) * HEAD_DIM)
-        key_t = load(kv, 0, 0, 2 * WINDOW, lanes).T
-        for start in range(0, WINDOW, TILE):
-            keys = slice(start, start + 3 * TILE)
-            mine = slice(start, start + TILE)
-            qb, gb = (load(qg, t, start, start + TILE, lanes) for t in range(2))
-            kb, vb = (load(kv, t, start, start + 3 * TILE, lanes) for t in range(2))
-            p_low, ds, stats = softmax_block(qb, gb, kb, vb, bias, WINDOW - start)
-            dq[mine, lanes] = (dot(key_t[:, keys], ds, NN) * SCALE).T.astype(jnp.bfloat16)
-            own = slice(0, start + TILE)
-            acc[0, own, lanes] += dot(ds[WINDOW - start :], qb, NN)
-            acc[1, own, lanes] += dot(p_low[WINDOW - start :], gb, NN)
-            for c, rows_of in enumerate(stats):
-                at = slice(start + c * HALF, start + (c + 1) * HALF)
-                for k, value in enumerate(rows_of):
-                    stat[3 * h + k : 3 * h + k + 1, at] = value
+    blocks = [(h, start) for h in range(heads) for start in range(0, WINDOW, TILE)]
+    lanes_of = [slice(h * HEAD_DIM, (h + 1) * HEAD_DIM) for h in range(heads)]
+    key_ts = [load(kv, 0, 0, 2 * WINDOW, lanes).T for lanes in lanes_of]
+
+    def products(h, start):
+        qb, gb = (load(qg, t, start, start + TILE, lanes_of[h]) for t in range(2))
+        kb, vb = (load(kv, t, start, start + 3 * TILE, lanes_of[h]) for t in range(2))
+        return dot(kb, qb, NT), dot(vb, gb, NT)
+
+    def probabilities(h, start, s, dp):
+        p_low, ds, stats = softmax_block(s, dp, bias, WINDOW - start)
+        for c, rows_of in enumerate(stats):
+            at = slice(start + c * HALF, start + (c + 1) * HALF)
+            for k, value in enumerate(rows_of):
+                stat[3 * h + k : 3 * h + k + 1, at] = value
+        return p_low, ds
+
+    def gradients(h, start, p_low, ds):
+        lanes = lanes_of[h]
+        keys = slice(start, start + 3 * TILE)
+        qb, gb = (load(qg, t, start, start + TILE, lanes) for t in range(2))
+        dq[slice(start, start + TILE), lanes] = (
+            (dot(key_ts[h][:, keys], ds, NN) * SCALE).T.astype(jnp.bfloat16)
+        )
+        own = slice(0, start + TILE)
+        acc[0, own, lanes] += dot(ds[WINDOW - start :], qb, NN)
+        acc[1, own, lanes] += dot(p_low[WINDOW - start :], gb, NN)
+
+    staged(blocks, products, probabilities, gradients)
     for m in range(n):
         dq_out[m // 2][m % 2] = dq[pl.ds(aligned(jnp.bitwise_xor(me, m), rows), rows)]
     front[0] = (acc[0] * SCALE).astype(jnp.bfloat16)
@@ -360,7 +391,6 @@
         [vmem(bf16(2, rows, width))] * (n // 2) + [end, stat_out],
         [vmem(bf16(total, width)), vmem(f32(2, WINDOW, width))], 0,
         *held((qg_early, qg_late, kv_early, kv_late, kv_halo, dq_late, partial)),
-        *([qg_halo] if QG_FIRST else []),
     )
     stat_halo = lax.ppermute(stat, "chunk", backward)
     dq = exchanged(DQ_ORDER, dq, 2)

time: 64.2 us -> 62.5 us (0.974)
  Pallas kernels: 11 us -> 9.52 us
  starting transfers between devices: 37.6 us -> 36.5 us
  waiting for transfers between devices: 14.6 us -> 15.3 us
    ppermute x1, starting transfers between devices: 3.31 us -> 0.76 us  [per_device(): other = lax.ppermute(other, GROUP, [(i, i ^ 1) for i in range(n)])]
    pallas_call x7, Pallas kernels: 11 us -> 9.52 us  [call(): pl.pallas_call(kernel, out_shape=outs, in_specs=[held if isinstance(x, tu...]
    ppermute x24, starting transfers between devices: 26.9 us -> 28.4 us  [exchanged(): lax.ppermute(pieces[m], GROUP, [(i, i ^ step * m) for i in range(step * n)])]
    ppermute x1, waiting for transfers between devices: 0.2 us -> 0.98 us  [per_device(): kv_halo = lax.ppermute(kv_send, 'chunk', forward)]
  transfers between devices with their start and end apart: 28 -> 28, of which waited for: 10 -> 10; matrix products, arithmetic and copies ran while one was open for 0% -> 0% of each run, Pallas kernels for 13% -> 11%
where the time goes in v5:
time: 62.5 us; the launch traced here: 62 us
  starting transfers between devices  36.5 us (58%)
  waiting for transfers between devices  15.3 us (24%)
  Pallas kernels  9.52 us (15%)
  between operations  0.74 us (1%)
    ppermute x24, starting transfers between devices, exchanged(): lax.ppermute(pieces[m], GROUP, [(i, i ^ step * m) for i in range(step * n)])  28.4 us
    ppermute x24, waiting for transfers between devices, exchanged(): lax.ppermute(pieces[m], GROUP, [(i, i ^ step * m) for i in range(step * n)])  14.3 us
    pallas_call x7, Pallas kernels, call(): pl.pallas_call(kernel, out_shape=outs, in_specs=[held if isinstance(x, tu...  9.52 us
    ppermute x1, starting transfers between devices, per_device(): kv_halo = lax.ppermute(kv_send, 'chunk', forward)  3.2 us
    ppermute x1, starting transfers between devices, per_device(): qg_halo = lax.ppermute(qg_send, 'chunk', backward)  2.08 us
    ppermute x1, starting transfers between devices, per_device(): stat_halo = lax.ppermute(stat, 'chunk', backward)  2.08 us
  transfers between devices with their start and end apart: 28, of which 10 were waited for; matrix products, arithmetic and copies ran while one was open for 0% of the time, Pallas kernels for 11%

profile of v5, /device:TPU:17, one launch (start us, length us, event | category | flops | bytes accessed | tf_op | source)
XLA Modules:
  0.0 62.0 jit_solution(5725151792392200028)
XLA Ops:
  0.6 1.6 %shard_map.67 = (bf16[2,128,256]{2,1,0:T(8,128)(2,1)S(1)}, bf16[2,128,256]{2,1,0:T(8,128)(2,1)S(1)}, bf16[2,128,256]{2,1,0:T(8,128)(2,1)S(1)}, bf16[2,128,256]{2...) custom-call(bf16[128,2048]{1,0:T(8,128)(2,1)} %refs_0_.1, ...), custom_call_target="tpu_custom_call" | custom-call | tf_op jit(solution)/shard_map/pallas_call | solution.py:316
  2.3 2.2 %collective-permute-start = (bf16[2,128,256]{2,1,0:T(8,128)(2,1)S(1)}, bf16[2,128,256]{2,1,0:T(8,128)(2,1)S(1)}, u32[]{:S(2)}, u32[]{:S(2)}) collective-permute-start(bf16[2,128,256]{2,1,0:T(8,128)(2,1)S(1)} %get-tuple-element.40), channel_id=1, source_target_pairs={{0,6},{1,7},{2,4},{3,5},{4,2},{5,3},{6,0},{7,1},{8,14},{9,15},{10,... | collective-permute-start | bytes 393224 | tf_op jit(solution)/shard_map/ppermute | solution.py:347
  4.5 1.0 %collective-permute-start.1 = (bf16[2,128,256]{2,1,0:T(8,128)(2,1)S(1)}, bf16[2,128,256]{2,1,0:T(8,128)(2,1)S(1)}, u32[]{:S(2)}, u32[]{:S(2)}) collective-permute-start(bf16[2,128,256]{2,1,0:T(8,128)(2,1)S(1)} %get-tuple-element.41), channel_id=1, source_target_pairs={{0,7},{1,6},{2,5},{3,4},{4,3},{5,2},{6,1},{7,0},{8,15},{9,14},{10,... | collective-permute-start | bytes 393224 | tf_op jit(solution)/shard_map/ppermute | solution.py:347
  5.6 1.2 %collective-permute-start.2 = (bf16[2,128,256]{2,1,0:T(8,128)(2,1)S(1)}, bf16[2,128,256]{2,1,0:T(8,128)(2,1)S(1)}, u32[]{:S(2)}, u32[]{:S(2)}) collective-permute-start(bf16[2,128,256]{2,1,0:T(8,128)(2,1)S(1)} %get-tuple-element.42), channel_id=1, source_target_pairs={{0,2},{1,3},{2,0},{3,1},{4,6},{5,7},{6,4},{7,5},{8,10},{9,11},{10,... | collective-permute-start | bytes 393224 | tf_op jit(solution)/shard_map/ppermute | solution.py:347
  6.8 1.2 %collective-permute-start.3 = (bf16[2,128,256]{2,1,0:T(8,128)(2,1)S(1)}, bf16[2,128,256]{2,1,0:T(8,128)(2,1)S(1)}, u32[]{:S(2)}, u32[]{:S(2)}) collective-permute-start(bf16[2,128,256]{2,1,0:T(8,128)(2,1)S(1)} %get-tuple-element.43), channel_id=1, source_target_pairs={{0,4},{1,5},{2,6},{3,7},{4,0},{5,1},{6,2},{7,3},{8,12},{9,13},{10,... | collective-permute-start | bytes 393224 | tf_op jit(solution)/shard_map/ppermute | solution.py:347
  8.0 0.1 collective-permute-start.4
  8.1 0.0 collective-permute-done.refs_1_
  8.1 3.0 %collective-permute-start.5 = (bf16[2,128,256]{2,1,0:T(8,128)(2,1)S(1)}, bf16[2,128,256]{2,1,0:T(8,128)(2,1)S(1)}, u32[]{:S(2)}, u32[]{:S(2)}) collective-permute-start(bf16[2,128,256]{2,1,0:T(8,128)(2,1)S(1)} %get-tuple-element.45), channel_id=1, source_target_pairs={{0,3},{1,2},{2,1},{3,0},{4,7},{5,6},{6,5},{7,4},{8,11},{9,10},{10,... | collective-permute-start | bytes 393224 | tf_op jit(solution)/shard_map/ppermute | solution.py:347
  11.1 0.2 collective-permute-done.1.refs_2_
  11.3 1.0 %collective-permute-start.6 = (bf16[2,128,256]{2,1,0:T(8,128)(2,1)S(1)}, bf16[2,128,256]{2,1,0:T(8,128)(2,1)S(1)}, u32[]{:S(2)}, u32[]{:S(2)}) collective-permute-start(bf16[2,128,256]{2,1,0:T(8,128)(2,1)S(1)} %get-tuple-element.46), channel_id=1, source_target_pairs={{0,5},{1,4},{2,7},{3,6},{4,1},{5,0},{6,3},{7,2},{8,13},{9,12},{10,... | collective-permute-start | bytes 393224 | tf_op jit(solution)/shard_map/ppermute | solution.py:347
  12.4 1.2 %collective-permute-done.2.refs_3_ = bf16[2,128,256]{2,1,0:T(8,128)(2,1)S(1)} collective-permute-done((bf16[2,128,256]{2,1,0:T(8,128)(2,1)S(1)}, bf16[2,128,256]{2,1,0:T(8,128)(2,1)S(1)}, u32[]{:S(2)}, u32[]{:S(2)}) %collective-permute-start.2) | collective-permute-done | bytes 131104 | tf_op jit(solution)/shard_map/ppermute | solution.py:347
  13.6 1.3 %collective-permute-start.10 = (bf16[2,128,256]{2,1,0:T(8,128)(2,1)S(1)}, bf16[2,128,256]{2,1,0:T(8,128)(2,1)S(1)}, u32[]{:S(2)}, u32[]{:S(2)}) collective-permute-start(bf16[2,128,256]{2,1,0:T(8,128)(2,1)S(1)} %get-tuple-element.52), channel_id=1, source_target_pairs={{0,6},{1,7},{2,4},{3,5},{4,2},{5,3},{6,0},{7,1},{8,14},{9,15},{10,... | collective-permute-start | bytes 393224 | tf_op jit(solution)/shard_map/ppermute | solution.py:347
  14.9 0.0 collective-permute-done.3.refs_4_
  14.9 3.3 %collective-permute-start.11 = (bf16[2,128,256]{2,1,0:T(8,128)(2,1)S(1)}, bf16[2,128,256]{2,1,0:T(8,128)(2,1)S(1)}, u32[]{:S(2)}, u32[]{:S(2)}) collective-permute-start(bf16[2,128,256]{2,1,0:T(8,128)(2,1)S(1)} %get-tuple-element.53), channel_id=1, source_target_pairs={{0,7},{1,6},{2,5},{3,4},{4,3},{5,2},{6,1},{7,0},{8,15},{9,14},{10,... | collective-permute-start | bytes 393224 | tf_op jit(solution)/shard_map/ppermute | solution.py:347
  18.2 0.0 collective-permute-done.4.refs_5_
  18.2 1.6 %collective-permute-start.12 = (bf16[2,128,256]{2,1,0:T(8,128)(2,1)S(1)}, bf16[2,128,256]{2,1,0:T(8,128)(2,1)S(1)}, u32[]{:S(2)}, u32[]{:S(2)}) collective-permute-start(bf16[2,128,256]{2,1,0:T(8,128)(2,1)S(1)} %get-tuple-element.54), channel_id=1, source_target_pairs={{0,2},{1,3},{2,0},{3,1},{4,6},{5,7},{6,4},{7,5},{8,10},{9,11},{10,... | collective-permute-start | bytes 393224 | tf_op jit(solution)/shard_map/ppermute | solution.py:347
  19.8 0.0 collective-permute-done.5.refs_6_
  19.8 0.0 collective-permute-start.13
  19.8 0.0 collective-permute-done.6.refs_7_
  19.8 0.1 shard_map.68
  19.9 3.2 %collective-permute-start.14 = (bf16[2,512,256]{2,1,0:T(8,128)(2,1)S(1)}, bf16[2,512,256]{2,1,0:T(8,128)(2,1)S(1)}, u32[]{:S(2)}, u32[]{:S(2)}) collective-permute-start(bf16[2,512,256]{2,1,0:T(8,128)(2,1)S(1)} %get-tuple-element.56.refs_8_.refs_3_.refs_1_), channel_id=1, source_target_pairs={{0,8},{8,16},{16,24},{1,9},{9,17},{17,25},{2,10},{10,18},{18,26},{... | collective-permute-start | bytes 1572872 | tf_op jit(solution)/shard_map/ppermute | solution.py:379
  23.1 0.0 collective-permute-done.10.refs_4_
  23.1 2.1 %collective-permute-start.19 = (bf16[2,512,256]{2,1,0:T(8,128)(2,1)S(1)}, bf16[2,512,256]{2,1,0:T(8,128)(2,1)S(1)}, u32[]{:S(2)}, u32[]{:S(2)}) collective-permute-start(bf16[2,512,256]{2,1,0:T(8,128)(2,1)S(1)} %get-tuple-element.47.refs_9_.refs_0_), channel_id=1, source_target_pairs={{8,0},{16,8},{24,16},{9,1},{17,9},{25,17},{10,2},{18,10},{26,18},{... | collective-permute-start | bytes 1572872 | tf_op jit(solution)/shard_map/ppermute | solution.py:380
  25.2 0.0 collective-permute-done.11.refs_5_
  25.2 1.6 %collective-permute-start.7 = (bf16[2,128,256]{2,1,0:T(8,128)(2,1)S(1)}, bf16[2,128,256]{2,1,0:T(8,128)(2,1)S(1)}, u32[]{:S(2)}, u32[]{:S(2)}) collective-permute-start(bf16[2,128,256]{2,1,0:T(8,128)(2,1)S(1)} %get-tuple-element.49), channel_id=1, source_target_pairs={{0,3},{1,2},{2,1},{3,0},{4,7},{5,6},{6,5},{7,4},{8,11},{9,10},{10,... | collective-permute-start | bytes 393224 | tf_op jit(solution)/shard_map/ppermute | solution.py:347
  26.7 0.0 collective-permute-done.12.refs_6_
  26.8 0.6 collective-permute-start.8
  27.4 0.0 collective-permute-done.13.refs_7_
  27.4 0.0 collective-permute-start.9
  27.4 3.3 %collective-permute-done.7.refs_1_ = bf16[2,128,256]{2,1,0:T(8,128)(2,1)S(1)} collective-permute-done((bf16[2,128,256]{2,1,0:T(8,128)(2,1)S(1)}, bf16[2,128,256]{2,1,0:T(8,128)(2,1)S(1)}, u32[]{:S(2)}, u32[]{:S(2)}) %collective-permute-start.7) | collective-permute-done | bytes 131104 | tf_op jit(solution)/shard_map/ppermute | solution.py:347
  30.7 1.3 %collective-permute-done.8.refs_2_ = bf16[2,128,256]{2,1,0:T(8,128)(2,1)S(1)} collective-permute-done((bf16[2,128,256]{2,1,0:T(8,128)(2,1)S(1)}, bf16[2,128,256]{2,1,0:T(8,128)(2,1)S(1)}, u32[]{:S(2)}, u32[]{:S(2)}) %collective-permute-start.8) | collective-permute-done | bytes 131104 | tf_op jit(solution)/shard_map/ppermute | solution.py:347
  31.9 0.0 collective-permute-done.9.refs_3_
  31.9 2.7 %shard_map.69 = (bf16[2,512,256]{2,1,0:T(8,128)(2,1)S(1)}, bf16[2,512,256]{2,1,0:T(8,128)(2,1)S(1)}, bf16[512,256]{1,0:T(8,128)(2,1)S(1)}, f32[2,1024,256]{2,1,0:T(8,128)S(1)}) custom-call(bf16[2,128,256]{2,1,0:T(8,128)(2,1)S(1)} %get-tuple-element.48.refs_0_, bf16[2,128,256]{2,1,0:T(8,128)(2,1)S(1)} %collective-permute-done.7.refs_1_, ...), custom_call_target="tpu_custom_call" | custom-call | flops 4000000000 | tf_op jit(solution)/shard_map/pallas_call | solution.py:316
  34.6 1.0 %collective-permute-done.14.refs_4_ = bf16[2,512,256]{2,1,0:T(8,128)(2,1)S(1)} collective-permute-done((bf16[2,512,256]{2,1,0:T(8,128)(2,1)S(1)}, bf16[2,512,256]{2,1,0:T(8,128)(2,1)S(1)}, u32[]{:S(2)}, u32[]{:S(2)}) %collective-permute-start.14) | collective-permute-done | bytes 524320 | tf_op jit(solution)/shard_map/ppermute | solution.py:379
  35.6 2.5 %shard_map.70 = (bf16[2,128,256]{2,1,0:T(8,128)(2,1)S(1)}, bf16[2,128,256]{2,1,0:T(8,128)(2,1)S(1)}, bf16[2,128,256]{2,1,0:T(8,128)(2,1)S(1)}, bf16[2,128,256]{2...) custom-call(bf16[2,512,256]{2,1,0:T(8,128)(2,1)S(1)} %get-tuple-element.47.refs_9_.refs_0_, ...), custom_call_target="tpu_custom_call" | custom-call | tf_op jit(solution)/shard_map/pallas_call | solution.py:316
  38.1 2.1 %collective-permute-start.20 = (f32[8,512]{1,0:T(8,128)S(1)}, f32[8,512]{1,0:T(8,128)S(1)}, u32[]{:S(2)}, u32[]{:S(2)}) collective-permute-start(f32[8,512]{1,0:T(8,128)S(1)} %get-tuple-element.66), channel_id=1, source_target_pairs={{8,0},{16,8},{24,16},{9,1},{17,9},{25,17},{10,2},{18,10},{26,18},{... | collective-permute-start | bytes 49160 | tf_op jit(solution)/shard_map/ppermute | solution.py:395
  40.2 1.1 %collective-permute-start.15 = (bf16[2,128,256]{2,1,0:T(8,128)(2,1)S(1)}, bf16[2,128,256]{2,1,0:T(8,128)(2,1)S(1)}, u32[]{:S(2)}, u32[]{:S(2)}) collective-permute-start(bf16[2,128,256]{2,1,0:T(8,128)(2,1)S(1)} %get-tuple-element.62), channel_id=1, source_target_pairs={{0,6},{1,7},{2,4},{3,5},{4,2},{5,3},{6,0},{7,1},{8,14},{9,15},{10,... | collective-permute-start | bytes 393224 | tf_op jit(solution)/shard_map/ppermute | solution.py:347
  41.3 0.3 collective-permute-start.16
  41.6 1.3 %collective-permute-start.17 = (bf16[2,128,256]{2,1,0:T(8,128)(2,1)S(1)}, bf16[2,128,256]{2,1,0:T(8,128)(2,1)S(1)}, u32[]{:S(2)}, u32[]{:S(2)}) collective-permute-start(bf16[2,128,256]{2,1,0:T(8,128)(2,1)S(1)} %get-tuple-element.64), channel_id=1, source_target_pairs={{0,4},{1,5},{2,6},{3,7},{4,0},{5,1},{6,2},{7,3},{8,12},{9,13},{10,... | collective-permute-start | bytes 393224 | tf_op jit(solution)/shard_map/ppermute | solution.py:347
  42.9 0.0 collective-permute-done.19.refs_2_
  42.9 0.0 collective-permute-done.20.refs_5_
  42.9 1.2 %shard_map.72 = (bf16[2,128,256]{2,1,0:T(8,128)(2,1)S(1)}, bf16[2,128,256]{2,1,0:T(8,128)(2,1)S(1)}, bf16[2,128,256]{2,1,0:T(8,128)(2,1)S(1)}, bf16[2,128,256]{2...) custom-call(bf16[2,512,256]{2,1,0:T(8,128)(2,1)S(1)} %get-tuple-elem, ...), custom_call_target="tpu_custom_call" | custom-call | flops 4000000000 | tf_op jit(solution)/shard_map/pallas_call | solution.py:316
  44.2 1.1 %collective-permute-start.21 = (bf16[2,128,256]{2,1,0:T(8,128)(2,1)S(1)}, bf16[2,128,256]{2,1,0:T(8,128)(2,1)S(1)}, u32[]{:S(2)}, u32[]{:S(2)}) collective-permute-start(bf16[2,128,256]{2,1,0:T(8,128)(2,1)S(1)} %get-tuple-element.68), channel_id=1, source_target_pairs={{0,6},{1,7},{2,4},{3,5},{4,2},{5,3},{6,0},{7,1},{8,14},{9,15},{10,... | collective-permute-start | bytes 393224 | tf_op jit(solution)/shard_map/ppermute | solution.py:347
  45.3 0.3 collective-permute-start.22
  45.5 0.1 collective-permute-done.15.refs_1_
  45.6 1.2 %collective-permute-start.23 = (bf16[2,128,256]{2,1,0:T(8,128)(2,1)S(1)}, bf16[2,128,256]{2,1,0:T(8,128)(2,1)S(1)}, u32[]{:S(2)}, u32[]{:S(2)}) collective-permute-start(bf16[2,128,256]{2,1,0:T(8,128)(2,1)S(1)} %get-tuple-element.70), channel_id=1, source_target_pairs={{0,4},{1,5},{2,6},{3,7},{4,0},{5,1},{6,2},{7,3},{8,12},{9,13},{10,... | collective-permute-start | bytes 393224 | tf_op jit(solution)/shard_map/ppermute | solution.py:347
  46.9 0.6 collective-permute-done.16.refs_2_
  47.5 2.8 %collective-permute-done.17.refs_3_ = bf16[2,128,256]{2,1,0:T(8,128)(2,1)S(1)} collective-permute-done((bf16[2,128,256]{2,1,0:T(8,128)(2,1)S(1)}, bf16[2,128,256]{2,1,0:T(8,128)(2,1)S(1)}, u32[]{:S(2)}, u32[]{:S(2)}) %collective-permute-start.17) | collective-permute-done | bytes 131104 | tf_op jit(solution)/shard_map/ppermute | solution.py:347
  50.3 0.8 %collective-permute-start.18 = (bf16[4,128,256]{2,1,0:T(8,128)(2,1)S(1)}, bf16[4,128,256]{2,1,0:T(8,128)(2,1)S(1)}, u32[]{:S(2)}, u32[]{:S(2)}) collective-permute-start(bf16[4,128,256]{2,1,0:T(8,128)(2,1)S(1)} %shard_map.71), channel_id=1, source_target_pairs={{0,1},{1,0},{2,3},{3,2},{4,5},{5,4},{6,7},{7,6},{8,9},{9,8},{10,11... | collective-permute-start | bytes 786440 | tf_op jit(solution)/shard_map/ppermute | solution.py:400
  51.1 2.3 %collective-permute-start.24 = (bf16[2,128,256]{2,1,0:T(8,128)(2,1)S(1)}, bf16[2,128,256]{2,1,0:T(8,128)(2,1)S(1)}, u32[]{:S(2)}, u32[]{:S(2)}) collective-permute-start(bf16[2,128,256]{2,1,0:T(8,128)(2,1)S(1)} %get-tuple-element.71), channel_id=1, source_target_pairs={{0,7},{1,6},{2,5},{3,4},{4,3},{5,2},{6,1},{7,0},{8,15},{9,14},{10,... | collective-permute-start | bytes 393224 | tf_op jit(solution)/shard_map/ppermute | solution.py:347
  53.4 0.0 collective-permute-done.21.refs_6_
  53.4 0.8 %collective-permute-start.25 = (bf16[2,128,256]{2,1,0:T(8,128)(2,1)S(1)}, bf16[2,128,256]{2,1,0:T(8,128)(2,1)S(1)}, u32[]{:S(2)}, u32[]{:S(2)}) collective-permute-start(bf16[2,128,256]{2,1,0:T(8,128)(2,1)S(1)} %get-tuple-element.72), channel_id=1, source_target_pairs={{0,3},{1,2},{2,1},{3,0},{4,7},{5,6},{6,5},{7,4},{8,11},{9,10},{10,... | collective-permute-start | bytes 393224 | tf_op jit(solution)/shard_map/ppermute | solution.py:347
  54.3 0.0 collective-permute-done.22.refs_7_
  54.3 1.7 %collective-permute-start.26 = (bf16[2,128,256]{2,1,0:T(8,128)(2,1)S(1)}, bf16[2,128,256]{2,1,0:T(8,128)(2,1)S(1)}, u32[]{:S(2)}, u32[]{:S(2)}) collective-permute-start(bf16[2,128,256]{2,1,0:T(8,128)(2,1)S(1)} %get-tuple-element.73), channel_id=1, source_target_pairs={{0,5},{1,4},{2,7},{3,6},{4,1},{5,0},{6,3},{7,2},{8,13},{9,12},{10,... | collective-permute-start | bytes 393224 | tf_op jit(solution)/shard_map/ppermute | solution.py:347
  56.0 0.0 collective-permute-done.23.refs_8_
  56.0 0.0 collective-permute-start.27
  56.0 1.9 %collective-permute-done.24.refs_9_ = bf16[2,128,256]{2,1,0:T(8,128)(2,1)S(1)} collective-permute-done((bf16[2,128,256]{2,1,0:T(8,128)(2,1)S(1)}, bf16[2,128,256]{2,1,0:T(8,128)(2,1)S(1)}, u32[]{:S(2)}, u32[]{:S(2)}) %collective-permute-start.24) | collective-permute-done | bytes 131104 | tf_op jit(solution)/shard_map/ppermute | solution.py:347
  57.9 2.7 %collective-permute-done.25.refs_10_ = bf16[2,128,256]{2,1,0:T(8,128)(2,1)S(1)} collective-permute-done((bf16[2,128,256]{2,1,0:T(8,128)(2,1)S(1)}, bf16[2,128,256]{2,1,0:T(8,128)(2,1)S(1)}, u32[]{:S(2)}, u32[]{:S(2)}) %collective-permute-start.25) | collective-permute-done | bytes 131104 | tf_op jit(solution)/shard_map/ppermute | solution.py:347
  60.7 0.0 collective-permute-done.26.refs_11_
  60.7 0.0 collective-permute-done.27.refs_12_
  60.7 0.0 collective-permute-done.18.refs_4_
  60.7 1.3 %shard_map.73 = (bf16[128,2048]{1,0:T(8,128)(2,1)}, bf16[128,2048]{1,0:T(8,128)(2,1)}, bf16[128,2048]{1,0:T(8,128)(2,1)}) custom-call(bf16[2,128,256]{2,1,0:T(8,128)(2,1)S(1)} %get-tuple-element.61.refs_0_, bf16[2,128,256]{2,1,0:T(8,128)(2,1)S(1)} %collective-permute-done.15.refs_1_, bf16[2,128,256]{2,1,0:T(8,128)(2,1)S(1)} %collective-permute-done.16.refs_2_, ...), custom_call_target="tpu_custom_call" | custom-call | tf_op jit(solution)/shard_map/pallas_call | solution.py:316
  (1 shorter events, 0.0 us)
Async XLA Ops:
  2.3 5.8 %collective-permute-start = (bf16[2,128,256]{2,1,0:T(8,128)(2,1)S(1)}, bf16[2,128,256]{2,1,0:T(8,128)(2,1)S(1)}, u32[]{:S(2)}, u32[]{:S(2)}) collective-permute-start(bf16[2,128,256]{2,1,0:T(8,128)(2,1)S(1)} %get-tuple-element.40), channel_id=1, source_target_pairs={{0,6},{1,7},{2,4},{3,5},{4,2},{5,3},{6,0},{7,1},{8,14},{9,15},{10,... | collective-permute-start | bytes 393224 | tf_op jit(solution)/shard_map/ppermute | solution.py:347
  4.5 6.8 %collective-permute-start.1 = (bf16[2,128,256]{2,1,0:T(8,128)(2,1)S(1)}, bf16[2,128,256]{2,1,0:T(8,128)(2,1)S(1)}, u32[]{:S(2)}, u32[]{:S(2)}) collective-permute-start(bf16[2,128,256]{2,1,0:T(8,128)(2,1)S(1)} %get-tuple-element.41), channel_id=1, source_target_pairs={{0,7},{1,6},{2,5},{3,4},{4,3},{5,2},{6,1},{7,0},{8,15},{9,14},{10,... | collective-permute-start | bytes 393224 | tf_op jit(solution)/shard_map/ppermute | solution.py:347
  5.6 8.0 %collective-permute-start.2 = (bf16[2,128,256]{2,1,0:T(8,128)(2,1)S(1)}, bf16[2,128,256]{2,1,0:T(8,128)(2,1)S(1)}, u32[]{:S(2)}, u32[]{:S(2)}) collective-permute-start(bf16[2,128,256]{2,1,0:T(8,128)(2,1)S(1)} %get-tuple-element.42), channel_id=1, source_target_pairs={{0,2},{1,3},{2,0},{3,1},{4,6},{5,7},{6,4},{7,5},{8,10},{9,11},{10,... | collective-permute-start | bytes 393224 | tf_op jit(solution)/shard_map/ppermute | solution.py:347
  6.8 8.1 %collective-permute-start.3 = (bf16[2,128,256]{2,1,0:T(8,128)(2,1)S(1)}, bf16[2,128,256]{2,1,0:T(8,128)(2,1)S(1)}, u32[]{:S(2)}, u32[]{:S(2)}) collective-permute-start(bf16[2,128,256]{2,1,0:T(8,128)(2,1)S(1)} %get-tuple-element.43), channel_id=1, source_target_pairs={{0,4},{1,5},{2,6},{3,7},{4,0},{5,1},{6,2},{7,3},{8,12},{9,13},{10,... | collective-permute-start | bytes 393224 | tf_op jit(solution)/shard_map/ppermute | solution.py:347
  8.0 10.2 %collective-permute-start.4 = (bf16[2,128,256]{2,1,0:T(8,128)(2,1)S(1)}, bf16[2,128,256]{2,1,0:T(8,128)(2,1)S(1)}, u32[]{:S(2)}, u32[]{:S(2)}) collective-permute-start(bf16[2,128,256]{2,1,0:T(8,128)(2,1)S(1)} %get-tuple-element.44), channel_id=1, source_target_pairs={{0,1},{1,0},{2,3},{3,2},{4,5},{5,4},{6,7},{7,6},{8,9},{9,8},{10,11... | collective-permute-start | bytes 393224 | tf_op jit(solution)/shard_map/ppermute | solution.py:347
  8.1 11.7 %collective-permute-start.5 = (bf16[2,128,256]{2,1,0:T(8,128)(2,1)S(1)}, bf16[2,128,256]{2,1,0:T(8,128)(2,1)S(1)}, u32[]{:S(2)}, u32[]{:S(2)}) collective-permute-start(bf16[2,128,256]{2,1,0:T(8,128)(2,1)S(1)} %get-tuple-element.45), channel_id=1, source_target_pairs={{0,3},{1,2},{2,1},{3,0},{4,7},{5,6},{6,5},{7,4},{8,11},{9,10},{10,... | collective-permute-start | bytes 393224 | tf_op jit(solution)/shard_map/ppermute | solution.py:347
  11.3 8.4 %collective-permute-start.6 = (bf16[2,128,256]{2,1,0:T(8,128)(2,1)S(1)}, bf16[2,128,256]{2,1,0:T(8,128)(2,1)S(1)}, u32[]{:S(2)}, u32[]{:S(2)}) collective-permute-start(bf16[2,128,256]{2,1,0:T(8,128)(2,1)S(1)} %get-tuple-element.46), channel_id=1, source_target_pairs={{0,5},{1,4},{2,7},{3,6},{4,1},{5,0},{6,3},{7,2},{8,13},{9,12},{10,... | collective-permute-start | bytes 393224 | tf_op jit(solution)/shard_map/ppermute | solution.py:347
  13.6 9.5 %collective-permute-start.10 = (bf16[2,128,256]{2,1,0:T(8,128)(2,1)S(1)}, bf16[2,128,256]{2,1,0:T(8,128)(2,1)S(1)}, u32[]{:S(2)}, u32[]{:S(2)}) collective-permute-start(bf16[2,128,256]{2,1,0:T(8,128)(2,1)S(1)} %get-tuple-element.52), channel_id=1, source_target_pairs={{0,6},{1,7},{2,4},{3,5},{4,2},{5,3},{6,0},{7,1},{8,14},{9,15},{10,... | collective-permute-start | bytes 393224 | tf_op jit(solution)/shard_map/ppermute | solution.py:347
  14.9 10.3 %collective-permute-start.11 = (bf16[2,128,256]{2,1,0:T(8,128)(2,1)S(1)}, bf16[2,128,256]{2,1,0:T(8,128)(2,1)S(1)}, u32[]{:S(2)}, u32[]{:S(2)}) collective-permute-start(bf16[2,128,256]{2,1,0:T(8,128)(2,1)S(1)} %get-tuple-element.53), channel_id=1, source_target_pairs={{0,7},{1,6},{2,5},{3,4},{4,3},{5,2},{6,1},{7,0},{8,15},{9,14},{10,... | collective-permute-start | bytes 393224 | tf_op jit(solution)/shard_map/ppermute | solution.py:347
  18.2 8.6 %collective-permute-start.12 = (bf16[2,128,256]{2,1,0:T(8,128)(2,1)S(1)}, bf16[2,128,256]{2,1,0:T(8,128)(2,1)S(1)}, u32[]{:S(2)}, u32[]{:S(2)}) collective-permute-start(bf16[2,128,256]{2,1,0:T(8,128)(2,1)S(1)} %get-tuple-element.54), channel_id=1, source_target_pairs={{0,2},{1,3},{2,0},{3,1},{4,6},{5,7},{6,4},{7,5},{8,10},{9,11},{10,... | collective-permute-start | bytes 393224 | tf_op jit(solution)/shard_map/ppermute | solution.py:347
  19.8 7.6 %collective-permute-start.13 = (bf16[2,128,256]{2,1,0:T(8,128)(2,1)S(1)}, bf16[2,128,256]{2,1,0:T(8,128)(2,1)S(1)}, u32[]{:S(2)}, u32[]{:S(2)}) collective-permute-start(bf16[2,128,256]{2,1,0:T(8,128)(2,1)S(1)} %get-tuple-element.55), channel_id=1, source_target_pairs={{0,4},{1,5},{2,6},{3,7},{4,0},{5,1},{6,2},{7,3},{8,12},{9,13},{10,... | collective-permute-start | bytes 393224 | tf_op jit(solution)/shard_map/ppermute | solution.py:347
  19.9 15.7 %collective-permute-start.14 = (bf16[2,512,256]{2,1,0:T(8,128)(2,1)S(1)}, bf16[2,512,256]{2,1,0:T(8,128)(2,1)S(1)}, u32[]{:S(2)}, u32[]{:S(2)}) collective-permute-start(bf16[2,512,256]{2,1,0:T(8,128)(2,1)S(1)} %get-tuple-element.56.refs_8_.refs_3_.refs_1_), channel_id=1, source_target_pairs={{0,8},{8,16},{16,24},{1,9},{9,17},{17,25},{2,10},{10,18},{18,26},{... | collective-permute-start | bytes 1572872 | tf_op jit(solution)/shard_map/ppermute | solution.py:379
  23.1 19.8 %collective-permute-start.19 = (bf16[2,512,256]{2,1,0:T(8,128)(2,1)S(1)}, bf16[2,512,256]{2,1,0:T(8,128)(2,1)S(1)}, u32[]{:S(2)}, u32[]{:S(2)}) collective-permute-start(bf16[2,512,256]{2,1,0:T(8,128)(2,1)S(1)} %get-tuple-element.47.refs_9_.refs_0_), channel_id=1, source_target_pairs={{8,0},{16,8},{24,16},{9,1},{17,9},{25,17},{10,2},{18,10},{26,18},{... | collective-permute-start | bytes 1572872 | tf_op jit(solution)/shard_map/ppermute | solution.py:380
  25.2 5.5 %collective-permute-start.7 = (bf16[2,128,256]{2,1,0:T(8,128)(2,1)S(1)}, bf16[2,128,256]{2,1,0:T(8,128)(2,1)S(1)}, u32[]{:S(2)}, u32[]{:S(2)}) collective-permute-start(bf16[2,128,256]{2,1,0:T(8,128)(2,1)S(1)} %get-tuple-element.49), channel_id=1, source_target_pairs={{0,3},{1,2},{2,1},{3,0},{4,7},{5,6},{6,5},{7,4},{8,11},{9,10},{10,... | collective-permute-start | bytes 393224 | tf_op jit(solution)/shard_map/ppermute | solution.py:347
  26.8 5.2 %collective-permute-start.8 = (bf16[2,128,256]{2,1,0:T(8,128)(2,1)S(1)}, bf16[2,128,256]{2,1,0:T(8,128)(2,1)S(1)}, u32[]{:S(2)}, u32[]{:S(2)}) collective-permute-start(bf16[2,128,256]{2,1,0:T(8,128)(2,1)S(1)} %get-tuple-element.50), channel_id=1, source_target_pairs={{0,5},{1,4},{2,7},{3,6},{4,1},{5,0},{6,3},{7,2},{8,13},{9,12},{10,... | collective-permute-start | bytes 393224 | tf_op jit(solution)/shard_map/ppermute | solution.py:347
  27.4 4.6 %collective-permute-start.9 = (bf16[2,128,256]{2,1,0:T(8,128)(2,1)S(1)}, bf16[2,128,256]{2,1,0:T(8,128)(2,1)S(1)}, u32[]{:S(2)}, u32[]{:S(2)}) collective-permute-start(bf16[2,128,256]{2,1,0:T(8,128)(2,1)S(1)} %get-tuple-element.51), channel_id=1, source_target_pairs={{0,1},{1,0},{2,3},{3,2},{4,5},{5,4},{6,7},{7,6},{8,9},{9,8},{10,11... | collective-permute-start | bytes 393224 | tf_op jit(solution)/shard_map/ppermute | solution.py:347
  38.1 4.8 %collective-permute-start.20 = (f32[8,512]{1,0:T(8,128)S(1)}, f32[8,512]{1,0:T(8,128)S(1)}, u32[]{:S(2)}, u32[]{:S(2)}) collective-permute-start(f32[8,512]{1,0:T(8,128)S(1)} %get-tuple-element.66), channel_id=1, source_target_pairs={{8,0},{16,8},{24,16},{9,1},{17,9},{25,17},{10,2},{18,10},{26,18},{... | collective-permute-start | bytes 49160 | tf_op jit(solution)/shard_map/ppermute | solution.py:395
  40.2 5.5 %collective-permute-start.15 = (bf16[2,128,256]{2,1,0:T(8,128)(2,1)S(1)}, bf16[2,128,256]{2,1,0:T(8,128)(2,1)S(1)}, u32[]{:S(2)}, u32[]{:S(2)}) collective-permute-start(bf16[2,128,256]{2,1,0:T(8,128)(2,1)S(1)} %get-tuple-element.62), channel_id=1, source_target_pairs={{0,6},{1,7},{2,4},{3,5},{4,2},{5,3},{6,0},{7,1},{8,14},{9,15},{10,... | collective-permute-start | bytes 393224 | tf_op jit(solution)/shard_map/ppermute | solution.py:347
  41.3 6.2 %collective-permute-start.16 = (bf16[2,128,256]{2,1,0:T(8,128)(2,1)S(1)}, bf16[2,128,256]{2,1,0:T(8,128)(2,1)S(1)}, u32[]{:S(2)}, u32[]{:S(2)}) collective-permute-start(bf16[2,128,256]{2,1,0:T(8,128)(2,1)S(1)} %get-tuple-element.63), channel_id=1, source_target_pairs={{0,2},{1,3},{2,0},{3,1},{4,6},{5,7},{6,4},{7,5},{8,10},{9,11},{10,... | collective-permute-start | bytes 393224 | tf_op jit(solution)/shard_map/ppermute | solution.py:347
  41.6 8.7 %collective-permute-start.17 = (bf16[2,128,256]{2,1,0:T(8,128)(2,1)S(1)}, bf16[2,128,256]{2,1,0:T(8,128)(2,1)S(1)}, u32[]{:S(2)}, u32[]{:S(2)}) collective-permute-start(bf16[2,128,256]{2,1,0:T(8,128)(2,1)S(1)} %get-tuple-element.64), channel_id=1, source_target_pairs={{0,4},{1,5},{2,6},{3,7},{4,0},{5,1},{6,2},{7,3},{8,12},{9,13},{10,... | collective-permute-start | bytes 393224 | tf_op jit(solution)/shard_map/ppermute | solution.py:347
  44.2 9.3 %collective-permute-start.21 = (bf16[2,128,256]{2,1,0:T(8,128)(2,1)S(1)}, bf16[2,128,256]{2,1,0:T(8,128)(2,1)S(1)}, u32[]{:S(2)}, u32[]{:S(2)}) collective-permute-start(bf16[2,128,256]{2,1,0:T(8,128)(2,1)S(1)} %get-tuple-element.68), channel_id=1, source_target_pairs={{0,6},{1,7},{2,4},{3,5},{4,2},{5,3},{6,0},{7,1},{8,14},{9,15},{10,... | collective-permute-start | bytes 393224 | tf_op jit(solution)/shard_map/ppermute | solution.py:347
  45.3 9.0 %collective-permute-start.22 = (bf16[2,128,256]{2,1,0:T(8,128)(2,1)S(1)}, bf16[2,128,256]{2,1,0:T(8,128)(2,1)S(1)}, u32[]{:S(2)}, u32[]{:S(2)}) collective-permute-start(bf16[2,128,256]{2,1,0:T(8,128)(2,1)S(1)} %get-tuple-element.69), channel_id=1, source_target_pairs={{0,2},{1,3},{2,0},{3,1},{4,6},{5,7},{6,4},{7,5},{8,10},{9,11},{10,... | collective-permute-start | bytes 393224 | tf_op jit(solution)/shard_map/ppermute | solution.py:347
  45.6 10.3 %collective-permute-start.23 = (bf16[2,128,256]{2,1,0:T(8,128)(2,1)S(1)}, bf16[2,128,256]{2,1,0:T(8,128)(2,1)S(1)}, u32[]{:S(2)}, u32[]{:S(2)}) collective-permute-start(bf16[2,128,256]{2,1,0:T(8,128)(2,1)S(1)} %get-tuple-element.70), channel_id=1, source_target_pairs={{0,4},{1,5},{2,6},{3,7},{4,0},{5,1},{6,2},{7,3},{8,12},{9,13},{10,... | collective-permute-start | bytes 393224 | tf_op jit(solution)/shard_map/ppermute | solution.py:347
  50.3 10.3 %collective-permute-start.18 = (bf16[4,128,256]{2,1,0:T(8,128)(2,1)S(1)}, bf16[4,128,256]{2,1,0:T(8,128)(2,1)S(1)}, u32[]{:S(2)}, u32[]{:S(2)}) collective-permute-start(bf16[4,128,256]{2,1,0:T(8,128)(2,1)S(1)} %shard_map.71), channel_id=1, source_target_pairs={{0,1},{1,0},{2,3},{3,2},{4,5},{5,4},{6,7},{7,6},{8,9},{9,8},{10,11... | collective-permute-start | bytes 786440 | tf_op jit(solution)/shard_map/ppermute | solution.py:400
  51.1 6.8 %collective-permute-start.24 = (bf16[2,128,256]{2,1,0:T(8,128)(2,1)S(1)}, bf16[2,128,256]{2,1,0:T(8,128)(2,1)S(1)}, u32[]{:S(2)}, u32[]{:S(2)}) collective-permute-start(bf16[2,128,256]{2,1,0:T(8,128)(2,1)S(1)} %get-tuple-element.71), channel_id=1, source_target_pairs={{0,7},{1,6},{2,5},{3,4},{4,3},{5,2},{6,1},{7,0},{8,15},{9,14},{10,... | collective-permute-start | bytes 393224 | tf_op jit(solution)/shard_map/ppermute | solution.py:347
  53.4 7.2 %collective-permute-start.25 = (bf16[2,128,256]{2,1,0:T(8,128)(2,1)S(1)}, bf16[2,128,256]{2,1,0:T(8,128)(2,1)S(1)}, u32[]{:S(2)}, u32[]{:S(2)}) collective-permute-start(bf16[2,128,256]{2,1,0:T(8,128)(2,1)S(1)} %get-tuple-element.72), channel_id=1, source_target_pairs={{0,3},{1,2},{2,1},{3,0},{4,7},{5,6},{6,5},{7,4},{8,11},{9,10},{10,... | collective-permute-start | bytes 393224 | tf_op jit(solution)/shard_map/ppermute | solution.py:347
  54.3 6.4 %collective-permute-start.26 = (bf16[2,128,256]{2,1,0:T(8,128)(2,1)S(1)}, bf16[2,128,256]{2,1,0:T(8,128)(2,1)S(1)}, u32[]{:S(2)}, u32[]{:S(2)}) collective-permute-start(bf16[2,128,256]{2,1,0:T(8,128)(2,1)S(1)} %get-tuple-element.73), channel_id=1, source_target_pairs={{0,5},{1,4},{2,7},{3,6},{4,1},{5,0},{6,3},{7,2},{8,13},{9,12},{10,... | collective-permute-start | bytes 393224 | tf_op jit(solution)/shard_map/ppermute | solution.py:347
  56.0 4.7 %collective-permute-start.27 = (bf16[2,128,256]{2,1,0:T(8,128)(2,1)S(1)}, bf16[2,128,256]{2,1,0:T(8,128)(2,1)S(1)}, u32[]{:S(2)}, u32[]{:S(2)}) collective-permute-start(bf16[2,128,256]{2,1,0:T(8,128)(2,1)S(1)} %get-tuple-element.74), channel_id=1, source_target_pairs={{0,1},{1,0},{2,3},{3,2},{4,5},{5,4},{6,7},{7,6},{8,9},{9,8},{10,11... | collective-permute-start | bytes 393224 | tf_op jit(solution)/shard_map/ppermute | solution.py:347

commit v6 on v5

--- a/solution.py
+++ b/solution.py
@@ -23,8 +23,8 @@
 NN = ((1,), (0,))
 CRIT_ORDER = (0, 6, 7, 2, 4, 1, 3, 5)
 REST_ORDER = (0, 3, 5, 1, 6, 7, 2, 4)
-DQ_ORDER = (0, 3, 1, 2)
-DKV_ORDER = (0, 6, 2, 4, 7, 3, 5, 1)
+DQ_ORDER = (0, 2, 1, 3)
+DKV_ORDER = (0, 7, 3, 4, 6, 2, 5, 1)
 DEPTH = 2
 EDGE_FLOPS = 4000000000
 LATE_FLOPS = 4000000000
@@ -62,34 +62,32 @@
     return lax.dot_general(a, b, (dims, ((), ())), preferred_element_type=jnp.float32)
 
 
-def pack_kernel(n, *refs):
-    q, g, k, v = refs[:4]
-    crit = refs[4 : 4 + n]
-    rest = refs[4 + n : 4 + 2 * n]
-    stage, sems = refs[4 + 2 * n :]
+def pack_kernel(n, late_pair, early_pair, *refs):
+    out = refs[4 : 4 + n]
+    stage, sems = refs[4 + n :]
     me = group_index()
     width = stage.shape[2] // n
 
-    def run(first, second):
+    def run(pair):
         loads = [
-            pltpu.make_async_copy(source, stage.at[i], sems.at[i])
-            for i, source in enumerate((*first, *second))
+            pltpu.make_async_copy(refs[source], stage.at[t], sems.at[t])
+            for t, source in enumerate(pair)
         ]
         for load in loads:
             load.start()
-        for i, load in enumerate(loads):
+        for t, load in enumerate(loads):
             load.wait()
             for m in range(n):
                 cols = pl.ds(aligned(jnp.bitwise_xor(me, m), width), width)
-                (crit if i < 2 else rest)[m][i % 2] = stage[i, :, cols]
+                out[m][t] = stage[t, :, cols]
 
     @pl.when(me >= n // 2)
     def _():
-        run((k, v), (q, g))
+        run(late_pair)
 
     @pl.when(me < n // 2)
     def _():
-        run((q, g), (k, v))
+        run(early_pair)
 
 
 def place_all(pieces, late, early, me):
@@ -253,8 +251,9 @@
 
 def edge_kernel(n, heads, *refs):
     kv_early, kv_late, qg, front, dkv_in, stat = refs[:6]
-    out = refs[6 : 6 + n]
-    full, acc = refs[6 + n :]
+    refs = refs[6:]
+    out = refs[:n]
+    full, acc = refs[n:]
     me = group_index()
     total = dkv_in.shape[1]
     done = total - WINDOW
@@ -358,13 +357,15 @@
     total = n * rows
     done = total - WINDOW
     piece = bf16(2, rows, width)
-    packed = call(
-        functools.partial(pack_kernel, n),
-        [vmem(piece)] * (2 * n),
-        [vmem(bf16(4, rows, model))], 4,
-        queries, grad_output, key_vectors, value_vectors, space=pltpu.HBM, limit=None,
-    )
-    crit = exchanged(CRIT_ORDER, packed[:n])
+    arguments = (queries, grad_output, key_vectors, value_vectors)
+
+    def packed(late_pair, early_pair):
+        return call(
+            functools.partial(pack_kernel, n, late_pair, early_pair), [vmem(piece)] * n,
+            [vmem(bf16(2, rows, model))], 2, *arguments, space=pltpu.HBM, limit=None,
+        )
+
+    crit = exchanged(CRIT_ORDER, packed((2, 3), (0, 1)))
     half = total // 2
     end = vmem(bf16(2, WINDOW, width))
     halves = vmem(bf16(2, half, width))
@@ -378,7 +379,7 @@
     backward = [(i + 1, i) for i in range(chunks - 1)]
     kv_halo = lax.ppermute(kv_send, "chunk", forward)
     qg_halo = lax.ppermute(qg_send, "chunk", backward)
-    rest = exchanged(REST_ORDER, packed[n:])
+    rest = exchanged(REST_ORDER, packed((0, 1), (2, 3)))
     stat_out = vmem(f32(-(-3 * heads // 8) * 8, WINDOW))
     qg_late, kv_early, dq_late, partial = call(
         functools.partial(late_kernel, n, heads),

time: 62.5 us -> 61.7 us (0.987)
  waiting for transfers between devices: 15.3 us -> 13.1 us
  Pallas kernels: 9.52 us -> 10.5 us
  starting transfers between devices: 36.5 us -> 37.2 us
    ppermute x24, waiting for transfers between devices: 14.3 us -> 12.3 us  [exchanged(): lax.ppermute(pieces[m], GROUP, [(i, i ^ step * m) for i in range(step * n)])]
    ppermute x1, starting transfers between devices: 0.76 us -> 2.75 us  [per_device(): other = lax.ppermute(other, GROUP, [(i, i ^ 1) for i in range(n)])]
    ppermute x24, starting transfers between devices: 28.4 us -> 27.1 us  [exchanged(): lax.ppermute(pieces[m], GROUP, [(i, i ^ step * m) for i in range(step * n)])]
    pallas_call x7 -> x8, Pallas kernels: 9.52 us -> 10.5 us  [call(): pl.pallas_call(kernel, out_shape=outs, in_specs=[held if isinstance(x, tu...]
  transfers between devices with their start and end apart: 28 -> 28, of which waited for: 10 -> 10; matrix products, arithmetic and copies ran while one was open for 0% -> 0% of each run, Pallas kernels for 11% -> 13%
where the time goes in v6:
time: 61.7 us; the launch traced here: 61.5 us
  starting transfers between devices  37.2 us (60%)
  waiting for transfers between devices  13.1 us (21%)
  Pallas kernels  10.5 us (17%)
  between operations  0.75 us (1%)
    ppermute x24, starting transfers between devices, exchanged(): lax.ppermute(pieces[m], GROUP, [(i, i ^ step * m) for i in range(step * n)])  27.1 us
    ppermute x24, waiting for transfers between devices, exchanged(): lax.ppermute(pieces[m], GROUP, [(i, i ^ step * m) for i in range(step * n)])  12.3 us
    pallas_call x8, Pallas kernels, call(): pl.pallas_call(kernel, out_shape=outs, in_specs=[held if isinstance(x, tu...  10.5 us
    ppermute x1, starting transfers between devices, per_device(): kv_halo = lax.ppermute(kv_send, 'chunk', forward)  3.2 us
    ppermute x1, starting transfers between devices, per_device(): other = lax.ppermute(other, GROUP, [(i, i ^ 1) for i in range(n)])  2.75 us
    ppermute x1, starting transfers between devices, per_device(): qg_halo = lax.ppermute(qg_send, 'chunk', backward)  2.1 us
    ppermute x1, starting transfers between devices, per_device(): stat_halo = lax.ppermute(stat, 'chunk', backward)  2.08 us
  transfers between devices with their start and end apart: 28, of which 10 were waited for; matrix products, arithmetic and copies ran while one was open for 0% of the time, Pallas kernels for 13%

profile of v6, /device:TPU:17, one launch (start us, length us, event | category | flops | bytes accessed | tf_op | source)
XLA Modules:
  0.0 61.5 jit_solution(1736314129013344760)
XLA Ops:
  0.6 1.3 %shard_map.67 = (bf16[2,128,256]{2,1,0:T(8,128)(2,1)S(1)}, bf16[2,128,256]{2,1,0:T(8,128)(2,1)S(1)}, bf16[2,128,256]{2,1,0:T(8,128)(2,1)S(1)}, bf16[2,128,256]{2...) custom-call(bf16[128,2048]{1,0:T(8,128)(2,1)} %refs_0_.3, ...), custom_call_target="tpu_custom_call" | custom-call | tf_op jit(solution)/shard_map/pallas_call | solution.py:315
  1.9 2.2 %collective-permute-start = (bf16[2,128,256]{2,1,0:T(8,128)(2,1)S(1)}, bf16[2,128,256]{2,1,0:T(8,128)(2,1)S(1)}, u32[]{:S(2)}, u32[]{:S(2)}) collective-permute-start(bf16[2,128,256]{2,1,0:T(8,128)(2,1)S(1)} %get-tuple-element.40), channel_id=1, source_target_pairs={{0,6},{1,7},{2,4},{3,5},{4,2},{5,3},{6,0},{7,1},{8,14},{9,15},{10,... | collective-permute-start | bytes 393224 | tf_op jit(solution)/shard_map/ppermute | solution.py:346
  4.2 1.0 %collective-permute-start.1 = (bf16[2,128,256]{2,1,0:T(8,128)(2,1)S(1)}, bf16[2,128,256]{2,1,0:T(8,128)(2,1)S(1)}, u32[]{:S(2)}, u32[]{:S(2)}) collective-permute-start(bf16[2,128,256]{2,1,0:T(8,128)(2,1)S(1)} %get-tuple-element.41), channel_id=1, source_target_pairs={{0,7},{1,6},{2,5},{3,4},{4,3},{5,2},{6,1},{7,0},{8,15},{9,14},{10,... | collective-permute-start | bytes 393224 | tf_op jit(solution)/shard_map/ppermute | solution.py:346
  5.2 1.2 %collective-permute-start.2 = (bf16[2,128,256]{2,1,0:T(8,128)(2,1)S(1)}, bf16[2,128,256]{2,1,0:T(8,128)(2,1)S(1)}, u32[]{:S(2)}, u32[]{:S(2)}) collective-permute-start(bf16[2,128,256]{2,1,0:T(8,128)(2,1)S(1)} %get-tuple-element.42), channel_id=1, source_target_pairs={{0,2},{1,3},{2,0},{3,1},{4,6},{5,7},{6,4},{7,5},{8,10},{9,11},{10,... | collective-permute-start | bytes 393224 | tf_op jit(solution)/shard_map/ppermute | solution.py:346
  6.4 1.2 %collective-permute-start.3 = (bf16[2,128,256]{2,1,0:T(8,128)(2,1)S(1)}, bf16[2,128,256]{2,1,0:T(8,128)(2,1)S(1)}, u32[]{:S(2)}, u32[]{:S(2)}) collective-permute-start(bf16[2,128,256]{2,1,0:T(8,128)(2,1)S(1)} %get-tuple-element.43), channel_id=1, source_target_pairs={{0,4},{1,5},{2,6},{3,7},{4,0},{5,1},{6,2},{7,3},{8,12},{9,13},{10,... | collective-permute-start | bytes 393224 | tf_op jit(solution)/shard_map/ppermute | solution.py:346
  7.7 0.1 collective-permute-start.4
  7.8 0.0 collective-permute-done.refs_1_
  7.8 3.0 %collective-permute-start.5 = (bf16[2,128,256]{2,1,0:T(8,128)(2,1)S(1)}, bf16[2,128,256]{2,1,0:T(8,128)(2,1)S(1)}, u32[]{:S(2)}, u32[]{:S(2)}) collective-permute-start(bf16[2,128,256]{2,1,0:T(8,128)(2,1)S(1)} %get-tuple-element.45), channel_id=1, source_target_pairs={{0,3},{1,2},{2,1},{3,0},{4,7},{5,6},{6,5},{7,4},{8,11},{9,10},{10,... | collective-permute-start | bytes 393224 | tf_op jit(solution)/shard_map/ppermute | solution.py:346
  10.8 0.2 collective-permute-done.1.refs_2_
  11.0 1.0 %collective-permute-start.6 = (bf16[2,128,256]{2,1,0:T(8,128)(2,1)S(1)}, bf16[2,128,256]{2,1,0:T(8,128)(2,1)S(1)}, u32[]{:S(2)}, u32[]{:S(2)}) collective-permute-start(bf16[2,128,256]{2,1,0:T(8,128)(2,1)S(1)} %get-tuple-element.46), channel_id=1, source_target_pairs={{0,5},{1,4},{2,7},{3,6},{4,1},{5,0},{6,3},{7,2},{8,13},{9,12},{10,... | collective-permute-start | bytes 393224 | tf_op jit(solution)/shard_map/ppermute | solution.py:346
  12.0 1.3 %shard_map.69 = (bf16[2,128,256]{2,1,0:T(8,128)(2,1)S(1)}, bf16[2,128,256]{2,1,0:T(8,128)(2,1)S(1)}, bf16[2,128,256]{2,1,0:T(8,128)(2,1)S(1)}, bf16[2,128,256]{2...) custom-call(bf16[128,2048]{1,0:T(8,128)(2,1)} %refs_0_.3, ...), custom_call_target="tpu_custom_call" | custom-call | tf_op jit(solution)/shard_map/pallas_call | solution.py:315
  13.3 0.0 collective-permute-done.2.refs_3_
  13.3 2.3 %collective-permute-start.10 = (bf16[2,128,256]{2,1,0:T(8,128)(2,1)S(1)}, bf16[2,128,256]{2,1,0:T(8,128)(2,1)S(1)}, u32[]{:S(2)}, u32[]{:S(2)}) collective-permute-start(bf16[2,128,256]{2,1,0:T(8,128)(2,1)S(1)} %get-tuple-element.52), channel_id=1, source_target_pairs={{0,6},{1,7},{2,4},{3,5},{4,2},{5,3},{6,0},{7,1},{8,14},{9,15},{10,... | collective-permute-start | bytes 393224 | tf_op jit(solution)/shard_map/ppermute | solution.py:346
  15.7 0.0 collective-permute-done.3.refs_4_
  15.7 2.2 %collective-permute-start.11 = (bf16[2,128,256]{2,1,0:T(8,128)(2,1)S(1)}, bf16[2,128,256]{2,1,0:T(8,128)(2,1)S(1)}, u32[]{:S(2)}, u32[]{:S(2)}) collective-permute-start(bf16[2,128,256]{2,1,0:T(8,128)(2,1)S(1)} %get-tuple-element.53), channel_id=1, source_target_pairs={{0,7},{1,6},{2,5},{3,4},{4,3},{5,2},{6,1},{7,0},{8,15},{9,14},{10,... | collective-permute-start | bytes 393224 | tf_op jit(solution)/shard_map/ppermute | solution.py:346
  17.9 0.0 collective-permute-done.4.refs_5_
  17.9 1.6 %collective-permute-start.12 = (bf16[2,128,256]{2,1,0:T(8,128)(2,1)S(1)}, bf16[2,128,256]{2,1,0:T(8,128)(2,1)S(1)}, u32[]{:S(2)}, u32[]{:S(2)}) collective-permute-start(bf16[2,128,256]{2,1,0:T(8,128)(2,1)S(1)} %get-tuple-element.54), channel_id=1, source_target_pairs={{0,2},{1,3},{2,0},{3,1},{4,6},{5,7},{6,4},{7,5},{8,10},{9,11},{10,... | collective-permute-start | bytes 393224 | tf_op jit(solution)/shard_map/ppermute | solution.py:346
  19.4 0.0 collective-permute-done.5.refs_6_
  19.4 0.0 collective-permute-start.13
  19.4 0.0 collective-permute-done.6.refs_7_
  19.4 0.1 shard_map.68
  19.5 3.2 %collective-permute-start.14 = (bf16[2,512,256]{2,1,0:T(8,128)(2,1)S(1)}, bf16[2,512,256]{2,1,0:T(8,128)(2,1)S(1)}, u32[]{:S(2)}, u32[]{:S(2)}) collective-permute-start(bf16[2,512,256]{2,1,0:T(8,128)(2,1)S(1)} %get-tuple-element.56.refs_8_.refs_3_.refs_1_), channel_id=1, source_target_pairs={{0,8},{8,16},{16,24},{1,9},{9,17},{17,25},{2,10},{10,18},{18,26},{... | collective-permute-start | bytes 1572872 | tf_op jit(solution)/shard_map/ppermute | solution.py:380
  22.8 0.0 collective-permute-done.10.refs_4_
  22.8 2.1 %collective-permute-start.19 = (bf16[2,512,256]{2,1,0:T(8,128)(2,1)S(1)}, bf16[2,512,256]{2,1,0:T(8,128)(2,1)S(1)}, u32[]{:S(2)}, u32[]{:S(2)}) collective-permute-start(bf16[2,512,256]{2,1,0:T(8,128)(2,1)S(1)} %get-tuple-element.47.refs_9_.refs_0_), channel_id=1, source_target_pairs={{8,0},{16,8},{24,16},{9,1},{17,9},{25,17},{10,2},{18,10},{26,18},{... | collective-permute-start | bytes 1572872 | tf_op jit(solution)/shard_map/ppermute | solution.py:381
  24.9 0.0 collective-permute-done.11.refs_5_
  24.9 1.5 %collective-permute-start.7 = (bf16[2,128,256]{2,1,0:T(8,128)(2,1)S(1)}, bf16[2,128,256]{2,1,0:T(8,128)(2,1)S(1)}, u32[]{:S(2)}, u32[]{:S(2)}) collective-permute-start(bf16[2,128,256]{2,1,0:T(8,128)(2,1)S(1)} %get-tuple-element.49), channel_id=1, source_target_pairs={{0,3},{1,2},{2,1},{3,0},{4,7},{5,6},{6,5},{7,4},{8,11},{9,10},{10,... | collective-permute-start | bytes 393224 | tf_op jit(solution)/shard_map/ppermute | solution.py:346
  26.4 0.0 collective-permute-done.12.refs_6_
  26.4 0.6 collective-permute-start.8
  27.0 0.0 collective-permute-done.13.refs_7_
  27.0 0.0 collective-permute-start.9
  27.0 3.7 %collective-permute-done.7.refs_1_ = bf16[2,128,256]{2,1,0:T(8,128)(2,1)S(1)} collective-permute-done((bf16[2,128,256]{2,1,0:T(8,128)(2,1)S(1)}, bf16[2,128,256]{2,1,0:T(8,128)(2,1)S(1)}, u32[]{:S(2)}, u32[]{:S(2)}) %collective-permute-start.7) | collective-permute-done | bytes 131104 | tf_op jit(solution)/shard_map/ppermute | solution.py:346
  30.7 0.9 %collective-permute-done.8.refs_2_ = bf16[2,128,256]{2,1,0:T(8,128)(2,1)S(1)} collective-permute-done((bf16[2,128,256]{2,1,0:T(8,128)(2,1)S(1)}, bf16[2,128,256]{2,1,0:T(8,128)(2,1)S(1)}, u32[]{:S(2)}, u32[]{:S(2)}) %collective-permute-start.8) | collective-permute-done | bytes 131104 | tf_op jit(solution)/shard_map/ppermute | solution.py:346
  31.6 0.0 collective-permute-done.9.refs_3_
  31.6 2.7 %shard_map.70 = (bf16[2,512,256]{2,1,0:T(8,128)(2,1)S(1)}, bf16[2,512,256]{2,1,0:T(8,128)(2,1)S(1)}, bf16[512,256]{1,0:T(8,128)(2,1)S(1)}, f32[2,1024,256]{2,1,0:T(8,128)S(1)}) custom-call(bf16[2,128,256]{2,1,0:T(8,128)(2,1)S(1)} %get-tuple-element.48.refs_0_, bf16[2,128,256]{2,1,0:T(8,128)(2,1)S(1)} %collective-permute-done.7.refs_1_, ...), custom_call_target="tpu_custom_call" | custom-call | flops 4000000000 | tf_op jit(solution)/shard_map/pallas_call | solution.py:315
  34.3 0.8 %collective-permute-done.14.refs_4_ = bf16[2,512,256]{2,1,0:T(8,128)(2,1)S(1)} collective-permute-done((bf16[2,512,256]{2,1,0:T(8,128)(2,1)S(1)}, bf16[2,512,256]{2,1,0:T(8,128)(2,1)S(1)}, u32[]{:S(2)}, u32[]{:S(2)}) %collective-permute-start.14) | collective-permute-done | bytes 524320 | tf_op jit(solution)/shard_map/ppermute | solution.py:380
  35.1 2.5 %shard_map.71 = (bf16[2,128,256]{2,1,0:T(8,128)(2,1)S(1)}, bf16[2,128,256]{2,1,0:T(8,128)(2,1)S(1)}, bf16[2,128,256]{2,1,0:T(8,128)(2,1)S(1)}, bf16[2,128,256]{2...) custom-call(bf16[2,512,256]{2,1,0:T(8,128)(2,1)S(1)} %get-tuple-element.47.refs_9_.refs_0_, ...), custom_call_target="tpu_custom_call" | custom-call | tf_op jit(solution)/shard_map/pallas_call | solution.py:315
  37.6 2.1 %collective-permute-start.20 = (f32[8,512]{1,0:T(8,128)S(1)}, f32[8,512]{1,0:T(8,128)S(1)}, u32[]{:S(2)}, u32[]{:S(2)}) collective-permute-start(f32[8,512]{1,0:T(8,128)S(1)} %get-tuple-element.66), channel_id=1, source_target_pairs={{8,0},{16,8},{24,16},{9,1},{17,9},{25,17},{10,2},{18,10},{26,18},{... | collective-permute-start | bytes 49160 | tf_op jit(solution)/shard_map/ppermute | solution.py:396
  39.7 0.5 collective-permute-start.15
  40.2 1.1 %collective-permute-start.16 = (bf16[2,128,256]{2,1,0:T(8,128)(2,1)S(1)}, bf16[2,128,256]{2,1,0:T(8,128)(2,1)S(1)}, u32[]{:S(2)}, u32[]{:S(2)}) collective-permute-start(bf16[2,128,256]{2,1,0:T(8,128)(2,1)S(1)} %get-tuple-element.63), channel_id=1, source_target_pairs={{0,2},{1,3},{2,0},{3,1},{4,6},{5,7},{6,4},{7,5},{8,10},{9,11},{10,... | collective-permute-start | bytes 393224 | tf_op jit(solution)/shard_map/ppermute | solution.py:346
  41.2 1.1 %collective-permute-start.17 = (bf16[2,128,256]{2,1,0:T(8,128)(2,1)S(1)}, bf16[2,128,256]{2,1,0:T(8,128)(2,1)S(1)}, u32[]{:S(2)}, u32[]{:S(2)}) collective-permute-start(bf16[2,128,256]{2,1,0:T(8,128)(2,1)S(1)} %get-tuple-element.64), channel_id=1, source_target_pairs={{0,6},{1,7},{2,4},{3,5},{4,2},{5,3},{6,0},{7,1},{8,14},{9,15},{10,... | collective-permute-start | bytes 393224 | tf_op jit(solution)/shard_map/ppermute | solution.py:346
  42.4 0.0 collective-permute-done.19.refs_2_
  42.4 0.0 collective-permute-done.20.refs_5_
  42.4 1.2 %shard_map.73 = (bf16[2,128,256]{2,1,0:T(8,128)(2,1)S(1)}, bf16[2,128,256]{2,1,0:T(8,128)(2,1)S(1)}, bf16[2,128,256]{2,1,0:T(8,128)(2,1)S(1)}, bf16[2,128,256]{2...) custom-call(bf16[2,512,256]{2,1,0:T(8,128)(2,1)S(1)} %get-tuple-elem, ...), custom_call_target="tpu_custom_call" | custom-call | flops 4000000000 | tf_op jit(solution)/shard_map/pallas_call | solution.py:315
  43.7 2.4 %collective-permute-start.21 = (bf16[2,128,256]{2,1,0:T(8,128)(2,1)S(1)}, bf16[2,128,256]{2,1,0:T(8,128)(2,1)S(1)}, u32[]{:S(2)}, u32[]{:S(2)}) collective-permute-start(bf16[2,128,256]{2,1,0:T(8,128)(2,1)S(1)} %get-tuple-element.68), channel_id=1, source_target_pairs={{0,7},{1,6},{2,5},{3,4},{4,3},{5,2},{6,1},{7,0},{8,15},{9,14},{10,... | collective-permute-start | bytes 393224 | tf_op jit(solution)/shard_map/ppermute | solution.py:346
  46.0 0.0 collective-permute-start.22
  46.0 0.0 collective-permute-done.15.refs_1_
  46.0 0.8 %collective-permute-start.23 = (bf16[2,128,256]{2,1,0:T(8,128)(2,1)S(1)}, bf16[2,128,256]{2,1,0:T(8,128)(2,1)S(1)}, u32[]{:S(2)}, u32[]{:S(2)}) collective-permute-start(bf16[2,128,256]{2,1,0:T(8,128)(2,1)S(1)} %get-tuple-element.70), channel_id=1, source_target_pairs={{0,4},{1,5},{2,6},{3,7},{4,0},{5,1},{6,2},{7,3},{8,12},{9,13},{10,... | collective-permute-start | bytes 393224 | tf_op jit(solution)/shard_map/ppermute | solution.py:346
  46.9 0.0 collective-permute-done.16.refs_2_
  46.9 0.3 collective-permute-done.17.refs_3_
  47.2 2.7 %collective-permute-start.18 = (bf16[4,128,256]{2,1,0:T(8,128)(2,1)S(1)}, bf16[4,128,256]{2,1,0:T(8,128)(2,1)S(1)}, u32[]{:S(2)}, u32[]{:S(2)}) collective-permute-start(bf16[4,128,256]{2,1,0:T(8,128)(2,1)S(1)} %shard_map.72), channel_id=1, source_target_pairs={{0,1},{1,0},{2,3},{3,2},{4,5},{5,4},{6,7},{7,6},{8,9},{9,8},{10,11... | collective-permute-start | bytes 786440 | tf_op jit(solution)/shard_map/ppermute | solution.py:401
  50.0 1.9 %collective-permute-start.24 = (bf16[2,128,256]{2,1,0:T(8,128)(2,1)S(1)}, bf16[2,128,256]{2,1,0:T(8,128)(2,1)S(1)}, u32[]{:S(2)}, u32[]{:S(2)}) collective-permute-start(bf16[2,128,256]{2,1,0:T(8,128)(2,1)S(1)} %get-tuple-element.71), channel_id=1, source_target_pairs={{0,6},{1,7},{2,4},{3,5},{4,2},{5,3},{6,0},{7,1},{8,14},{9,15},{10,... | collective-permute-start | bytes 393224 | tf_op jit(solution)/shard_map/ppermute | solution.py:346
  51.8 0.1 collective-permute-done.21.refs_6_
  51.9 0.3 collective-permute-start.25
  52.2 2.5 %collective-permute-done.22.refs_7_ = bf16[2,128,256]{2,1,0:T(8,128)(2,1)S(1)} collective-permute-done((bf16[2,128,256]{2,1,0:T(8,128)(2,1)S(1)}, bf16[2,128,256]{2,1,0:T(8,128)(2,1)S(1)}, u32[]{:S(2)}, u32[]{:S(2)}) %collective-permute-start.22) | collective-permute-done | bytes 131104 | tf_op jit(solution)/shard_map/ppermute | solution.py:346
  54.8 0.5 collective-permute-start.26
  55.3 0.0 collective-permute-done.23.refs_8_
  55.3 0.5 collective-permute-start.27
  55.7 1.8 %collective-permute-done.24.refs_9_ = bf16[2,128,256]{2,1,0:T(8,128)(2,1)S(1)} collective-permute-done((bf16[2,128,256]{2,1,0:T(8,128)(2,1)S(1)}, bf16[2,128,256]{2,1,0:T(8,128)(2,1)S(1)}, u32[]{:S(2)}, u32[]{:S(2)}) %collective-permute-start.24) | collective-permute-done | bytes 131104 | tf_op jit(solution)/shard_map/ppermute | solution.py:346
  57.5 1.7 %collective-permute-done.25.refs_10_ = bf16[2,128,256]{2,1,0:T(8,128)(2,1)S(1)} collective-permute-done((bf16[2,128,256]{2,1,0:T(8,128)(2,1)S(1)}, bf16[2,128,256]{2,1,0:T(8,128)(2,1)S(1)}, u32[]{:S(2)}, u32[]{:S(2)}) %collective-permute-start.25) | collective-permute-done | bytes 131104 | tf_op jit(solution)/shard_map/ppermute | solution.py:346
  59.2 1.0 %collective-permute-done.26.refs_11_ = bf16[2,128,256]{2,1,0:T(8,128)(2,1)S(1)} collective-permute-done((bf16[2,128,256]{2,1,0:T(8,128)(2,1)S(1)}, bf16[2,128,256]{2,1,0:T(8,128)(2,1)S(1)}, u32[]{:S(2)}, u32[]{:S(2)}) %collective-permute-start.26) | collective-permute-done | bytes 131104 | tf_op jit(solution)/shard_map/ppermute | solution.py:346
  60.2 0.0 collective-permute-done.27.refs_12_
  60.2 0.0 collective-permute-done.18.refs_4_
  60.2 1.3 %shard_map.74 = (bf16[128,2048]{1,0:T(8,128)(2,1)}, bf16[128,2048]{1,0:T(8,128)(2,1)}, bf16[128,2048]{1,0:T(8,128)(2,1)}) custom-call(bf16[2,128,256]{2,1,0:T(8,128)(2,1)S(1)} %get-tuple-element.61.refs_0_, bf16[2,128,256]{2,1,0:T(8,128)(2,1)S(1)} %collective-permute-done.15.refs_1_, bf16[2,128,256]{2,1,0:T(8,128)(2,1)S(1)} %collective-permute-done.16.refs_2_, ...), custom_call_target="tpu_custom_call" | custom-call | tf_op jit(solution)/shard_map/pallas_call | solution.py:315
  (1 shorter events, 0.0 us)
Async XLA Ops:
  1.9 5.8 %collective-permute-start = (bf16[2,128,256]{2,1,0:T(8,128)(2,1)S(1)}, bf16[2,128,256]{2,1,0:T(8,128)(2,1)S(1)}, u32[]{:S(2)}, u32[]{:S(2)}) collective-permute-start(bf16[2,128,256]{2,1,0:T(8,128)(2,1)S(1)} %get-tuple-element.40), channel_id=1, source_target_pairs={{0,6},{1,7},{2,4},{3,5},{4,2},{5,3},{6,0},{7,1},{8,14},{9,15},{10,... | collective-permute-start | bytes 393224 | tf_op jit(solution)/shard_map/ppermute | solution.py:346
  4.2 6.8 %collective-permute-start.1 = (bf16[2,128,256]{2,1,0:T(8,128)(2,1)S(1)}, bf16[2,128,256]{2,1,0:T(8,128)(2,1)S(1)}, u32[]{:S(2)}, u32[]{:S(2)}) collective-permute-start(bf16[2,128,256]{2,1,0:T(8,128)(2,1)S(1)} %get-tuple-element.41), channel_id=1, source_target_pairs={{0,7},{1,6},{2,5},{3,4},{4,3},{5,2},{6,1},{7,0},{8,15},{9,14},{10,... | collective-permute-start | bytes 393224 | tf_op jit(solution)/shard_map/ppermute | solution.py:346
  5.2 8.1 %collective-permute-start.2 = (bf16[2,128,256]{2,1,0:T(8,128)(2,1)S(1)}, bf16[2,128,256]{2,1,0:T(8,128)(2,1)S(1)}, u32[]{:S(2)}, u32[]{:S(2)}) collective-permute-start(bf16[2,128,256]{2,1,0:T(8,128)(2,1)S(1)} %get-tuple-element.42), channel_id=1, source_target_pairs={{0,2},{1,3},{2,0},{3,1},{4,6},{5,7},{6,4},{7,5},{8,10},{9,11},{10,... | collective-permute-start | bytes 393224 | tf_op jit(solution)/shard_map/ppermute | solution.py:346
  6.4 9.2 %collective-permute-start.3 = (bf16[2,128,256]{2,1,0:T(8,128)(2,1)S(1)}, bf16[2,128,256]{2,1,0:T(8,128)(2,1)S(1)}, u32[]{:S(2)}, u32[]{:S(2)}) collective-permute-start(bf16[2,128,256]{2,1,0:T(8,128)(2,1)S(1)} %get-tuple-element.43), channel_id=1, source_target_pairs={{0,4},{1,5},{2,6},{3,7},{4,0},{5,1},{6,2},{7,3},{8,12},{9,13},{10,... | collective-permute-start | bytes 393224 | tf_op jit(solution)/shard_map/ppermute | solution.py:346
  7.7 10.2 %collective-permute-start.4 = (bf16[2,128,256]{2,1,0:T(8,128)(2,1)S(1)}, bf16[2,128,256]{2,1,0:T(8,128)(2,1)S(1)}, u32[]{:S(2)}, u32[]{:S(2)}) collective-permute-start(bf16[2,128,256]{2,1,0:T(8,128)(2,1)S(1)} %get-tuple-element.44), channel_id=1, source_target_pairs={{0,1},{1,0},{2,3},{3,2},{4,5},{5,4},{6,7},{7,6},{8,9},{9,8},{10,11... | collective-permute-start | bytes 393224 | tf_op jit(solution)/shard_map/ppermute | solution.py:346
  7.8 11.7 %collective-permute-start.5 = (bf16[2,128,256]{2,1,0:T(8,128)(2,1)S(1)}, bf16[2,128,256]{2,1,0:T(8,128)(2,1)S(1)}, u32[]{:S(2)}, u32[]{:S(2)}) collective-permute-start(bf16[2,128,256]{2,1,0:T(8,128)(2,1)S(1)} %get-tuple-element.45), channel_id=1, source_target_pairs={{0,3},{1,2},{2,1},{3,0},{4,7},{5,6},{6,5},{7,4},{8,11},{9,10},{10,... | collective-permute-start | bytes 393224 | tf_op jit(solution)/shard_map/ppermute | solution.py:346
  11.0 8.4 %collective-permute-start.6 = (bf16[2,128,256]{2,1,0:T(8,128)(2,1)S(1)}, bf16[2,128,256]{2,1,0:T(8,128)(2,1)S(1)}, u32[]{:S(2)}, u32[]{:S(2)}) collective-permute-start(bf16[2,128,256]{2,1,0:T(8,128)(2,1)S(1)} %get-tuple-element.46), channel_id=1, source_target_pairs={{0,5},{1,4},{2,7},{3,6},{4,1},{5,0},{6,3},{7,2},{8,13},{9,12},{10,... | collective-permute-start | bytes 393224 | tf_op jit(solution)/shard_map/ppermute | solution.py:346
  13.3 9.4 %collective-permute-start.10 = (bf16[2,128,256]{2,1,0:T(8,128)(2,1)S(1)}, bf16[2,128,256]{2,1,0:T(8,128)(2,1)S(1)}, u32[]{:S(2)}, u32[]{:S(2)}) collective-permute-start(bf16[2,128,256]{2,1,0:T(8,128)(2,1)S(1)} %get-tuple-element.52), channel_id=1, source_target_pairs={{0,6},{1,7},{2,4},{3,5},{4,2},{5,3},{6,0},{7,1},{8,14},{9,15},{10,... | collective-permute-start | bytes 393224 | tf_op jit(solution)/shard_map/ppermute | solution.py:346
  15.7 9.2 %collective-permute-start.11 = (bf16[2,128,256]{2,1,0:T(8,128)(2,1)S(1)}, bf16[2,128,256]{2,1,0:T(8,128)(2,1)S(1)}, u32[]{:S(2)}, u32[]{:S(2)}) collective-permute-start(bf16[2,128,256]{2,1,0:T(8,128)(2,1)S(1)} %get-tuple-element.53), channel_id=1, source_target_pairs={{0,7},{1,6},{2,5},{3,4},{4,3},{5,2},{6,1},{7,0},{8,15},{9,14},{10,... | collective-permute-start | bytes 393224 | tf_op jit(solution)/shard_map/ppermute | solution.py:346
  17.9 8.6 %collective-permute-start.12 = (bf16[2,128,256]{2,1,0:T(8,128)(2,1)S(1)}, bf16[2,128,256]{2,1,0:T(8,128)(2,1)S(1)}, u32[]{:S(2)}, u32[]{:S(2)}) collective-permute-start(bf16[2,128,256]{2,1,0:T(8,128)(2,1)S(1)} %get-tuple-element.54), channel_id=1, source_target_pairs={{0,2},{1,3},{2,0},{3,1},{4,6},{5,7},{6,4},{7,5},{8,10},{9,11},{10,... | collective-permute-start | bytes 393224 | tf_op jit(solution)/shard_map/ppermute | solution.py:346
  19.4 7.6 %collective-permute-start.13 = (bf16[2,128,256]{2,1,0:T(8,128)(2,1)S(1)}, bf16[2,128,256]{2,1,0:T(8,128)(2,1)S(1)}, u32[]{:S(2)}, u32[]{:S(2)}) collective-permute-start(bf16[2,128,256]{2,1,0:T(8,128)(2,1)S(1)} %get-tuple-element.55), channel_id=1, source_target_pairs={{0,4},{1,5},{2,6},{3,7},{4,0},{5,1},{6,2},{7,3},{8,12},{9,13},{10,... | collective-permute-start | bytes 393224 | tf_op jit(solution)/shard_map/ppermute | solution.py:346
  19.5 15.6 %collective-permute-start.14 = (bf16[2,512,256]{2,1,0:T(8,128)(2,1)S(1)}, bf16[2,512,256]{2,1,0:T(8,128)(2,1)S(1)}, u32[]{:S(2)}, u32[]{:S(2)}) collective-permute-start(bf16[2,512,256]{2,1,0:T(8,128)(2,1)S(1)} %get-tuple-element.56.refs_8_.refs_3_.refs_1_), channel_id=1, source_target_pairs={{0,8},{8,16},{16,24},{1,9},{9,17},{17,25},{2,10},{10,18},{18,26},{... | collective-permute-start | bytes 1572872 | tf_op jit(solution)/shard_map/ppermute | solution.py:380
  22.8 19.6 %collective-permute-start.19 = (bf16[2,512,256]{2,1,0:T(8,128)(2,1)S(1)}, bf16[2,512,256]{2,1,0:T(8,128)(2,1)S(1)}, u32[]{:S(2)}, u32[]{:S(2)}) collective-permute-start(bf16[2,512,256]{2,1,0:T(8,128)(2,1)S(1)} %get-tuple-element.47.refs_9_.refs_0_), channel_id=1, source_target_pairs={{8,0},{16,8},{24,16},{9,1},{17,9},{25,17},{10,2},{18,10},{26,18},{... | collective-permute-start | bytes 1572872 | tf_op jit(solution)/shard_map/ppermute | solution.py:381
  24.9 5.8 %collective-permute-start.7 = (bf16[2,128,256]{2,1,0:T(8,128)(2,1)S(1)}, bf16[2,128,256]{2,1,0:T(8,128)(2,1)S(1)}, u32[]{:S(2)}, u32[]{:S(2)}) collective-permute-start(bf16[2,128,256]{2,1,0:T(8,128)(2,1)S(1)} %get-tuple-element.49), channel_id=1, source_target_pairs={{0,3},{1,2},{2,1},{3,0},{4,7},{5,6},{6,5},{7,4},{8,11},{9,10},{10,... | collective-permute-start | bytes 393224 | tf_op jit(solution)/shard_map/ppermute | solution.py:346
  26.4 5.2 %collective-permute-start.8 = (bf16[2,128,256]{2,1,0:T(8,128)(2,1)S(1)}, bf16[2,128,256]{2,1,0:T(8,128)(2,1)S(1)}, u32[]{:S(2)}, u32[]{:S(2)}) collective-permute-start(bf16[2,128,256]{2,1,0:T(8,128)(2,1)S(1)} %get-tuple-element.50), channel_id=1, source_target_pairs={{0,5},{1,4},{2,7},{3,6},{4,1},{5,0},{6,3},{7,2},{8,13},{9,12},{10,... | collective-permute-start | bytes 393224 | tf_op jit(solution)/shard_map/ppermute | solution.py:346
  27.0 4.6 %collective-permute-start.9 = (bf16[2,128,256]{2,1,0:T(8,128)(2,1)S(1)}, bf16[2,128,256]{2,1,0:T(8,128)(2,1)S(1)}, u32[]{:S(2)}, u32[]{:S(2)}) collective-permute-start(bf16[2,128,256]{2,1,0:T(8,128)(2,1)S(1)} %get-tuple-element.51), channel_id=1, source_target_pairs={{0,1},{1,0},{2,3},{3,2},{4,5},{5,4},{6,7},{7,6},{8,9},{9,8},{10,11... | collective-permute-start | bytes 393224 | tf_op jit(solution)/shard_map/ppermute | solution.py:346
  37.6 4.8 %collective-permute-start.20 = (f32[8,512]{1,0:T(8,128)S(1)}, f32[8,512]{1,0:T(8,128)S(1)}, u32[]{:S(2)}, u32[]{:S(2)}) collective-permute-start(f32[8,512]{1,0:T(8,128)S(1)} %get-tuple-element.66), channel_id=1, source_target_pairs={{8,0},{16,8},{24,16},{9,1},{17,9},{25,17},{10,2},{18,10},{26,18},{... | collective-permute-start | bytes 49160 | tf_op jit(solution)/shard_map/ppermute | solution.py:396
  39.7 6.3 %collective-permute-start.15 = (bf16[2,128,256]{2,1,0:T(8,128)(2,1)S(1)}, bf16[2,128,256]{2,1,0:T(8,128)(2,1)S(1)}, u32[]{:S(2)}, u32[]{:S(2)}) collective-permute-start(bf16[2,128,256]{2,1,0:T(8,128)(2,1)S(1)} %get-tuple-element.62), channel_id=1, source_target_pairs={{0,4},{1,5},{2,6},{3,7},{4,0},{5,1},{6,2},{7,3},{8,12},{9,13},{10,... | collective-permute-start | bytes 393224 | tf_op jit(solution)/shard_map/ppermute | solution.py:346
  40.2 6.7 %collective-permute-start.16 = (bf16[2,128,256]{2,1,0:T(8,128)(2,1)S(1)}, bf16[2,128,256]{2,1,0:T(8,128)(2,1)S(1)}, u32[]{:S(2)}, u32[]{:S(2)}) collective-permute-start(bf16[2,128,256]{2,1,0:T(8,128)(2,1)S(1)} %get-tuple-element.63), channel_id=1, source_target_pairs={{0,2},{1,3},{2,0},{3,1},{4,6},{5,7},{6,4},{7,5},{8,10},{9,11},{10,... | collective-permute-start | bytes 393224 | tf_op jit(solution)/shard_map/ppermute | solution.py:346
  41.2 6.0 %collective-permute-start.17 = (bf16[2,128,256]{2,1,0:T(8,128)(2,1)S(1)}, bf16[2,128,256]{2,1,0:T(8,128)(2,1)S(1)}, u32[]{:S(2)}, u32[]{:S(2)}) collective-permute-start(bf16[2,128,256]{2,1,0:T(8,128)(2,1)S(1)} %get-tuple-element.64), channel_id=1, source_target_pairs={{0,6},{1,7},{2,4},{3,5},{4,2},{5,3},{6,0},{7,1},{8,14},{9,15},{10,... | collective-permute-start | bytes 393224 | tf_op jit(solution)/shard_map/ppermute | solution.py:346
  43.7 8.3 %collective-permute-start.21 = (bf16[2,128,256]{2,1,0:T(8,128)(2,1)S(1)}, bf16[2,128,256]{2,1,0:T(8,128)(2,1)S(1)}, u32[]{:S(2)}, u32[]{:S(2)}) collective-permute-start(bf16[2,128,256]{2,1,0:T(8,128)(2,1)S(1)} %get-tuple-element.68), channel_id=1, source_target_pairs={{0,7},{1,6},{2,5},{3,4},{4,3},{5,2},{6,1},{7,0},{8,15},{9,14},{10,... | collective-permute-start | bytes 393224 | tf_op jit(solution)/shard_map/ppermute | solution.py:346
  46.0 8.8 %collective-permute-start.22 = (bf16[2,128,256]{2,1,0:T(8,128)(2,1)S(1)}, bf16[2,128,256]{2,1,0:T(8,128)(2,1)S(1)}, u32[]{:S(2)}, u32[]{:S(2)}) collective-permute-start(bf16[2,128,256]{2,1,0:T(8,128)(2,1)S(1)} %get-tuple-element.69), channel_id=1, source_target_pairs={{0,3},{1,2},{2,1},{3,0},{4,7},{5,6},{6,5},{7,4},{8,11},{9,10},{10,... | collective-permute-start | bytes 393224 | tf_op jit(solution)/shard_map/ppermute | solution.py:346
  46.0 9.2 %collective-permute-start.23 = (bf16[2,128,256]{2,1,0:T(8,128)(2,1)S(1)}, bf16[2,128,256]{2,1,0:T(8,128)(2,1)S(1)}, u32[]{:S(2)}, u32[]{:S(2)}) collective-permute-start(bf16[2,128,256]{2,1,0:T(8,128)(2,1)S(1)} %get-tuple-element.70), channel_id=1, source_target_pairs={{0,4},{1,5},{2,6},{3,7},{4,0},{5,1},{6,2},{7,3},{8,12},{9,13},{10,... | collective-permute-start | bytes 393224 | tf_op jit(solution)/shard_map/ppermute | solution.py:346
  47.2 13.0 %collective-permute-start.18 = (bf16[4,128,256]{2,1,0:T(8,128)(2,1)S(1)}, bf16[4,128,256]{2,1,0:T(8,128)(2,1)S(1)}, u32[]{:S(2)}, u32[]{:S(2)}) collective-permute-start(bf16[4,128,256]{2,1,0:T(8,128)(2,1)S(1)} %shard_map.72), channel_id=1, source_target_pairs={{0,1},{1,0},{2,3},{3,2},{4,5},{5,4},{6,7},{7,6},{8,9},{9,8},{10,11... | collective-permute-start | bytes 786440 | tf_op jit(solution)/shard_map/ppermute | solution.py:401
  50.0 7.5 %collective-permute-start.24 = (bf16[2,128,256]{2,1,0:T(8,128)(2,1)S(1)}, bf16[2,128,256]{2,1,0:T(8,128)(2,1)S(1)}, u32[]{:S(2)}, u32[]{:S(2)}) collective-permute-start(bf16[2,128,256]{2,1,0:T(8,128)(2,1)S(1)} %get-tuple-element.71), channel_id=1, source_target_pairs={{0,6},{1,7},{2,4},{3,5},{4,2},{5,3},{6,0},{7,1},{8,14},{9,15},{10,... | collective-permute-start | bytes 393224 | tf_op jit(solution)/shard_map/ppermute | solution.py:346
  51.9 7.2 %collective-permute-start.25 = (bf16[2,128,256]{2,1,0:T(8,128)(2,1)S(1)}, bf16[2,128,256]{2,1,0:T(8,128)(2,1)S(1)}, u32[]{:S(2)}, u32[]{:S(2)}) collective-permute-start(bf16[2,128,256]{2,1,0:T(8,128)(2,1)S(1)} %get-tuple-element.72), channel_id=1, source_target_pairs={{0,2},{1,3},{2,0},{3,1},{4,6},{5,7},{6,4},{7,5},{8,10},{9,11},{10,... | collective-permute-start | bytes 393224 | tf_op jit(solution)/shard_map/ppermute | solution.py:346
  54.8 5.4 %collective-permute-start.26 = (bf16[2,128,256]{2,1,0:T(8,128)(2,1)S(1)}, bf16[2,128,256]{2,1,0:T(8,128)(2,1)S(1)}, u32[]{:S(2)}, u32[]{:S(2)}) collective-permute-start(bf16[2,128,256]{2,1,0:T(8,128)(2,1)S(1)} %get-tuple-element.73), channel_id=1, source_target_pairs={{0,5},{1,4},{2,7},{3,6},{4,1},{5,0},{6,3},{7,2},{8,13},{9,12},{10,... | collective-permute-start | bytes 393224 | tf_op jit(solution)/shard_map/ppermute | solution.py:346
  55.3 4.9 %collective-permute-start.27 = (bf16[2,128,256]{2,1,0:T(8,128)(2,1)S(1)}, bf16[2,128,256]{2,1,0:T(8,128)(2,1)S(1)}, u32[]{:S(2)}, u32[]{:S(2)}) collective-permute-start(bf16[2,128,256]{2,1,0:T(8,128)(2,1)S(1)} %get-tuple-element.74), channel_id=1, source_target_pairs={{0,1},{1,0},{2,3},{3,2},{4,5},{5,4},{6,7},{7,6},{8,9},{9,8},{10,11... | collective-permute-start | bytes 393224 | tf_op jit(solution)/shard_map/ppermute | solution.py:346

commit v7 on v6

--- a/solution.py
+++ b/solution.py
@@ -188,7 +188,7 @@
         mine = slice(start + WINDOW, start + WINDOW + TILE)
         qb, gb = (load(qg, t, start + WINDOW, start + WINDOW + TILE, lanes) for t in range(2))
         dq[slice(start, start + TILE), lanes] = (
-            (dot(key_ts[h][:, keys], ds, NN) * SCALE).T.astype(jnp.bfloat16)
+            (dot(key_ts[h][:, keys], ds, NN) * SCALE).astype(jnp.bfloat16).T
         )
         for t, add in enumerate((dot(ds, qb, NN), dot(p_low, gb, NN))):
             if start == 0:
@@ -236,7 +236,7 @@
         keys = slice(start, start + 3 * TILE)
         qb, gb = (load(qg, t, start, start + TILE, lanes) for t in range(2))
         dq[slice(start, start + TILE), lanes] = (
-            (dot(key_ts[h][:, keys], ds, NN) * SCALE).T.astype(jnp.bfloat16)
+            (dot(key_ts[h][:, keys], ds, NN) * SCALE).astype(jnp.bfloat16).T
         )
         own = slice(0, start + TILE)
         acc[0, own, lanes] += dot(ds[WINDOW - start :], qb, NN)
@@ -262,22 +262,29 @@
     row = lax.broadcasted_iota(jnp.int32, (TILE, TILE), 0)
     col = lax.broadcasted_iota(jnp.int32, (TILE, TILE), 1)
     acc[...] = dkv_in[:, WINDOW:]
-    for h in range(heads):
-        lanes = slice(h * HEAD_DIM, (h + 1) * HEAD_DIM)
-        for start in range(0, WINDOW, TILE):
-            mine = slice(start, start + TILE)
-            qb, gb = qg[0, mine, lanes], qg[1, mine, lanes]
-            kb, vb = (load(kv, t, done + start, total, lanes) for t in range(2))
-            s = dot(kb, qb, NT)
-            newest = jnp.where(row > col, s[:TILE], MASKED)
-            s = newest if len(s) == TILE else jnp.concatenate([newest, s[TILE:]], axis=0)
-            top, inverse, dots = (stat[3 * h + k : 3 * h + k + 1, mine] for k in range(3))
-            p = jnp.exp2(s * SCALE_LOG2 - top) * inverse
-            dp = dot(vb, gb, NT)
-            ds = (p * (dp - dots)).astype(jnp.bfloat16)
-            at = slice(done - WINDOW + start, done)
-            acc[0, at, lanes] += dot(ds, qb, NN)
-            acc[1, at, lanes] += dot(p.astype(jnp.bfloat16), gb, NN)
+    blocks = [(h, start) for h in range(heads) for start in range(0, WINDOW, TILE)]
+    lanes_of = [slice(h * HEAD_DIM, (h + 1) * HEAD_DIM) for h in range(heads)]
+
+    def products(h, start):
+        mine = slice(start, start + TILE)
+        kb, vb = (load(kv, t, done + start, total, lanes_of[h]) for t in range(2))
+        return dot(kb, qg[0, mine, lanes_of[h]], NT), dot(vb, qg[1, mine, lanes_of[h]], NT)
+
+    def probabilities(h, start, s, dp):
+        mine = slice(start, start + TILE)
+        newest = jnp.where(row > col, s[:TILE], MASKED)
+        s = newest if len(s) == TILE else jnp.concatenate([newest, s[TILE:]], axis=0)
+        top, inverse, dots = (stat[3 * h + k : 3 * h + k + 1, mine] for k in range(3))
+        p = jnp.exp2(s * SCALE_LOG2 - top) * inverse
+        return p.astype(jnp.bfloat16), (p * (dp - dots)).astype(jnp.bfloat16)
+
+    def gradients(h, start, p_low, ds):
+        mine = slice(start, start + TILE)
+        at = slice(done - WINDOW + start, done)
+        acc[0, at, lanes_of[h]] += dot(ds, qg[0, mine, lanes_of[h]], NN)
+        acc[1, at, lanes_of[h]] += dot(p_low, qg[1, mine, lanes_of[h]], NN)
+
+    staged(blocks, products, probabilities, gradients)
     full[:, :WINDOW] = front[...]
     full[0, WINDOW:] = (acc[0] * SCALE).astype(jnp.bfloat16)
     full[1, WINDOW:] = acc[1].astype(jnp.bfloat16)

time: 61.7 us -> 61.8 us (level)
  transfers between devices with their start and end apart: 28 -> 28, of which waited for: 10 -> 11; matrix products, arithmetic and copies ran while one was open for 0% -> 0% of each run, Pallas kernels for 13% -> 12%
where the time goes in v7:
time: 61.8 us; the launch traced here: 61.5 us
  starting transfers between devices  37.8 us (61%)
  waiting for transfers between devices  12.7 us (21%)
  Pallas kernels  10.3 us (17%)
  between operations  0.76 us (1%)
    ppermute x24, starting transfers between devices, exchanged(): lax.ppermute(pieces[m], GROUP, [(i, i ^ step * m) for i in range(step * n)])  27.5 us
    ppermute x24, waiting for transfers between devices, exchanged(): lax.ppermute(pieces[m], GROUP, [(i, i ^ step * m) for i in range(step * n)])  11.9 us
    pallas_call x8, Pallas kernels, call(): pl.pallas_call(kernel, out_shape=outs, in_specs=[held if isinstance(x, tu...  10.3 us
    ppermute x1, starting transfers between devices, per_device(): kv_halo = lax.ppermute(kv_send, 'chunk', forward)  3.2 us
    ppermute x1, starting transfers between devices, per_device(): other = lax.ppermute(other, GROUP, [(i, i ^ 1) for i in range(n)])  2.93 us
    ppermute x1, starting transfers between devices, per_device(): qg_halo = lax.ppermute(qg_send, 'chunk', backward)  2.1 us
    ppermute x1, starting transfers between devices, per_device(): stat_halo = lax.ppermute(stat, 'chunk', backward)  2.08 us
  transfers between devices with their start and end apart: 28, of which 11 were waited for; matrix products, arithmetic and copies ran while one was open for 0% of the time, Pallas kernels for 12%

profile of v7, /device:TPU:17, one launch (start us, length us, event | category | flops | bytes accessed | tf_op | source)
XLA Modules:
  0.0 61.5 jit_solution(13197066949670208244)
XLA Ops:
  0.6 1.3 %shard_map.67 = (bf16[2,128,256]{2,1,0:T(8,128)(2,1)S(1)}, bf16[2,128,256]{2,1,0:T(8,128)(2,1)S(1)}, bf16[2,128,256]{2,1,0:T(8,128)(2,1)S(1)}, bf16[2,128,256]{2...) custom-call(bf16[128,2048]{1,0:T(8,128)(2,1)} %refs_0_.3, ...), custom_call_target="tpu_custom_call" | custom-call | tf_op jit(solution)/shard_map/pallas_call | solution.py:322
  1.9 2.2 %collective-permute-start = (bf16[2,128,256]{2,1,0:T(8,128)(2,1)S(1)}, bf16[2,128,256]{2,1,0:T(8,128)(2,1)S(1)}, u32[]{:S(2)}, u32[]{:S(2)}) collective-permute-start(bf16[2,128,256]{2,1,0:T(8,128)(2,1)S(1)} %get-tuple-element.40), channel_id=1, source_target_pairs={{0,6},{1,7},{2,4},{3,5},{4,2},{5,3},{6,0},{7,1},{8,14},{9,15},{10,... | collective-permute-start | bytes 393224 | tf_op jit(solution)/shard_map/ppermute | solution.py:353
  4.2 1.0 %collective-permute-start.1 = (bf16[2,128,256]{2,1,0:T(8,128)(2,1)S(1)}, bf16[2,128,256]{2,1,0:T(8,128)(2,1)S(1)}, u32[]{:S(2)}, u32[]{:S(2)}) collective-permute-start(bf16[2,128,256]{2,1,0:T(8,128)(2,1)S(1)} %get-tuple-element.41), channel_id=1, source_target_pairs={{0,7},{1,6},{2,5},{3,4},{4,3},{5,2},{6,1},{7,0},{8,15},{9,14},{10,... | collective-permute-start | bytes 393224 | tf_op jit(solution)/shard_map/ppermute | solution.py:353
  5.2 1.2 %collective-permute-start.2 = (bf16[2,128,256]{2,1,0:T(8,128)(2,1)S(1)}, bf16[2,128,256]{2,1,0:T(8,128)(2,1)S(1)}, u32[]{:S(2)}, u32[]{:S(2)}) collective-permute-start(bf16[2,128,256]{2,1,0:T(8,128)(2,1)S(1)} %get-tuple-element.42), channel_id=1, source_target_pairs={{0,2},{1,3},{2,0},{3,1},{4,6},{5,7},{6,4},{7,5},{8,10},{9,11},{10,... | collective-permute-start | bytes 393224 | tf_op jit(solution)/shard_map/ppermute | solution.py:353
  6.4 1.2 %collective-permute-start.3 = (bf16[2,128,256]{2,1,0:T(8,128)(2,1)S(1)}, bf16[2,128,256]{2,1,0:T(8,128)(2,1)S(1)}, u32[]{:S(2)}, u32[]{:S(2)}) collective-permute-start(bf16[2,128,256]{2,1,0:T(8,128)(2,1)S(1)} %get-tuple-element.43), channel_id=1, source_target_pairs={{0,4},{1,5},{2,6},{3,7},{4,0},{5,1},{6,2},{7,3},{8,12},{9,13},{10,... | collective-permute-start | bytes 393224 | tf_op jit(solution)/shard_map/ppermute | solution.py:353
  7.7 0.1 collective-permute-start.4
  7.8 0.0 collective-permute-done.refs_1_
  7.8 3.0 %collective-permute-start.5 = (bf16[2,128,256]{2,1,0:T(8,128)(2,1)S(1)}, bf16[2,128,256]{2,1,0:T(8,128)(2,1)S(1)}, u32[]{:S(2)}, u32[]{:S(2)}) collective-permute-start(bf16[2,128,256]{2,1,0:T(8,128)(2,1)S(1)} %get-tuple-element.45), channel_id=1, source_target_pairs={{0,3},{1,2},{2,1},{3,0},{4,7},{5,6},{6,5},{7,4},{8,11},{9,10},{10,... | collective-permute-start | bytes 393224 | tf_op jit(solution)/shard_map/ppermute | solution.py:353
  10.8 0.2 collective-permute-done.1.refs_2_
  11.0 1.0 %collective-permute-start.6 = (bf16[2,128,256]{2,1,0:T(8,128)(2,1)S(1)}, bf16[2,128,256]{2,1,0:T(8,128)(2,1)S(1)}, u32[]{:S(2)}, u32[]{:S(2)}) collective-permute-start(bf16[2,128,256]{2,1,0:T(8,128)(2,1)S(1)} %get-tuple-element.46), channel_id=1, source_target_pairs={{0,5},{1,4},{2,7},{3,6},{4,1},{5,0},{6,3},{7,2},{8,13},{9,12},{10,... | collective-permute-start | bytes 393224 | tf_op jit(solution)/shard_map/ppermute | solution.py:353
  12.0 1.3 %shard_map.69 = (bf16[2,128,256]{2,1,0:T(8,128)(2,1)S(1)}, bf16[2,128,256]{2,1,0:T(8,128)(2,1)S(1)}, bf16[2,128,256]{2,1,0:T(8,128)(2,1)S(1)}, bf16[2,128,256]{2...) custom-call(bf16[128,2048]{1,0:T(8,128)(2,1)} %refs_0_.3, ...), custom_call_target="tpu_custom_call" | custom-call | tf_op jit(solution)/shard_map/pallas_call | solution.py:322
  13.3 0.0 collective-permute-done.2.refs_3_
  13.3 2.3 %collective-permute-start.10 = (bf16[2,128,256]{2,1,0:T(8,128)(2,1)S(1)}, bf16[2,128,256]{2,1,0:T(8,128)(2,1)S(1)}, u32[]{:S(2)}, u32[]{:S(2)}) collective-permute-start(bf16[2,128,256]{2,1,0:T(8,128)(2,1)S(1)} %get-tuple-element.52), channel_id=1, source_target_pairs={{0,6},{1,7},{2,4},{3,5},{4,2},{5,3},{6,0},{7,1},{8,14},{9,15},{10,... | collective-permute-start | bytes 393224 | tf_op jit(solution)/shard_map/ppermute | solution.py:353
  15.7 0.0 collective-permute-done.3.refs_4_
  15.7 2.2 %collective-permute-start.11 = (bf16[2,128,256]{2,1,0:T(8,128)(2,1)S(1)}, bf16[2,128,256]{2,1,0:T(8,128)(2,1)S(1)}, u32[]{:S(2)}, u32[]{:S(2)}) collective-permute-start(bf16[2,128,256]{2,1,0:T(8,128)(2,1)S(1)} %get-tuple-element.53), channel_id=1, source_target_pairs={{0,7},{1,6},{2,5},{3,4},{4,3},{5,2},{6,1},{7,0},{8,15},{9,14},{10,... | collective-permute-start | bytes 393224 | tf_op jit(solution)/shard_map/ppermute | solution.py:353
  17.9 0.0 collective-permute-done.4.refs_5_
  17.9 1.6 %collective-permute-start.12 = (bf16[2,128,256]{2,1,0:T(8,128)(2,1)S(1)}, bf16[2,128,256]{2,1,0:T(8,128)(2,1)S(1)}, u32[]{:S(2)}, u32[]{:S(2)}) collective-permute-start(bf16[2,128,256]{2,1,0:T(8,128)(2,1)S(1)} %get-tuple-element.54), channel_id=1, source_target_pairs={{0,2},{1,3},{2,0},{3,1},{4,6},{5,7},{6,4},{7,5},{8,10},{9,11},{10,... | collective-permute-start | bytes 393224 | tf_op jit(solution)/shard_map/ppermute | solution.py:353
  19.4 0.0 collective-permute-done.5.refs_6_
  19.4 0.0 collective-permute-start.13
  19.4 0.0 collective-permute-done.6.refs_7_
  19.4 0.1 shard_map.68
  19.5 3.2 %collective-permute-start.14 = (bf16[2,512,256]{2,1,0:T(8,128)(2,1)S(1)}, bf16[2,512,256]{2,1,0:T(8,128)(2,1)S(1)}, u32[]{:S(2)}, u32[]{:S(2)}) collective-permute-start(bf16[2,512,256]{2,1,0:T(8,128)(2,1)S(1)} %get-tuple-element.56.refs_8_.refs_3_.refs_1_), channel_id=1, source_target_pairs={{0,8},{8,16},{16,24},{1,9},{9,17},{17,25},{2,10},{10,18},{18,26},{... | collective-permute-start | bytes 1572872 | tf_op jit(solution)/shard_map/ppermute | solution.py:387
  22.8 0.0 collective-permute-done.10.refs_4_
  22.8 2.1 %collective-permute-start.19 = (bf16[2,512,256]{2,1,0:T(8,128)(2,1)S(1)}, bf16[2,512,256]{2,1,0:T(8,128)(2,1)S(1)}, u32[]{:S(2)}, u32[]{:S(2)}) collective-permute-start(bf16[2,512,256]{2,1,0:T(8,128)(2,1)S(1)} %get-tuple-element.47.refs_9_.refs_0_), channel_id=1, source_target_pairs={{8,0},{16,8},{24,16},{9,1},{17,9},{25,17},{10,2},{18,10},{26,18},{... | collective-permute-start | bytes 1572872 | tf_op jit(solution)/shard_map/ppermute | solution.py:388
  24.9 0.0 collective-permute-done.11.refs_5_
  24.9 1.5 %collective-permute-start.7 = (bf16[2,128,256]{2,1,0:T(8,128)(2,1)S(1)}, bf16[2,128,256]{2,1,0:T(8,128)(2,1)S(1)}, u32[]{:S(2)}, u32[]{:S(2)}) collective-permute-start(bf16[2,128,256]{2,1,0:T(8,128)(2,1)S(1)} %get-tuple-element.49), channel_id=1, source_target_pairs={{0,3},{1,2},{2,1},{3,0},{4,7},{5,6},{6,5},{7,4},{8,11},{9,10},{10,... | collective-permute-start | bytes 393224 | tf_op jit(solution)/shard_map/ppermute | solution.py:353
  26.4 0.0 collective-permute-done.12.refs_6_
  26.4 0.6 collective-permute-start.8
  27.0 0.0 collective-permute-done.13.refs_7_
  27.0 0.0 collective-permute-start.9
  27.0 3.7 %collective-permute-done.7.refs_1_ = bf16[2,128,256]{2,1,0:T(8,128)(2,1)S(1)} collective-permute-done((bf16[2,128,256]{2,1,0:T(8,128)(2,1)S(1)}, bf16[2,128,256]{2,1,0:T(8,128)(2,1)S(1)}, u32[]{:S(2)}, u32[]{:S(2)}) %collective-permute-start.7) | collective-permute-done | bytes 131104 | tf_op jit(solution)/shard_map/ppermute | solution.py:353
  30.7 0.9 %collective-permute-done.8.refs_2_ = bf16[2,128,256]{2,1,0:T(8,128)(2,1)S(1)} collective-permute-done((bf16[2,128,256]{2,1,0:T(8,128)(2,1)S(1)}, bf16[2,128,256]{2,1,0:T(8,128)(2,1)S(1)}, u32[]{:S(2)}, u32[]{:S(2)}) %collective-permute-start.8) | collective-permute-done | bytes 131104 | tf_op jit(solution)/shard_map/ppermute | solution.py:353
  31.6 0.0 collective-permute-done.9.refs_3_
  31.6 2.7 %shard_map.70 = (bf16[2,512,256]{2,1,0:T(8,128)(2,1)S(1)}, bf16[2,512,256]{2,1,0:T(8,128)(2,1)S(1)}, bf16[512,256]{1,0:T(8,128)(2,1)S(1)}, f32[2,1024,256]{2,1,0:T(8,128)S(1)}) custom-call(bf16[2,128,256]{2,1,0:T(8,128)(2,1)S(1)} %get-tuple-element.48.refs_0_, bf16[2,128,256]{2,1,0:T(8,128)(2,1)S(1)} %collective-permute-done.7.refs_1_, ...), custom_call_target="tpu_custom_call" | custom-call | flops 4000000000 | tf_op jit(solution)/shard_map/pallas_call | solution.py:322
  34.3 0.8 %collective-permute-done.14.refs_4_ = bf16[2,512,256]{2,1,0:T(8,128)(2,1)S(1)} collective-permute-done((bf16[2,512,256]{2,1,0:T(8,128)(2,1)S(1)}, bf16[2,512,256]{2,1,0:T(8,128)(2,1)S(1)}, u32[]{:S(2)}, u32[]{:S(2)}) %collective-permute-start.14) | collective-permute-done | bytes 524320 | tf_op jit(solution)/shard_map/ppermute | solution.py:387
  35.1 2.5 %shard_map.71 = (bf16[2,128,256]{2,1,0:T(8,128)(2,1)S(1)}, bf16[2,128,256]{2,1,0:T(8,128)(2,1)S(1)}, bf16[2,128,256]{2,1,0:T(8,128)(2,1)S(1)}, bf16[2,128,256]{2...) custom-call(bf16[2,512,256]{2,1,0:T(8,128)(2,1)S(1)} %get-tuple-element.47.refs_9_.refs_0_, ...), custom_call_target="tpu_custom_call" | custom-call | tf_op jit(solution)/shard_map/pallas_call | solution.py:322
  37.6 2.1 %collective-permute-start.20 = (f32[8,512]{1,0:T(8,128)S(1)}, f32[8,512]{1,0:T(8,128)S(1)}, u32[]{:S(2)}, u32[]{:S(2)}) collective-permute-start(f32[8,512]{1,0:T(8,128)S(1)} %get-tuple-element.66), channel_id=1, source_target_pairs={{8,0},{16,8},{24,16},{9,1},{17,9},{25,17},{10,2},{18,10},{26,18},{... | collective-permute-start | bytes 49160 | tf_op jit(solution)/shard_map/ppermute | solution.py:403
  39.7 0.5 collective-permute-start.15
  40.2 1.1 %collective-permute-start.16 = (bf16[2,128,256]{2,1,0:T(8,128)(2,1)S(1)}, bf16[2,128,256]{2,1,0:T(8,128)(2,1)S(1)}, u32[]{:S(2)}, u32[]{:S(2)}) collective-permute-start(bf16[2,128,256]{2,1,0:T(8,128)(2,1)S(1)} %get-tuple-element.63), channel_id=1, source_target_pairs={{0,2},{1,3},{2,0},{3,1},{4,6},{5,7},{6,4},{7,5},{8,10},{9,11},{10,... | collective-permute-start | bytes 393224 | tf_op jit(solution)/shard_map/ppermute | solution.py:353
  41.2 1.1 %collective-permute-start.17 = (bf16[2,128,256]{2,1,0:T(8,128)(2,1)S(1)}, bf16[2,128,256]{2,1,0:T(8,128)(2,1)S(1)}, u32[]{:S(2)}, u32[]{:S(2)}) collective-permute-start(bf16[2,128,256]{2,1,0:T(8,128)(2,1)S(1)} %get-tuple-element.64), channel_id=1, source_target_pairs={{0,6},{1,7},{2,4},{3,5},{4,2},{5,3},{6,0},{7,1},{8,14},{9,15},{10,... | collective-permute-start | bytes 393224 | tf_op jit(solution)/shard_map/ppermute | solution.py:353
  42.4 0.0 collective-permute-done.19.refs_2_
  42.4 0.0 collective-permute-done.20.refs_5_
  42.4 1.1 %shard_map.73 = (bf16[2,128,256]{2,1,0:T(8,128)(2,1)S(1)}, bf16[2,128,256]{2,1,0:T(8,128)(2,1)S(1)}, bf16[2,128,256]{2,1,0:T(8,128)(2,1)S(1)}, bf16[2,128,256]{2...) custom-call(bf16[2,512,256]{2,1,0:T(8,128)(2,1)S(1)} %get-tuple-elem, ...), custom_call_target="tpu_custom_call" | custom-call | flops 4000000000 | tf_op jit(solution)/shard_map/pallas_call | solution.py:322
  43.5 2.4 %collective-permute-start.21 = (bf16[2,128,256]{2,1,0:T(8,128)(2,1)S(1)}, bf16[2,128,256]{2,1,0:T(8,128)(2,1)S(1)}, u32[]{:S(2)}, u32[]{:S(2)}) collective-permute-start(bf16[2,128,256]{2,1,0:T(8,128)(2,1)S(1)} %get-tuple-element.68), channel_id=1, source_target_pairs={{0,7},{1,6},{2,5},{3,4},{4,3},{5,2},{6,1},{7,0},{8,15},{9,14},{10,... | collective-permute-start | bytes 393224 | tf_op jit(solution)/shard_map/ppermute | solution.py:353
  45.8 0.0 collective-permute-start.22
  45.8 0.0 collective-permute-done.15.refs_1_
  45.8 0.8 %collective-permute-start.23 = (bf16[2,128,256]{2,1,0:T(8,128)(2,1)S(1)}, bf16[2,128,256]{2,1,0:T(8,128)(2,1)S(1)}, u32[]{:S(2)}, u32[]{:S(2)}) collective-permute-start(bf16[2,128,256]{2,1,0:T(8,128)(2,1)S(1)} %get-tuple-element.70), channel_id=1, source_target_pairs={{0,4},{1,5},{2,6},{3,7},{4,0},{5,1},{6,2},{7,3},{8,12},{9,13},{10,... | collective-permute-start | bytes 393224 | tf_op jit(solution)/shard_map/ppermute | solution.py:353
  46.7 0.0 collective-permute-done.16.refs_2_
  46.7 0.5 collective-permute-done.17.refs_3_
  47.2 2.9 %collective-permute-start.18 = (bf16[4,128,256]{2,1,0:T(8,128)(2,1)S(1)}, bf16[4,128,256]{2,1,0:T(8,128)(2,1)S(1)}, u32[]{:S(2)}, u32[]{:S(2)}) collective-permute-start(bf16[4,128,256]{2,1,0:T(8,128)(2,1)S(1)} %shard_map.72), channel_id=1, source_target_pairs={{0,1},{1,0},{2,3},{3,2},{4,5},{5,4},{6,7},{7,6},{8,9},{9,8},{10,11... | collective-permute-start | bytes 786440 | tf_op jit(solution)/shard_map/ppermute | solution.py:408
  50.1 1.9 %collective-permute-start.24 = (bf16[2,128,256]{2,1,0:T(8,128)(2,1)S(1)}, bf16[2,128,256]{2,1,0:T(8,128)(2,1)S(1)}, u32[]{:S(2)}, u32[]{:S(2)}) collective-permute-start(bf16[2,128,256]{2,1,0:T(8,128)(2,1)S(1)} %get-tuple-element.71), channel_id=1, source_target_pairs={{0,6},{1,7},{2,4},{3,5},{4,2},{5,3},{6,0},{7,1},{8,14},{9,15},{10,... | collective-permute-start | bytes 393224 | tf_op jit(solution)/shard_map/ppermute | solution.py:353
  52.0 0.1 collective-permute-done.21.refs_6_
  52.1 0.3 collective-permute-start.25
  52.4 2.2 %collective-permute-done.22.refs_7_ = bf16[2,128,256]{2,1,0:T(8,128)(2,1)S(1)} collective-permute-done((bf16[2,128,256]{2,1,0:T(8,128)(2,1)S(1)}, bf16[2,128,256]{2,1,0:T(8,128)(2,1)S(1)}, u32[]{:S(2)}, u32[]{:S(2)}) %collective-permute-start.22) | collective-permute-done | bytes 131104 | tf_op jit(solution)/shard_map/ppermute | solution.py:353
  54.6 0.5 collective-permute-start.26
  55.1 0.1 collective-permute-done.23.refs_8_
  55.1 0.8 %collective-permute-start.27 = (bf16[2,128,256]{2,1,0:T(8,128)(2,1)S(1)}, bf16[2,128,256]{2,1,0:T(8,128)(2,1)S(1)}, u32[]{:S(2)}, u32[]{:S(2)}) collective-permute-start(bf16[2,128,256]{2,1,0:T(8,128)(2,1)S(1)} %get-tuple-element.74), channel_id=1, source_target_pairs={{0,1},{1,0},{2,3},{3,2},{4,5},{5,4},{6,7},{7,6},{8,9},{9,8},{10,11... | collective-permute-start | bytes 393224 | tf_op jit(solution)/shard_map/ppermute | solution.py:353
  55.9 1.4 %collective-permute-done.24.refs_9_ = bf16[2,128,256]{2,1,0:T(8,128)(2,1)S(1)} collective-permute-done((bf16[2,128,256]{2,1,0:T(8,128)(2,1)S(1)}, bf16[2,128,256]{2,1,0:T(8,128)(2,1)S(1)}, u32[]{:S(2)}, u32[]{:S(2)}) %collective-permute-start.24) | collective-permute-done | bytes 131104 | tf_op jit(solution)/shard_map/ppermute | solution.py:353
  57.3 2.0 %collective-permute-done.25.refs_10_ = bf16[2,128,256]{2,1,0:T(8,128)(2,1)S(1)} collective-permute-done((bf16[2,128,256]{2,1,0:T(8,128)(2,1)S(1)}, bf16[2,128,256]{2,1,0:T(8,128)(2,1)S(1)}, u32[]{:S(2)}, u32[]{:S(2)}) %collective-permute-start.25) | collective-permute-done | bytes 131104 | tf_op jit(solution)/shard_map/ppermute | solution.py:353
  59.4 0.9 %collective-permute-done.26.refs_11_ = bf16[2,128,256]{2,1,0:T(8,128)(2,1)S(1)} collective-permute-done((bf16[2,128,256]{2,1,0:T(8,128)(2,1)S(1)}, bf16[2,128,256]{2,1,0:T(8,128)(2,1)S(1)}, u32[]{:S(2)}, u32[]{:S(2)}) %collective-permute-start.26) | collective-permute-done | bytes 131104 | tf_op jit(solution)/shard_map/ppermute | solution.py:353
  60.2 0.0 collective-permute-done.27.refs_12_
  60.2 0.0 collective-permute-done.18.refs_4_
  60.2 1.3 %shard_map.74 = (bf16[128,2048]{1,0:T(8,128)(2,1)}, bf16[128,2048]{1,0:T(8,128)(2,1)}, bf16[128,2048]{1,0:T(8,128)(2,1)}) custom-call(bf16[2,128,256]{2,1,0:T(8,128)(2,1)S(1)} %get-tuple-element.61.refs_0_, bf16[2,128,256]{2,1,0:T(8,128)(2,1)S(1)} %collective-permute-done.15.refs_1_, bf16[2,128,256]{2,1,0:T(8,128)(2,1)S(1)} %collective-permute-done.16.refs_2_, ...), custom_call_target="tpu_custom_call" | custom-call | tf_op jit(solution)/shard_map/pallas_call | solution.py:322
  (1 shorter events, 0.0 us)
Async XLA Ops:
  1.9 5.8 %collective-permute-start = (bf16[2,128,256]{2,1,0:T(8,128)(2,1)S(1)}, bf16[2,128,256]{2,1,0:T(8,128)(2,1)S(1)}, u32[]{:S(2)}, u32[]{:S(2)}) collective-permute-start(bf16[2,128,256]{2,1,0:T(8,128)(2,1)S(1)} %get-tuple-element.40), channel_id=1, source_target_pairs={{0,6},{1,7},{2,4},{3,5},{4,2},{5,3},{6,0},{7,1},{8,14},{9,15},{10,... | collective-permute-start | bytes 393224 | tf_op jit(solution)/shard_map/ppermute | solution.py:353
  4.2 6.8 %collective-permute-start.1 = (bf16[2,128,256]{2,1,0:T(8,128)(2,1)S(1)}, bf16[2,128,256]{2,1,0:T(8,128)(2,1)S(1)}, u32[]{:S(2)}, u32[]{:S(2)}) collective-permute-start(bf16[2,128,256]{2,1,0:T(8,128)(2,1)S(1)} %get-tuple-element.41), channel_id=1, source_target_pairs={{0,7},{1,6},{2,5},{3,4},{4,3},{5,2},{6,1},{7,0},{8,15},{9,14},{10,... | collective-permute-start | bytes 393224 | tf_op jit(solution)/shard_map/ppermute | solution.py:353
  5.2 8.1 %collective-permute-start.2 = (bf16[2,128,256]{2,1,0:T(8,128)(2,1)S(1)}, bf16[2,128,256]{2,1,0:T(8,128)(2,1)S(1)}, u32[]{:S(2)}, u32[]{:S(2)}) collective-permute-start(bf16[2,128,256]{2,1,0:T(8,128)(2,1)S(1)} %get-tuple-element.42), channel_id=1, source_target_pairs={{0,2},{1,3},{2,0},{3,1},{4,6},{5,7},{6,4},{7,5},{8,10},{9,11},{10,... | collective-permute-start | bytes 393224 | tf_op jit(solution)/shard_map/ppermute | solution.py:353
  6.4 9.2 %collective-permute-start.3 = (bf16[2,128,256]{2,1,0:T(8,128)(2,1)S(1)}, bf16[2,128,256]{2,1,0:T(8,128)(2,1)S(1)}, u32[]{:S(2)}, u32[]{:S(2)}) collective-permute-start(bf16[2,128,256]{2,1,0:T(8,128)(2,1)S(1)} %get-tuple-element.43), channel_id=1, source_target_pairs={{0,4},{1,5},{2,6},{3,7},{4,0},{5,1},{6,2},{7,3},{8,12},{9,13},{10,... | collective-permute-start | bytes 393224 | tf_op jit(solution)/shard_map/ppermute | solution.py:353
  7.7 10.2 %collective-permute-start.4 = (bf16[2,128,256]{2,1,0:T(8,128)(2,1)S(1)}, bf16[2,128,256]{2,1,0:T(8,128)(2,1)S(1)}, u32[]{:S(2)}, u32[]{:S(2)}) collective-permute-start(bf16[2,128,256]{2,1,0:T(8,128)(2,1)S(1)} %get-tuple-element.44), channel_id=1, source_target_pairs={{0,1},{1,0},{2,3},{3,2},{4,5},{5,4},{6,7},{7,6},{8,9},{9,8},{10,11... | collective-permute-start | bytes 393224 | tf_op jit(solution)/shard_map/ppermute | solution.py:353
  7.8 11.7 %collective-permute-start.5 = (bf16[2,128,256]{2,1,0:T(8,128)(2,1)S(1)}, bf16[2,128,256]{2,1,0:T(8,128)(2,1)S(1)}, u32[]{:S(2)}, u32[]{:S(2)}) collective-permute-start(bf16[2,128,256]{2,1,0:T(8,128)(2,1)S(1)} %get-tuple-element.45), channel_id=1, source_target_pairs={{0,3},{1,2},{2,1},{3,0},{4,7},{5,6},{6,5},{7,4},{8,11},{9,10},{10,... | collective-permute-start | bytes 393224 | tf_op jit(solution)/shard_map/ppermute | solution.py:353
  11.0 8.4 %collective-permute-start.6 = (bf16[2,128,256]{2,1,0:T(8,128)(2,1)S(1)}, bf16[2,128,256]{2,1,0:T(8,128)(2,1)S(1)}, u32[]{:S(2)}, u32[]{:S(2)}) collective-permute-start(bf16[2,128,256]{2,1,0:T(8,128)(2,1)S(1)} %get-tuple-element.46), channel_id=1, source_target_pairs={{0,5},{1,4},{2,7},{3,6},{4,1},{5,0},{6,3},{7,2},{8,13},{9,12},{10,... | collective-permute-start | bytes 393224 | tf_op jit(solution)/shard_map/ppermute | solution.py:353
  13.3 9.4 %collective-permute-start.10 = (bf16[2,128,256]{2,1,0:T(8,128)(2,1)S(1)}, bf16[2,128,256]{2,1,0:T(8,128)(2,1)S(1)}, u32[]{:S(2)}, u32[]{:S(2)}) collective-permute-start(bf16[2,128,256]{2,1,0:T(8,128)(2,1)S(1)} %get-tuple-element.52), channel_id=1, source_target_pairs={{0,6},{1,7},{2,4},{3,5},{4,2},{5,3},{6,0},{7,1},{8,14},{9,15},{10,... | collective-permute-start | bytes 393224 | tf_op jit(solution)/shard_map/ppermute | solution.py:353
  15.7 9.2 %collective-permute-start.11 = (bf16[2,128,256]{2,1,0:T(8,128)(2,1)S(1)}, bf16[2,128,256]{2,1,0:T(8,128)(2,1)S(1)}, u32[]{:S(2)}, u32[]{:S(2)}) collective-permute-start(bf16[2,128,256]{2,1,0:T(8,128)(2,1)S(1)} %get-tuple-element.53), channel_id=1, source_target_pairs={{0,7},{1,6},{2,5},{3,4},{4,3},{5,2},{6,1},{7,0},{8,15},{9,14},{10,... | collective-permute-start | bytes 393224 | tf_op jit(solution)/shard_map/ppermute | solution.py:353
  17.9 8.6 %collective-permute-start.12 = (bf16[2,128,256]{2,1,0:T(8,128)(2,1)S(1)}, bf16[2,128,256]{2,1,0:T(8,128)(2,1)S(1)}, u32[]{:S(2)}, u32[]{:S(2)}) collective-permute-start(bf16[2,128,256]{2,1,0:T(8,128)(2,1)S(1)} %get-tuple-element.54), channel_id=1, source_target_pairs={{0,2},{1,3},{2,0},{3,1},{4,6},{5,7},{6,4},{7,5},{8,10},{9,11},{10,... | collective-permute-start | bytes 393224 | tf_op jit(solution)/shard_map/ppermute | solution.py:353
  19.4 7.6 %collective-permute-start.13 = (bf16[2,128,256]{2,1,0:T(8,128)(2,1)S(1)}, bf16[2,128,256]{2,1,0:T(8,128)(2,1)S(1)}, u32[]{:S(2)}, u32[]{:S(2)}) collective-permute-start(bf16[2,128,256]{2,1,0:T(8,128)(2,1)S(1)} %get-tuple-element.55), channel_id=1, source_target_pairs={{0,4},{1,5},{2,6},{3,7},{4,0},{5,1},{6,2},{7,3},{8,12},{9,13},{10,... | collective-permute-start | bytes 393224 | tf_op jit(solution)/shard_map/ppermute | solution.py:353
  19.5 15.6 %collective-permute-start.14 = (bf16[2,512,256]{2,1,0:T(8,128)(2,1)S(1)}, bf16[2,512,256]{2,1,0:T(8,128)(2,1)S(1)}, u32[]{:S(2)}, u32[]{:S(2)}) collective-permute-start(bf16[2,512,256]{2,1,0:T(8,128)(2,1)S(1)} %get-tuple-element.56.refs_8_.refs_3_.refs_1_), channel_id=1, source_target_pairs={{0,8},{8,16},{16,24},{1,9},{9,17},{17,25},{2,10},{10,18},{18,26},{... | collective-permute-start | bytes 1572872 | tf_op jit(solution)/shard_map/ppermute | solution.py:387
  22.8 19.6 %collective-permute-start.19 = (bf16[2,512,256]{2,1,0:T(8,128)(2,1)S(1)}, bf16[2,512,256]{2,1,0:T(8,128)(2,1)S(1)}, u32[]{:S(2)}, u32[]{:S(2)}) collective-permute-start(bf16[2,512,256]{2,1,0:T(8,128)(2,1)S(1)} %get-tuple-element.47.refs_9_.refs_0_), channel_id=1, source_target_pairs={{8,0},{16,8},{24,16},{9,1},{17,9},{25,17},{10,2},{18,10},{26,18},{... | collective-permute-start | bytes 1572872 | tf_op jit(solution)/shard_map/ppermute | solution.py:388
  24.9 5.8 %collective-permute-start.7 = (bf16[2,128,256]{2,1,0:T(8,128)(2,1)S(1)}, bf16[2,128,256]{2,1,0:T(8,128)(2,1)S(1)}, u32[]{:S(2)}, u32[]{:S(2)}) collective-permute-start(bf16[2,128,256]{2,1,0:T(8,128)(2,1)S(1)} %get-tuple-element.49), channel_id=1, source_target_pairs={{0,3},{1,2},{2,1},{3,0},{4,7},{5,6},{6,5},{7,4},{8,11},{9,10},{10,... | collective-permute-start | bytes 393224 | tf_op jit(solution)/shard_map/ppermute | solution.py:353
  26.4 5.2 %collective-permute-start.8 = (bf16[2,128,256]{2,1,0:T(8,128)(2,1)S(1)}, bf16[2,128,256]{2,1,0:T(8,128)(2,1)S(1)}, u32[]{:S(2)}, u32[]{:S(2)}) collective-permute-start(bf16[2,128,256]{2,1,0:T(8,128)(2,1)S(1)} %get-tuple-element.50), channel_id=1, source_target_pairs={{0,5},{1,4},{2,7},{3,6},{4,1},{5,0},{6,3},{7,2},{8,13},{9,12},{10,... | collective-permute-start | bytes 393224 | tf_op jit(solution)/shard_map/ppermute | solution.py:353
  27.0 4.6 %collective-permute-start.9 = (bf16[2,128,256]{2,1,0:T(8,128)(2,1)S(1)}, bf16[2,128,256]{2,1,0:T(8,128)(2,1)S(1)}, u32[]{:S(2)}, u32[]{:S(2)}) collective-permute-start(bf16[2,128,256]{2,1,0:T(8,128)(2,1)S(1)} %get-tuple-element.51), channel_id=1, source_target_pairs={{0,1},{1,0},{2,3},{3,2},{4,5},{5,4},{6,7},{7,6},{8,9},{9,8},{10,11... | collective-permute-start | bytes 393224 | tf_op jit(solution)/shard_map/ppermute | solution.py:353
  37.6 4.8 %collective-permute-start.20 = (f32[8,512]{1,0:T(8,128)S(1)}, f32[8,512]{1,0:T(8,128)S(1)}, u32[]{:S(2)}, u32[]{:S(2)}) collective-permute-start(f32[8,512]{1,0:T(8,128)S(1)} %get-tuple-element.66), channel_id=1, source_target_pairs={{8,0},{16,8},{24,16},{9,1},{17,9},{25,17},{10,2},{18,10},{26,18},{... | collective-permute-start | bytes 49160 | tf_op jit(solution)/shard_map/ppermute | solution.py:403
  39.7 6.2 %collective-permute-start.15 = (bf16[2,128,256]{2,1,0:T(8,128)(2,1)S(1)}, bf16[2,128,256]{2,1,0:T(8,128)(2,1)S(1)}, u32[]{:S(2)}, u32[]{:S(2)}) collective-permute-start(bf16[2,128,256]{2,1,0:T(8,128)(2,1)S(1)} %get-tuple-element.62), channel_id=1, source_target_pairs={{0,4},{1,5},{2,6},{3,7},{4,0},{5,1},{6,2},{7,3},{8,12},{9,13},{10,... | collective-permute-start | bytes 393224 | tf_op jit(solution)/shard_map/ppermute | solution.py:353
  40.2 6.5 %collective-permute-start.16 = (bf16[2,128,256]{2,1,0:T(8,128)(2,1)S(1)}, bf16[2,128,256]{2,1,0:T(8,128)(2,1)S(1)}, u32[]{:S(2)}, u32[]{:S(2)}) collective-permute-start(bf16[2,128,256]{2,1,0:T(8,128)(2,1)S(1)} %get-tuple-element.63), channel_id=1, source_target_pairs={{0,2},{1,3},{2,0},{3,1},{4,6},{5,7},{6,4},{7,5},{8,10},{9,11},{10,... | collective-permute-start | bytes 393224 | tf_op jit(solution)/shard_map/ppermute | solution.py:353
  41.2 6.0 %collective-permute-start.17 = (bf16[2,128,256]{2,1,0:T(8,128)(2,1)S(1)}, bf16[2,128,256]{2,1,0:T(8,128)(2,1)S(1)}, u32[]{:S(2)}, u32[]{:S(2)}) collective-permute-start(bf16[2,128,256]{2,1,0:T(8,128)(2,1)S(1)} %get-tuple-element.64), channel_id=1, source_target_pairs={{0,6},{1,7},{2,4},{3,5},{4,2},{5,3},{6,0},{7,1},{8,14},{9,15},{10,... | collective-permute-start | bytes 393224 | tf_op jit(solution)/shard_map/ppermute | solution.py:353
  43.5 8.7 %collective-permute-start.21 = (bf16[2,128,256]{2,1,0:T(8,128)(2,1)S(1)}, bf16[2,128,256]{2,1,0:T(8,128)(2,1)S(1)}, u32[]{:S(2)}, u32[]{:S(2)}) collective-permute-start(bf16[2,128,256]{2,1,0:T(8,128)(2,1)S(1)} %get-tuple-element.68), channel_id=1, source_target_pairs={{0,7},{1,6},{2,5},{3,4},{4,3},{5,2},{6,1},{7,0},{8,15},{9,14},{10,... | collective-permute-start | bytes 393224 | tf_op jit(solution)/shard_map/ppermute | solution.py:353
  45.8 8.8 %collective-permute-start.22 = (bf16[2,128,256]{2,1,0:T(8,128)(2,1)S(1)}, bf16[2,128,256]{2,1,0:T(8,128)(2,1)S(1)}, u32[]{:S(2)}, u32[]{:S(2)}) collective-permute-start(bf16[2,128,256]{2,1,0:T(8,128)(2,1)S(1)} %get-tuple-element.69), channel_id=1, source_target_pairs={{0,3},{1,2},{2,1},{3,0},{4,7},{5,6},{6,5},{7,4},{8,11},{9,10},{10,... | collective-permute-start | bytes 393224 | tf_op jit(solution)/shard_map/ppermute | solution.py:353
  45.8 9.3 %collective-permute-start.23 = (bf16[2,128,256]{2,1,0:T(8,128)(2,1)S(1)}, bf16[2,128,256]{2,1,0:T(8,128)(2,1)S(1)}, u32[]{:S(2)}, u32[]{:S(2)}) collective-permute-start(bf16[2,128,256]{2,1,0:T(8,128)(2,1)S(1)} %get-tuple-element.70), channel_id=1, source_target_pairs={{0,4},{1,5},{2,6},{3,7},{4,0},{5,1},{6,2},{7,3},{8,12},{9,13},{10,... | collective-permute-start | bytes 393224 | tf_op jit(solution)/shard_map/ppermute | solution.py:353
  47.2 13.0 %collective-permute-start.18 = (bf16[4,128,256]{2,1,0:T(8,128)(2,1)S(1)}, bf16[4,128,256]{2,1,0:T(8,128)(2,1)S(1)}, u32[]{:S(2)}, u32[]{:S(2)}) collective-permute-start(bf16[4,128,256]{2,1,0:T(8,128)(2,1)S(1)} %shard_map.72), channel_id=1, source_target_pairs={{0,1},{1,0},{2,3},{3,2},{4,5},{5,4},{6,7},{7,6},{8,9},{9,8},{10,11... | collective-permute-start | bytes 786440 | tf_op jit(solution)/shard_map/ppermute | solution.py:408
  50.1 7.2 %collective-permute-start.24 = (bf16[2,128,256]{2,1,0:T(8,128)(2,1)S(1)}, bf16[2,128,256]{2,1,0:T(8,128)(2,1)S(1)}, u32[]{:S(2)}, u32[]{:S(2)}) collective-permute-start(bf16[2,128,256]{2,1,0:T(8,128)(2,1)S(1)} %get-tuple-element.71), channel_id=1, source_target_pairs={{0,6},{1,7},{2,4},{3,5},{4,2},{5,3},{6,0},{7,1},{8,14},{9,15},{10,... | collective-permute-start | bytes 393224 | tf_op jit(solution)/shard_map/ppermute | solution.py:353
  52.1 7.2 %collective-permute-start.25 = (bf16[2,128,256]{2,1,0:T(8,128)(2,1)S(1)}, bf16[2,128,256]{2,1,0:T(8,128)(2,1)S(1)}, u32[]{:S(2)}, u32[]{:S(2)}) collective-permute-start(bf16[2,128,256]{2,1,0:T(8,128)(2,1)S(1)} %get-tuple-element.72), channel_id=1, source_target_pairs={{0,2},{1,3},{2,0},{3,1},{4,6},{5,7},{6,4},{7,5},{8,10},{9,11},{10,... | collective-permute-start | bytes 393224 | tf_op jit(solution)/shard_map/ppermute | solution.py:353
  54.6 5.6 %collective-permute-start.26 = (bf16[2,128,256]{2,1,0:T(8,128)(2,1)S(1)}, bf16[2,128,256]{2,1,0:T(8,128)(2,1)S(1)}, u32[]{:S(2)}, u32[]{:S(2)}) collective-permute-start(bf16[2,128,256]{2,1,0:T(8,128)(2,1)S(1)} %get-tuple-element.73), channel_id=1, source_target_pairs={{0,5},{1,4},{2,7},{3,6},{4,1},{5,0},{6,3},{7,2},{8,13},{9,12},{10,... | collective-permute-start | bytes 393224 | tf_op jit(solution)/shard_map/ppermute | solution.py:353
  55.1 5.1 %collective-permute-start.27 = (bf16[2,128,256]{2,1,0:T(8,128)(2,1)S(1)}, bf16[2,128,256]{2,1,0:T(8,128)(2,1)S(1)}, u32[]{:S(2)}, u32[]{:S(2)}) collective-permute-start(bf16[2,128,256]{2,1,0:T(8,128)(2,1)S(1)} %get-tuple-element.74), channel_id=1, source_target_pairs={{0,1},{1,0},{2,3},{3,2},{4,5},{5,4},{6,7},{7,6},{8,9},{9,8},{10,11... | collective-permute-start | bytes 393224 | tf_op jit(solution)/shard_map/ppermute | solution.py:353

commit v8 on v7

--- a/solution.py
+++ b/solution.py
@@ -169,13 +169,15 @@
 
 def late_kernel(n, heads, *refs):
     rest = by_slot(REST_ORDER, refs[:n])
-    kv_late, qg_early, qg_late, kv_early, dq, dkv = refs[n:]
+    kv_late, qg_early, qg_late, kv_early, dq, dkv, turned = refs[n:]
     place_all(rest, qg_late, kv_early, group_index())
     total = dkv.shape[1]
     qg, kv = (qg_early, qg_late), (kv_early, kv_late)
     blocks = [(h, start) for h in range(heads) for start in range(0, total - WINDOW, TILE)]
     lanes_of = [slice(h * HEAD_DIM, (h + 1) * HEAD_DIM) for h in range(heads)]
     key_ts = [load(kv, 0, 0, total, lanes).T for lanes in lanes_of]
+    for h in range(heads):
+        turned[h] = key_ts[h][:, :WINDOW]
 
     def products(h, start):
         qb, gb = (load(qg, t, start + WINDOW, start + WINDOW + TILE, lanes_of[h]) for t in range(2))
@@ -202,8 +204,8 @@
 
 
 def early_kernel(n, heads, *refs):
-    qg_early, qg_late, kv_early, kv_late, kv_halo, dq_in, dkv_in = refs[:7]
-    refs = refs[7:]
+    qg_early, qg_late, kv_early, kv_late, kv_halo, dq_in, dkv_in, turned = refs[:8]
+    refs = refs[8:]
     dq_out = refs[: n // 2]
     front, stat, dq, acc = refs[n // 2 :]
     me = group_index()
@@ -216,7 +218,10 @@
     qg, kv = (qg_early, qg_late), (kv_halo, kv_early, kv_late)
     blocks = [(h, start) for h in range(heads) for start in range(0, WINDOW, TILE)]
     lanes_of = [slice(h * HEAD_DIM, (h + 1) * HEAD_DIM) for h in range(heads)]
-    key_ts = [load(kv, 0, 0, 2 * WINDOW, lanes).T for lanes in lanes_of]
+    key_ts = [
+        jnp.concatenate([kv_halo[0, :, lanes].T, turned[h]], axis=1)
+        for h, lanes in enumerate(lanes_of)
+    ]
 
     def products(h, start):
         qb, gb = (load(qg, t, start, start + TILE, lanes_of[h]) for t in range(2))
@@ -388,9 +393,12 @@
     qg_halo = lax.ppermute(qg_send, "chunk", backward)
     rest = exchanged(REST_ORDER, packed((0, 1), (2, 3)))
     stat_out = vmem(f32(-(-3 * heads // 8) * 8, WINDOW))
-    qg_late, kv_early, dq_late, partial = call(
+    qg_late, kv_early, dq_late, partial, turned = call(
         functools.partial(late_kernel, n, heads),
-        [halves, halves, vmem(bf16(done, width)), vmem(f32(2, total, width))],
+        [
+            halves, halves, vmem(bf16(done, width)), vmem(f32(2, total, width)),
+            vmem(bf16(heads, HEAD_DIM, WINDOW)),
+        ],
         [], 0,
         *held(rest), (kv_late,), (qg_early,), flops=LATE_FLOPS,
     )
@@ -398,7 +406,7 @@
         functools.partial(early_kernel, n, heads),
         [vmem(bf16(2, rows, width))] * (n // 2) + [end, stat_out],
         [vmem(bf16(total, width)), vmem(f32(2, WINDOW, width))], 0,
-        *held((qg_early, qg_late, kv_early, kv_late, kv_halo, dq_late, partial)),
+        *held((qg_early, qg_late, kv_early, kv_late, kv_halo, dq_late, partial, turned)),
     )
     stat_halo = lax.ppermute(stat, "chunk", backward)
     dq = exchanged(DQ_ORDER, dq, 2)

time: 61.8 us -> 64.7 us (1.047)
  Pallas kernels: 10.3 us -> 12.1 us
  local copies, waits for them, and re-layouts: 0 us -> 1.35 us
  starting transfers between devices: 37.8 us -> 36.5 us
    pallas_call x8, Pallas kernels: 10.3 us -> 12.1 us  [call(): pl.pallas_call(kernel, out_shape=outs, in_specs=[held if isinstance(x, tu...]
    unnamed x0 -> x4, local copies, waits for them, and re-layouts: none -> 1.35 us
    ppermute x24, waiting for transfers between devices: 11.9 us -> 13.3 us  [exchanged(): lax.ppermute(pieces[m], GROUP, [(i, i ^ step * m) for i in range(step * n)])]
    ppermute x24, starting transfers between devices: 27.5 us -> 26.5 us  [exchanged(): lax.ppermute(pieces[m], GROUP, [(i, i ^ step * m) for i in range(step * n)])]
    ppermute x1, waiting for transfers between devices: 0.8 us -> 0.01 us  [per_device(): kv_halo = lax.ppermute(kv_send, 'chunk', forward)]
  transfers between devices with their start and end apart: 28 -> 28, of which waited for: 11 -> 9; matrix products, arithmetic and copies ran while one was open for 0% -> 0% of each run, Pallas kernels for 12% -> 15%
where the time goes in v8:
time: 64.7 us; the launch traced here: 63.9 us
  starting transfers between devices  36.5 us (56%)
  waiting for transfers between devices  13.3 us (21%)
  Pallas kernels  12.1 us (19%)
  local copies, waits for them, and re-layouts  1.35 us (2%)
  between operations  0.76 us (1%)
    ppermute x24, starting transfers between devices, exchanged(): lax.ppermute(pieces[m], GROUP, [(i, i ^ step * m) for i in range(step * n)])  26.5 us
    ppermute x24, waiting for transfers between devices, exchanged(): lax.ppermute(pieces[m], GROUP, [(i, i ^ step * m) for i in range(step * n)])  13.3 us
    pallas_call x8, Pallas kernels, call(): pl.pallas_call(kernel, out_shape=outs, in_specs=[held if isinstance(x, tu...  12.1 us
    ppermute x1, starting transfers between devices, per_device(): kv_halo = lax.ppermute(kv_send, 'chunk', forward)  3.2 us
    ppermute x1, starting transfers between devices, per_device(): other = lax.ppermute(other, GROUP, [(i, i ^ 1) for i in range(n)])  2.62 us
    ppermute x1, starting transfers between devices, per_device(): stat_halo = lax.ppermute(stat, 'chunk', backward)  2.1 us
    ppermute x1, starting transfers between devices, per_device(): qg_halo = lax.ppermute(qg_send, 'chunk', backward)  2.1 us
    unnamed x4, local copies, waits for them, and re-layouts  1.35 us
  transfers between devices with their start and end apart: 28, of which 9 were waited for; matrix products, arithmetic and copies ran while one was open for 0% of the time, Pallas kernels for 15%

profile of v8, /device:TPU:17, one launch (start us, length us, event | category | flops | bytes accessed | tf_op | source)
XLA Modules:
  0.0 63.9 jit_solution(5105277565694308662)
XLA Ops:
  0.6 1.3 %shard_map.67 = (bf16[2,128,256]{2,1,0:T(8,128)(2,1)S(1)}, bf16[2,128,256]{2,1,0:T(8,128)(2,1)S(1)}, bf16[2,128,256]{2,1,0:T(8,128)(2,1)S(1)}, bf16[2,128,256]{2...) custom-call(bf16[128,2048]{1,0:T(8,128)(2,1)} %refs_0_.3, ...), custom_call_target="tpu_custom_call" | custom-call | tf_op jit(solution)/shard_map/pallas_call | solution.py:327
  1.9 2.2 %collective-permute-start = (bf16[2,128,256]{2,1,0:T(8,128)(2,1)S(1)}, bf16[2,128,256]{2,1,0:T(8,128)(2,1)S(1)}, u32[]{:S(2)}, u32[]{:S(2)}) collective-permute-start(bf16[2,128,256]{2,1,0:T(8,128)(2,1)S(1)} %get-tuple-element.41), channel_id=1, source_target_pairs={{0,6},{1,7},{2,4},{3,5},{4,2},{5,3},{6,0},{7,1},{8,14},{9,15},{10,... | collective-permute-start | bytes 393224 | tf_op jit(solution)/shard_map/ppermute | solution.py:358
  4.2 1.0 %collective-permute-start.1 = (bf16[2,128,256]{2,1,0:T(8,128)(2,1)S(1)}, bf16[2,128,256]{2,1,0:T(8,128)(2,1)S(1)}, u32[]{:S(2)}, u32[]{:S(2)}) collective-permute-start(bf16[2,128,256]{2,1,0:T(8,128)(2,1)S(1)} %get-tuple-element.42), channel_id=1, source_target_pairs={{0,7},{1,6},{2,5},{3,4},{4,3},{5,2},{6,1},{7,0},{8,15},{9,14},{10,... | collective-permute-start | bytes 393224 | tf_op jit(solution)/shard_map/ppermute | solution.py:358
  5.2 1.2 %collective-permute-start.2 = (bf16[2,128,256]{2,1,0:T(8,128)(2,1)S(1)}, bf16[2,128,256]{2,1,0:T(8,128)(2,1)S(1)}, u32[]{:S(2)}, u32[]{:S(2)}) collective-permute-start(bf16[2,128,256]{2,1,0:T(8,128)(2,1)S(1)} %get-tuple-element.43), channel_id=1, source_target_pairs={{0,2},{1,3},{2,0},{3,1},{4,6},{5,7},{6,4},{7,5},{8,10},{9,11},{10,... | collective-permute-start | bytes 393224 | tf_op jit(solution)/shard_map/ppermute | solution.py:358
  6.4 1.2 %collective-permute-start.3 = (bf16[2,128,256]{2,1,0:T(8,128)(2,1)S(1)}, bf16[2,128,256]{2,1,0:T(8,128)(2,1)S(1)}, u32[]{:S(2)}, u32[]{:S(2)}) collective-permute-start(bf16[2,128,256]{2,1,0:T(8,128)(2,1)S(1)} %get-tuple-element.44), channel_id=1, source_target_pairs={{0,4},{1,5},{2,6},{3,7},{4,0},{5,1},{6,2},{7,3},{8,12},{9,13},{10,... | collective-permute-start | bytes 393224 | tf_op jit(solution)/shard_map/ppermute | solution.py:358
  7.7 0.1 collective-permute-start.4
  7.8 0.0 collective-permute-done.refs_1_
  7.8 3.0 %collective-permute-start.5 = (bf16[2,128,256]{2,1,0:T(8,128)(2,1)S(1)}, bf16[2,128,256]{2,1,0:T(8,128)(2,1)S(1)}, u32[]{:S(2)}, u32[]{:S(2)}) collective-permute-start(bf16[2,128,256]{2,1,0:T(8,128)(2,1)S(1)} %get-tuple-element.46), channel_id=1, source_target_pairs={{0,3},{1,2},{2,1},{3,0},{4,7},{5,6},{6,5},{7,4},{8,11},{9,10},{10,... | collective-permute-start | bytes 393224 | tf_op jit(solution)/shard_map/ppermute | solution.py:358
  10.8 0.2 collective-permute-done.1.refs_2_
  11.0 1.0 %collective-permute-start.6 = (bf16[2,128,256]{2,1,0:T(8,128)(2,1)S(1)}, bf16[2,128,256]{2,1,0:T(8,128)(2,1)S(1)}, u32[]{:S(2)}, u32[]{:S(2)}) collective-permute-start(bf16[2,128,256]{2,1,0:T(8,128)(2,1)S(1)} %get-tuple-element.47), channel_id=1, source_target_pairs={{0,5},{1,4},{2,7},{3,6},{4,1},{5,0},{6,3},{7,2},{8,13},{9,12},{10,... | collective-permute-start | bytes 393224 | tf_op jit(solution)/shard_map/ppermute | solution.py:358
  12.0 1.3 %shard_map.69 = (bf16[2,128,256]{2,1,0:T(8,128)(2,1)S(1)}, bf16[2,128,256]{2,1,0:T(8,128)(2,1)S(1)}, bf16[2,128,256]{2,1,0:T(8,128)(2,1)S(1)}, bf16[2,128,256]{2...) custom-call(bf16[128,2048]{1,0:T(8,128)(2,1)} %refs_0_.3, ...), custom_call_target="tpu_custom_call" | custom-call | tf_op jit(solution)/shard_map/pallas_call | solution.py:327
  13.3 0.0 collective-permute-done.2.refs_3_
  13.3 2.3 %collective-permute-start.10 = (bf16[2,128,256]{2,1,0:T(8,128)(2,1)S(1)}, bf16[2,128,256]{2,1,0:T(8,128)(2,1)S(1)}, u32[]{:S(2)}, u32[]{:S(2)}) collective-permute-start(bf16[2,128,256]{2,1,0:T(8,128)(2,1)S(1)} %get-tuple-element.53), channel_id=1, source_target_pairs={{0,6},{1,7},{2,4},{3,5},{4,2},{5,3},{6,0},{7,1},{8,14},{9,15},{10,... | collective-permute-start | bytes 393224 | tf_op jit(solution)/shard_map/ppermute | solution.py:358
  15.7 0.0 collective-permute-done.3.refs_4_
  15.7 2.2 %collective-permute-start.11 = (bf16[2,128,256]{2,1,0:T(8,128)(2,1)S(1)}, bf16[2,128,256]{2,1,0:T(8,128)(2,1)S(1)}, u32[]{:S(2)}, u32[]{:S(2)}) collective-permute-start(bf16[2,128,256]{2,1,0:T(8,128)(2,1)S(1)} %get-tuple-element.54), channel_id=1, source_target_pairs={{0,7},{1,6},{2,5},{3,4},{4,3},{5,2},{6,1},{7,0},{8,15},{9,14},{10,... | collective-permute-start | bytes 393224 | tf_op jit(solution)/shard_map/ppermute | solution.py:358
  17.9 0.0 collective-permute-done.4.refs_5_
  17.9 1.6 %collective-permute-start.12 = (bf16[2,128,256]{2,1,0:T(8,128)(2,1)S(1)}, bf16[2,128,256]{2,1,0:T(8,128)(2,1)S(1)}, u32[]{:S(2)}, u32[]{:S(2)}) collective-permute-start(bf16[2,128,256]{2,1,0:T(8,128)(2,1)S(1)} %get-tuple-element.55), channel_id=1, source_target_pairs={{0,2},{1,3},{2,0},{3,1},{4,6},{5,7},{6,4},{7,5},{8,10},{9,11},{10,... | collective-permute-start | bytes 393224 | tf_op jit(solution)/shard_map/ppermute | solution.py:358
  19.4 0.0 collective-permute-done.5.refs_6_
  19.4 0.0 collective-permute-start.13
  19.4 0.0 collective-permute-done.6.refs_7_
  19.4 0.1 shard_map.68
  19.5 3.2 %collective-permute-start.14 = (bf16[2,512,256]{2,1,0:T(8,128)(2,1)S(1)}, bf16[2,512,256]{2,1,0:T(8,128)(2,1)S(1)}, u32[]{:S(2)}, u32[]{:S(2)}) collective-permute-start(bf16[2,512,256]{2,1,0:T(8,128)(2,1)S(1)} %get-tuple-element.57.refs_8_.refs_3_.refs_1_), channel_id=1, source_target_pairs={{0,8},{8,16},{16,24},{1,9},{9,17},{17,25},{2,10},{10,18},{18,26},{... | collective-permute-start | bytes 1572872 | tf_op jit(solution)/shard_map/ppermute | solution.py:392
  22.8 0.0 collective-permute-done.10.refs_4_
  22.8 2.1 %collective-permute-start.19 = (bf16[2,512,256]{2,1,0:T(8,128)(2,1)S(1)}, bf16[2,512,256]{2,1,0:T(8,128)(2,1)S(1)}, u32[]{:S(2)}, u32[]{:S(2)}) collective-permute-start(bf16[2,512,256]{2,1,0:T(8,128)(2,1)S(1)} %get-tuple-element.48.refs_9_.refs_0_), channel_id=1, source_target_pairs={{8,0},{16,8},{24,16},{9,1},{17,9},{25,17},{10,2},{18,10},{26,18},{... | collective-permute-start | bytes 1572872 | tf_op jit(solution)/shard_map/ppermute | solution.py:393
  24.9 0.0 collective-permute-done.11.refs_5_
  24.9 1.5 %collective-permute-start.7 = (bf16[2,128,256]{2,1,0:T(8,128)(2,1)S(1)}, bf16[2,128,256]{2,1,0:T(8,128)(2,1)S(1)}, u32[]{:S(2)}, u32[]{:S(2)}) collective-permute-start(bf16[2,128,256]{2,1,0:T(8,128)(2,1)S(1)} %get-tuple-element.50), channel_id=1, source_target_pairs={{0,3},{1,2},{2,1},{3,0},{4,7},{5,6},{6,5},{7,4},{8,11},{9,10},{10,... | collective-permute-start | bytes 393224 | tf_op jit(solution)/shard_map/ppermute | solution.py:358
  26.4 0.0 collective-permute-done.12.refs_6_
  26.4 0.6 collective-permute-start.8
  27.0 0.0 collective-permute-done.13.refs_7_
  27.0 0.0 collective-permute-start.9
  27.0 3.7 %collective-permute-done.7.refs_1_ = bf16[2,128,256]{2,1,0:T(8,128)(2,1)S(1)} collective-permute-done((bf16[2,128,256]{2,1,0:T(8,128)(2,1)S(1)}, bf16[2,128,256]{2,1,0:T(8,128)(2,1)S(1)}, u32[]{:S(2)}, u32[]{:S(2)}) %collective-permute-start.7) | collective-permute-done | bytes 131104 | tf_op jit(solution)/shard_map/ppermute | solution.py:358
  30.7 0.9 %collective-permute-done.8.refs_2_ = bf16[2,128,256]{2,1,0:T(8,128)(2,1)S(1)} collective-permute-done((bf16[2,128,256]{2,1,0:T(8,128)(2,1)S(1)}, bf16[2,128,256]{2,1,0:T(8,128)(2,1)S(1)}, u32[]{:S(2)}, u32[]{:S(2)}) %collective-permute-start.8) | collective-permute-done | bytes 131104 | tf_op jit(solution)/shard_map/ppermute | solution.py:358
  31.6 0.0 collective-permute-done.9.refs_3_
  31.6 2.7 %shard_map.70 = (bf16[2,512,256]{2,1,0:T(8,128)(2,1)S(1)}, bf16[2,512,256]{2,1,0:T(8,128)(2,1)S(1)}, bf16[512,256]{1,0:T(8,128)(2,1)S(1)}, f32[2,1024,256]{2,1,0:T(8,128)S(1)}, bf16[2,128,512]{2,1,0:T(8,128)(2,1)S(1)}) custom-call(bf16[2,128,256]{2,1,0:T(8,128)(2,1)S(1)} %get-tuple-element.49.refs_0_, ...), custom_call_target="tpu_custom_call" | custom-call | flops 4000000000 | tf_op jit(solution)/shard_map/pallas_call | solution.py:327
  34.3 1.3 %copy-done = f32[2,1024,256]{2,1,0:T(8,128)} copy-done((f32[2,1024,256]{2,1,0:T(8,128)}, f32[2,1024,256]{2,1,0:T(8,128)S(1)}, u32[]{:S(2)}) %copy-start) | copy-done | bytes 2097176
  35.7 0.0 collective-permute-done.14.refs_4_
  35.7 4.2 %shard_map.71 = (bf16[2,128,256]{2,1,0:T(8,128)(2,1)S(1)}, bf16[2,128,256]{2,1,0:T(8,128)(2,1)S(1)}, bf16[2,128,256]{2,1,0:T(8,128)(2,1)S(1)}, bf16[2,128,256]{2...) custom-call(bf16[2,512,256]{2,1,0:T(8,128)(2,1)S(1)} %get-tuple-element.48.refs_9_.refs_0_, ...), custom_call_target="tpu_custom_call" | custom-call | tf_op jit(solution)/shard_map/pallas_call | solution.py:327
  39.9 2.1 %collective-permute-start.20 = (f32[8,512]{1,0:T(8,128)S(1)}, f32[8,512]{1,0:T(8,128)S(1)}, u32[]{:S(2)}, u32[]{:S(2)}) collective-permute-start(f32[8,512]{1,0:T(8,128)S(1)} %get-tuple-element.68), channel_id=1, source_target_pairs={{8,0},{16,8},{24,16},{9,1},{17,9},{25,17},{10,2},{18,10},{26,18},{... | collective-permute-start | bytes 49160 | tf_op jit(solution)/shard_map/ppermute | solution.py:411
  42.0 1.0 %collective-permute-start.15 = (bf16[2,128,256]{2,1,0:T(8,128)(2,1)S(1)}, bf16[2,128,256]{2,1,0:T(8,128)(2,1)S(1)}, u32[]{:S(2)}, u32[]{:S(2)}) collective-permute-start(bf16[2,128,256]{2,1,0:T(8,128)(2,1)S(1)} %get-tuple-element.64), channel_id=1, source_target_pairs={{0,4},{1,5},{2,6},{3,7},{4,0},{5,1},{6,2},{7,3},{8,12},{9,13},{10,... | collective-permute-start | bytes 393224 | tf_op jit(solution)/shard_map/ppermute | solution.py:358
  43.0 0.2 collective-permute-start.16
  43.2 1.5 %collective-permute-start.17 = (bf16[2,128,256]{2,1,0:T(8,128)(2,1)S(1)}, bf16[2,128,256]{2,1,0:T(8,128)(2,1)S(1)}, u32[]{:S(2)}, u32[]{:S(2)}) collective-permute-start(bf16[2,128,256]{2,1,0:T(8,128)(2,1)S(1)} %get-tuple-element.66), channel_id=1, source_target_pairs={{0,6},{1,7},{2,4},{3,5},{4,2},{5,3},{6,0},{7,1},{8,14},{9,15},{10,... | collective-permute-start | bytes 393224 | tf_op jit(solution)/shard_map/ppermute | solution.py:358
  44.8 0.0 collective-permute-done.19.refs_2_
  44.8 0.0 collective-permute-done.20.refs_5_
  44.8 1.1 %shard_map.73 = (bf16[2,128,256]{2,1,0:T(8,128)(2,1)S(1)}, bf16[2,128,256]{2,1,0:T(8,128)(2,1)S(1)}, bf16[2,128,256]{2,1,0:T(8,128)(2,1)S(1)}, bf16[2,128,256]{2...) custom-call(bf16[2,512,256]{2,1,0:T(8,128)(2,1)S(1)} %get-tuple-elem, ...), custom_call_target="tpu_custom_call" | custom-call | flops 4000000000 | tf_op jit(solution)/shard_map/pallas_call | solution.py:327
  45.8 2.5 %collective-permute-start.21 = (bf16[2,128,256]{2,1,0:T(8,128)(2,1)S(1)}, bf16[2,128,256]{2,1,0:T(8,128)(2,1)S(1)}, u32[]{:S(2)}, u32[]{:S(2)}) collective-permute-start(bf16[2,128,256]{2,1,0:T(8,128)(2,1)S(1)} %get-tuple-element.70), channel_id=1, source_target_pairs={{0,7},{1,6},{2,5},{3,4},{4,3},{5,2},{6,1},{7,0},{8,15},{9,14},{10,... | collective-permute-start | bytes 393224 | tf_op jit(solution)/shard_map/ppermute | solution.py:358
  48.4 0.0 collective-permute-start.22
  48.4 0.0 collective-permute-done.15.refs_1_
  48.4 1.0 %collective-permute-start.23 = (bf16[2,128,256]{2,1,0:T(8,128)(2,1)S(1)}, bf16[2,128,256]{2,1,0:T(8,128)(2,1)S(1)}, u32[]{:S(2)}, u32[]{:S(2)}) collective-permute-start(bf16[2,128,256]{2,1,0:T(8,128)(2,1)S(1)} %get-tuple-element.72), channel_id=1, source_target_pairs={{0,4},{1,5},{2,6},{3,7},{4,0},{5,1},{6,2},{7,3},{8,12},{9,13},{10,... | collective-permute-start | bytes 393224 | tf_op jit(solution)/shard_map/ppermute | solution.py:358
  49.4 0.0 collective-permute-done.16.refs_2_
  49.4 1.1 %collective-permute-done.17.refs_3_ = bf16[2,128,256]{2,1,0:T(8,128)(2,1)S(1)} collective-permute-done((bf16[2,128,256]{2,1,0:T(8,128)(2,1)S(1)}, bf16[2,128,256]{2,1,0:T(8,128)(2,1)S(1)}, u32[]{:S(2)}, u32[]{:S(2)}) %collective-permute-start.17) | collective-permute-done | bytes 131104 | tf_op jit(solution)/shard_map/ppermute | solution.py:358
  50.5 2.6 %collective-permute-start.18 = (bf16[4,128,256]{2,1,0:T(8,128)(2,1)S(1)}, bf16[4,128,256]{2,1,0:T(8,128)(2,1)S(1)}, u32[]{:S(2)}, u32[]{:S(2)}) collective-permute-start(bf16[4,128,256]{2,1,0:T(8,128)(2,1)S(1)} %shard_map.72), channel_id=1, source_target_pairs={{0,1},{1,0},{2,3},{3,2},{4,5},{5,4},{6,7},{7,6},{8,9},{9,8},{10,11... | collective-permute-start | bytes 786440 | tf_op jit(solution)/shard_map/ppermute | solution.py:416
  53.2 0.5 collective-permute-start.24
  53.7 1.5 %collective-permute-done.21.refs_6_ = bf16[2,128,256]{2,1,0:T(8,128)(2,1)S(1)} collective-permute-done((bf16[2,128,256]{2,1,0:T(8,128)(2,1)S(1)}, bf16[2,128,256]{2,1,0:T(8,128)(2,1)S(1)}, u32[]{:S(2)}, u32[]{:S(2)}) %collective-permute-start.21) | collective-permute-done | bytes 131104 | tf_op jit(solution)/shard_map/ppermute | solution.py:358
  55.1 0.8 %collective-permute-start.25 = (bf16[2,128,256]{2,1,0:T(8,128)(2,1)S(1)}, bf16[2,128,256]{2,1,0:T(8,128)(2,1)S(1)}, u32[]{:S(2)}, u32[]{:S(2)}) collective-permute-start(bf16[2,128,256]{2,1,0:T(8,128)(2,1)S(1)} %get-tuple-element.74), channel_id=1, source_target_pairs={{0,2},{1,3},{2,0},{3,1},{4,6},{5,7},{6,4},{7,5},{8,10},{9,11},{10,... | collective-permute-start | bytes 393224 | tf_op jit(solution)/shard_map/ppermute | solution.py:358
  56.0 1.6 %collective-permute-done.22.refs_7_ = bf16[2,128,256]{2,1,0:T(8,128)(2,1)S(1)} collective-permute-done((bf16[2,128,256]{2,1,0:T(8,128)(2,1)S(1)}, bf16[2,128,256]{2,1,0:T(8,128)(2,1)S(1)}, u32[]{:S(2)}, u32[]{:S(2)}) %collective-permute-start.22) | collective-permute-done | bytes 131104 | tf_op jit(solution)/shard_map/ppermute | solution.py:358
  57.6 0.0 collective-permute-start.26
  57.6 0.0 collective-permute-done.23.refs_8_
  57.6 0.8 %collective-permute-start.27 = (bf16[2,128,256]{2,1,0:T(8,128)(2,1)S(1)}, bf16[2,128,256]{2,1,0:T(8,128)(2,1)S(1)}, u32[]{:S(2)}, u32[]{:S(2)}) collective-permute-start(bf16[2,128,256]{2,1,0:T(8,128)(2,1)S(1)} %get-tuple-element.76), channel_id=1, source_target_pairs={{0,1},{1,0},{2,3},{3,2},{4,5},{5,4},{6,7},{7,6},{8,9},{9,8},{10,11... | collective-permute-start | bytes 393224 | tf_op jit(solution)/shard_map/ppermute | solution.py:358
  58.4 1.3 %collective-permute-done.24.refs_9_ = bf16[2,128,256]{2,1,0:T(8,128)(2,1)S(1)} collective-permute-done((bf16[2,128,256]{2,1,0:T(8,128)(2,1)S(1)}, bf16[2,128,256]{2,1,0:T(8,128)(2,1)S(1)}, u32[]{:S(2)}, u32[]{:S(2)}) %collective-permute-start.24) | collective-permute-done | bytes 131104 | tf_op jit(solution)/shard_map/ppermute | solution.py:358
  59.7 2.3 %collective-permute-done.25.refs_10_ = bf16[2,128,256]{2,1,0:T(8,128)(2,1)S(1)} collective-permute-done((bf16[2,128,256]{2,1,0:T(8,128)(2,1)S(1)}, bf16[2,128,256]{2,1,0:T(8,128)(2,1)S(1)}, u32[]{:S(2)}, u32[]{:S(2)}) %collective-permute-start.25) | collective-permute-done | bytes 131104 | tf_op jit(solution)/shard_map/ppermute | solution.py:358
  61.9 0.7 %collective-permute-done.26.refs_11_ = bf16[2,128,256]{2,1,0:T(8,128)(2,1)S(1)} collective-permute-done((bf16[2,128,256]{2,1,0:T(8,128)(2,1)S(1)}, bf16[2,128,256]{2,1,0:T(8,128)(2,1)S(1)}, u32[]{:S(2)}, u32[]{:S(2)}) %collective-permute-start.26) | collective-permute-done | bytes 131104 | tf_op jit(solution)/shard_map/ppermute | solution.py:358
  62.6 0.0 collective-permute-done.27.refs_12_
  62.6 0.0 collective-permute-done.18.refs_4_
  62.6 1.3 %shard_map.74 = (bf16[128,2048]{1,0:T(8,128)(2,1)}, bf16[128,2048]{1,0:T(8,128)(2,1)}, bf16[128,2048]{1,0:T(8,128)(2,1)}) custom-call(bf16[2,128,256]{2,1,0:T(8,128)(2,1)S(1)} %get-tuple-element.63.refs_0_, bf16[2,128,256]{2,1,0:T(8,128)(2,1)S(1)} %collective-permute-done.15.refs_1_, bf16[2,128,256]{2,1,0:T(8,128)(2,1)S(1)} %collective-permute-done.16.refs_2_, ...), custom_call_target="tpu_custom_call" | custom-call | tf_op jit(solution)/shard_map/pallas_call | solution.py:327
  (4 shorter events, 0.0 us)
Async XLA Ops:
  1.9 5.8 %collective-permute-start = (bf16[2,128,256]{2,1,0:T(8,128)(2,1)S(1)}, bf16[2,128,256]{2,1,0:T(8,128)(2,1)S(1)}, u32[]{:S(2)}, u32[]{:S(2)}) collective-permute-start(bf16[2,128,256]{2,1,0:T(8,128)(2,1)S(1)} %get-tuple-element.41), channel_id=1, source_target_pairs={{0,6},{1,7},{2,4},{3,5},{4,2},{5,3},{6,0},{7,1},{8,14},{9,15},{10,... | collective-permute-start | bytes 393224 | tf_op jit(solution)/shard_map/ppermute | solution.py:358
  4.2 6.8 %collective-permute-start.1 = (bf16[2,128,256]{2,1,0:T(8,128)(2,1)S(1)}, bf16[2,128,256]{2,1,0:T(8,128)(2,1)S(1)}, u32[]{:S(2)}, u32[]{:S(2)}) collective-permute-start(bf16[2,128,256]{2,1,0:T(8,128)(2,1)S(1)} %get-tuple-element.42), channel_id=1, source_target_pairs={{0,7},{1,6},{2,5},{3,4},{4,3},{5,2},{6,1},{7,0},{8,15},{9,14},{10,... | collective-permute-start | bytes 393224 | tf_op jit(solution)/shard_map/ppermute | solution.py:358
  5.2 8.1 %collective-permute-start.2 = (bf16[2,128,256]{2,1,0:T(8,128)(2,1)S(1)}, bf16[2,128,256]{2,1,0:T(8,128)(2,1)S(1)}, u32[]{:S(2)}, u32[]{:S(2)}) collective-permute-start(bf16[2,128,256]{2,1,0:T(8,128)(2,1)S(1)} %get-tuple-element.43), channel_id=1, source_target_pairs={{0,2},{1,3},{2,0},{3,1},{4,6},{5,7},{6,4},{7,5},{8,10},{9,11},{10,... | collective-permute-start | bytes 393224 | tf_op jit(solution)/shard_map/ppermute | solution.py:358
  6.4 9.2 %collective-permute-start.3 = (bf16[2,128,256]{2,1,0:T(8,128)(2,1)S(1)}, bf16[2,128,256]{2,1,0:T(8,128)(2,1)S(1)}, u32[]{:S(2)}, u32[]{:S(2)}) collective-permute-start(bf16[2,128,256]{2,1,0:T(8,128)(2,1)S(1)} %get-tuple-element.44), channel_id=1, source_target_pairs={{0,4},{1,5},{2,6},{3,7},{4,0},{5,1},{6,2},{7,3},{8,12},{9,13},{10,... | collective-permute-start | bytes 393224 | tf_op jit(solution)/shard_map/ppermute | solution.py:358
  7.7 10.2 %collective-permute-start.4 = (bf16[2,128,256]{2,1,0:T(8,128)(2,1)S(1)}, bf16[2,128,256]{2,1,0:T(8,128)(2,1)S(1)}, u32[]{:S(2)}, u32[]{:S(2)}) collective-permute-start(bf16[2,128,256]{2,1,0:T(8,128)(2,1)S(1)} %get-tuple-element.45), channel_id=1, source_target_pairs={{0,1},{1,0},{2,3},{3,2},{4,5},{5,4},{6,7},{7,6},{8,9},{9,8},{10,11... | collective-permute-start | bytes 393224 | tf_op jit(solution)/shard_map/ppermute | solution.py:358
  7.8 11.7 %collective-permute-start.5 = (bf16[2,128,256]{2,1,0:T(8,128)(2,1)S(1)}, bf16[2,128,256]{2,1,0:T(8,128)(2,1)S(1)}, u32[]{:S(2)}, u32[]{:S(2)}) collective-permute-start(bf16[2,128,256]{2,1,0:T(8,128)(2,1)S(1)} %get-tuple-element.46), channel_id=1, source_target_pairs={{0,3},{1,2},{2,1},{3,0},{4,7},{5,6},{6,5},{7,4},{8,11},{9,10},{10,... | collective-permute-start | bytes 393224 | tf_op jit(solution)/shard_map/ppermute | solution.py:358
  11.0 8.4 %collective-permute-start.6 = (bf16[2,128,256]{2,1,0:T(8,128)(2,1)S(1)}, bf16[2,128,256]{2,1,0:T(8,128)(2,1)S(1)}, u32[]{:S(2)}, u32[]{:S(2)}) collective-permute-start(bf16[2,128,256]{2,1,0:T(8,128)(2,1)S(1)} %get-tuple-element.47), channel_id=1, source_target_pairs={{0,5},{1,4},{2,7},{3,6},{4,1},{5,0},{6,3},{7,2},{8,13},{9,12},{10,... | collective-permute-start | bytes 393224 | tf_op jit(solution)/shard_map/ppermute | solution.py:358
  13.3 9.4 %collective-permute-start.10 = (bf16[2,128,256]{2,1,0:T(8,128)(2,1)S(1)}, bf16[2,128,256]{2,1,0:T(8,128)(2,1)S(1)}, u32[]{:S(2)}, u32[]{:S(2)}) collective-permute-start(bf16[2,128,256]{2,1,0:T(8,128)(2,1)S(1)} %get-tuple-element.53), channel_id=1, source_target_pairs={{0,6},{1,7},{2,4},{3,5},{4,2},{5,3},{6,0},{7,1},{8,14},{9,15},{10,... | collective-permute-start | bytes 393224 | tf_op jit(solution)/shard_map/ppermute | solution.py:358
  15.7 9.2 %collective-permute-start.11 = (bf16[2,128,256]{2,1,0:T(8,128)(2,1)S(1)}, bf16[2,128,256]{2,1,0:T(8,128)(2,1)S(1)}, u32[]{:S(2)}, u32[]{:S(2)}) collective-permute-start(bf16[2,128,256]{2,1,0:T(8,128)(2,1)S(1)} %get-tuple-element.54), channel_id=1, source_target_pairs={{0,7},{1,6},{2,5},{3,4},{4,3},{5,2},{6,1},{7,0},{8,15},{9,14},{10,... | collective-permute-start | bytes 393224 | tf_op jit(solution)/shard_map/ppermute | solution.py:358
  17.9 8.6 %collective-permute-start.12 = (bf16[2,128,256]{2,1,0:T(8,128)(2,1)S(1)}, bf16[2,128,256]{2,1,0:T(8,128)(2,1)S(1)}, u32[]{:S(2)}, u32[]{:S(2)}) collective-permute-start(bf16[2,128,256]{2,1,0:T(8,128)(2,1)S(1)} %get-tuple-element.55), channel_id=1, source_target_pairs={{0,2},{1,3},{2,0},{3,1},{4,6},{5,7},{6,4},{7,5},{8,10},{9,11},{10,... | collective-permute-start | bytes 393224 | tf_op jit(solution)/shard_map/ppermute | solution.py:358
  19.4 7.6 %collective-permute-start.13 = (bf16[2,128,256]{2,1,0:T(8,128)(2,1)S(1)}, bf16[2,128,256]{2,1,0:T(8,128)(2,1)S(1)}, u32[]{:S(2)}, u32[]{:S(2)}) collective-permute-start(bf16[2,128,256]{2,1,0:T(8,128)(2,1)S(1)} %get-tuple-element.56), channel_id=1, source_target_pairs={{0,4},{1,5},{2,6},{3,7},{4,0},{5,1},{6,2},{7,3},{8,12},{9,13},{10,... | collective-permute-start | bytes 393224 | tf_op jit(solution)/shard_map/ppermute | solution.py:358
  19.5 16.2 %collective-permute-start.14 = (bf16[2,512,256]{2,1,0:T(8,128)(2,1)S(1)}, bf16[2,512,256]{2,1,0:T(8,128)(2,1)S(1)}, u32[]{:S(2)}, u32[]{:S(2)}) collective-permute-start(bf16[2,512,256]{2,1,0:T(8,128)(2,1)S(1)} %get-tuple-element.57.refs_8_.refs_3_.refs_1_), channel_id=1, source_target_pairs={{0,8},{8,16},{16,24},{1,9},{9,17},{17,25},{2,10},{10,18},{18,26},{... | collective-permute-start | bytes 1572872 | tf_op jit(solution)/shard_map/ppermute | solution.py:392
  22.8 22.0 %collective-permute-start.19 = (bf16[2,512,256]{2,1,0:T(8,128)(2,1)S(1)}, bf16[2,512,256]{2,1,0:T(8,128)(2,1)S(1)}, u32[]{:S(2)}, u32[]{:S(2)}) collective-permute-start(bf16[2,512,256]{2,1,0:T(8,128)(2,1)S(1)} %get-tuple-element.48.refs_9_.refs_0_), channel_id=1, source_target_pairs={{8,0},{16,8},{24,16},{9,1},{17,9},{25,17},{10,2},{18,10},{26,18},{... | collective-permute-start | bytes 1572872 | tf_op jit(solution)/shard_map/ppermute | solution.py:393
  24.9 5.8 %collective-permute-start.7 = (bf16[2,128,256]{2,1,0:T(8,128)(2,1)S(1)}, bf16[2,128,256]{2,1,0:T(8,128)(2,1)S(1)}, u32[]{:S(2)}, u32[]{:S(2)}) collective-permute-start(bf16[2,128,256]{2,1,0:T(8,128)(2,1)S(1)} %get-tuple-element.50), channel_id=1, source_target_pairs={{0,3},{1,2},{2,1},{3,0},{4,7},{5,6},{6,5},{7,4},{8,11},{9,10},{10,... | collective-permute-start | bytes 393224 | tf_op jit(solution)/shard_map/ppermute | solution.py:358
  26.4 5.2 %collective-permute-start.8 = (bf16[2,128,256]{2,1,0:T(8,128)(2,1)S(1)}, bf16[2,128,256]{2,1,0:T(8,128)(2,1)S(1)}, u32[]{:S(2)}, u32[]{:S(2)}) collective-permute-start(bf16[2,128,256]{2,1,0:T(8,128)(2,1)S(1)} %get-tuple-element.51), channel_id=1, source_target_pairs={{0,5},{1,4},{2,7},{3,6},{4,1},{5,0},{6,3},{7,2},{8,13},{9,12},{10,... | collective-permute-start | bytes 393224 | tf_op jit(solution)/shard_map/ppermute | solution.py:358
  27.0 4.6 %collective-permute-start.9 = (bf16[2,128,256]{2,1,0:T(8,128)(2,1)S(1)}, bf16[2,128,256]{2,1,0:T(8,128)(2,1)S(1)}, u32[]{:S(2)}, u32[]{:S(2)}) collective-permute-start(bf16[2,128,256]{2,1,0:T(8,128)(2,1)S(1)} %get-tuple-element.52), channel_id=1, source_target_pairs={{0,1},{1,0},{2,3},{3,2},{4,5},{5,4},{6,7},{7,6},{8,9},{9,8},{10,11... | collective-permute-start | bytes 393224 | tf_op jit(solution)/shard_map/ppermute | solution.py:358
  34.3 1.4 %copy-start = (f32[2,1024,256]{2,1,0:T(8,128)}, f32[2,1024,256]{2,1,0:T(8,128)S(1)}, u32[]{:S(2)}) copy-start(f32[2,1024,256]{2,1,0:T(8,128)S(1)} %get-tuple-element.61.refs_6_.refs_4_) | copy-start | bytes 6291460
  35.7 9.1 %copy-start.1 = (f32[2,1024,256]{2,1,0:T(8,128)S(1)}, f32[2,1024,256]{2,1,0:T(8,128)}, u32[]{:S(2)}) copy-start(f32[2,1024,256]{2,1,0:T(8,128)} %copy-done) | copy-start | bytes 6291460
  39.9 4.8 %collective-permute-start.20 = (f32[8,512]{1,0:T(8,128)S(1)}, f32[8,512]{1,0:T(8,128)S(1)}, u32[]{:S(2)}, u32[]{:S(2)}) collective-permute-start(f32[8,512]{1,0:T(8,128)S(1)} %get-tuple-element.68), channel_id=1, source_target_pairs={{8,0},{16,8},{24,16},{9,1},{17,9},{25,17},{10,2},{18,10},{26,18},{... | collective-permute-start | bytes 49160 | tf_op jit(solution)/shard_map/ppermute | solution.py:411
  42.0 6.3 %collective-permute-start.15 = (bf16[2,128,256]{2,1,0:T(8,128)(2,1)S(1)}, bf16[2,128,256]{2,1,0:T(8,128)(2,1)S(1)}, u32[]{:S(2)}, u32[]{:S(2)}) collective-permute-start(bf16[2,128,256]{2,1,0:T(8,128)(2,1)S(1)} %get-tuple-element.64), channel_id=1, source_target_pairs={{0,4},{1,5},{2,6},{3,7},{4,0},{5,1},{6,2},{7,3},{8,12},{9,13},{10,... | collective-permute-start | bytes 393224 | tf_op jit(solution)/shard_map/ppermute | solution.py:358
  43.0 6.4 %collective-permute-start.16 = (bf16[2,128,256]{2,1,0:T(8,128)(2,1)S(1)}, bf16[2,128,256]{2,1,0:T(8,128)(2,1)S(1)}, u32[]{:S(2)}, u32[]{:S(2)}) collective-permute-start(bf16[2,128,256]{2,1,0:T(8,128)(2,1)S(1)} %get-tuple-element.65), channel_id=1, source_target_pairs={{0,2},{1,3},{2,0},{3,1},{4,6},{5,7},{6,4},{7,5},{8,10},{9,11},{10,... | collective-permute-start | bytes 393224 | tf_op jit(solution)/shard_map/ppermute | solution.py:358
  43.2 7.3 %collective-permute-start.17 = (bf16[2,128,256]{2,1,0:T(8,128)(2,1)S(1)}, bf16[2,128,256]{2,1,0:T(8,128)(2,1)S(1)}, u32[]{:S(2)}, u32[]{:S(2)}) collective-permute-start(bf16[2,128,256]{2,1,0:T(8,128)(2,1)S(1)} %get-tuple-element.66), channel_id=1, source_target_pairs={{0,6},{1,7},{2,4},{3,5},{4,2},{5,3},{6,0},{7,1},{8,14},{9,15},{10,... | collective-permute-start | bytes 393224 | tf_op jit(solution)/shard_map/ppermute | solution.py:358
  45.8 9.3 %collective-permute-start.21 = (bf16[2,128,256]{2,1,0:T(8,128)(2,1)S(1)}, bf16[2,128,256]{2,1,0:T(8,128)(2,1)S(1)}, u32[]{:S(2)}, u32[]{:S(2)}) collective-permute-start(bf16[2,128,256]{2,1,0:T(8,128)(2,1)S(1)} %get-tuple-element.70), channel_id=1, source_target_pairs={{0,7},{1,6},{2,5},{3,4},{4,3},{5,2},{6,1},{7,0},{8,15},{9,14},{10,... | collective-permute-start | bytes 393224 | tf_op jit(solution)/shard_map/ppermute | solution.py:358
  48.4 9.3 %collective-permute-start.22 = (bf16[2,128,256]{2,1,0:T(8,128)(2,1)S(1)}, bf16[2,128,256]{2,1,0:T(8,128)(2,1)S(1)}, u32[]{:S(2)}, u32[]{:S(2)}) collective-permute-start(bf16[2,128,256]{2,1,0:T(8,128)(2,1)S(1)} %get-tuple-element.71), channel_id=1, source_target_pairs={{0,3},{1,2},{2,1},{3,0},{4,7},{5,6},{6,5},{7,4},{8,11},{9,10},{10,... | collective-permute-start | bytes 393224 | tf_op jit(solution)/shard_map/ppermute | solution.py:358
  48.4 9.3 %collective-permute-start.23 = (bf16[2,128,256]{2,1,0:T(8,128)(2,1)S(1)}, bf16[2,128,256]{2,1,0:T(8,128)(2,1)S(1)}, u32[]{:S(2)}, u32[]{:S(2)}) collective-permute-start(bf16[2,128,256]{2,1,0:T(8,128)(2,1)S(1)} %get-tuple-element.72), channel_id=1, source_target_pairs={{0,4},{1,5},{2,6},{3,7},{4,0},{5,1},{6,2},{7,3},{8,12},{9,13},{10,... | collective-permute-start | bytes 393224 | tf_op jit(solution)/shard_map/ppermute | solution.py:358
  50.5 12.1 %collective-permute-start.18 = (bf16[4,128,256]{2,1,0:T(8,128)(2,1)S(1)}, bf16[4,128,256]{2,1,0:T(8,128)(2,1)S(1)}, u32[]{:S(2)}, u32[]{:S(2)}) collective-permute-start(bf16[4,128,256]{2,1,0:T(8,128)(2,1)S(1)} %shard_map.72), channel_id=1, source_target_pairs={{0,1},{1,0},{2,3},{3,2},{4,5},{5,4},{6,7},{7,6},{8,9},{9,8},{10,11... | collective-permute-start | bytes 786440 | tf_op jit(solution)/shard_map/ppermute | solution.py:416
  53.2 6.5 %collective-permute-start.24 = (bf16[2,128,256]{2,1,0:T(8,128)(2,1)S(1)}, bf16[2,128,256]{2,1,0:T(8,128)(2,1)S(1)}, u32[]{:S(2)}, u32[]{:S(2)}) collective-permute-start(bf16[2,128,256]{2,1,0:T(8,128)(2,1)S(1)} %get-tuple-element.73), channel_id=1, source_target_pairs={{0,6},{1,7},{2,4},{3,5},{4,2},{5,3},{6,0},{7,1},{8,14},{9,15},{10,... | collective-permute-start | bytes 393224 | tf_op jit(solution)/shard_map/ppermute | solution.py:358
  55.1 6.8 %collective-permute-start.25 = (bf16[2,128,256]{2,1,0:T(8,128)(2,1)S(1)}, bf16[2,128,256]{2,1,0:T(8,128)(2,1)S(1)}, u32[]{:S(2)}, u32[]{:S(2)}) collective-permute-start(bf16[2,128,256]{2,1,0:T(8,128)(2,1)S(1)} %get-tuple-element.74), channel_id=1, source_target_pairs={{0,2},{1,3},{2,0},{3,1},{4,6},{5,7},{6,4},{7,5},{8,10},{9,11},{10,... | collective-permute-start | bytes 393224 | tf_op jit(solution)/shard_map/ppermute | solution.py:358
  57.6 5.0 %collective-permute-start.26 = (bf16[2,128,256]{2,1,0:T(8,128)(2,1)S(1)}, bf16[2,128,256]{2,1,0:T(8,128)(2,1)S(1)}, u32[]{:S(2)}, u32[]{:S(2)}) collective-permute-start(bf16[2,128,256]{2,1,0:T(8,128)(2,1)S(1)} %get-tuple-element.75), channel_id=1, source_target_pairs={{0,5},{1,4},{2,7},{3,6},{4,1},{5,0},{6,3},{7,2},{8,13},{9,12},{10,... | collective-permute-start | bytes 393224 | tf_op jit(solution)/shard_map/ppermute | solution.py:358
  57.6 5.0 %collective-permute-start.27 = (bf16[2,128,256]{2,1,0:T(8,128)(2,1)S(1)}, bf16[2,128,256]{2,1,0:T(8,128)(2,1)S(1)}, u32[]{:S(2)}, u32[]{:S(2)}) collective-permute-start(bf16[2,128,256]{2,1,0:T(8,128)(2,1)S(1)} %get-tuple-element.76), channel_id=1, source_target_pairs={{0,1},{1,0},{2,3},{3,2},{4,5},{5,4},{6,7},{7,6},{8,9},{9,8},{10,11... | collective-permute-start | bytes 393224 | tf_op jit(solution)/shard_map/ppermute | solution.py:358

commit v9 on v8

--- a/solution.py
+++ b/solution.py
@@ -18,7 +18,7 @@
 SCALE = HEAD_DIM ** (-0.5)
 SCALE_LOG2 = SCALE * math.log2(math.e)
 MASKED = -1e30
-VMEM_LIMIT = 48 * 1024 * 1024
+VMEM_LIMIT = 28 * 1024 * 1024
 NT = ((1,), (1,))
 NN = ((1,), (0,))
 CRIT_ORDER = (0, 6, 7, 2, 4, 1, 3, 5)

time: 64.7 us -> 61.8 us (0.955)
  Pallas kernels: 12.1 us -> 10.3 us
  local copies, waits for them, and re-layouts: 1.35 us -> 0 us
  starting transfers between devices: 36.5 us -> 37.7 us
    pallas_call x8, Pallas kernels: 12.1 us -> 10.3 us  [call(): pl.pallas_call(kernel, out_shape=outs, in_specs=[held if isinstance(x, tu...]
    unnamed x4 -> x0, local copies, waits for them, and re-layouts: 1.35 us -> none
    ppermute x24, waiting for transfers between devices: 13.3 us -> 12 us  [exchanged(): lax.ppermute(pieces[m], GROUP, [(i, i ^ step * m) for i in range(step * n)])]
    ppermute x24, starting transfers between devices: 26.5 us -> 27.4 us  [exchanged(): lax.ppermute(pieces[m], GROUP, [(i, i ^ step * m) for i in range(step * n)])]
    ppermute x1, waiting for transfers between devices: 0.01 us -> 0.76 us  [per_device(): kv_halo = lax.ppermute(kv_send, 'chunk', forward)]
  transfers between devices with their start and end apart: 28 -> 28, of which waited for: 9 -> 11; matrix products, arithmetic and copies ran while one was open for 0% -> 0% of each run, Pallas kernels for 15% -> 13%
where the time goes in v9:
time: 61.8 us; the launch traced here: 61.6 us
  starting transfers between devices  37.7 us (61%)
  waiting for transfers between devices  12.7 us (21%)
  Pallas kernels  10.3 us (17%)
  between operations  0.75 us (1%)
    ppermute x24, starting transfers between devices, exchanged(): lax.ppermute(pieces[m], GROUP, [(i, i ^ step * m) for i in range(step * n)])  27.4 us
    ppermute x24, waiting for transfers between devices, exchanged(): lax.ppermute(pieces[m], GROUP, [(i, i ^ step * m) for i in range(step * n)])  12 us
    pallas_call x8, Pallas kernels, call(): pl.pallas_call(kernel, out_shape=outs, in_specs=[held if isinstance(x, tu...  10.3 us
    ppermute x1, starting transfers between devices, per_device(): kv_halo = lax.ppermute(kv_send, 'chunk', forward)  3.2 us
    ppermute x1, starting transfers between devices, per_device(): other = lax.ppermute(other, GROUP, [(i, i ^ 1) for i in range(n)])  2.93 us
    ppermute x1, starting transfers between devices, per_device(): qg_halo = lax.ppermute(qg_send, 'chunk', backward)  2.1 us
    ppermute x1, starting transfers between devices, per_device(): stat_halo = lax.ppermute(stat, 'chunk', backward)  2.08 us
  transfers between devices with their start and end apart: 28, of which 11 were waited for; matrix products, arithmetic and copies ran while one was open for 0% of the time, Pallas kernels for 13%

profile of v9, /device:TPU:17, one launch (start us, length us, event | category | flops | bytes accessed | tf_op | source)
XLA Modules:
  0.0 61.6 jit_solution(5713961703713817131)
XLA Ops:
  0.6 1.3 %shard_map.67 = (bf16[2,128,256]{2,1,0:T(8,128)(2,1)S(1)}, bf16[2,128,256]{2,1,0:T(8,128)(2,1)S(1)}, bf16[2,128,256]{2,1,0:T(8,128)(2,1)S(1)}, bf16[2,128,256]{2...) custom-call(bf16[128,2048]{1,0:T(8,128)(2,1)} %refs_0_.3, ...), custom_call_target="tpu_custom_call" | custom-call | tf_op jit(solution)/shard_map/pallas_call | solution.py:327
  1.9 2.2 %collective-permute-start = (bf16[2,128,256]{2,1,0:T(8,128)(2,1)S(1)}, bf16[2,128,256]{2,1,0:T(8,128)(2,1)S(1)}, u32[]{:S(2)}, u32[]{:S(2)}) collective-permute-start(bf16[2,128,256]{2,1,0:T(8,128)(2,1)S(1)} %get-tuple-element.41), channel_id=1, source_target_pairs={{0,6},{1,7},{2,4},{3,5},{4,2},{5,3},{6,0},{7,1},{8,14},{9,15},{10,... | collective-permute-start | bytes 393224 | tf_op jit(solution)/shard_map/ppermute | solution.py:358
  4.2 1.0 %collective-permute-start.1 = (bf16[2,128,256]{2,1,0:T(8,128)(2,1)S(1)}, bf16[2,128,256]{2,1,0:T(8,128)(2,1)S(1)}, u32[]{:S(2)}, u32[]{:S(2)}) collective-permute-start(bf16[2,128,256]{2,1,0:T(8,128)(2,1)S(1)} %get-tuple-element.42), channel_id=1, source_target_pairs={{0,7},{1,6},{2,5},{3,4},{4,3},{5,2},{6,1},{7,0},{8,15},{9,14},{10,... | collective-permute-start | bytes 393224 | tf_op jit(solution)/shard_map/ppermute | solution.py:358
  5.2 1.2 %collective-permute-start.2 = (bf16[2,128,256]{2,1,0:T(8,128)(2,1)S(1)}, bf16[2,128,256]{2,1,0:T(8,128)(2,1)S(1)}, u32[]{:S(2)}, u32[]{:S(2)}) collective-permute-start(bf16[2,128,256]{2,1,0:T(8,128)(2,1)S(1)} %get-tuple-element.43), channel_id=1, source_target_pairs={{0,2},{1,3},{2,0},{3,1},{4,6},{5,7},{6,4},{7,5},{8,10},{9,11},{10,... | collective-permute-start | bytes 393224 | tf_op jit(solution)/shard_map/ppermute | solution.py:358
  6.4 1.2 %collective-permute-start.3 = (bf16[2,128,256]{2,1,0:T(8,128)(2,1)S(1)}, bf16[2,128,256]{2,1,0:T(8,128)(2,1)S(1)}, u32[]{:S(2)}, u32[]{:S(2)}) collective-permute-start(bf16[2,128,256]{2,1,0:T(8,128)(2,1)S(1)} %get-tuple-element.44), channel_id=1, source_target_pairs={{0,4},{1,5},{2,6},{3,7},{4,0},{5,1},{6,2},{7,3},{8,12},{9,13},{10,... | collective-permute-start | bytes 393224 | tf_op jit(solution)/shard_map/ppermute | solution.py:358
  7.7 0.1 collective-permute-start.4
  7.8 0.0 collective-permute-done.refs_1_
  7.8 3.0 %collective-permute-start.5 = (bf16[2,128,256]{2,1,0:T(8,128)(2,1)S(1)}, bf16[2,128,256]{2,1,0:T(8,128)(2,1)S(1)}, u32[]{:S(2)}, u32[]{:S(2)}) collective-permute-start(bf16[2,128,256]{2,1,0:T(8,128)(2,1)S(1)} %get-tuple-element.46), channel_id=1, source_target_pairs={{0,3},{1,2},{2,1},{3,0},{4,7},{5,6},{6,5},{7,4},{8,11},{9,10},{10,... | collective-permute-start | bytes 393224 | tf_op jit(solution)/shard_map/ppermute | solution.py:358
  10.8 0.2 collective-permute-done.1.refs_2_
  11.0 1.0 %collective-permute-start.6 = (bf16[2,128,256]{2,1,0:T(8,128)(2,1)S(1)}, bf16[2,128,256]{2,1,0:T(8,128)(2,1)S(1)}, u32[]{:S(2)}, u32[]{:S(2)}) collective-permute-start(bf16[2,128,256]{2,1,0:T(8,128)(2,1)S(1)} %get-tuple-element.47), channel_id=1, source_target_pairs={{0,5},{1,4},{2,7},{3,6},{4,1},{5,0},{6,3},{7,2},{8,13},{9,12},{10,... | collective-permute-start | bytes 393224 | tf_op jit(solution)/shard_map/ppermute | solution.py:358
  12.0 1.3 %shard_map.69 = (bf16[2,128,256]{2,1,0:T(8,128)(2,1)S(1)}, bf16[2,128,256]{2,1,0:T(8,128)(2,1)S(1)}, bf16[2,128,256]{2,1,0:T(8,128)(2,1)S(1)}, bf16[2,128,256]{2...) custom-call(bf16[128,2048]{1,0:T(8,128)(2,1)} %refs_0_.3, ...), custom_call_target="tpu_custom_call" | custom-call | tf_op jit(solution)/shard_map/pallas_call | solution.py:327
  13.3 0.0 collective-permute-done.2.refs_3_
  13.3 2.3 %collective-permute-start.10 = (bf16[2,128,256]{2,1,0:T(8,128)(2,1)S(1)}, bf16[2,128,256]{2,1,0:T(8,128)(2,1)S(1)}, u32[]{:S(2)}, u32[]{:S(2)}) collective-permute-start(bf16[2,128,256]{2,1,0:T(8,128)(2,1)S(1)} %get-tuple-element.53), channel_id=1, source_target_pairs={{0,6},{1,7},{2,4},{3,5},{4,2},{5,3},{6,0},{7,1},{8,14},{9,15},{10,... | collective-permute-start | bytes 393224 | tf_op jit(solution)/shard_map/ppermute | solution.py:358
  15.7 0.0 collective-permute-done.3.refs_4_
  15.7 2.2 %collective-permute-start.11 = (bf16[2,128,256]{2,1,0:T(8,128)(2,1)S(1)}, bf16[2,128,256]{2,1,0:T(8,128)(2,1)S(1)}, u32[]{:S(2)}, u32[]{:S(2)}) collective-permute-start(bf16[2,128,256]{2,1,0:T(8,128)(2,1)S(1)} %get-tuple-element.54), channel_id=1, source_target_pairs={{0,7},{1,6},{2,5},{3,4},{4,3},{5,2},{6,1},{7,0},{8,15},{9,14},{10,... | collective-permute-start | bytes 393224 | tf_op jit(solution)/shard_map/ppermute | solution.py:358
  17.9 0.0 collective-permute-done.4.refs_5_
  17.9 1.6 %collective-permute-start.12 = (bf16[2,128,256]{2,1,0:T(8,128)(2,1)S(1)}, bf16[2,128,256]{2,1,0:T(8,128)(2,1)S(1)}, u32[]{:S(2)}, u32[]{:S(2)}) collective-permute-start(bf16[2,128,256]{2,1,0:T(8,128)(2,1)S(1)} %get-tuple-element.55), channel_id=1, source_target_pairs={{0,2},{1,3},{2,0},{3,1},{4,6},{5,7},{6,4},{7,5},{8,10},{9,11},{10,... | collective-permute-start | bytes 393224 | tf_op jit(solution)/shard_map/ppermute | solution.py:358
  19.4 0.0 collective-permute-done.5.refs_6_
  19.4 0.0 collective-permute-start.13
  19.4 0.0 collective-permute-done.6.refs_7_
  19.4 0.1 shard_map.68
  19.5 3.2 %collective-permute-start.14 = (bf16[2,512,256]{2,1,0:T(8,128)(2,1)S(1)}, bf16[2,512,256]{2,1,0:T(8,128)(2,1)S(1)}, u32[]{:S(2)}, u32[]{:S(2)}) collective-permute-start(bf16[2,512,256]{2,1,0:T(8,128)(2,1)S(1)} %get-tuple-element.57.refs_8_.refs_3_.refs_1_), channel_id=1, source_target_pairs={{0,8},{8,16},{16,24},{1,9},{9,17},{17,25},{2,10},{10,18},{18,26},{... | collective-permute-start | bytes 1572872 | tf_op jit(solution)/shard_map/ppermute | solution.py:392
  22.8 0.0 collective-permute-done.10.refs_4_
  22.8 2.1 %collective-permute-start.19 = (bf16[2,512,256]{2,1,0:T(8,128)(2,1)S(1)}, bf16[2,512,256]{2,1,0:T(8,128)(2,1)S(1)}, u32[]{:S(2)}, u32[]{:S(2)}) collective-permute-start(bf16[2,512,256]{2,1,0:T(8,128)(2,1)S(1)} %get-tuple-element.48.refs_9_.refs_0_), channel_id=1, source_target_pairs={{8,0},{16,8},{24,16},{9,1},{17,9},{25,17},{10,2},{18,10},{26,18},{... | collective-permute-start | bytes 1572872 | tf_op jit(solution)/shard_map/ppermute | solution.py:393
  24.9 0.0 collective-permute-done.11.refs_5_
  24.9 1.5 %collective-permute-start.7 = (bf16[2,128,256]{2,1,0:T(8,128)(2,1)S(1)}, bf16[2,128,256]{2,1,0:T(8,128)(2,1)S(1)}, u32[]{:S(2)}, u32[]{:S(2)}) collective-permute-start(bf16[2,128,256]{2,1,0:T(8,128)(2,1)S(1)} %get-tuple-element.50), channel_id=1, source_target_pairs={{0,3},{1,2},{2,1},{3,0},{4,7},{5,6},{6,5},{7,4},{8,11},{9,10},{10,... | collective-permute-start | bytes 393224 | tf_op jit(solution)/shard_map/ppermute | solution.py:358
  26.4 0.0 collective-permute-done.12.refs_6_
  26.4 0.6 collective-permute-start.8
  27.0 0.0 collective-permute-done.13.refs_7_
  27.0 0.0 collective-permute-start.9
  27.0 3.7 %collective-permute-done.7.refs_1_ = bf16[2,128,256]{2,1,0:T(8,128)(2,1)S(1)} collective-permute-done((bf16[2,128,256]{2,1,0:T(8,128)(2,1)S(1)}, bf16[2,128,256]{2,1,0:T(8,128)(2,1)S(1)}, u32[]{:S(2)}, u32[]{:S(2)}) %collective-permute-start.7) | collective-permute-done | bytes 131104 | tf_op jit(solution)/shard_map/ppermute | solution.py:358
  30.7 0.9 %collective-permute-done.8.refs_2_ = bf16[2,128,256]{2,1,0:T(8,128)(2,1)S(1)} collective-permute-done((bf16[2,128,256]{2,1,0:T(8,128)(2,1)S(1)}, bf16[2,128,256]{2,1,0:T(8,128)(2,1)S(1)}, u32[]{:S(2)}, u32[]{:S(2)}) %collective-permute-start.8) | collective-permute-done | bytes 131104 | tf_op jit(solution)/shard_map/ppermute | solution.py:358
  31.6 0.0 collective-permute-done.9.refs_3_
  31.6 2.7 %shard_map.70 = (bf16[2,512,256]{2,1,0:T(8,128)(2,1)S(1)}, bf16[2,512,256]{2,1,0:T(8,128)(2,1)S(1)}, bf16[512,256]{1,0:T(8,128)(2,1)S(1)}, f32[2,1024,256]{2,1,0:T(8,128)S(1)}, bf16[2,128,512]{2,1,0:T(8,128)(2,1)S(1)}) custom-call(bf16[2,128,256]{2,1,0:T(8,128)(2,1)S(1)} %get-tuple-element.49.refs_0_, ...), custom_call_target="tpu_custom_call" | custom-call | flops 4000000000 | tf_op jit(solution)/shard_map/pallas_call | solution.py:327
  34.3 0.8 %collective-permute-done.14.refs_4_ = bf16[2,512,256]{2,1,0:T(8,128)(2,1)S(1)} collective-permute-done((bf16[2,512,256]{2,1,0:T(8,128)(2,1)S(1)}, bf16[2,512,256]{2,1,0:T(8,128)(2,1)S(1)}, u32[]{:S(2)}, u32[]{:S(2)}) %collective-permute-start.14) | collective-permute-done | bytes 524320 | tf_op jit(solution)/shard_map/ppermute | solution.py:392
  35.1 2.5 %shard_map.71 = (bf16[2,128,256]{2,1,0:T(8,128)(2,1)S(1)}, bf16[2,128,256]{2,1,0:T(8,128)(2,1)S(1)}, bf16[2,128,256]{2,1,0:T(8,128)(2,1)S(1)}, bf16[2,128,256]{2...) custom-call(bf16[2,512,256]{2,1,0:T(8,128)(2,1)S(1)} %get-tuple-element.48.refs_9_.refs_0_, ...), custom_call_target="tpu_custom_call" | custom-call | tf_op jit(solution)/shard_map/pallas_call | solution.py:327
  37.6 2.1 %collective-permute-start.20 = (f32[8,512]{1,0:T(8,128)S(1)}, f32[8,512]{1,0:T(8,128)S(1)}, u32[]{:S(2)}, u32[]{:S(2)}) collective-permute-start(f32[8,512]{1,0:T(8,128)S(1)} %get-tuple-element.68), channel_id=1, source_target_pairs={{8,0},{16,8},{24,16},{9,1},{17,9},{25,17},{10,2},{18,10},{26,18},{... | collective-permute-start | bytes 49160 | tf_op jit(solution)/shard_map/ppermute | solution.py:411
  39.7 0.5 collective-permute-start.15
  40.2 1.1 %collective-permute-start.16 = (bf16[2,128,256]{2,1,0:T(8,128)(2,1)S(1)}, bf16[2,128,256]{2,1,0:T(8,128)(2,1)S(1)}, u32[]{:S(2)}, u32[]{:S(2)}) collective-permute-start(bf16[2,128,256]{2,1,0:T(8,128)(2,1)S(1)} %get-tuple-element.65), channel_id=1, source_target_pairs={{0,2},{1,3},{2,0},{3,1},{4,6},{5,7},{6,4},{7,5},{8,10},{9,11},{10,... | collective-permute-start | bytes 393224 | tf_op jit(solution)/shard_map/ppermute | solution.py:358
  41.3 1.1 %collective-permute-start.17 = (bf16[2,128,256]{2,1,0:T(8,128)(2,1)S(1)}, bf16[2,128,256]{2,1,0:T(8,128)(2,1)S(1)}, u32[]{:S(2)}, u32[]{:S(2)}) collective-permute-start(bf16[2,128,256]{2,1,0:T(8,128)(2,1)S(1)} %get-tuple-element.66), channel_id=1, source_target_pairs={{0,6},{1,7},{2,4},{3,5},{4,2},{5,3},{6,0},{7,1},{8,14},{9,15},{10,... | collective-permute-start | bytes 393224 | tf_op jit(solution)/shard_map/ppermute | solution.py:358
  42.4 0.0 collective-permute-done.19.refs_2_
  42.4 0.0 collective-permute-done.20.refs_5_
  42.4 1.1 %shard_map.73 = (bf16[2,128,256]{2,1,0:T(8,128)(2,1)S(1)}, bf16[2,128,256]{2,1,0:T(8,128)(2,1)S(1)}, bf16[2,128,256]{2,1,0:T(8,128)(2,1)S(1)}, bf16[2,128,256]{2...) custom-call(bf16[2,512,256]{2,1,0:T(8,128)(2,1)S(1)} %get-tuple-elem, ...), custom_call_target="tpu_custom_call" | custom-call | flops 4000000000 | tf_op jit(solution)/shard_map/pallas_call | solution.py:327
  43.5 2.4 %collective-permute-start.21 = (bf16[2,128,256]{2,1,0:T(8,128)(2,1)S(1)}, bf16[2,128,256]{2,1,0:T(8,128)(2,1)S(1)}, u32[]{:S(2)}, u32[]{:S(2)}) collective-permute-start(bf16[2,128,256]{2,1,0:T(8,128)(2,1)S(1)} %get-tuple-element.70), channel_id=1, source_target_pairs={{0,7},{1,6},{2,5},{3,4},{4,3},{5,2},{6,1},{7,0},{8,15},{9,14},{10,... | collective-permute-start | bytes 393224 | tf_op jit(solution)/shard_map/ppermute | solution.py:358
  45.9 0.0 collective-permute-start.22
  45.9 0.0 collective-permute-done.15.refs_1_
  45.9 0.8 %collective-permute-start.23 = (bf16[2,128,256]{2,1,0:T(8,128)(2,1)S(1)}, bf16[2,128,256]{2,1,0:T(8,128)(2,1)S(1)}, u32[]{:S(2)}, u32[]{:S(2)}) collective-permute-start(bf16[2,128,256]{2,1,0:T(8,128)(2,1)S(1)} %get-tuple-element.72), channel_id=1, source_target_pairs={{0,4},{1,5},{2,6},{3,7},{4,0},{5,1},{6,2},{7,3},{8,12},{9,13},{10,... | collective-permute-start | bytes 393224 | tf_op jit(solution)/shard_map/ppermute | solution.py:358
  46.7 0.0 collective-permute-done.16.refs_2_
  46.7 0.5 collective-permute-done.17.refs_3_
  47.2 2.9 %collective-permute-start.18 = (bf16[4,128,256]{2,1,0:T(8,128)(2,1)S(1)}, bf16[4,128,256]{2,1,0:T(8,128)(2,1)S(1)}, u32[]{:S(2)}, u32[]{:S(2)}) collective-permute-start(bf16[4,128,256]{2,1,0:T(8,128)(2,1)S(1)} %shard_map.72), channel_id=1, source_target_pairs={{0,1},{1,0},{2,3},{3,2},{4,5},{5,4},{6,7},{7,6},{8,9},{9,8},{10,11... | collective-permute-start | bytes 786440 | tf_op jit(solution)/shard_map/ppermute | solution.py:416
  50.2 1.9 %collective-permute-start.24 = (bf16[2,128,256]{2,1,0:T(8,128)(2,1)S(1)}, bf16[2,128,256]{2,1,0:T(8,128)(2,1)S(1)}, u32[]{:S(2)}, u32[]{:S(2)}) collective-permute-start(bf16[2,128,256]{2,1,0:T(8,128)(2,1)S(1)} %get-tuple-element.73), channel_id=1, source_target_pairs={{0,6},{1,7},{2,4},{3,5},{4,2},{5,3},{6,0},{7,1},{8,14},{9,15},{10,... | collective-permute-start | bytes 393224 | tf_op jit(solution)/shard_map/ppermute | solution.py:358
  52.0 0.1 collective-permute-done.21.refs_6_
  52.2 0.4 collective-permute-start.25
  52.5 2.2 %collective-permute-done.22.refs_7_ = bf16[2,128,256]{2,1,0:T(8,128)(2,1)S(1)} collective-permute-done((bf16[2,128,256]{2,1,0:T(8,128)(2,1)S(1)}, bf16[2,128,256]{2,1,0:T(8,128)(2,1)S(1)}, u32[]{:S(2)}, u32[]{:S(2)}) %collective-permute-start.22) | collective-permute-done | bytes 131104 | tf_op jit(solution)/shard_map/ppermute | solution.py:358
  54.7 0.4 collective-permute-start.26
  55.1 0.1 collective-permute-done.23.refs_8_
  55.2 0.8 %collective-permute-start.27 = (bf16[2,128,256]{2,1,0:T(8,128)(2,1)S(1)}, bf16[2,128,256]{2,1,0:T(8,128)(2,1)S(1)}, u32[]{:S(2)}, u32[]{:S(2)}) collective-permute-start(bf16[2,128,256]{2,1,0:T(8,128)(2,1)S(1)} %get-tuple-element.76), channel_id=1, source_target_pairs={{0,1},{1,0},{2,3},{3,2},{4,5},{5,4},{6,7},{7,6},{8,9},{9,8},{10,11... | collective-permute-start | bytes 393224 | tf_op jit(solution)/shard_map/ppermute | solution.py:358
  55.9 1.4 %collective-permute-done.24.refs_9_ = bf16[2,128,256]{2,1,0:T(8,128)(2,1)S(1)} collective-permute-done((bf16[2,128,256]{2,1,0:T(8,128)(2,1)S(1)}, bf16[2,128,256]{2,1,0:T(8,128)(2,1)S(1)}, u32[]{:S(2)}, u32[]{:S(2)}) %collective-permute-start.24) | collective-permute-done | bytes 131104 | tf_op jit(solution)/shard_map/ppermute | solution.py:358
  57.3 2.0 %collective-permute-done.25.refs_10_ = bf16[2,128,256]{2,1,0:T(8,128)(2,1)S(1)} collective-permute-done((bf16[2,128,256]{2,1,0:T(8,128)(2,1)S(1)}, bf16[2,128,256]{2,1,0:T(8,128)(2,1)S(1)}, u32[]{:S(2)}, u32[]{:S(2)}) %collective-permute-start.25) | collective-permute-done | bytes 131104 | tf_op jit(solution)/shard_map/ppermute | solution.py:358
  59.3 0.9 %collective-permute-done.26.refs_11_ = bf16[2,128,256]{2,1,0:T(8,128)(2,1)S(1)} collective-permute-done((bf16[2,128,256]{2,1,0:T(8,128)(2,1)S(1)}, bf16[2,128,256]{2,1,0:T(8,128)(2,1)S(1)}, u32[]{:S(2)}, u32[]{:S(2)}) %collective-permute-start.26) | collective-permute-done | bytes 131104 | tf_op jit(solution)/shard_map/ppermute | solution.py:358
  60.2 0.0 collective-permute-done.27.refs_12_
  60.2 0.0 collective-permute-done.18.refs_4_
  60.2 1.3 %shard_map.74 = (bf16[128,2048]{1,0:T(8,128)(2,1)}, bf16[128,2048]{1,0:T(8,128)(2,1)}, bf16[128,2048]{1,0:T(8,128)(2,1)}) custom-call(bf16[2,128,256]{2,1,0:T(8,128)(2,1)S(1)} %get-tuple-element.63.refs_0_, bf16[2,128,256]{2,1,0:T(8,128)(2,1)S(1)} %collective-permute-done.15.refs_1_, bf16[2,128,256]{2,1,0:T(8,128)(2,1)S(1)} %collective-permute-done.16.refs_2_, ...), custom_call_target="tpu_custom_call" | custom-call | tf_op jit(solution)/shard_map/pallas_call | solution.py:327
  (1 shorter events, 0.0 us)
Async XLA Ops:
  1.9 5.8 %collective-permute-start = (bf16[2,128,256]{2,1,0:T(8,128)(2,1)S(1)}, bf16[2,128,256]{2,1,0:T(8,128)(2,1)S(1)}, u32[]{:S(2)}, u32[]{:S(2)}) collective-permute-start(bf16[2,128,256]{2,1,0:T(8,128)(2,1)S(1)} %get-tuple-element.41), channel_id=1, source_target_pairs={{0,6},{1,7},{2,4},{3,5},{4,2},{5,3},{6,0},{7,1},{8,14},{9,15},{10,... | collective-permute-start | bytes 393224 | tf_op jit(solution)/shard_map/ppermute | solution.py:358
  4.2 6.8 %collective-permute-start.1 = (bf16[2,128,256]{2,1,0:T(8,128)(2,1)S(1)}, bf16[2,128,256]{2,1,0:T(8,128)(2,1)S(1)}, u32[]{:S(2)}, u32[]{:S(2)}) collective-permute-start(bf16[2,128,256]{2,1,0:T(8,128)(2,1)S(1)} %get-tuple-element.42), channel_id=1, source_target_pairs={{0,7},{1,6},{2,5},{3,4},{4,3},{5,2},{6,1},{7,0},{8,15},{9,14},{10,... | collective-permute-start | bytes 393224 | tf_op jit(solution)/shard_map/ppermute | solution.py:358
  5.2 8.1 %collective-permute-start.2 = (bf16[2,128,256]{2,1,0:T(8,128)(2,1)S(1)}, bf16[2,128,256]{2,1,0:T(8,128)(2,1)S(1)}, u32[]{:S(2)}, u32[]{:S(2)}) collective-permute-start(bf16[2,128,256]{2,1,0:T(8,128)(2,1)S(1)} %get-tuple-element.43), channel_id=1, source_target_pairs={{0,2},{1,3},{2,0},{3,1},{4,6},{5,7},{6,4},{7,5},{8,10},{9,11},{10,... | collective-permute-start | bytes 393224 | tf_op jit(solution)/shard_map/ppermute | solution.py:358
  6.4 9.2 %collective-permute-start.3 = (bf16[2,128,256]{2,1,0:T(8,128)(2,1)S(1)}, bf16[2,128,256]{2,1,0:T(8,128)(2,1)S(1)}, u32[]{:S(2)}, u32[]{:S(2)}) collective-permute-start(bf16[2,128,256]{2,1,0:T(8,128)(2,1)S(1)} %get-tuple-element.44), channel_id=1, source_target_pairs={{0,4},{1,5},{2,6},{3,7},{4,0},{5,1},{6,2},{7,3},{8,12},{9,13},{10,... | collective-permute-start | bytes 393224 | tf_op jit(solution)/shard_map/ppermute | solution.py:358
  7.7 10.2 %collective-permute-start.4 = (bf16[2,128,256]{2,1,0:T(8,128)(2,1)S(1)}, bf16[2,128,256]{2,1,0:T(8,128)(2,1)S(1)}, u32[]{:S(2)}, u32[]{:S(2)}) collective-permute-start(bf16[2,128,256]{2,1,0:T(8,128)(2,1)S(1)} %get-tuple-element.45), channel_id=1, source_target_pairs={{0,1},{1,0},{2,3},{3,2},{4,5},{5,4},{6,7},{7,6},{8,9},{9,8},{10,11... | collective-permute-start | bytes 393224 | tf_op jit(solution)/shard_map/ppermute | solution.py:358
  7.8 11.7 %collective-permute-start.5 = (bf16[2,128,256]{2,1,0:T(8,128)(2,1)S(1)}, bf16[2,128,256]{2,1,0:T(8,128)(2,1)S(1)}, u32[]{:S(2)}, u32[]{:S(2)}) collective-permute-start(bf16[2,128,256]{2,1,0:T(8,128)(2,1)S(1)} %get-tuple-element.46), channel_id=1, source_target_pairs={{0,3},{1,2},{2,1},{3,0},{4,7},{5,6},{6,5},{7,4},{8,11},{9,10},{10,... | collective-permute-start | bytes 393224 | tf_op jit(solution)/shard_map/ppermute | solution.py:358
  11.0 8.4 %collective-permute-start.6 = (bf16[2,128,256]{2,1,0:T(8,128)(2,1)S(1)}, bf16[2,128,256]{2,1,0:T(8,128)(2,1)S(1)}, u32[]{:S(2)}, u32[]{:S(2)}) collective-permute-start(bf16[2,128,256]{2,1,0:T(8,128)(2,1)S(1)} %get-tuple-element.47), channel_id=1, source_target_pairs={{0,5},{1,4},{2,7},{3,6},{4,1},{5,0},{6,3},{7,2},{8,13},{9,12},{10,... | collective-permute-start | bytes 393224 | tf_op jit(solution)/shard_map/ppermute | solution.py:358
  13.3 9.4 %collective-permute-start.10 = (bf16[2,128,256]{2,1,0:T(8,128)(2,1)S(1)}, bf16[2,128,256]{2,1,0:T(8,128)(2,1)S(1)}, u32[]{:S(2)}, u32[]{:S(2)}) collective-permute-start(bf16[2,128,256]{2,1,0:T(8,128)(2,1)S(1)} %get-tuple-element.53), channel_id=1, source_target_pairs={{0,6},{1,7},{2,4},{3,5},{4,2},{5,3},{6,0},{7,1},{8,14},{9,15},{10,... | collective-permute-start | bytes 393224 | tf_op jit(solution)/shard_map/ppermute | solution.py:358
  15.7 9.2 %collective-permute-start.11 = (bf16[2,128,256]{2,1,0:T(8,128)(2,1)S(1)}, bf16[2,128,256]{2,1,0:T(8,128)(2,1)S(1)}, u32[]{:S(2)}, u32[]{:S(2)}) collective-permute-start(bf16[2,128,256]{2,1,0:T(8,128)(2,1)S(1)} %get-tuple-element.54), channel_id=1, source_target_pairs={{0,7},{1,6},{2,5},{3,4},{4,3},{5,2},{6,1},{7,0},{8,15},{9,14},{10,... | collective-permute-start | bytes 393224 | tf_op jit(solution)/shard_map/ppermute | solution.py:358
  17.9 8.6 %collective-permute-start.12 = (bf16[2,128,256]{2,1,0:T(8,128)(2,1)S(1)}, bf16[2,128,256]{2,1,0:T(8,128)(2,1)S(1)}, u32[]{:S(2)}, u32[]{:S(2)}) collective-permute-start(bf16[2,128,256]{2,1,0:T(8,128)(2,1)S(1)} %get-tuple-element.55), channel_id=1, source_target_pairs={{0,2},{1,3},{2,0},{3,1},{4,6},{5,7},{6,4},{7,5},{8,10},{9,11},{10,... | collective-permute-start | bytes 393224 | tf_op jit(solution)/shard_map/ppermute | solution.py:358
  19.4 7.6 %collective-permute-start.13 = (bf16[2,128,256]{2,1,0:T(8,128)(2,1)S(1)}, bf16[2,128,256]{2,1,0:T(8,128)(2,1)S(1)}, u32[]{:S(2)}, u32[]{:S(2)}) collective-permute-start(bf16[2,128,256]{2,1,0:T(8,128)(2,1)S(1)} %get-tuple-element.56), channel_id=1, source_target_pairs={{0,4},{1,5},{2,6},{3,7},{4,0},{5,1},{6,2},{7,3},{8,12},{9,13},{10,... | collective-permute-start | bytes 393224 | tf_op jit(solution)/shard_map/ppermute | solution.py:358
  19.5 15.6 %collective-permute-start.14 = (bf16[2,512,256]{2,1,0:T(8,128)(2,1)S(1)}, bf16[2,512,256]{2,1,0:T(8,128)(2,1)S(1)}, u32[]{:S(2)}, u32[]{:S(2)}) collective-permute-start(bf16[2,512,256]{2,1,0:T(8,128)(2,1)S(1)} %get-tuple-element.57.refs_8_.refs_3_.refs_1_), channel_id=1, source_target_pairs={{0,8},{8,16},{16,24},{1,9},{9,17},{17,25},{2,10},{10,18},{18,26},{... | collective-permute-start | bytes 1572872 | tf_op jit(solution)/shard_map/ppermute | solution.py:392
  22.8 19.7 %collective-permute-start.19 = (bf16[2,512,256]{2,1,0:T(8,128)(2,1)S(1)}, bf16[2,512,256]{2,1,0:T(8,128)(2,1)S(1)}, u32[]{:S(2)}, u32[]{:S(2)}) collective-permute-start(bf16[2,512,256]{2,1,0:T(8,128)(2,1)S(1)} %get-tuple-element.48.refs_9_.refs_0_), channel_id=1, source_target_pairs={{8,0},{16,8},{24,16},{9,1},{17,9},{25,17},{10,2},{18,10},{26,18},{... | collective-permute-start | bytes 1572872 | tf_op jit(solution)/shard_map/ppermute | solution.py:393
  24.9 5.8 %collective-permute-start.7 = (bf16[2,128,256]{2,1,0:T(8,128)(2,1)S(1)}, bf16[2,128,256]{2,1,0:T(8,128)(2,1)S(1)}, u32[]{:S(2)}, u32[]{:S(2)}) collective-permute-start(bf16[2,128,256]{2,1,0:T(8,128)(2,1)S(1)} %get-tuple-element.50), channel_id=1, source_target_pairs={{0,3},{1,2},{2,1},{3,0},{4,7},{5,6},{6,5},{7,4},{8,11},{9,10},{10,... | collective-permute-start | bytes 393224 | tf_op jit(solution)/shard_map/ppermute | solution.py:358
  26.4 5.2 %collective-permute-start.8 = (bf16[2,128,256]{2,1,0:T(8,128)(2,1)S(1)}, bf16[2,128,256]{2,1,0:T(8,128)(2,1)S(1)}, u32[]{:S(2)}, u32[]{:S(2)}) collective-permute-start(bf16[2,128,256]{2,1,0:T(8,128)(2,1)S(1)} %get-tuple-element.51), channel_id=1, source_target_pairs={{0,5},{1,4},{2,7},{3,6},{4,1},{5,0},{6,3},{7,2},{8,13},{9,12},{10,... | collective-permute-start | bytes 393224 | tf_op jit(solution)/shard_map/ppermute | solution.py:358
  27.0 4.6 %collective-permute-start.9 = (bf16[2,128,256]{2,1,0:T(8,128)(2,1)S(1)}, bf16[2,128,256]{2,1,0:T(8,128)(2,1)S(1)}, u32[]{:S(2)}, u32[]{:S(2)}) collective-permute-start(bf16[2,128,256]{2,1,0:T(8,128)(2,1)S(1)} %get-tuple-element.52), channel_id=1, source_target_pairs={{0,1},{1,0},{2,3},{3,2},{4,5},{5,4},{6,7},{7,6},{8,9},{9,8},{10,11... | collective-permute-start | bytes 393224 | tf_op jit(solution)/shard_map/ppermute | solution.py:358
  37.6 4.8 %collective-permute-start.20 = (f32[8,512]{1,0:T(8,128)S(1)}, f32[8,512]{1,0:T(8,128)S(1)}, u32[]{:S(2)}, u32[]{:S(2)}) collective-permute-start(f32[8,512]{1,0:T(8,128)S(1)} %get-tuple-element.68), channel_id=1, source_target_pairs={{8,0},{16,8},{24,16},{9,1},{17,9},{25,17},{10,2},{18,10},{26,18},{... | collective-permute-start | bytes 49160 | tf_op jit(solution)/shard_map/ppermute | solution.py:411
  39.7 6.2 %collective-permute-start.15 = (bf16[2,128,256]{2,1,0:T(8,128)(2,1)S(1)}, bf16[2,128,256]{2,1,0:T(8,128)(2,1)S(1)}, u32[]{:S(2)}, u32[]{:S(2)}) collective-permute-start(bf16[2,128,256]{2,1,0:T(8,128)(2,1)S(1)} %get-tuple-element.64), channel_id=1, source_target_pairs={{0,4},{1,5},{2,6},{3,7},{4,0},{5,1},{6,2},{7,3},{8,12},{9,13},{10,... | collective-permute-start | bytes 393224 | tf_op jit(solution)/shard_map/ppermute | solution.py:358
  40.2 6.5 %collective-permute-start.16 = (bf16[2,128,256]{2,1,0:T(8,128)(2,1)S(1)}, bf16[2,128,256]{2,1,0:T(8,128)(2,1)S(1)}, u32[]{:S(2)}, u32[]{:S(2)}) collective-permute-start(bf16[2,128,256]{2,1,0:T(8,128)(2,1)S(1)} %get-tuple-element.65), channel_id=1, source_target_pairs={{0,2},{1,3},{2,0},{3,1},{4,6},{5,7},{6,4},{7,5},{8,10},{9,11},{10,... | collective-permute-start | bytes 393224 | tf_op jit(solution)/shard_map/ppermute | solution.py:358
  41.3 6.0 %collective-permute-start.17 = (bf16[2,128,256]{2,1,0:T(8,128)(2,1)S(1)}, bf16[2,128,256]{2,1,0:T(8,128)(2,1)S(1)}, u32[]{:S(2)}, u32[]{:S(2)}) collective-permute-start(bf16[2,128,256]{2,1,0:T(8,128)(2,1)S(1)} %get-tuple-element.66), channel_id=1, source_target_pairs={{0,6},{1,7},{2,4},{3,5},{4,2},{5,3},{6,0},{7,1},{8,14},{9,15},{10,... | collective-permute-start | bytes 393224 | tf_op jit(solution)/shard_map/ppermute | solution.py:358
  43.5 8.7 %collective-permute-start.21 = (bf16[2,128,256]{2,1,0:T(8,128)(2,1)S(1)}, bf16[2,128,256]{2,1,0:T(8,128)(2,1)S(1)}, u32[]{:S(2)}, u32[]{:S(2)}) collective-permute-start(bf16[2,128,256]{2,1,0:T(8,128)(2,1)S(1)} %get-tuple-element.70), channel_id=1, source_target_pairs={{0,7},{1,6},{2,5},{3,4},{4,3},{5,2},{6,1},{7,0},{8,15},{9,14},{10,... | collective-permute-start | bytes 393224 | tf_op jit(solution)/shard_map/ppermute | solution.py:358
  45.9 8.8 %collective-permute-start.22 = (bf16[2,128,256]{2,1,0:T(8,128)(2,1)S(1)}, bf16[2,128,256]{2,1,0:T(8,128)(2,1)S(1)}, u32[]{:S(2)}, u32[]{:S(2)}) collective-permute-start(bf16[2,128,256]{2,1,0:T(8,128)(2,1)S(1)} %get-tuple-element.71), channel_id=1, source_target_pairs={{0,3},{1,2},{2,1},{3,0},{4,7},{5,6},{6,5},{7,4},{8,11},{9,10},{10,... | collective-permute-start | bytes 393224 | tf_op jit(solution)/shard_map/ppermute | solution.py:358
  45.9 9.3 %collective-permute-start.23 = (bf16[2,128,256]{2,1,0:T(8,128)(2,1)S(1)}, bf16[2,128,256]{2,1,0:T(8,128)(2,1)S(1)}, u32[]{:S(2)}, u32[]{:S(2)}) collective-permute-start(bf16[2,128,256]{2,1,0:T(8,128)(2,1)S(1)} %get-tuple-element.72), channel_id=1, source_target_pairs={{0,4},{1,5},{2,6},{3,7},{4,0},{5,1},{6,2},{7,3},{8,12},{9,13},{10,... | collective-permute-start | bytes 393224 | tf_op jit(solution)/shard_map/ppermute | solution.py:358
  47.2 13.0 %collective-permute-start.18 = (bf16[4,128,256]{2,1,0:T(8,128)(2,1)S(1)}, bf16[4,128,256]{2,1,0:T(8,128)(2,1)S(1)}, u32[]{:S(2)}, u32[]{:S(2)}) collective-permute-start(bf16[4,128,256]{2,1,0:T(8,128)(2,1)S(1)} %shard_map.72), channel_id=1, source_target_pairs={{0,1},{1,0},{2,3},{3,2},{4,5},{5,4},{6,7},{7,6},{8,9},{9,8},{10,11... | collective-permute-start | bytes 786440 | tf_op jit(solution)/shard_map/ppermute | solution.py:416
  50.2 7.1 %collective-permute-start.24 = (bf16[2,128,256]{2,1,0:T(8,128)(2,1)S(1)}, bf16[2,128,256]{2,1,0:T(8,128)(2,1)S(1)}, u32[]{:S(2)}, u32[]{:S(2)}) collective-permute-start(bf16[2,128,256]{2,1,0:T(8,128)(2,1)S(1)} %get-tuple-element.73), channel_id=1, source_target_pairs={{0,6},{1,7},{2,4},{3,5},{4,2},{5,3},{6,0},{7,1},{8,14},{9,15},{10,... | collective-permute-start | bytes 393224 | tf_op jit(solution)/shard_map/ppermute | solution.py:358
  52.2 7.1 %collective-permute-start.25 = (bf16[2,128,256]{2,1,0:T(8,128)(2,1)S(1)}, bf16[2,128,256]{2,1,0:T(8,128)(2,1)S(1)}, u32[]{:S(2)}, u32[]{:S(2)}) collective-permute-start(bf16[2,128,256]{2,1,0:T(8,128)(2,1)S(1)} %get-tuple-element.74), channel_id=1, source_target_pairs={{0,2},{1,3},{2,0},{3,1},{4,6},{5,7},{6,4},{7,5},{8,10},{9,11},{10,... | collective-permute-start | bytes 393224 | tf_op jit(solution)/shard_map/ppermute | solution.py:358
  54.7 5.5 %collective-permute-start.26 = (bf16[2,128,256]{2,1,0:T(8,128)(2,1)S(1)}, bf16[2,128,256]{2,1,0:T(8,128)(2,1)S(1)}, u32[]{:S(2)}, u32[]{:S(2)}) collective-permute-start(bf16[2,128,256]{2,1,0:T(8,128)(2,1)S(1)} %get-tuple-element.75), channel_id=1, source_target_pairs={{0,5},{1,4},{2,7},{3,6},{4,1},{5,0},{6,3},{7,2},{8,13},{9,12},{10,... | collective-permute-start | bytes 393224 | tf_op jit(solution)/shard_map/ppermute | solution.py:358
  55.2 5.1 %collective-permute-start.27 = (bf16[2,128,256]{2,1,0:T(8,128)(2,1)S(1)}, bf16[2,128,256]{2,1,0:T(8,128)(2,1)S(1)}, u32[]{:S(2)}, u32[]{:S(2)}) collective-permute-start(bf16[2,128,256]{2,1,0:T(8,128)(2,1)S(1)} %get-tuple-element.76), channel_id=1, source_target_pairs={{0,1},{1,0},{2,3},{3,2},{4,5},{5,4},{6,7},{7,6},{8,9},{9,8},{10,11... | collective-permute-start | bytes 393224 | tf_op jit(solution)/shard_map/ppermute | solution.py:358
